TPU v7x, 32 devices: a whole 2x2x4 slice. The times are simulated.
32 devices in a mesh: grp: 4 (over y, x), blk: 8 (over z, core).
Axes of the slice: x: 2, y: 2, z: 4, core: 2. Of those that a mesh axis runs over, the one named last changes fastest.
Arguments:
- walkers: bfloat16 [128, 32, 768], P('blk', 'grp'), may hold values from -6 to 6
- one_body: bfloat16 [768, 768], replicated, may hold values from -0.21875 to 0.21875
- fields: float32 [32, 96], P('grp', 'blk'), may hold values from -6 to 6
- field_diag: float32 [96, 768], P('blk'), may hold values from -0.875 to 0.875
- chol: bfloat16 [96, 128, 768], P('blk'), may hold values from -0.25 to 0.25
- weights: float32 [32], P('grp'), may hold values from 0.25 to 12, as said below
- target: int32 [32], P('grp'), may hold values from 0 to 16, as said below
Outputs:
- fock: bfloat16 [128, 32, 768], P('blk', 'grp')
Inputs may be any that keep to these rules, and one draw needn't show every extreme that they name: `target`: each list of 8 slots (the slots of one index of grp) holds its live walkers in its first slots. The live walkers of all lists, in order of list and slot, carry the numbers 0 to 15, each once; a dead slot holds 16. A list holds 0 to 8 live walkers, and some list holds exactly 8. `weights`: Positive.
All inputs are finite; a program needn't handle non-finite values.
Results may differ from a plain program's by a relative error of at most 0.018.
Values may be sent and summed in bfloat16 or wider, within the bound.
No kernel may reach another device: no remote copies, remote signals or barrier semaphores. Data moves between devices by JAX's collectives and lax.ppermute only.
A program may use at most 64 MiB of HBM per device.

v0:
```python
import jax
import jax.numpy as jnp
from jax import lax
from jax.sharding import PartitionSpec as P


def measure(blocks, chol):
    vec_count = chol.shape[0]
    occupied = chol.shape[1]
    vectors = chol.reshape(-1, chol.shape[2])
    portion = lax.all_gather(blocks, "blk", axis=0, tiled=True)
    flat = portion.reshape(-1, portion.shape[2])
    result = lax.dot_general(
        vectors, flat, (((1,), (1,)), ((), ())), preferred_element_type=jnp.float32
    )
    result = result.reshape(vec_count, occupied, portion.shape[0], portion.shape[1])
    coupling = jnp.transpose(result, (1, 3, 0, 2)).astype(jnp.bfloat16)
    amount = blocks.shape[0] * lax.axis_size("blk")
    result = jnp.dot(
        coupling.reshape(amount * coupling.shape[1], -1),
        vectors,
        preferred_element_type=jnp.float32,
    )
    return lax.psum_scatter(
        result.reshape(amount, coupling.shape[1], -1).astype(jnp.bfloat16),
        "blk",
        scatter_dimension=0,
        tiled=True,
    ).astype(jnp.float32)


def body(walkers, one_body, fields, field_diag, chol, weights, target):
    slot_count = walkers.shape[1]
    orbitals = walkers.shape[2]
    field_part = jnp.dot(fields, field_diag, precision=lax.Precision.HIGHEST)
    exponent = lax.psum(field_part, "blk")
    scaled = (walkers.astype(jnp.float32) * jnp.exp(exponent)[None]).astype(jnp.bfloat16)
    propagated = jnp.dot(scaled.reshape(-1, orbitals), one_body, preferred_element_type=jnp.float32)
    propagated = propagated.astype(jnp.bfloat16).reshape(walkers.shape)
    live_total = slot_count // 2 * lax.axis_size("grp")
    active = target < live_total
    weight_sum = lax.psum(jnp.sum(jnp.where(active, weights, jnp.float32(0.0))), "grp")
    factor = jnp.where(active, weights * live_total / weight_sum, jnp.float32(0.0))
    fock_raw = lax.optimization_barrier(measure(propagated, chol).astype(jnp.bfloat16)).astype(
        jnp.float32
    )
    return (fock_raw * factor[None, :, None]).astype(jnp.bfloat16)


def solution(mesh):
    in_specs = (
        P("blk", "grp", None),
        P(),
        P("grp", "blk"),
        P("blk", None),
        P("blk", None, None),
        P("grp"),
        P("grp"),
    )
    out_specs = P("blk", "grp", None)
    return jax.shard_map(body, mesh=mesh, in_specs=in_specs, out_specs=out_specs, check_vma=False)
```

profile of v0, /device:TPU:0, one launch (start us, length us, event | category | flops | bytes accessed | tf_op | source)
XLA Modules:
  0.0 123.1 jit_solution(16725986775379016172)
XLA Ops:
  6.5 0.0 copy-start
  6.5 0.0 all-gather.2.cloned.1.call-start
  6.5 1.1 fusion.14
  7.7 30.3 %psum.14 = f32[8,768]{1,0:T(8,128)S(1)} all-reduce(f32[8,768]{1,0:T(8,128)S(1)} %fusion.14), channel_id=1, replica_groups=mesh['grp'=4,'blk'=8] {'blk'}, use_global_device_ids=true, to_apply=%region_0.0 | all-reduce | flops 6144 | bytes 49152 | tf_op jit(solution)/shard_map/psum | solution.py:36
  37.9 2.4 %fusion.9 = bf16[16,8,768]{2,1,0:T(8,128)(2,1)} fusion(bf16[768,768]{1,0:T(8,128)(2,1)} %param.8, bf16[16,8,768]{2,1,0:T(8,128)(2,1)} %param.7, f32[8,768]{1,0:T(8,128)S(1)} %exp.3), kind=kOutput, calls=%fused_computation.8 | convolution fusion | flops 151388160 | bytes 1597440 | tf_op jit(solution)/shard_map/dot_general | solution.py:38
  40.3 0.0 all-gather.2.cloned.1.call-update
  40.4 0.0 reduce-scatter.2.cloned.1.call-start
  40.4 23.4 %all-gather.2.cloned.1.call-done = bf16[128,8,768]{2,1,0:T(8,128)(2,1)} async-done(((bf16[16,8,768]{2,1,0:T(8,128)(2,1)}), bf16[128,8,768]{2,1,0:T(8,128)(2,1)}) %all-gather.2.cloned.1.call-update) | async-done | bytes 1572880 | tf_op jit(solution)/shard_map/all_gather | solution.py:11
  63.8 0.0 copy-done
  63.8 5.5 %fusion.3 = bf16[12,128,128,8]{1,3,0,2:T(8,128)(2,1)} fusion(bf16[1536,768]{1,0:T(8,128)(2,1)S(1)} %bitcast.30, bf16[128,8,768]{2,1,0:T(8,128)(2,1)} %all-gather.2.cloned.1.call-done), kind=kOutput, calls=%fused_computation.5 | convolution fusion | flops 2417491968 | bytes 7077888 | tf_op jit(solution)/shard_map/dot_general | solution.py:13
  69.2 5.0 %copy.10 = bf16[12,128,128,8]{2,1,0,3:T(8,128)(2,1)} copy(bf16[12,128,128,8]{1,3,0,2:T(8,128)(2,1)} %fusion.3) | data formatting | bytes 6291456 | tf_op jit(solution)/shard_map/convert_element_type | solution.py:17
  74.2 0.0 copy-start.1
  74.2 0.0 copy-start.2
  74.2 6.5 %bitcast_convert_fusion = bf16[128,8,768]{2,0,1:T(8,128)(2,1)} fusion(bf16[12,128,768]{2,1,0:T(8,128)(2,1)S(1)} %copy-done, bf16[12,128,128,8]{2,1,0,3:T(8,128)(2,1)} %copy.10), kind=kOutput, calls=%fused_computation.1 | convolution fusion | flops 2416705536 | bytes 7077888 | tf_op jit(solution)/shard_map/dot_general | solution.py:19
  80.7 0.0 reduce-scatter.2.cloned.1.call-update
  80.7 0.0 copy-done.1
  80.7 0.0 copy-done.2
  80.8 0.6 fusion.13
  81.4 10.4 %psum.15 = f32[]{:T(128)} all-reduce(f32[]{:T(128)} %fusion.13), channel_id=1, replica_groups=mesh['grp'=4,'blk'=8] {'grp'}, use_global_device_ids=true, to_apply=%region_3.4 | all-reduce | flops 1 | bytes 8 | tf_op jit(solution)/shard_map/psum | solution.py:42
  91.8 0.6 compare_select_fusion
  92.5 22.0 %reduce-scatter.2.cloned.1.call-done = bf16[16,8,768]{2,0,1:T(8,128)(2,1)} async-done(((bf16[128,8,768]{2,0,1:T(8,128)(2,1)}), bf16[16,8,768]{2,0,1:T(8,128)(2,1)}) %reduce-scatter.2.cloned.1.call-update) | async-done | bytes 196624 | tf_op jit(solution)/shard_map/reduce_scatter | solution.py:24
  114.5 1.0 multiply_convert_fusion
  115.5 0.7 copy.11
  (1 shorter events, 0.0 us)
Async XLA Ops:
  6.5 57.3 %copy-start = (bf16[12,128,768]{2,1,0:T(8,128)(2,1)S(1)}, bf16[12,128,768]{2,1,0:T(8,128)(2,1)}, u32[]{:S(2)}) copy-start(bf16[12,128,768]{2,1,0:T(8,128)(2,1)} %param.11) | copy-start | bytes 7077892
  6.5 57.2 %all-gather.2.cloned.1.call-start = ((), (), s32[]{:S(2)}) async-start(), calls=%async_computation.1 | async-start | bytes 1769472 | tf_op jit(solution)/shard_map/all_gather | solution.py:11
  40.4 74.1 %reduce-scatter.2.cloned.1.call-start = ((), (), s32[]{:S(2)}) async-start(), calls=%async_computation.2 | async-start | bytes 1769472 | tf_op jit(solution)/shard_map/reduce_scatter | solution.py:24
  74.2 6.5 %copy-start.1 = (s32[8]{0:T(128)S(1)}, s32[8]{0:T(128)}, u32[]{:S(2)}) copy-start(s32[8]{0:T(128)} %param.13) | copy-start | bytes 100
  74.2 6.5 %copy-start.2 = (f32[8]{0:T(128)S(1)}, f32[8]{0:T(128)}, u32[]{:S(2)}) copy-start(f32[8]{0:T(128)} %param.12) | copy-start | bytes 100
Sparse Core Ops, SparseCore 0:
  40.5 23.2 all-gather.1
  80.9 33.5 reduce-scatter.1
where the time goes:
time: 123 us
  waiting for transfers between devices  45.4 us (37%)
  blocking collectives  40.7 us (33%)
  matrix products  15.5 us (13%)
  between operations  13.4 us (11%)
  local copies, waits for them, and re-layouts  5.73 us (5%)
  other arithmetic  2.28 us (2%)
    psum x1, blocking collectives, body(): exponent = lax.psum(field_part, 'blk')  30.3 us
    all_gather x1, waiting for transfers between devices, measure(): portion = lax.all_gather(blocks, 'blk', axis=0, tiled=True)  23.4 us
    reduce_scatter x1, waiting for transfers between devices, measure(): lax.psum_scatter(result.reshape(amount, coupling.shape[1], -1).astype(jnp...  22 us
    psum x1, blocking collectives, body(): lax.psum(jnp.sum(jnp.where(active, weights, jnp.float32(0.0))), 'grp')  10.4 us
    dot_general x1, matrix products, measure(): jnp.dot(coupling.reshape(amount * coupling.shape[1], -1), vectors, prefer...  6.49 us
    dot_general x1, matrix products, measure(): lax.dot_general(vectors, flat, (((1,), (1,)), ((), ())), preferred_elemen...  5.46 us
    convert_element_type x1, local copies, waits for them, and re-layouts, measure(): coupling = jnp.transpose(result, (1, 3, 0, 2)).astype(jnp.bfloat16)  4.97 us
  transfers between devices with their start and end apart: 2, of which 2 were waited for; matrix products, arithmetic and copies ran while one was open for 1% of the time, Pallas kernels for 0%

commit v1 on v0

v1 whole, which is shorter than its diff:
```python
import functools
import jax
import jax.numpy as jnp
from jax import lax
from jax.experimental import pallas as pl
from jax.experimental.pallas import tpu as pltpu
from jax.sharding import PartitionSpec as P

F32 = jnp.float32
BF16 = jnp.bfloat16


def pack_kernel(walkers_ref, fields_ref, diag_ref, out_ref, wide):
    rows, slots, orbitals = walkers_ref.shape
    vec_count = fields_ref.shape[1]
    half = slots // 2
    wide[...] = walkers_ref[...].astype(F32)
    part = fields_ref[:, 0:1] * diag_ref[0:1, :]
    for g in range(1, vec_count):
        part = part + fields_ref[:, g : g + 1] * diag_ref[g : g + 1, :]
    high = part.astype(BF16).astype(F32)
    low = part - high
    for h in range(2):
        pieces = [wide[:, h * half + w, :] for w in range(half)]
        pieces += [high[h * half : (h + 1) * half], low[h * half : (h + 1) * half]]
        out_ref[h] = jnp.concatenate(pieces, axis=0).astype(BF16)


def fock_kernel(rows, half, recv_ref, body_ref, own_ref, sib_ref, out_ref, prop, turned, coup):
    n = recv_ref.shape[0]
    vec_count, occupied, orbitals = own_ref.shape
    slab = rows * half
    exponent = jnp.zeros((half, orbitals), F32)
    for s in range(n):
        tail = recv_ref[s, slab:, :].astype(F32)
        exponent = exponent + (tail[:half] + tail[half:])
    growth = jnp.exp(exponent)
    for s in range(n):
        for w in range(half):
            block = recv_ref[s, w * rows : (w + 1) * rows, :].astype(F32)
            prop[w * occupied + s * rows : w * occupied + (s + 1) * rows, :] = (
                block * growth[w : w + 1]
            ).astype(BF16)
    for w in range(half):
        piece = prop[w * occupied : (w + 1) * occupied, :]
        done = jnp.dot(piece, body_ref[...], preferred_element_type=F32)
        turned[:, w * occupied : (w + 1) * occupied] = done.T.astype(BF16)
    pair = 2 if vec_count % 2 == 0 else 1
    for c, ref in enumerate((own_ref, sib_ref)):
        for g in range(0, vec_count, pair):
            left = ref[g : g + pair].reshape(pair * occupied, orbitals)
            s = jnp.dot(left, turned[...], preferred_element_type=F32).astype(BF16)
            for k in range(pair):
                for w in range(half):
                    coup[
                        w * occupied : (w + 1) * occupied,
                        (c * vec_count + g + k) * occupied : (c * vec_count + g + k + 1) * occupied,
                    ] = s[k * occupied : (k + 1) * occupied, w * occupied : (w + 1) * occupied]
    tile = 256 if orbitals % 256 == 0 else orbitals
    depth = vec_count * occupied
    for t in range(0, orbitals, tile):
        total = jnp.dot(
            coup[:, :depth],
            own_ref[:, :, t : t + tile].reshape(depth, tile),
            preferred_element_type=F32,
        )
        total = total + jnp.dot(
            coup[:, depth:],
            sib_ref[:, :, t : t + tile].reshape(depth, tile),
            preferred_element_type=F32,
        )
        total = total.astype(BF16)
        for s in range(n):
            for w in range(half):
                out_ref[s, w * rows : (w + 1) * rows, t : t + tile] = total[
                    w * occupied + s * rows : w * occupied + (s + 1) * rows, :
                ]


def sum_kernel(recv_ref, factor_ref, out_ref, wide):
    n = recv_ref.shape[0]
    rows, slots, orbitals = out_ref.shape
    half = slots // 2
    for h in range(2):
        total = recv_ref[h].astype(F32)
        for s in range(h + 2, n, 2):
            total = total + recv_ref[s].astype(F32)
        for w in range(half):
            slot = h * half + w
            raw = total[w * rows : (w + 1) * rows].astype(BF16).astype(F32)
            wide[:, slot, :] = raw * factor_ref[slot]
    out_ref[...] = wide[...].astype(BF16)


def axis_sum(value, name):
    size = lax.axis_size(name)
    if size & (size - 1) == 0:
        step = 1
        while step < size:
            value = value + lax.ppermute(value, name, [(i, i ^ step) for i in range(size)])
            step *= 2
        return value
    total = value
    for step in range(1, size):
        total = total + lax.ppermute(value, name, [(i, (i + step) % size) for i in range(size)])
    return total


def vmem():
    return pl.BlockSpec(memory_space=pltpu.VMEM)


def params():
    return pltpu.CompilerParams(vmem_limit_bytes=40 * 2**20)


def body(walkers, one_body, fields, field_diag, chol, weights, target):
    rows, slots, orbitals = walkers.shape
    vec_count, occupied, _ = chol.shape
    half = slots // 2
    n = lax.axis_size("blk")
    slab = rows * half
    packed = pl.pallas_call(
        pack_kernel,
        out_shape=jax.ShapeDtypeStruct((2, slab + slots, orbitals), BF16),
        in_specs=[vmem()] * 3,
        out_specs=vmem(),
        scratch_shapes=[pltpu.VMEM((rows, slots, orbitals), F32)],
        compiler_params=params(),
        name="pack",
    )(walkers, fields, field_diag)
    send = jnp.broadcast_to(packed[None], (n // 2,) + packed.shape).reshape((n,) + packed.shape[1:])
    sibling = lax.ppermute(chol, "blk", [(i, i ^ 1) for i in range(n)])
    recv = lax.all_to_all(send, "blk", 0, 0, tiled=True)
    live_total = slots // 2 * lax.axis_size("grp")
    active = target < live_total
    weight_sum = axis_sum(jnp.sum(jnp.where(active, weights, F32(0.0)), keepdims=True), "grp")
    factor = jnp.where(active, weights * live_total / weight_sum, F32(0.0))
    flops = 2 * n * slab * orbitals * (orbitals + 4 * vec_count * occupied)
    part = pl.pallas_call(
        functools.partial(fock_kernel, rows, half),
        out_shape=jax.ShapeDtypeStruct((n, slab, orbitals), BF16),
        in_specs=[vmem()] * 4,
        out_specs=vmem(),
        scratch_shapes=[
            pltpu.VMEM((half * occupied, orbitals), BF16),
            pltpu.VMEM((orbitals, half * occupied), BF16),
            pltpu.VMEM((half * occupied, 2 * vec_count * occupied), BF16),
        ],
        compiler_params=params(),
        cost_estimate=pl.CostEstimate(flops=flops, bytes_accessed=8 * 2**20, transcendentals=0),
        name="fock",
    )(recv, one_body, chol, sibling)
    back = lax.all_to_all(part, "blk", 0, 0, tiled=True)
    return pl.pallas_call(
        sum_kernel,
        out_shape=jax.ShapeDtypeStruct(walkers.shape, BF16),
        in_specs=[vmem(), pl.BlockSpec(memory_space=pltpu.SMEM)],
        out_specs=vmem(),
        scratch_shapes=[pltpu.VMEM(walkers.shape, F32)],
        compiler_params=params(),
        name="sum",
    )(back, factor)


def solution(mesh):
    in_specs = (
        P("blk", "grp", None),
        P(),
        P("grp", "blk"),
        P("blk", None),
        P("blk", None, None),
        P("grp"),
        P("grp"),
    )
    out_specs = P("blk", "grp", None)
    return jax.shard_map(body, mesh=mesh, in_specs=in_specs, out_specs=out_specs, check_vma=False)
```

time: 123 us -> 66.6 us (0.54)
  waiting for transfers between devices: 45.4 us -> 14 us
  matrix products: 15.5 us -> 0 us
  blocking collectives: 40.7 us -> 29 us
  between operations: 13.4 us -> 1.96 us
  Pallas kernels: 0 us -> 8.52 us
  starting transfers between devices: 0.04 us -> 8.4 us
  local copies, waits for them, and re-layouts: 5.73 us -> 3.75 us
  other arithmetic: 2.28 us -> 0.61 us
    psum x2 -> x0, blocking collectives: 40.7 us -> none  [the longest x1 30.3 us: body(): exponent = lax.psum(field_part, 'blk')]
    all_to_all x0 -> x1, blocking collectives: none -> 29 us  [body(): recv = lax.all_to_all(send, 'blk', 0, 0, tiled=True)]
    all_gather x1 -> x0, waiting for transfers between devices: 23.4 us -> none  [measure(): portion = lax.all_gather(blocks, 'blk', axis=0, tiled=True)]
    reduce_scatter x1 -> x0, waiting for transfers between devices: 22 us -> none  [measure(): lax.psum_scatter(result.reshape(amount, coupling.shape[1], -1).astype(jnp...]
    dot_general x4 -> x0, matrix products: 15.5 us -> none  [the longest x1 6.49 us: measure(): jnp.dot(coupling.reshape(amount * coupling.shape[1], -1), vectors, prefer...]
    all_to_all x0 -> x1, waiting for transfers between devices: none -> 11.1 us  [body(): back = lax.all_to_all(part, 'blk', 0, 0, tiled=True)]
    pallas_call x0 -> x3, Pallas kernels: none -> 8.52 us  [the longest x1 6.8 us: body(): pl.pallas_call(functools.partial(fock_kernel, rows, half), out_shape=jax....]
    convert_element_type x2 -> x0, local copies, waits for them, and re-layouts: 5.71 us -> none  [the longest x1 4.97 us: measure(): coupling = jnp.transpose(result, (1, 3, 0, 2)).astype(jnp.bfloat16)]
  transfers between devices with their start and end apart: 2 -> 4, of which waited for: 2 -> 3; matrix products, arithmetic and copies ran while one was open for 1% -> 1% of each run, Pallas kernels for 0% -> 0%
where the time goes in v1:
time: 66.6 us; the launch traced here: 66.2 us
  blocking collectives  29 us (44%)
  waiting for transfers between devices  14 us (21%)
  Pallas kernels  8.52 us (13%)
  starting transfers between devices  8.4 us (13%)
  local copies, waits for them, and re-layouts  3.75 us (6%)
  between operations  1.96 us (3%)
    all_to_all x1, blocking collectives, body(): recv = lax.all_to_all(send, 'blk', 0, 0, tiled=True)  29 us
    all_to_all x1, waiting for transfers between devices, body(): back = lax.all_to_all(part, 'blk', 0, 0, tiled=True)  11.1 us
    pallas_call x1, Pallas kernels, body(): pl.pallas_call(functools.partial(fock_kernel, rows, half), out_shape=jax....  6.8 us
    ppermute x2, starting transfers between devices, axis_sum(): lax.ppermute(value, name, [(i, i ^ step) for i in range(size)])  4.4 us
    unnamed x14, local copies, waits for them, and re-layouts  3.69 us
    all_to_all x1, starting transfers between devices, body(): back = lax.all_to_all(part, 'blk', 0, 0, tiled=True)  3.55 us
    ppermute x2, waiting for transfers between devices, axis_sum(): lax.ppermute(value, name, [(i, i ^ step) for i in range(size)])  2.81 us
    pallas_call x1, Pallas kernels, body(): pl.pallas_call(sum_kernel, out_shape=jax.ShapeDtypeStruct(walkers.shape,...  1.5 us
  transfers between devices with their start and end apart: 4, of which 3 were waited for; matrix products, arithmetic and copies ran while one was open for 1% of the time, Pallas kernels for 0%

profile of v1, /device:TPU:0, one launch (start us, length us, event | category | flops | bytes accessed | tf_op | source)
XLA Modules:
  0.0 66.2 jit_solution(10804164708663740835)
XLA Ops:
  0.0 0.5 collective-permute-start
  0.5 0.0 copy-start
  0.5 0.9 %copy-done = bf16[16,8,768]{2,1,0:T(8,128)(2,1)S(1)} copy-done((bf16[16,8,768]{2,1,0:T(8,128)(2,1)S(1)}, bf16[16,8,768]{2,1,0:T(8,128)(2,1)}, u32[]{:S(2)}) %copy-start) | copy-done | bytes 196632
  1.4 0.0 copy-start.1
  1.4 0.8 %copy-done.1 = f32[12,768]{1,0:T(8,128)S(1)} copy-done((f32[12,768]{1,0:T(8,128)S(1)}, f32[12,768]{1,0:T(8,128)}, u32[]{:S(2)}) %copy-start.1) | copy-done | bytes 36888
  2.2 0.0 copy-start.2
  2.2 0.7 %copy-done.2 = f32[8,12]{1,0:T(8,128)S(1)} copy-done((f32[8,12]{1,0:T(8,128)S(1)}, f32[8,12]{1,0:T(8,128)}, u32[]{:S(2)}) %copy-start.2) | copy-done | bytes 408
  2.9 0.0 copy-start.3
  2.9 0.2 pack.1
  3.1 0.1 broadcast_in_dim.14
  3.2 29.0 %all_to_all.10.recv_ref = bf16[8,72,768]{2,1,0:T(8,128)(2,1)S(1)} all-to-all(bf16[8,72,768]{2,1,0:T(8,128)(2,1)S(1)} %bitcast.3), channel_id=1, replica_groups=mesh['grp'=4,'blk'=8] {'blk'}, dimensions={0} | all-to-all | bytes 1769472 | tf_op jit(solution)/shard_map/all_to_all | solution.py:134
  32.2 0.0 collective-permute-done.sib_ref
  32.2 0.0 copy-done.3
  32.2 0.0 copy-start.4
  32.2 1.3 %copy-done.4 = bf16[768,768]{1,0:T(8,128)(2,1)S(1)} copy-done((bf16[768,768]{1,0:T(8,128)(2,1)S(1)}, bf16[768,768]{1,0:T(8,128)(2,1)}, u32[]{:S(2)}) %copy-start.4) | copy-done | bytes 1179672
  33.4 0.0 copy-start.5
  33.5 0.0 copy-start.6
  33.5 6.8 %fock.1 = bf16[8,64,768]{2,1,0:T(8,128)(2,1)} custom-call(bf16[8,72,768]{2,1,0:T(8,128)(2,1)S(1)} %all_to_all.10.recv_ref, bf16[768,768]{1,0:T(8,128)(2,1)S(1)} %copy-done.4, bf16[12,128,768]{2,1,0:T(8,128)(2,1)S(1)} %copy-done.3, bf16[12,128,768]{2,1,0:T(8,128)(2,1)S(1)} %collective-permute-done.sib_ref), custom_call_target="tpu_custom_call" | custom-call | flops 5435817984 | bytes 8388608 | tf_op jit(solution)/shard_map/fock/pallas_call | solution.py:140
  40.2 3.5 %all-to-all-start.1 = ((bf16[8,64,768]{2,1,0:T(8,128)(2,1)}), bf16[8,64,768]{2,1,0:T(8,128)(2,1)S(1)}, u32[]{:S(2)}, u32[]{:S(2)}) async-start(bf16[8,64,768]{2,1,0:T(8,128)(2,1)} %fock.1), calls=%async_computation.1 | async-start | bytes 1572864 | tf_op jit(solution)/shard_map/all_to_all | solution.py:154
  43.8 0.0 copy-done.5
  43.8 0.0 copy-done.6
  43.8 0.6 fusion
  44.4 1.5 %collective-permute-start.1 = (f32[1]{0:T(128)}, f32[1]{0:T(128)}, u32[]{:S(2)}, u32[]{:S(2)}) collective-permute-start(f32[1]{0:T(128)} %bitcast.1), channel_id=1, source_target_pairs={{0,8},{8,0},{16,24},{24,16},{1,9},{9,1},{17,25},{25,17},{2,10},{10... | collective-permute-start | bytes 20 | tf_op jit(solution)/shard_map/ppermute | solution.py:100
  45.9 2.1 %collective-permute-done.1 = f32[1]{0:T(128)} collective-permute-done((f32[1]{0:T(128)}, f32[1]{0:T(128)}, u32[]{:S(2)}, u32[]{:S(2)}) %collective-permute-start.1) | collective-permute-done | bytes 36 | tf_op jit(solution)/shard_map/ppermute | solution.py:100
  49.4 2.9 %collective-permute-start.2 = (f32[1]{0:T(128)}, f32[1]{0:T(128)}, u32[]{:S(2)}, u32[]{:S(2)}) collective-permute-start(f32[1]{0:T(128)} %add.6), channel_id=1, source_target_pairs={{0,16},{8,24},{16,0},{24,8},{1,17},{9,25},{17,1},{25,9},{2,18},{10... | collective-permute-start | bytes 20 | tf_op jit(solution)/shard_map/ppermute | solution.py:100
  52.2 0.7 %collective-permute-done.2 = f32[1]{0:T(128)} collective-permute-done((f32[1]{0:T(128)}, f32[1]{0:T(128)}, u32[]{:S(2)}, u32[]{:S(2)}) %collective-permute-start.2) | collective-permute-done | bytes 36 | tf_op jit(solution)/shard_map/ppermute | solution.py:100
  53.6 11.1 %all-to-all-done.1.recv_ref = bf16[8,64,768]{2,1,0:T(8,128)(2,1)S(1)} async-done(((bf16[8,64,768]{2,1,0:T(8,128)(2,1)}), bf16[8,64,768]{2,1,0:T(8,128)(2,1)S(1)}, u32[]{:S(2)}, u32[]{:S(2)}) %all-to-all-start.1) | async-done | bytes 786464 | tf_op jit(solution)/shard_map/all_to_all | solution.py:154
  64.7 1.5 %sum.1 = bf16[16,8,768]{2,1,0:T(8,128)(2,1)} custom-call(bf16[8,64,768]{2,1,0:T(8,128)(2,1)S(1)} %all-to-all-done.1.recv_ref, f32[8]{0:T(128)S(1)} %compare_select_fusion.factor_ref), custom_call_target="tpu_custom_call" | custom-call | tf_op jit(solution)/shard_map/sum/pallas_call | solution.py:155
  (1 shorter events, 0.0 us)
Async XLA Ops:
  0.0 32.2 %collective-permute-start = (bf16[12,128,768]{2,1,0:T(8,128)(2,1)}, bf16[12,128,768]{2,1,0:T(8,128)(2,1)S(1)}, u32[]{:S(2)}, u32[]{:S(2)}) collective-permute-start(bf16[12,128,768]{2,1,0:T(8,128)(2,1)} %own_ref.1), channel_id=1, source_target_pairs={{0,1},{1,0},{2,3},{3,2},{4,5},{5,4},{6,7},{7,6},{8,9},{9,8},{10,11... | collective-permute-start | bytes 7077896 | tf_op jit(solution)/shard_map/ppermute | solution.py:133
  0.5 0.9 %copy-start = (bf16[16,8,768]{2,1,0:T(8,128)(2,1)S(1)}, bf16[16,8,768]{2,1,0:T(8,128)(2,1)}, u32[]{:S(2)}) copy-start(bf16[16,8,768]{2,1,0:T(8,128)(2,1)} %walkers_ref.1) | copy-start | bytes 589828
  1.4 0.8 %copy-start.1 = (f32[12,768]{1,0:T(8,128)S(1)}, f32[12,768]{1,0:T(8,128)}, u32[]{:S(2)}) copy-start(f32[12,768]{1,0:T(8,128)} %diag_ref.1) | copy-start | bytes 110596
  2.2 0.7 %copy-start.2 = (f32[8,12]{1,0:T(8,128)S(1)}, f32[8,12]{1,0:T(8,128)}, u32[]{:S(2)}) copy-start(f32[8,12]{1,0:T(8,128)} %fields_ref.1) | copy-start | bytes 1156
  2.9 29.3 %copy-start.3 = (bf16[12,128,768]{2,1,0:T(8,128)(2,1)S(1)}, bf16[12,128,768]{2,1,0:T(8,128)(2,1)}, u32[]{:S(2)}) copy-start(bf16[12,128,768]{2,1,0:T(8,128)(2,1)} %own_ref.1) | copy-start | bytes 7077892
  32.2 1.3 %copy-start.4 = (bf16[768,768]{1,0:T(8,128)(2,1)S(1)}, bf16[768,768]{1,0:T(8,128)(2,1)}, u32[]{:S(2)}) copy-start(bf16[768,768]{1,0:T(8,128)(2,1)} %body_ref.1) | copy-start | bytes 3538948
  33.4 10.4 %copy-start.5 = (s32[8]{0:T(128)S(1)}, s32[8]{0:T(128)}, u32[]{:S(2)}) copy-start(s32[8]{0:T(128)} %param.13) | copy-start | bytes 100
  33.5 10.4 %copy-start.6 = (f32[8]{0:T(128)S(1)}, f32[8]{0:T(128)}, u32[]{:S(2)}) copy-start(f32[8]{0:T(128)} %param.12) | copy-start | bytes 100
  40.2 24.4 %all-to-all-start.1 = ((bf16[8,64,768]{2,1,0:T(8,128)(2,1)}), bf16[8,64,768]{2,1,0:T(8,128)(2,1)S(1)}, u32[]{:S(2)}, u32[]{:S(2)}) async-start(bf16[8,64,768]{2,1,0:T(8,128)(2,1)} %fock.1), calls=%async_computation.1 | async-start | bytes 1572864 | tf_op jit(solution)/shard_map/all_to_all | solution.py:154
  44.4 3.7 %collective-permute-start.1 = (f32[1]{0:T(128)}, f32[1]{0:T(128)}, u32[]{:S(2)}, u32[]{:S(2)}) collective-permute-start(f32[1]{0:T(128)} %bitcast.1), channel_id=1, source_target_pairs={{0,8},{8,0},{16,24},{24,16},{1,9},{9,1},{17,25},{25,17},{2,10},{10... | collective-permute-start | bytes 20 | tf_op jit(solution)/shard_map/ppermute | solution.py:100
  49.4 3.6 %collective-permute-start.2 = (f32[1]{0:T(128)}, f32[1]{0:T(128)}, u32[]{:S(2)}, u32[]{:S(2)}) collective-permute-start(f32[1]{0:T(128)} %add.6), channel_id=1, source_target_pairs={{0,16},{8,24},{16,0},{24,8},{1,17},{9,25},{17,1},{25,9},{2,18},{10... | collective-permute-start | bytes 20 | tf_op jit(solution)/shard_map/ppermute | solution.py:100

commit v2 on v0

v2 whole, which is shorter than its diff:
```python
import functools
import jax
import jax.numpy as jnp
from jax import lax
from jax.experimental import pallas as pl
from jax.experimental.pallas import tpu as pltpu
from jax.sharding import PartitionSpec as P

F32 = jnp.float32
BF16 = jnp.bfloat16
LANES = 128


def terms(value, count):
    out = []
    for _ in range(count):
        term = value.astype(BF16).astype(F32)
        out.append(term)
        value = value - term
    return out


def padded(pieces, rows):
    have = sum(p.shape[0] for p in pieces)
    if have < rows:
        pieces = list(pieces) + [jnp.zeros((rows - have, pieces[0].shape[1]), F32)]
    return jnp.concatenate(pieces, axis=0)


def route_kernel(keep, me_ref, target_ref, weights_ref, walkers_ref, fields_ref, *refs):
    rows, slots, orbitals = walkers_ref.shape
    vec_count = fields_ref.shape[1]
    *outs, wide, blocks, lines = refs
    groups = len(outs)
    live = groups * keep
    wide[...] = walkers_ref[...].astype(F32)
    blocks[...] = jnp.zeros(blocks.shape, F32)
    lines[...] = jnp.zeros(lines.shape, F32)
    weight = F32(0.0)
    for slot in range(slots):
        t = jnp.minimum(target_ref[slot], live)
        weight = weight + jnp.where(t < live, weights_ref[slot], F32(0.0))
        blocks[t] = wide[:, slot, :]
        lines[t, :, 0:vec_count] = fields_ref[slot : slot + 1, :]
    sums = terms(jnp.full((1, LANES), weight, F32), 3)
    for s, out in enumerate(outs):
        base = lax.rem(me_ref[0] + s, groups) * keep
        out[:, 0:orbitals] = jnp.concatenate([blocks[base + k] for k in range(keep)], axis=0).astype(BF16)
        line = jnp.concatenate([lines[base + k] for k in range(keep)], axis=0)
        out[:, orbitals:] = padded(terms(line, 3) + sums, keep * rows).astype(BF16)


def merge_kernel(keep, groups, core_ref, diag_ref, *refs):
    ins, (same_ref, other_ref, weight_ref) = refs[:groups], refs[groups:]
    vec_count, orbitals = diag_ref.shape
    half = keep // 2
    slab = same_ref.shape[0]
    total = ins[0][...].astype(F32)
    for ref in ins[1:]:
        total = total + ref[...].astype(F32)
    tail = total[:, orbitals:]
    line = tail[0:keep] + tail[keep : 2 * keep] + tail[2 * keep : 3 * keep]
    weight = jnp.zeros((1, LANES), F32)
    for ref in ins:
        part = ref[:, orbitals:].astype(F32)
        weight = weight + (part[3 * keep : 3 * keep + 1] + part[3 * keep + 1 : 3 * keep + 2] + part[3 * keep + 2 : 3 * keep + 3])
    weight_ref[...] = jnp.broadcast_to(weight, weight_ref.shape)
    exponent = line[:, 0:1] * diag_ref[0:1, :]
    for g in range(1, vec_count):
        exponent = exponent + line[:, g : g + 1] * diag_ref[g : g + 1, :]
    full = []
    for h in range(2):
        pieces = []
        for term in terms(exponent[h * half : (h + 1) * half], 2):
            pieces += [term[k : k + 1, c : c + LANES] for k in range(half) for c in range(0, orbitals, LANES)]
        parts = [total[h * slab : (h + 1) * slab, 0:orbitals]]
        for b in range(0, len(pieces), slab):
            parts.append(padded(pieces[b : b + slab], slab))
        full.append(jnp.concatenate(parts, axis=1))
    first = core_ref[0] == 0
    same_ref[...] = jnp.where(first, full[0], full[1]).astype(BF16)
    other_ref[...] = jnp.where(first, full[1], full[0]).astype(BF16)


def hops(n):
    return [(s, e) for s in range(n // 2) for e in range(2)]


def partner(blk, s, e, n, sign):
    chip = lax.rem(lax.div(blk, 2) + (s if sign > 0 else n // 2 - s), n // 2)
    core = lax.rem(blk, 2)
    return 2 * chip + (core if e == 0 else 1 - core)


def fock_kernel(n, half, blk_ref, body_ref, own_ref, sib_ref, *refs):
    ins, outs = refs[:n], refs[n : 2 * n]
    prop, turned, coup, result = refs[2 * n :]
    vec_count, occupied, orbitals = own_ref.shape
    slab = outs[0].shape[0]
    rows = slab // half
    blocks = orbitals // LANES
    blk = blk_ref[0]
    exponent = jnp.zeros((2 * half * blocks, LANES), F32)
    for ref in ins:
        pieces = [ref[:, c : c + LANES].astype(F32) for c in range(orbitals, ref.shape[1], LANES)]
        exponent = exponent + jnp.concatenate(pieces, axis=0)[0 : 2 * half * blocks]
    growth = jnp.exp(exponent[0 : half * blocks] + exponent[half * blocks :])
    for ref, (s, e) in zip(ins, hops(n)):
        source = partner(blk, s, e, n, -1)
        for w in range(half):
            for c in range(blocks):
                piece = ref[w * rows : (w + 1) * rows, c * LANES : (c + 1) * LANES].astype(F32)
                prop[w, source, :, c * LANES : (c + 1) * LANES] = piece * growth[w * blocks + c : w * blocks + c + 1]
    for w in range(half):
        piece = jnp.concatenate([prop[w, i] for i in range(n)], axis=0).astype(BF16)
        done = jnp.dot(piece, body_ref[...], preferred_element_type=F32)
        turned[:, w * occupied : (w + 1) * occupied] = done.T.astype(BF16)
    pair = 2 if vec_count % 2 == 0 else 1
    for c, ref in enumerate((own_ref, sib_ref)):
        for g in range(0, vec_count, pair):
            left = ref[g : g + pair].reshape(pair * occupied, orbitals)
            s = jnp.dot(left, turned[...], preferred_element_type=F32).astype(BF16)
            for k in range(pair):
                at = (c * vec_count + g + k) * occupied
                for w in range(half):
                    coup[w * occupied : (w + 1) * occupied, at : at + occupied] = s[
                        k * occupied : (k + 1) * occupied, w * occupied : (w + 1) * occupied
                    ]
    tile = 256 if orbitals % 256 == 0 else orbitals
    depth = vec_count * occupied
    for t in range(0, orbitals, tile):
        total = jnp.dot(
            coup[:, :depth],
            own_ref[:, :, t : t + tile].reshape(depth, tile),
            preferred_element_type=F32,
        )
        total = total + jnp.dot(
            coup[:, depth:],
            sib_ref[:, :, t : t + tile].reshape(depth, tile),
            preferred_element_type=F32,
        )
        for w in range(half):
            for i in range(n):
                at = w * occupied + i * rows
                result[w, i, :, t : t + tile] = total[at : at + rows]
    for out, (s, e) in zip(outs, hops(n)):
        to = partner(blk, s, e, n, 1)
        for w in range(half):
            out[w * rows : (w + 1) * rows, :] = result[w, to].astype(BF16)


def sum_kernel(n, core_ref, *refs):
    ins, out_ref = refs[:n], refs[n]
    slab = ins[0].shape[0]
    halves = []
    for e in range(2):
        total = ins[e][...].astype(F32)
        for ref in ins[e + 2 :: 2]:
            total = total + ref[...].astype(F32)
        halves.append(total)
    first = core_ref[0] == 0
    out_ref[0:slab, :] = jnp.where(first, halves[0], halves[1]).astype(BF16)
    out_ref[slab:, :] = jnp.where(first, halves[1], halves[0]).astype(BF16)


def deal_kernel(keep, groups, me_ref, target_ref, weights_ref, total_ref, *refs):
    ins, (out_ref, blocks, wide) = refs[:groups], refs[groups:]
    rows, slots, orbitals = out_ref.shape
    live = groups * keep
    for s, ref in enumerate(ins):
        base = lax.rem(me_ref[0] + groups - s, groups) * keep
        for k in range(keep):
            blocks[base + k] = ref[k * rows : (k + 1) * rows, :].astype(F32)
    blocks[live] = jnp.zeros((rows, orbitals), F32)
    for slot in range(slots):
        t = jnp.minimum(target_ref[slot], live)
        weight = jnp.where(t < live, weights_ref[slot], F32(0.0))
        factor = jnp.full((1, LANES), weight * live, F32) / total_ref[0:1, :]
        wide[:, slot, :] = blocks[t] * factor[:, 0:1]
    out_ref[...] = wide[...].astype(BF16)


def call(kernel, outs, scalars, arrays, scratch, name, flops=0, vmem=40):
    smem = pl.BlockSpec(memory_space=pltpu.SMEM)
    full = pl.BlockSpec(memory_space=pltpu.VMEM)
    size = sum(x.size * x.dtype.itemsize for x in list(arrays) + list(outs))
    return pl.pallas_call(
        kernel,
        out_shape=outs,
        in_specs=[smem] * len(scalars) + [full] * len(arrays),
        out_specs=[full] * len(outs),
        scratch_shapes=scratch,
        compiler_params=pltpu.CompilerParams(vmem_limit_bytes=vmem * 2**20),
        cost_estimate=pl.CostEstimate(flops=flops, bytes_accessed=size, transcendentals=0),
        name=name,
    )(*scalars, *arrays)


def body(walkers, one_body, fields, field_diag, chol, weights, target):
    rows, slots, orbitals = walkers.shape
    vec_count, occupied, _ = chol.shape
    n, groups = lax.axis_size("blk"), lax.axis_size("grp")
    keep = slots // 2
    half = keep // 2
    slab = half * rows
    shape = jax.ShapeDtypeStruct
    grp = lax.axis_index("grp").reshape(1)
    blk = lax.axis_index("blk").reshape(1)
    core = lax.rem(blk, 2)

    def to_list(x, s):
        return lax.ppermute(x, "grp", [(i, (i + s) % groups) for i in range(groups)]) if s else x

    def to_block(x, s, e):
        if not s and not e:
            return x
        return lax.ppermute(x, "blk", [(i, (2 * (i // 2 + s) + (i % 2 ^ e)) % n) for i in range(n)])

    sibling = to_block(chol, 0, 1)
    routed = call(
        functools.partial(route_kernel, keep),
        [shape((keep * rows, orbitals + LANES), BF16)] * groups,
        [grp, target, weights],
        [walkers, fields],
        [
            pltpu.VMEM((rows, slots, orbitals), F32),
            pltpu.VMEM((groups * keep + 1, rows, orbitals), F32),
            pltpu.VMEM((groups * keep + 1, 1, LANES), F32),
        ],
        "route",
    )
    routed = [to_list(x, s) for s, x in enumerate(routed)]
    extra = -(-2 * half * (orbitals // LANES) // slab)
    payload = shape((slab, orbitals + extra * LANES), BF16)
    same, other, weight_sum = call(
        functools.partial(merge_kernel, keep, groups),
        [payload, payload, shape((8, LANES), F32)],
        [core],
        [field_diag] + routed,
        [],
        "merge",
    )
    gathered = [to_block(other if e else same, s, e) for s, e in hops(n)]
    parts = call(
        functools.partial(fock_kernel, n, half),
        [shape((slab, orbitals), BF16)] * n,
        [blk],
        [one_body, chol, sibling] + gathered,
        [
            pltpu.VMEM((half, n, rows, orbitals), F32),
            pltpu.VMEM((orbitals, half * occupied), BF16),
            pltpu.VMEM((half * occupied, 2 * vec_count * occupied), BF16),
            pltpu.VMEM((half, n, rows, orbitals), F32),
        ],
        "fock",
        flops=2 * n * slab * orbitals * (orbitals + 4 * vec_count * occupied),
    )
    parts = [to_block(x, s, e) for x, (s, e) in zip(parts, hops(n))]
    (raw,) = call(
        functools.partial(sum_kernel, n),
        [shape((keep * rows, orbitals), BF16)],
        [core],
        parts,
        [],
        "sum",
    )
    back = [to_list(raw, s) for s in range(groups)]
    (out,) = call(
        functools.partial(deal_kernel, keep, groups),
        [shape(walkers.shape, BF16)],
        [grp, target, weights],
        [weight_sum] + back,
        [pltpu.VMEM((groups * keep + 1, rows, orbitals), F32), pltpu.VMEM(walkers.shape, F32)],
        "deal",
    )
    return out


def solution(mesh):
    in_specs = (
        P("blk", "grp", None),
        P(),
        P("grp", "blk"),
        P("blk", None),
        P("blk", None, None),
        P("grp"),
        P("grp"),
    )
    out_specs = P("blk", "grp", None)
    return jax.shard_map(body, mesh=mesh, in_specs=in_specs, out_specs=out_specs, check_vma=False)
```

time: 123 us -> 59.1 us (0.48)
  blocking collectives: 40.7 us -> 0 us
  starting transfers between devices: 0.04 us -> 27.4 us
  waiting for transfers between devices: 45.4 us -> 18.4 us
  matrix products: 15.5 us -> 0 us
  between operations: 13.4 us -> 0.06 us
  Pallas kernels: 0 us -> 6.32 us
  other arithmetic: 2.28 us -> 0 us
    psum x2 -> x0, blocking collectives: 40.7 us -> none  [the longest x1 30.3 us: body(): exponent = lax.psum(field_part, 'blk')]
    ppermute x0 -> x21, starting transfers between devices: none -> 27.4 us  [the longest x15 18.3 us: to_block(): lax.ppermute(x, 'blk', [(i, (2 * (i // 2 + s) + (i % 2 ^ e)) % n) for i i...]
    all_gather x1 -> x0, waiting for transfers between devices: 23.4 us -> none  [measure(): portion = lax.all_gather(blocks, 'blk', axis=0, tiled=True)]
    reduce_scatter x1 -> x0, waiting for transfers between devices: 22 us -> none  [measure(): lax.psum_scatter(result.reshape(amount, coupling.shape[1], -1).astype(jnp...]
    ppermute x0 -> x21, waiting for transfers between devices: none -> 18.4 us  [the longest x6 9.48 us: to_list(): lax.ppermute(x, 'grp', [(i, (i + s) % groups) for i in range(groups)])]
    dot_general x4 -> x0, matrix products: 15.5 us -> none  [the longest x1 6.49 us: measure(): jnp.dot(coupling.reshape(amount * coupling.shape[1], -1), vectors, prefer...]
    unnamed x6 -> x18, local copies, waits for them, and re-layouts: 0.01 us -> 6.66 us
    pallas_call x0 -> x5, Pallas kernels: none -> 6.32 us  [call(): pl.pallas_call(kernel, out_shape=outs, in_specs=[smem] * len(scalars) + [...]
  transfers between devices with their start and end apart: 2 -> 21, of which waited for: 2 -> 14; matrix products, arithmetic and copies ran while one was open for 1% -> 0% of each run, Pallas kernels for 0% -> 2%
where the time goes in v2:
time: 59.1 us; the launch traced here: 58.8 us
  starting transfers between devices  27.4 us (46%)
  waiting for transfers between devices  18.4 us (31%)
  local copies, waits for them, and re-layouts  6.66 us (11%)
  Pallas kernels  6.32 us (11%)
    ppermute x15, starting transfers between devices, to_block(): lax.ppermute(x, 'blk', [(i, (2 * (i // 2 + s) + (i % 2 ^ e)) % n) for i i...  18.3 us
    ppermute x6, waiting for transfers between devices, to_list(): lax.ppermute(x, 'grp', [(i, (i + s) % groups) for i in range(groups)])  9.48 us
    ppermute x6, starting transfers between devices, to_list(): lax.ppermute(x, 'grp', [(i, (i + s) % groups) for i in range(groups)])  9.09 us
    ppermute x15, waiting for transfers between devices, to_block(): lax.ppermute(x, 'blk', [(i, (2 * (i // 2 + s) + (i % 2 ^ e)) % n) for i i...  8.93 us
    unnamed x18, local copies, waits for them, and re-layouts  6.66 us
    pallas_call x5, Pallas kernels, call(): pl.pallas_call(kernel, out_shape=outs, in_specs=[smem] * len(scalars) + [...  6.32 us
  transfers between devices with their start and end apart: 21, of which 14 were waited for; matrix products, arithmetic and copies ran while one was open for 0% of the time, Pallas kernels for 2%

profile of v2, /device:TPU:0, one launch (start us, length us, event | category | flops | bytes accessed | tf_op | source)
XLA Modules:
  0.0 58.8 jit_solution(13883631499915408878)
XLA Ops:
  0.0 0.5 collective-permute-start.3
  0.5 0.9 %copy-done = bf16[16,8,768]{2,1,0:T(8,128)(2,1)S(1)} copy-done((bf16[16,8,768]{2,1,0:T(8,128)(2,1)S(1)}, bf16[16,8,768]{2,1,0:T(8,128)(2,1)}, u32[]{:S(2)}) %copy-start) | copy-done | bytes 196632
  1.4 0.7 %copy-done.2 = f32[8,12]{1,0:T(8,128)S(1)} copy-done((f32[8,12]{1,0:T(8,128)S(1)}, f32[8,12]{1,0:T(8,128)}, u32[]{:S(2)}) %copy-start.2) | copy-done | bytes 408
  2.1 0.7 %copy-done.3 = s32[8]{0:T(128)S(1)} copy-done((s32[8]{0:T(128)S(1)}, s32[8]{0:T(128)}, u32[]{:S(2)}) %copy-start.3) | copy-done | bytes 56
  2.7 0.7 %copy-done.5 = f32[8]{0:T(128)S(1)} copy-done((f32[8]{0:T(128)S(1)}, f32[8]{0:T(128)}, u32[]{:S(2)}) %copy-start.5) | copy-done | bytes 56
  3.4 0.8 %route.1 = (bf16[64,896]{1,0:T(8,128)(2,1)S(1)}, bf16[64,896]{1,0:T(8,128)(2,1)S(1)}, bf16[64,896]{1,0:T(8,128)(2,1)S(1)}, bf16[64,896]{1,0:T(8,128)(2,1)S(1)}) custom-call(s32[1]{0:T(128)} %bitcast.me_ref, s32[8]{0:T(128)S(1)} %copy-done.3, f32[8]{0:T(128)S(1)} %copy-done.5, bf16[16,8,768]{2,1,0:T(8,128)(2,1)S(1)} %copy-done, f32[8,12]{1,0:T(8,128)S(1)} %copy-done.2), custom_call_target="tpu_custom_call" | custom-call | bytes 655744 | tf_op jit(solution)/shard_map/route/pallas_call | solution.py:187
  4.2 2.5 %collective-permute-start = (bf16[64,896]{1,0:T(8,128)(2,1)S(1)}, bf16[64,896]{1,0:T(8,128)(2,1)S(1)}, u32[]{:S(2)}, u32[]{:S(2)}) collective-permute-start(bf16[64,896]{1,0:T(8,128)(2,1)S(1)} %get-tuple-element.21), channel_id=1, source_target_pairs={{0,8},{8,16},{16,24},{24,0},{1,9},{9,17},{17,25},{25,1},{2,10},{10... | collective-permute-start | bytes 344072 | tf_op jit(solution)/shard_map/ppermute | solution.py:212
  6.7 1.5 %collective-permute-start.1 = (bf16[64,896]{1,0:T(8,128)(2,1)S(1)}, bf16[64,896]{1,0:T(8,128)(2,1)S(1)}, u32[]{:S(2)}, u32[]{:S(2)}) collective-permute-start(bf16[64,896]{1,0:T(8,128)(2,1)S(1)} %get-tuple-element.22), channel_id=1, source_target_pairs={{0,16},{8,24},{16,0},{24,8},{1,17},{9,25},{17,1},{25,9},{2,18},{10... | collective-permute-start | bytes 344072 | tf_op jit(solution)/shard_map/ppermute | solution.py:212
  8.2 1.4 %collective-permute-start.2 = (bf16[64,896]{1,0:T(8,128)(2,1)S(1)}, bf16[64,896]{1,0:T(8,128)(2,1)S(1)}, u32[]{:S(2)}, u32[]{:S(2)}) collective-permute-start(bf16[64,896]{1,0:T(8,128)(2,1)S(1)} %get-tuple-element.23), channel_id=1, source_target_pairs={{0,24},{8,0},{16,8},{24,16},{1,25},{9,1},{17,9},{25,17},{2,26},{10... | collective-permute-start | bytes 344072 | tf_op jit(solution)/shard_map/ppermute | solution.py:212
  9.7 2.0 %collective-permute-done.refs_1_ = bf16[64,896]{1,0:T(8,128)(2,1)S(1)} collective-permute-done((bf16[64,896]{1,0:T(8,128)(2,1)S(1)}, bf16[64,896]{1,0:T(8,128)(2,1)S(1)}, u32[]{:S(2)}, u32[]{:S(2)}) %collective-permute-start) | collective-permute-done | bytes 114720 | tf_op jit(solution)/shard_map/ppermute | solution.py:212
  11.7 2.2 %collective-permute-done.1.refs_2_ = bf16[64,896]{1,0:T(8,128)(2,1)S(1)} collective-permute-done((bf16[64,896]{1,0:T(8,128)(2,1)S(1)}, bf16[64,896]{1,0:T(8,128)(2,1)S(1)}, u32[]{:S(2)}, u32[]{:S(2)}) %collective-permute-start.1) | collective-permute-done | bytes 114720 | tf_op jit(solution)/shard_map/ppermute | solution.py:212
  13.9 0.3 collective-permute-done.2.refs_3_
  14.2 0.8 %copy-done.1 = f32[12,768]{1,0:T(8,128)S(1)} copy-done((f32[12,768]{1,0:T(8,128)S(1)}, f32[12,768]{1,0:T(8,128)}, u32[]{:S(2)}) %copy-start.1) | copy-done | bytes 36888
  15.0 0.1 merge.1
  15.2 3.7 %collective-permute-start.9 = (bf16[32,896]{1,0:T(8,128)(2,1)S(1)}, bf16[32,896]{1,0:T(8,128)(2,1)S(1)}, u32[]{:S(2)}, u32[]{:S(2)}) collective-permute-start(bf16[32,896]{1,0:T(8,128)(2,1)S(1)} %get-tuple-element.25.refs_0_), channel_id=1, source_target_pairs={{0,6},{1,7},{2,0},{3,1},{4,2},{5,3},{6,4},{7,5},{8,14},{9,15},{10,... | collective-permute-start | bytes 172040 | tf_op jit(solution)/shard_map/ppermute | solution.py:217
  18.8 1.0 %collective-permute-start.5 = (bf16[32,896]{1,0:T(8,128)(2,1)S(1)}, bf16[32,896]{1,0:T(8,128)(2,1)S(1)}, u32[]{:S(2)}, u32[]{:S(2)}) collective-permute-start(bf16[32,896]{1,0:T(8,128)(2,1)S(1)} %get-tuple-element.25.refs_0_), channel_id=1, source_target_pairs={{0,2},{1,3},{2,4},{3,5},{4,6},{5,7},{6,0},{7,1},{8,10},{9,11},{10,... | collective-permute-start | bytes 172040 | tf_op jit(solution)/shard_map/ppermute | solution.py:217
  19.8 1.8 %collective-permute-start.10 = (bf16[32,896]{1,0:T(8,128)(2,1)S(1)}, bf16[32,896]{1,0:T(8,128)(2,1)S(1)}, u32[]{:S(2)}, u32[]{:S(2)}) collective-permute-start(bf16[32,896]{1,0:T(8,128)(2,1)S(1)} %get-tuple-element.26), channel_id=1, source_target_pairs={{0,7},{1,6},{2,1},{3,0},{4,3},{5,2},{6,5},{7,4},{8,15},{9,14},{10,... | collective-permute-start | bytes 172040 | tf_op jit(solution)/shard_map/ppermute | solution.py:217
  21.6 1.8 %collective-permute-start.8 = (bf16[32,896]{1,0:T(8,128)(2,1)S(1)}, bf16[32,896]{1,0:T(8,128)(2,1)S(1)}, u32[]{:S(2)}, u32[]{:S(2)}) collective-permute-start(bf16[32,896]{1,0:T(8,128)(2,1)S(1)} %get-tuple-element.26), channel_id=1, source_target_pairs={{0,5},{1,4},{2,7},{3,6},{4,1},{5,0},{6,3},{7,2},{8,13},{9,12},{10,... | collective-permute-start | bytes 172040 | tf_op jit(solution)/shard_map/ppermute | solution.py:217
  23.5 0.7 %collective-permute-done.7.refs_4_ = bf16[32,896]{1,0:T(8,128)(2,1)S(1)} collective-permute-done((bf16[32,896]{1,0:T(8,128)(2,1)S(1)}, bf16[32,896]{1,0:T(8,128)(2,1)S(1)}, u32[]{:S(2)}, u32[]{:S(2)}) %collective-permute-start.7) | collective-permute-done | bytes 57376 | tf_op jit(solution)/shard_map/ppermute | solution.py:217
  24.2 1.5 %collective-permute-start.6 = (bf16[32,896]{1,0:T(8,128)(2,1)S(1)}, bf16[32,896]{1,0:T(8,128)(2,1)S(1)}, u32[]{:S(2)}, u32[]{:S(2)}) collective-permute-start(bf16[32,896]{1,0:T(8,128)(2,1)S(1)} %get-tuple-element.26), channel_id=1, source_target_pairs={{0,3},{1,2},{2,5},{3,4},{4,7},{5,6},{6,1},{7,0},{8,11},{9,10},{10,... | collective-permute-start | bytes 172040 | tf_op jit(solution)/shard_map/ppermute | solution.py:217
  25.7 0.0 collective-permute-done.5.refs_2_
  25.7 0.0 collective-permute-start.4
  25.7 0.1 collective-permute-done.10.refs_7_
  25.8 2.3 %collective-permute-done.8.refs_5_ = bf16[32,896]{1,0:T(8,128)(2,1)S(1)} collective-permute-done((bf16[32,896]{1,0:T(8,128)(2,1)S(1)}, bf16[32,896]{1,0:T(8,128)(2,1)S(1)}, u32[]{:S(2)}, u32[]{:S(2)}) %collective-permute-start.8) | collective-permute-done | bytes 57376 | tf_op jit(solution)/shard_map/ppermute | solution.py:217
  28.1 1.5 %collective-permute-done.6.refs_3_ = bf16[32,896]{1,0:T(8,128)(2,1)S(1)} collective-permute-done((bf16[32,896]{1,0:T(8,128)(2,1)S(1)}, bf16[32,896]{1,0:T(8,128)(2,1)S(1)}, u32[]{:S(2)}, u32[]{:S(2)}) %collective-permute-start.6) | collective-permute-done | bytes 57376 | tf_op jit(solution)/shard_map/ppermute | solution.py:217
  29.6 0.0 collective-permute-done.4.refs_1_
  29.6 0.0 collective-permute-done.3.sib_ref
  29.6 1.7 %copy-done.7 = bf16[12,128,768]{2,1,0:T(8,128)(2,1)S(1)} copy-done((bf16[12,128,768]{2,1,0:T(8,128)(2,1)S(1)}, bf16[12,128,768]{2,1,0:T(8,128)(2,1)}, u32[]{:S(2)}) %copy-start.7) | copy-done | bytes 2359320
  31.3 1.3 %copy-done.8 = bf16[768,768]{1,0:T(8,128)(2,1)S(1)} copy-done((bf16[768,768]{1,0:T(8,128)(2,1)S(1)}, bf16[768,768]{1,0:T(8,128)(2,1)}, u32[]{:S(2)}) %copy-start.8) | copy-done | bytes 1179672
  32.6 3.9 %fock.1 = (bf16[32,768]{1,0:T(8,128)(2,1)S(1)}, bf16[32,768]{1,0:T(8,128)(2,1)S(1)}, bf16[32,768]{1,0:T(8,128)(2,1)S(1)}, bf16[32,768]{1,0:T(8,128)(2,1)S(1)}, b...) custom-call(s32[1]{0:T(128)} %bitcast.1.blk_ref, ...), custom_call_target="tpu_custom_call" | custom-call | flops 2717908992 | bytes 6750208 | tf_op jit(solution)/shard_map/fock/pallas_call | solution.py:187
  36.5 0.1 collective-permute-start.11
  36.6 2.0 %collective-permute-start.13 = (bf16[32,768]{1,0:T(8,128)(2,1)S(1)}, bf16[32,768]{1,0:T(8,128)(2,1)S(1)}, u32[]{:S(2)}, u32[]{:S(2)}) collective-permute-start(bf16[32,768]{1,0:T(8,128)(2,1)S(1)} %get-tuple-element.30), channel_id=1, source_target_pairs={{0,3},{1,2},{2,5},{3,4},{4,7},{5,6},{6,1},{7,0},{8,11},{9,10},{10,... | collective-permute-start | bytes 147464 | tf_op jit(solution)/shard_map/ppermute | solution.py:217
  38.7 2.1 %collective-permute-start.14 = (bf16[32,768]{1,0:T(8,128)(2,1)S(1)}, bf16[32,768]{1,0:T(8,128)(2,1)S(1)}, u32[]{:S(2)}, u32[]{:S(2)}) collective-permute-start(bf16[32,768]{1,0:T(8,128)(2,1)S(1)} %get-tuple-element.31), channel_id=1, source_target_pairs={{0,4},{1,5},{2,6},{3,7},{4,0},{5,1},{6,2},{7,3},{8,12},{9,13},{10,... | collective-permute-start | bytes 147464 | tf_op jit(solution)/shard_map/ppermute | solution.py:217
  40.8 0.5 collective-permute-start.15
  41.3 1.6 %collective-permute-start.16 = (bf16[32,768]{1,0:T(8,128)(2,1)S(1)}, bf16[32,768]{1,0:T(8,128)(2,1)S(1)}, u32[]{:S(2)}, u32[]{:S(2)}) collective-permute-start(bf16[32,768]{1,0:T(8,128)(2,1)S(1)} %get-tuple-element.33), channel_id=1, source_target_pairs={{0,6},{1,7},{2,0},{3,1},{4,2},{5,3},{6,4},{7,5},{8,14},{9,15},{10,... | collective-permute-start | bytes 147464 | tf_op jit(solution)/shard_map/ppermute | solution.py:217
  42.9 0.1 collective-permute-done.12.refs_2_
  43.0 1.6 %collective-permute-start.17 = (bf16[32,768]{1,0:T(8,128)(2,1)S(1)}, bf16[32,768]{1,0:T(8,128)(2,1)S(1)}, u32[]{:S(2)}, u32[]{:S(2)}) collective-permute-start(bf16[32,768]{1,0:T(8,128)(2,1)S(1)} %get-tuple-element.34), channel_id=1, source_target_pairs={{0,7},{1,6},{2,1},{3,0},{4,3},{5,2},{6,5},{7,4},{8,15},{9,14},{10,... | collective-permute-start | bytes 147464 | tf_op jit(solution)/shard_map/ppermute | solution.py:217
  44.6 2.2 %collective-permute-done.14.refs_4_ = bf16[32,768]{1,0:T(8,128)(2,1)S(1)} collective-permute-done((bf16[32,768]{1,0:T(8,128)(2,1)S(1)}, bf16[32,768]{1,0:T(8,128)(2,1)S(1)}, u32[]{:S(2)}, u32[]{:S(2)}) %collective-permute-start.14) | collective-permute-done | bytes 49184 | tf_op jit(solution)/shard_map/ppermute | solution.py:217
  46.9 1.0 %collective-permute-done.15.refs_5_ = bf16[32,768]{1,0:T(8,128)(2,1)S(1)} collective-permute-done((bf16[32,768]{1,0:T(8,128)(2,1)S(1)}, bf16[32,768]{1,0:T(8,128)(2,1)S(1)}, u32[]{:S(2)}, u32[]{:S(2)}) %collective-permute-start.15) | collective-permute-done | bytes 49184 | tf_op jit(solution)/shard_map/ppermute | solution.py:217
  47.8 1.0 %collective-permute-done.17.refs_7_ = bf16[32,768]{1,0:T(8,128)(2,1)S(1)} collective-permute-done((bf16[32,768]{1,0:T(8,128)(2,1)S(1)}, bf16[32,768]{1,0:T(8,128)(2,1)S(1)}, u32[]{:S(2)}, u32[]{:S(2)}) %collective-permute-start.17) | collective-permute-done | bytes 49184 | tf_op jit(solution)/shard_map/ppermute | solution.py:217
  48.8 0.1 sum.1.refs_0_
  48.8 1.5 %collective-permute-start.20 = (bf16[64,768]{1,0:T(8,128)(2,1)S(1)}, bf16[64,768]{1,0:T(8,128)(2,1)S(1)}, u32[]{:S(2)}, u32[]{:S(2)}) collective-permute-start(bf16[64,768]{1,0:T(8,128)(2,1)S(1)} %sum.1.refs_0_), channel_id=1, source_target_pairs={{0,24},{8,0},{16,8},{24,16},{1,25},{9,1},{17,9},{25,17},{2,26},{10... | collective-permute-start | bytes 294920 | tf_op jit(solution)/shard_map/ppermute | solution.py:212
  50.3 1.5 %collective-permute-start.19 = (bf16[64,768]{1,0:T(8,128)(2,1)S(1)}, bf16[64,768]{1,0:T(8,128)(2,1)S(1)}, u32[]{:S(2)}, u32[]{:S(2)}) collective-permute-start(bf16[64,768]{1,0:T(8,128)(2,1)S(1)} %sum.1.refs_0_), channel_id=1, source_target_pairs={{0,16},{8,24},{16,0},{24,8},{1,17},{9,25},{17,1},{25,9},{2,18},{10... | collective-permute-start | bytes 294920 | tf_op jit(solution)/shard_map/ppermute | solution.py:212
  51.8 0.6 %collective-permute-start.18 = (bf16[64,768]{1,0:T(8,128)(2,1)S(1)}, bf16[64,768]{1,0:T(8,128)(2,1)S(1)}, u32[]{:S(2)}, u32[]{:S(2)}) collective-permute-start(bf16[64,768]{1,0:T(8,128)(2,1)S(1)} %sum.1.refs_0_), channel_id=1, source_target_pairs={{0,8},{8,16},{16,24},{24,0},{1,9},{9,17},{17,25},{25,1},{2,10},{10... | collective-permute-start | bytes 294920 | tf_op jit(solution)/shard_map/ppermute | solution.py:212
  52.4 1.3 %collective-permute-done.20.refs_3_ = bf16[64,768]{1,0:T(8,128)(2,1)S(1)} collective-permute-done((bf16[64,768]{1,0:T(8,128)(2,1)S(1)}, bf16[64,768]{1,0:T(8,128)(2,1)S(1)}, u32[]{:S(2)}, u32[]{:S(2)}) %collective-permute-start.20) | collective-permute-done | bytes 98336 | tf_op jit(solution)/shard_map/ppermute | solution.py:212
  53.7 2.4 %collective-permute-done.19.refs_2_ = bf16[64,768]{1,0:T(8,128)(2,1)S(1)} collective-permute-done((bf16[64,768]{1,0:T(8,128)(2,1)S(1)}, bf16[64,768]{1,0:T(8,128)(2,1)S(1)}, u32[]{:S(2)}, u32[]{:S(2)}) %collective-permute-start.19) | collective-permute-done | bytes 98336 | tf_op jit(solution)/shard_map/ppermute | solution.py:212
  56.1 1.3 %collective-permute-done.18.refs_1_ = bf16[64,768]{1,0:T(8,128)(2,1)S(1)} collective-permute-done((bf16[64,768]{1,0:T(8,128)(2,1)S(1)}, bf16[64,768]{1,0:T(8,128)(2,1)S(1)}, u32[]{:S(2)}, u32[]{:S(2)}) %collective-permute-start.18) | collective-permute-done | bytes 98336 | tf_op jit(solution)/shard_map/ppermute | solution.py:212
  57.4 1.5 %deal.1 = bf16[16,8,768]{2,1,0:T(8,128)(2,1)} custom-call(s32[1]{0:T(128)} %bitcast.me_ref, s32[8]{0:T(128)S(1)} %copy-done.4, f32[8]{0:T(128)S(1)} %copy-done.6, f32[8,128]{1,0:T(8,128)S(1)} %get-tuple-element.24.total_ref, bf16[64,768]{1,0:T(8,128)(2,1)S(1)} %sum.1.refs_0_, bf16[64,768]{1,0:T(8,128)(2,1)S(1)} %collective-permute-done.18.refs_1_, ...), custom_call_target="tpu_custom_call" | custom-call | bytes 593920 | tf_op jit(solution)/shard_map/deal/pallas_call | solution.py:187
  (17 shorter events, 0.0 us)
Async XLA Ops:
  0.0 29.6 %collective-permute-start.3 = (bf16[12,128,768]{2,1,0:T(8,128)(2,1)}, bf16[12,128,768]{2,1,0:T(8,128)(2,1)S(1)}, u32[]{:S(2)}, u32[]{:S(2)}) collective-permute-start(bf16[12,128,768]{2,1,0:T(8,128)(2,1)} %own_ref.1), channel_id=1, source_target_pairs={{0,1},{1,0},{2,3},{3,2},{4,5},{5,4},{6,7},{7,6},{8,9},{9,8},{10,11... | collective-permute-start | bytes 7077896 | tf_op jit(solution)/shard_map/ppermute | solution.py:217
  0.5 0.9 %copy-start = (bf16[16,8,768]{2,1,0:T(8,128)(2,1)S(1)}, bf16[16,8,768]{2,1,0:T(8,128)(2,1)}, u32[]{:S(2)}) copy-start(bf16[16,8,768]{2,1,0:T(8,128)(2,1)} %walkers_ref.1) | copy-start | bytes 589828
  1.4 0.7 %copy-start.2 = (f32[8,12]{1,0:T(8,128)S(1)}, f32[8,12]{1,0:T(8,128)}, u32[]{:S(2)}) copy-start(f32[8,12]{1,0:T(8,128)} %fields_ref.1) | copy-start | bytes 1156
  2.1 0.7 %copy-start.3 = (s32[8]{0:T(128)S(1)}, s32[8]{0:T(128)}, u32[]{:S(2)}) copy-start(s32[8]{0:T(128)} %target_ref.3) | copy-start | bytes 100
  2.7 0.7 %copy-start.5 = (f32[8]{0:T(128)S(1)}, f32[8]{0:T(128)}, u32[]{:S(2)}) copy-start(f32[8]{0:T(128)} %weights_ref.3) | copy-start | bytes 100
  4.2 7.5 %collective-permute-start = (bf16[64,896]{1,0:T(8,128)(2,1)S(1)}, bf16[64,896]{1,0:T(8,128)(2,1)S(1)}, u32[]{:S(2)}, u32[]{:S(2)}) collective-permute-start(bf16[64,896]{1,0:T(8,128)(2,1)S(1)} %get-tuple-element.21), channel_id=1, source_target_pairs={{0,8},{8,16},{16,24},{24,0},{1,9},{9,17},{17,25},{25,1},{2,10},{10... | collective-permute-start | bytes 344072 | tf_op jit(solution)/shard_map/ppermute | solution.py:212
  6.7 7.2 %collective-permute-start.1 = (bf16[64,896]{1,0:T(8,128)(2,1)S(1)}, bf16[64,896]{1,0:T(8,128)(2,1)S(1)}, u32[]{:S(2)}, u32[]{:S(2)}) collective-permute-start(bf16[64,896]{1,0:T(8,128)(2,1)S(1)} %get-tuple-element.22), channel_id=1, source_target_pairs={{0,16},{8,24},{16,0},{24,8},{1,17},{9,25},{17,1},{25,9},{2,18},{10... | collective-permute-start | bytes 344072 | tf_op jit(solution)/shard_map/ppermute | solution.py:212
  8.2 6.0 %collective-permute-start.2 = (bf16[64,896]{1,0:T(8,128)(2,1)S(1)}, bf16[64,896]{1,0:T(8,128)(2,1)S(1)}, u32[]{:S(2)}, u32[]{:S(2)}) collective-permute-start(bf16[64,896]{1,0:T(8,128)(2,1)S(1)} %get-tuple-element.23), channel_id=1, source_target_pairs={{0,24},{8,0},{16,8},{24,16},{1,25},{9,1},{17,9},{25,17},{2,26},{10... | collective-permute-start | bytes 344072 | tf_op jit(solution)/shard_map/ppermute | solution.py:212
  14.2 0.8 %copy-start.1 = (f32[12,768]{1,0:T(8,128)S(1)}, f32[12,768]{1,0:T(8,128)}, u32[]{:S(2)}) copy-start(f32[12,768]{1,0:T(8,128)} %diag_ref.1) | copy-start | bytes 110596
  15.2 6.5 %collective-permute-start.9 = (bf16[32,896]{1,0:T(8,128)(2,1)S(1)}, bf16[32,896]{1,0:T(8,128)(2,1)S(1)}, u32[]{:S(2)}, u32[]{:S(2)}) collective-permute-start(bf16[32,896]{1,0:T(8,128)(2,1)S(1)} %get-tuple-element.25.refs_0_), channel_id=1, source_target_pairs={{0,6},{1,7},{2,0},{3,1},{4,2},{5,3},{6,4},{7,5},{8,14},{9,15},{10,... | collective-permute-start | bytes 172040 | tf_op jit(solution)/shard_map/ppermute | solution.py:217
  18.8 5.4 %collective-permute-start.7 = (bf16[32,896]{1,0:T(8,128)(2,1)S(1)}, bf16[32,896]{1,0:T(8,128)(2,1)S(1)}, u32[]{:S(2)}, u32[]{:S(2)}) collective-permute-start(bf16[32,896]{1,0:T(8,128)(2,1)S(1)} %get-tuple-element.25.refs_0_), channel_id=1, source_target_pairs={{0,4},{1,5},{2,6},{3,7},{4,0},{5,1},{6,2},{7,3},{8,12},{9,13},{10,... | collective-permute-start | bytes 172040 | tf_op jit(solution)/shard_map/ppermute | solution.py:217
  18.8 6.9 %collective-permute-start.5 = (bf16[32,896]{1,0:T(8,128)(2,1)S(1)}, bf16[32,896]{1,0:T(8,128)(2,1)S(1)}, u32[]{:S(2)}, u32[]{:S(2)}) collective-permute-start(bf16[32,896]{1,0:T(8,128)(2,1)S(1)} %get-tuple-element.25.refs_0_), channel_id=1, source_target_pairs={{0,2},{1,3},{2,4},{3,5},{4,6},{5,7},{6,0},{7,1},{8,10},{9,11},{10,... | collective-permute-start | bytes 172040 | tf_op jit(solution)/shard_map/ppermute | solution.py:217
  19.8 37.5 %copy-start.4 = (s32[8]{0:T(128)S(1)}, s32[8]{0:T(128)}, u32[]{:S(2)}) copy-start(s32[8]{0:T(128)} %target_ref.3) | copy-start | bytes 100
  19.8 37.5 %copy-start.6 = (f32[8]{0:T(128)S(1)}, f32[8]{0:T(128)}, u32[]{:S(2)}) copy-start(f32[8]{0:T(128)} %weights_ref.3) | copy-start | bytes 100
  19.8 6.0 %collective-permute-start.10 = (bf16[32,896]{1,0:T(8,128)(2,1)S(1)}, bf16[32,896]{1,0:T(8,128)(2,1)S(1)}, u32[]{:S(2)}, u32[]{:S(2)}) collective-permute-start(bf16[32,896]{1,0:T(8,128)(2,1)S(1)} %get-tuple-element.26), channel_id=1, source_target_pairs={{0,7},{1,6},{2,1},{3,0},{4,3},{5,2},{6,5},{7,4},{8,15},{9,14},{10,... | collective-permute-start | bytes 172040 | tf_op jit(solution)/shard_map/ppermute | solution.py:217
  21.6 6.4 %collective-permute-start.8 = (bf16[32,896]{1,0:T(8,128)(2,1)S(1)}, bf16[32,896]{1,0:T(8,128)(2,1)S(1)}, u32[]{:S(2)}, u32[]{:S(2)}) collective-permute-start(bf16[32,896]{1,0:T(8,128)(2,1)S(1)} %get-tuple-element.26), channel_id=1, source_target_pairs={{0,5},{1,4},{2,7},{3,6},{4,1},{5,0},{6,3},{7,2},{8,13},{9,12},{10,... | collective-permute-start | bytes 172040 | tf_op jit(solution)/shard_map/ppermute | solution.py:217
  24.2 5.4 %collective-permute-start.6 = (bf16[32,896]{1,0:T(8,128)(2,1)S(1)}, bf16[32,896]{1,0:T(8,128)(2,1)S(1)}, u32[]{:S(2)}, u32[]{:S(2)}) collective-permute-start(bf16[32,896]{1,0:T(8,128)(2,1)S(1)} %get-tuple-element.26), channel_id=1, source_target_pairs={{0,3},{1,2},{2,5},{3,4},{4,7},{5,6},{6,1},{7,0},{8,11},{9,10},{10,... | collective-permute-start | bytes 172040 | tf_op jit(solution)/shard_map/ppermute | solution.py:217
  25.7 3.9 %collective-permute-start.4 = (bf16[32,896]{1,0:T(8,128)(2,1)S(1)}, bf16[32,896]{1,0:T(8,128)(2,1)S(1)}, u32[]{:S(2)}, u32[]{:S(2)}) collective-permute-start(bf16[32,896]{1,0:T(8,128)(2,1)S(1)} %get-tuple-element.26), channel_id=1, source_target_pairs={{0,1},{1,0},{2,3},{3,2},{4,5},{5,4},{6,7},{7,6},{8,9},{9,8},{10,11... | collective-permute-start | bytes 172040 | tf_op jit(solution)/shard_map/ppermute | solution.py:217
  29.6 1.7 %copy-start.7 = (bf16[12,128,768]{2,1,0:T(8,128)(2,1)S(1)}, bf16[12,128,768]{2,1,0:T(8,128)(2,1)}, u32[]{:S(2)}) copy-start(bf16[12,128,768]{2,1,0:T(8,128)(2,1)} %own_ref.1) | copy-start | bytes 7077892
  31.3 1.3 %copy-start.8 = (bf16[768,768]{1,0:T(8,128)(2,1)S(1)}, bf16[768,768]{1,0:T(8,128)(2,1)}, u32[]{:S(2)}) copy-start(bf16[768,768]{1,0:T(8,128)(2,1)} %body_ref.1) | copy-start | bytes 3538948
  36.5 4.8 %collective-permute-start.11 = (bf16[32,768]{1,0:T(8,128)(2,1)S(1)}, bf16[32,768]{1,0:T(8,128)(2,1)S(1)}, u32[]{:S(2)}, u32[]{:S(2)}) collective-permute-start(bf16[32,768]{1,0:T(8,128)(2,1)S(1)} %get-tuple-element.28), channel_id=1, source_target_pairs={{0,1},{1,0},{2,3},{3,2},{4,5},{5,4},{6,7},{7,6},{8,9},{9,8},{10,11... | collective-permute-start | bytes 147464 | tf_op jit(solution)/shard_map/ppermute | solution.py:217
  36.6 6.4 %collective-permute-start.12 = (bf16[32,768]{1,0:T(8,128)(2,1)S(1)}, bf16[32,768]{1,0:T(8,128)(2,1)S(1)}, u32[]{:S(2)}, u32[]{:S(2)}) collective-permute-start(bf16[32,768]{1,0:T(8,128)(2,1)S(1)} %get-tuple-element.29), channel_id=1, source_target_pairs={{0,2},{1,3},{2,4},{3,5},{4,6},{5,7},{6,0},{7,1},{8,10},{9,11},{10,... | collective-permute-start | bytes 147464 | tf_op jit(solution)/shard_map/ppermute | solution.py:217
  36.6 8.0 %collective-permute-start.13 = (bf16[32,768]{1,0:T(8,128)(2,1)S(1)}, bf16[32,768]{1,0:T(8,128)(2,1)S(1)}, u32[]{:S(2)}, u32[]{:S(2)}) collective-permute-start(bf16[32,768]{1,0:T(8,128)(2,1)S(1)} %get-tuple-element.30), channel_id=1, source_target_pairs={{0,3},{1,2},{2,5},{3,4},{4,7},{5,6},{6,1},{7,0},{8,11},{9,10},{10,... | collective-permute-start | bytes 147464 | tf_op jit(solution)/shard_map/ppermute | solution.py:217
  38.7 8.2 %collective-permute-start.14 = (bf16[32,768]{1,0:T(8,128)(2,1)S(1)}, bf16[32,768]{1,0:T(8,128)(2,1)S(1)}, u32[]{:S(2)}, u32[]{:S(2)}) collective-permute-start(bf16[32,768]{1,0:T(8,128)(2,1)S(1)} %get-tuple-element.31), channel_id=1, source_target_pairs={{0,4},{1,5},{2,6},{3,7},{4,0},{5,1},{6,2},{7,3},{8,12},{9,13},{10,... | collective-permute-start | bytes 147464 | tf_op jit(solution)/shard_map/ppermute | solution.py:217
  40.8 7.0 %collective-permute-start.15 = (bf16[32,768]{1,0:T(8,128)(2,1)S(1)}, bf16[32,768]{1,0:T(8,128)(2,1)S(1)}, u32[]{:S(2)}, u32[]{:S(2)}) collective-permute-start(bf16[32,768]{1,0:T(8,128)(2,1)S(1)} %get-tuple-element.32), channel_id=1, source_target_pairs={{0,5},{1,4},{2,7},{3,6},{4,1},{5,0},{6,3},{7,2},{8,13},{9,12},{10,... | collective-permute-start | bytes 147464 | tf_op jit(solution)/shard_map/ppermute | solution.py:217
  41.3 6.5 %collective-permute-start.16 = (bf16[32,768]{1,0:T(8,128)(2,1)S(1)}, bf16[32,768]{1,0:T(8,128)(2,1)S(1)}, u32[]{:S(2)}, u32[]{:S(2)}) collective-permute-start(bf16[32,768]{1,0:T(8,128)(2,1)S(1)} %get-tuple-element.33), channel_id=1, source_target_pairs={{0,6},{1,7},{2,0},{3,1},{4,2},{5,3},{6,4},{7,5},{8,14},{9,15},{10,... | collective-permute-start | bytes 147464 | tf_op jit(solution)/shard_map/ppermute | solution.py:217
  43.0 5.8 %collective-permute-start.17 = (bf16[32,768]{1,0:T(8,128)(2,1)S(1)}, bf16[32,768]{1,0:T(8,128)(2,1)S(1)}, u32[]{:S(2)}, u32[]{:S(2)}) collective-permute-start(bf16[32,768]{1,0:T(8,128)(2,1)S(1)} %get-tuple-element.34), channel_id=1, source_target_pairs={{0,7},{1,6},{2,1},{3,0},{4,3},{5,2},{6,5},{7,4},{8,15},{9,14},{10,... | collective-permute-start | bytes 147464 | tf_op jit(solution)/shard_map/ppermute | solution.py:217
  48.8 4.9 %collective-permute-start.20 = (bf16[64,768]{1,0:T(8,128)(2,1)S(1)}, bf16[64,768]{1,0:T(8,128)(2,1)S(1)}, u32[]{:S(2)}, u32[]{:S(2)}) collective-permute-start(bf16[64,768]{1,0:T(8,128)(2,1)S(1)} %sum.1.refs_0_), channel_id=1, source_target_pairs={{0,24},{8,0},{16,8},{24,16},{1,25},{9,1},{17,9},{25,17},{2,26},{10... | collective-permute-start | bytes 294920 | tf_op jit(solution)/shard_map/ppermute | solution.py:212
  50.3 5.8 %collective-permute-start.19 = (bf16[64,768]{1,0:T(8,128)(2,1)S(1)}, bf16[64,768]{1,0:T(8,128)(2,1)S(1)}, u32[]{:S(2)}, u32[]{:S(2)}) collective-permute-start(bf16[64,768]{1,0:T(8,128)(2,1)S(1)} %sum.1.refs_0_), channel_id=1, source_target_pairs={{0,16},{8,24},{16,0},{24,8},{1,17},{9,25},{17,1},{25,9},{2,18},{10... | collective-permute-start | bytes 294920 | tf_op jit(solution)/shard_map/ppermute | solution.py:212
  51.8 5.5 %collective-permute-start.18 = (bf16[64,768]{1,0:T(8,128)(2,1)S(1)}, bf16[64,768]{1,0:T(8,128)(2,1)S(1)}, u32[]{:S(2)}, u32[]{:S(2)}) collective-permute-start(bf16[64,768]{1,0:T(8,128)(2,1)S(1)} %sum.1.refs_0_), channel_id=1, source_target_pairs={{0,8},{8,16},{16,24},{24,0},{1,9},{9,17},{17,25},{25,1},{2,10},{10... | collective-permute-start | bytes 294920 | tf_op jit(solution)/shard_map/ppermute | solution.py:212

commit v3 on v2

v3 whole, which is shorter than its diff:
```python
import functools
import jax
import jax.numpy as jnp
from jax import lax
from jax.experimental import pallas as pl
from jax.experimental.pallas import tpu as pltpu
from jax.sharding import PartitionSpec as P

F32 = jnp.float32
BF16 = jnp.bfloat16
LANES = 128


def terms(value, count):
    out = []
    for _ in range(count):
        term = value.astype(BF16).astype(F32)
        out.append(term)
        value = value - term
    return out


def tail_blocks(count, slab):
    return -(-count // slab)


def write_tail(out_ref, start, lines):
    slab = out_ref.shape[0]
    for b in range(tail_blocks(lines.shape[0], slab)):
        part = lines[b * slab : (b + 1) * slab]
        if part.shape[0] < slab:
            part = jnp.concatenate([part, jnp.zeros((slab - part.shape[0], LANES), F32)], axis=0)
        out_ref[:, start + b * LANES : start + (b + 1) * LANES] = part.astype(BF16)


def read_tail(ref, start, count):
    parts = [ref[:, c : c + LANES].astype(F32) for c in range(start, ref.shape[1], LANES)]
    whole = parts[0] if len(parts) == 1 else jnp.concatenate(parts, axis=0)
    return whole[0:count]


def wide_mask(line, width):
    return jnp.concatenate([line] * (width // LANES), axis=1) > 0


def stage_kernel(*refs):
    count = (len(refs) - 1) // 2
    sems = refs[-1]
    copies = [pltpu.make_async_copy(refs[i], refs[count + i], sems.at[i]) for i in range(count)]
    for copy in copies:
        copy.start()
    for copy in copies:
        copy.wait()


def route_kernel(keep, cap, me_ref, target_any, weights_any, walkers_any, fields_any, *refs):
    *outs, target_ref, weights_ref, walkers_ref, fields_ref, wide, blocks, lines, sems = refs
    pairs = (
        (walkers_any, walkers_ref),
        (target_any, target_ref),
        (weights_any, weights_ref),
        (fields_any, fields_ref),
    )
    copies = [pltpu.make_async_copy(a, b, sems.at[i]) for i, (a, b) in enumerate(pairs)]
    for copy in copies:
        copy.start()
    rows, slots, orbitals = walkers_ref.shape
    vec_count = fields_ref.shape[1]
    groups = len(outs)
    live = groups * keep
    blocks[...] = jnp.zeros(blocks.shape, F32)
    lines[...] = jnp.zeros(lines.shape, F32)
    for copy in copies:
        copy.wait()
    wide[...] = walkers_ref[...].astype(F32)
    weight = F32(0.0)
    lane = lax.broadcasted_iota(jnp.int32, (1, LANES), 1)
    for slot in range(slots):
        t = target_ref[slot]
        alive = t < live
        weight = weight + jnp.where(alive, weights_ref[slot], F32(0.0))
        turn = lax.div(t, groups)
        at = jnp.where(alive, lax.rem(t, groups) * cap + lax.rem(turn, cap), groups * cap)
        blocks[at] = wide[:, slot, :]
        lines[at] = jnp.where(lane == LANES - 1, (turn + 1).astype(F32), F32(0.0))
        lines[at, :, 0:vec_count] = fields_ref[slot : slot + 1, :]
    sums = terms(jnp.full((1, LANES), weight, F32), 3)
    for s, out in enumerate(outs):
        base = lax.rem(me_ref[0] + s, groups) * cap
        out[:, 0:orbitals] = jnp.concatenate([blocks[base + k] for k in range(cap)], axis=0).astype(BF16)
        line = jnp.concatenate([lines[base + k] for k in range(cap)], axis=0)
        write_tail(out, orbitals, jnp.concatenate(terms(line, 3) + sums, axis=0))


def merge_kernel(keep, cap, groups, core_ref, diag_ref, *refs):
    ins, (same_ref, other_ref, weight_ref, pick_ref) = refs[:groups], refs[groups:]
    vec_count, orbitals = diag_ref.shape
    half = keep // 2
    rows = ins[0].shape[0] // cap
    slab = half * rows
    weight = jnp.zeros((1, LANES), F32)
    walker = [jnp.zeros((rows, orbitals), F32)] * keep
    line = [jnp.zeros((1, LANES), F32)] * keep
    for s, ref in enumerate(ins):
        tail = read_tail(ref, orbitals, 3 * cap + 3)
        weight = weight + (tail[3 * cap : 3 * cap + 1] + tail[3 * cap + 1 : 3 * cap + 2] + tail[3 * cap + 2 :])
        for k in range(cap):
            fields = tail[k : k + 1] + tail[cap + k : cap + k + 1] + tail[2 * cap + k : 2 * cap + k + 1]
            flag = jnp.broadcast_to(fields[:, LANES - 1 : LANES], (1, LANES))
            block = ref[k * rows : (k + 1) * rows, 0:orbitals].astype(F32)
            for m in range(k, keep, cap):
                mine = jnp.where(flag == m + 1, F32(1.0), F32(0.0))
                pick_ref[s * keep + m : s * keep + m + 1, :] = mine
                walker[m] = jnp.where(wide_mask(mine, orbitals), block, walker[m])
                line[m] = jnp.where(mine > 0, fields, line[m])
    weight_ref[...] = jnp.broadcast_to(weight, weight_ref.shape)
    fields = jnp.concatenate(line, axis=0)
    exponent = fields[:, 0:1] * diag_ref[0:1, :]
    for g in range(1, vec_count):
        exponent = exponent + fields[:, g : g + 1] * diag_ref[g : g + 1, :]
    first = core_ref[0] == 0
    high, low = terms(exponent, 2)
    for out, order in ((same_ref, (0, 1)), (other_ref, (1, 0))):
        for k in range(half):
            picked = jnp.where(first, walker[order[0] * half + k], walker[order[1] * half + k])
            out[k * rows : (k + 1) * rows, 0:orbitals] = picked.astype(BF16)
        pieces = []
        for term in (high, low):
            for k in range(half):
                a, b = order[0] * half + k, order[1] * half + k
                picked = jnp.where(first, term[a : a + 1], term[b : b + 1])
                pieces += [picked[:, c : c + LANES] for c in range(0, orbitals, LANES)]
        write_tail(out, orbitals, jnp.concatenate(pieces, axis=0))


def hops(n):
    return [(s, e) for s in range(n // 2) for e in range(2)]


def partner(blk, s, e, n, sign):
    chip = lax.rem(lax.div(blk, 2) + (s if sign > 0 else n // 2 - s), n // 2)
    core = lax.rem(blk, 2)
    return 2 * chip + (core if e == 0 else 1 - core)


def fock_kernel(n, half, blk_ref, body_ref, own_ref, sib_ref, *refs):
    ins, outs = refs[:n], refs[n : 2 * n]
    prop, turned, coup, result = refs[2 * n :]
    vec_count, occupied, orbitals = own_ref.shape
    slab = outs[0].shape[0]
    rows = slab // half
    blocks = orbitals // LANES
    blk = blk_ref[0]
    exponent = jnp.zeros((2 * half * blocks, LANES), F32)
    for ref in ins:
        exponent = exponent + read_tail(ref, orbitals, 2 * half * blocks)
    growth = jnp.exp(exponent[0 : half * blocks] + exponent[half * blocks :])
    for ref, (s, e) in zip(ins, hops(n)):
        source = partner(blk, s, e, n, -1)
        for w in range(half):
            for c in range(blocks):
                piece = ref[w * rows : (w + 1) * rows, c * LANES : (c + 1) * LANES].astype(F32)
                prop[w, source, :, c * LANES : (c + 1) * LANES] = piece * growth[w * blocks + c : w * blocks + c + 1]
    for w in range(half):
        piece = jnp.concatenate([prop[w, i] for i in range(n)], axis=0).astype(BF16)
        done = jnp.dot(piece, body_ref[...], preferred_element_type=F32)
        turned[:, w * occupied : (w + 1) * occupied] = done.T.astype(BF16)
    pair = 2 if vec_count % 2 == 0 else 1
    for c, ref in enumerate((own_ref, sib_ref)):
        for g in range(0, vec_count, pair):
            left = ref[g : g + pair].reshape(pair * occupied, orbitals)
            s = jnp.dot(left, turned[...], preferred_element_type=F32).astype(BF16)
            for k in range(pair):
                at = (c * vec_count + g + k) * occupied
                for w in range(half):
                    coup[w * occupied : (w + 1) * occupied, at : at + occupied] = s[
                        k * occupied : (k + 1) * occupied, w * occupied : (w + 1) * occupied
                    ]
    tile = 256 if orbitals % 256 == 0 else orbitals
    depth = vec_count * occupied
    for t in range(0, orbitals, tile):
        total = jnp.dot(
            coup[:, :depth],
            own_ref[:, :, t : t + tile].reshape(depth, tile),
            preferred_element_type=F32,
        )
        total = total + jnp.dot(
            coup[:, depth:],
            sib_ref[:, :, t : t + tile].reshape(depth, tile),
            preferred_element_type=F32,
        )
        for w in range(half):
            for i in range(n):
                at = w * occupied + i * rows
                result[w, i, :, t : t + tile] = total[at : at + rows]
    for out, (s, e) in zip(outs, hops(n)):
        to = partner(blk, s, e, n, 1)
        for w in range(half):
            out[w * rows : (w + 1) * rows, :] = result[w, to].astype(BF16)


def sum_kernel(n, keep, cap, groups, core_ref, pick_ref, *refs):
    ins, outs = refs[:n], refs[n:]
    slab, orbitals = ins[0].shape
    half = keep // 2
    rows = slab // half
    halves = []
    for e in range(2):
        total = ins[e][...].astype(F32)
        for ref in ins[e + 2 :: 2]:
            total = total + ref[...].astype(F32)
        halves.append(total)
    first = core_ref[0] == 0
    whole = [jnp.where(first, halves[0], halves[1]), jnp.where(first, halves[1], halves[0])]
    walker = [whole[m // half][(m % half) * rows : (m % half + 1) * rows] for m in range(keep)]
    for s, out in enumerate(outs):
        source = (groups - s) % groups
        for k in range(cap):
            value = jnp.zeros((rows, orbitals), F32)
            for m in range(k, keep, cap):
                mine = pick_ref[source * keep + m : source * keep + m + 1, :]
                value = jnp.where(wide_mask(mine, orbitals), walker[m], value)
            out[k * rows : (k + 1) * rows, :] = value.astype(BF16)


def deal_kernel(keep, cap, groups, me_ref, target_ref, weights_ref, total_ref, *refs):
    ins, (out_ref, blocks, wide) = refs[:groups], refs[groups:]
    rows, slots, orbitals = out_ref.shape
    live = groups * keep
    for s, ref in enumerate(ins):
        base = lax.rem(me_ref[0] + groups - s, groups) * cap
        for k in range(cap):
            blocks[base + k] = ref[k * rows : (k + 1) * rows, :].astype(F32)
    blocks[groups * cap] = jnp.zeros((rows, orbitals), F32)
    for slot in range(slots):
        t = target_ref[slot]
        alive = t < live
        at = jnp.where(alive, lax.rem(t, groups) * cap + lax.rem(lax.div(t, groups), cap), groups * cap)
        weight = jnp.where(alive, weights_ref[slot], F32(0.0))
        factor = jnp.full((1, LANES), weight * live, F32) / total_ref[0:1, :]
        wide[:, slot, :] = blocks[at] * factor[:, 0:1]
    out_ref[...] = wide[...].astype(BF16)


def call(kernel, outs, scalars, held, arrays, scratch, name, flops=0, vmem=40):
    smem = pl.BlockSpec(memory_space=pltpu.SMEM)
    full = pl.BlockSpec(memory_space=pltpu.VMEM)
    size = sum(x.size * x.dtype.itemsize for x in list(arrays) + list(outs))
    return pl.pallas_call(
        kernel,
        out_shape=outs,
        in_specs=[smem] * len(scalars) + [pl.BlockSpec(memory_space=pl.ANY)] * len(held) + [full] * len(arrays),
        out_specs=[full] * len(outs),
        scratch_shapes=scratch,
        compiler_params=pltpu.CompilerParams(vmem_limit_bytes=vmem * 2**20),
        cost_estimate=pl.CostEstimate(flops=flops, bytes_accessed=size, transcendentals=0),
        name=name,
    )(*scalars, *held, *arrays)


def body(walkers, one_body, fields, field_diag, chol, weights, target):
    rows, slots, orbitals = walkers.shape
    vec_count, occupied, _ = chol.shape
    n, groups = lax.axis_size("blk"), lax.axis_size("grp")
    keep = slots // 2
    half = keep // 2
    cap = -(-slots // groups)
    slab = half * rows
    shape = jax.ShapeDtypeStruct
    grp = lax.axis_index("grp").reshape(1)
    blk = lax.axis_index("blk").reshape(1)
    core = lax.rem(blk, 2)

    def to_list(x, s):
        return lax.ppermute(x, "grp", [(i, (i + s) % groups) for i in range(groups)]) if s else x

    def to_block(x, s, e):
        if not s and not e:
            return x
        return lax.ppermute(x, "blk", [(i, (2 * (i // 2 + s) + (i % 2 ^ e)) % n) for i in range(n)])

    sibling = to_block(chol, 0, 1)
    own, held_body, diag = call(
        stage_kernel,
        [shape(x.shape, x.dtype) for x in (chol, one_body, field_diag)],
        [],
        [chol, one_body, field_diag],
        [],
        [pltpu.SemaphoreType.DMA((3,))],
        "stage",
    )
    width = orbitals + tail_blocks(3 * cap + 3, cap * rows) * LANES
    routed = call(
        functools.partial(route_kernel, keep, cap),
        [shape((cap * rows, width), BF16)] * groups,
        [grp],
        [target, weights, walkers, fields],
        [],
        [
            pltpu.SMEM(target.shape, target.dtype),
            pltpu.SMEM(weights.shape, weights.dtype),
            pltpu.VMEM(walkers.shape, walkers.dtype),
            pltpu.VMEM(fields.shape, fields.dtype),
            pltpu.VMEM((rows, slots, orbitals), F32),
            pltpu.VMEM((groups * cap + 1, rows, orbitals), F32),
            pltpu.VMEM((groups * cap + 1, 1, LANES), F32),
            pltpu.SemaphoreType.DMA((4,)),
        ],
        "route",
        vmem=56,
    )
    routed = [to_list(x, s) for s, x in enumerate(routed)]
    payload = shape((slab, orbitals + tail_blocks(2 * half * (orbitals // LANES), slab) * LANES), BF16)
    same, other, weight_sum, pick = call(
        functools.partial(merge_kernel, keep, cap, groups),
        [payload, payload, shape((8, LANES), F32), shape((groups * keep, LANES), F32)],
        [core],
        [],
        [diag] + routed,
        [],
        "merge",
    )
    gathered = [to_block(other if e else same, s, e) for s, e in hops(n)]
    parts = call(
        functools.partial(fock_kernel, n, half),
        [shape((slab, orbitals), BF16)] * n,
        [blk],
        [],
        [held_body, own, sibling] + gathered,
        [
            pltpu.VMEM((half, n, rows, orbitals), F32),
            pltpu.VMEM((orbitals, half * occupied), BF16),
            pltpu.VMEM((half * occupied, 2 * vec_count * occupied), BF16),
            pltpu.VMEM((half, n, rows, orbitals), F32),
        ],
        "fock",
        flops=2 * n * slab * orbitals * (orbitals + 4 * vec_count * occupied),
    )
    parts = [to_block(x, s, e) for x, (s, e) in zip(parts, hops(n))]
    back = call(
        functools.partial(sum_kernel, n, keep, cap, groups),
        [shape((cap * rows, orbitals), BF16)] * groups,
        [core],
        [],
        [pick] + parts,
        [],
        "sum",
    )
    back = [to_list(x, s) for s, x in enumerate(back)]
    (out,) = call(
        functools.partial(deal_kernel, keep, cap, groups),
        [shape(walkers.shape, BF16)],
        [grp, target, weights],
        [],
        [weight_sum] + back,
        [pltpu.VMEM((groups * cap + 1, rows, orbitals), F32), pltpu.VMEM(walkers.shape, F32)],
        "deal",
    )
    return out


def solution(mesh):
    in_specs = (
        P("blk", "grp", None),
        P(),
        P("grp", "blk"),
        P("blk", None),
        P("blk", None, None),
        P("grp"),
        P("grp"),
    )
    out_specs = P("blk", "grp", None)
    return jax.shard_map(body, mesh=mesh, in_specs=in_specs, out_specs=out_specs, check_vma=False)
```

time: 59.1 us -> 50.6 us (0.86)
  waiting for transfers between devices: 18.4 us -> 10.7 us
  local copies, waits for them, and re-layouts: 6.66 us -> 4.03 us
  Pallas kernels: 6.32 us -> 8.06 us
    ppermute x6, waiting for transfers between devices: 9.48 us -> 2.14 us  [to_list(): lax.ppermute(x, 'grp', [(i, (i + s) % groups) for i in range(groups)])]
    unnamed x18 -> x12, local copies, waits for them, and re-layouts: 6.66 us -> 4.03 us
    pallas_call x5 -> x6, Pallas kernels: 6.32 us -> 8.06 us  [call(): pl.pallas_call(kernel, out_shape=outs, in_specs=[smem] * len(scalars) + [...]
  transfers between devices with their start and end apart: 21 -> 21, of which waited for: 14 -> 9; matrix products, arithmetic and copies ran while one was open for 0% -> 0% of each run, Pallas kernels for 2% -> 5%
where the time goes in v3:
time: 50.6 us; the launch traced here: 50.3 us
  starting transfers between devices  27.4 us (54%)
  waiting for transfers between devices  10.7 us (21%)
  Pallas kernels  8.06 us (16%)
  local copies, waits for them, and re-layouts  4.03 us (8%)
    ppermute x15, starting transfers between devices, to_block(): lax.ppermute(x, 'blk', [(i, (2 * (i // 2 + s) + (i % 2 ^ e)) % n) for i i...  18.4 us
    ppermute x6, starting transfers between devices, to_list(): lax.ppermute(x, 'grp', [(i, (i + s) % groups) for i in range(groups)])  8.97 us
    ppermute x15, waiting for transfers between devices, to_block(): lax.ppermute(x, 'blk', [(i, (2 * (i // 2 + s) + (i % 2 ^ e)) % n) for i i...  8.55 us
    pallas_call x6, Pallas kernels, call(): pl.pallas_call(kernel, out_shape=outs, in_specs=[smem] * len(scalars) + [...  8.06 us
    unnamed x12, local copies, waits for them, and re-layouts  4.03 us
    ppermute x6, waiting for transfers between devices, to_list(): lax.ppermute(x, 'grp', [(i, (i + s) % groups) for i in range(groups)])  2.14 us
  transfers between devices with their start and end apart: 21, of which 9 were waited for; matrix products, arithmetic and copies ran while one was open for 0% of the time, Pallas kernels for 5%

profile of v3, /device:TPU:0, one launch (start us, length us, event | category | flops | bytes accessed | tf_op | source)
XLA Modules:
  0.0 50.3 jit_solution(10955371337788374991)
XLA Ops:
  0.0 0.5 collective-permute-start.3
  0.5 1.8 %route.1 = (bf16[32,896]{1,0:T(8,128)(2,1)}, bf16[32,896]{1,0:T(8,128)(2,1)}, bf16[32,896]{1,0:T(8,128)(2,1)}, bf16[32,896]{1,0:T(8,128)(2,1)}) custom-call(s32[1]{0:T(128)} %bitcast.me_ref, s32[8]{0:T(128)} %target_ref.1, f32[8]{0:T(128)} %weights_ref.1, bf16[16,8,768]{2,1,0:T(8,128)(2,1)} %walkers_any.1, f32[8,12]{1,0:T(8,128)} %fields_any.1), custom_call_target="tpu_custom_call" | custom-call | bytes 229376 | tf_op jit(solution)/shard_map/route/pallas_call | solution.py:249
  2.3 2.5 %collective-permute-start = (bf16[32,896]{1,0:T(8,128)(2,1)}, bf16[32,896]{1,0:T(8,128)(2,1)S(1)}, u32[]{:S(2)}, u32[]{:S(2)}) collective-permute-start(bf16[32,896]{1,0:T(8,128)(2,1)} %get-tuple-element.30), channel_id=1, source_target_pairs={{0,8},{8,16},{16,24},{24,0},{1,9},{9,17},{17,25},{25,1},{2,10},{10... | collective-permute-start | bytes 172040 | tf_op jit(solution)/shard_map/ppermute | solution.py:275
  4.8 1.5 %collective-permute-start.1 = (bf16[32,896]{1,0:T(8,128)(2,1)}, bf16[32,896]{1,0:T(8,128)(2,1)S(1)}, u32[]{:S(2)}, u32[]{:S(2)}) collective-permute-start(bf16[32,896]{1,0:T(8,128)(2,1)} %get-tuple-element.31), channel_id=1, source_target_pairs={{0,16},{8,24},{16,0},{24,8},{1,17},{9,25},{17,1},{25,9},{2,18},{10... | collective-permute-start | bytes 172040 | tf_op jit(solution)/shard_map/ppermute | solution.py:275
  6.3 1.4 %collective-permute-start.2 = (bf16[32,896]{1,0:T(8,128)(2,1)}, bf16[32,896]{1,0:T(8,128)(2,1)S(1)}, u32[]{:S(2)}, u32[]{:S(2)}) collective-permute-start(bf16[32,896]{1,0:T(8,128)(2,1)} %get-tuple-element.32), channel_id=1, source_target_pairs={{0,24},{8,0},{16,8},{24,16},{1,25},{9,1},{17,9},{25,17},{2,26},{10... | collective-permute-start | bytes 172040 | tf_op jit(solution)/shard_map/ppermute | solution.py:275
  7.8 1.7 %copy-done = bf16[12,128,768]{2,1,0:T(8,128)(2,1)S(1)} copy-done((bf16[12,128,768]{2,1,0:T(8,128)(2,1)S(1)}, bf16[12,128,768]{2,1,0:T(8,128)(2,1)}, u32[]{:S(2)}) %copy-start) | copy-done | bytes 2359320
  9.4 1.3 %copy-done.1 = bf16[768,768]{1,0:T(8,128)(2,1)S(1)} copy-done((bf16[768,768]{1,0:T(8,128)(2,1)S(1)}, bf16[768,768]{1,0:T(8,128)(2,1)}, u32[]{:S(2)}) %copy-start.1) | copy-done | bytes 1179672
  10.7 0.8 %copy-done.3 = f32[12,768]{1,0:T(8,128)S(1)} copy-done((f32[12,768]{1,0:T(8,128)S(1)}, f32[12,768]{1,0:T(8,128)}, u32[]{:S(2)}) %copy-start.3) | copy-done | bytes 36888
  11.5 0.5 stage.1
  12.0 0.0 collective-permute-done.refs_1_
  12.0 0.0 collective-permute-done.1.refs_2_
  12.0 0.0 collective-permute-done.2.refs_3_
  12.0 0.3 copy-done.2
  12.3 0.3 merge.1
  12.6 3.7 %collective-permute-start.9 = (bf16[32,896]{1,0:T(8,128)(2,1)S(1)}, bf16[32,896]{1,0:T(8,128)(2,1)S(1)}, u32[]{:S(2)}, u32[]{:S(2)}) collective-permute-start(bf16[32,896]{1,0:T(8,128)(2,1)S(1)} %get-tuple-element.37.refs_0_), channel_id=1, source_target_pairs={{0,6},{1,7},{2,0},{3,1},{4,2},{5,3},{6,4},{7,5},{8,14},{9,15},{10,... | collective-permute-start | bytes 172040 | tf_op jit(solution)/shard_map/ppermute | solution.py:280
  16.2 0.0 collective-permute-start.7
  16.2 1.0 %collective-permute-start.5 = (bf16[32,896]{1,0:T(8,128)(2,1)S(1)}, bf16[32,896]{1,0:T(8,128)(2,1)S(1)}, u32[]{:S(2)}, u32[]{:S(2)}) collective-permute-start(bf16[32,896]{1,0:T(8,128)(2,1)S(1)} %get-tuple-element.37.refs_0_), channel_id=1, source_target_pairs={{0,2},{1,3},{2,4},{3,5},{4,6},{5,7},{6,0},{7,1},{8,10},{9,11},{10,... | collective-permute-start | bytes 172040 | tf_op jit(solution)/shard_map/ppermute | solution.py:280
  17.3 1.5 %collective-permute-start.10 = (bf16[32,896]{1,0:T(8,128)(2,1)S(1)}, bf16[32,896]{1,0:T(8,128)(2,1)S(1)}, u32[]{:S(2)}, u32[]{:S(2)}) collective-permute-start(bf16[32,896]{1,0:T(8,128)(2,1)S(1)} %get-tuple-element.38), channel_id=1, source_target_pairs={{0,7},{1,6},{2,1},{3,0},{4,3},{5,2},{6,5},{7,4},{8,15},{9,14},{10,... | collective-permute-start | bytes 172040 | tf_op jit(solution)/shard_map/ppermute | solution.py:280
  18.8 2.1 %collective-permute-start.8 = (bf16[32,896]{1,0:T(8,128)(2,1)S(1)}, bf16[32,896]{1,0:T(8,128)(2,1)S(1)}, u32[]{:S(2)}, u32[]{:S(2)}) collective-permute-start(bf16[32,896]{1,0:T(8,128)(2,1)S(1)} %get-tuple-element.38), channel_id=1, source_target_pairs={{0,5},{1,4},{2,7},{3,6},{4,1},{5,0},{6,3},{7,2},{8,13},{9,12},{10,... | collective-permute-start | bytes 172040 | tf_op jit(solution)/shard_map/ppermute | solution.py:280
  20.9 0.5 collective-permute-done.7.refs_4_
  21.4 1.7 %collective-permute-start.6 = (bf16[32,896]{1,0:T(8,128)(2,1)S(1)}, bf16[32,896]{1,0:T(8,128)(2,1)S(1)}, u32[]{:S(2)}, u32[]{:S(2)}) collective-permute-start(bf16[32,896]{1,0:T(8,128)(2,1)S(1)} %get-tuple-element.38), channel_id=1, source_target_pairs={{0,3},{1,2},{2,5},{3,4},{4,7},{5,6},{6,1},{7,0},{8,11},{9,10},{10,... | collective-permute-start | bytes 172040 | tf_op jit(solution)/shard_map/ppermute | solution.py:280
  23.1 2.0 %collective-permute-done.8.refs_5_ = bf16[32,896]{1,0:T(8,128)(2,1)S(1)} collective-permute-done((bf16[32,896]{1,0:T(8,128)(2,1)S(1)}, bf16[32,896]{1,0:T(8,128)(2,1)S(1)}, u32[]{:S(2)}, u32[]{:S(2)}) %collective-permute-start.8) | collective-permute-done | bytes 57376 | tf_op jit(solution)/shard_map/ppermute | solution.py:280
  25.1 1.7 %collective-permute-done.6.refs_3_ = bf16[32,896]{1,0:T(8,128)(2,1)S(1)} collective-permute-done((bf16[32,896]{1,0:T(8,128)(2,1)S(1)}, bf16[32,896]{1,0:T(8,128)(2,1)S(1)}, u32[]{:S(2)}, u32[]{:S(2)}) %collective-permute-start.6) | collective-permute-done | bytes 57376 | tf_op jit(solution)/shard_map/ppermute | solution.py:280
  26.8 0.0 collective-permute-done.4.refs_1_
  26.8 0.0 collective-permute-done.3.sib_ref
  26.8 0.0 copy-start.5
  26.8 4.0 %fock.1 = (bf16[32,768]{1,0:T(8,128)(2,1)S(1)}, bf16[32,768]{1,0:T(8,128)(2,1)S(1)}, bf16[32,768]{1,0:T(8,128)(2,1)S(1)}, bf16[32,768]{1,0:T(8,128)(2,1)S(1)}, b...) custom-call(s32[1]{0:T(128)} %bitcast.1.blk_ref, ...), custom_call_target="tpu_custom_call" | custom-call | flops 2717908992 | bytes 6750208 | tf_op jit(solution)/shard_map/fock/pallas_call | solution.py:249
  30.8 0.2 collective-permute-start.11
  31.0 0.1 collective-permute-start.12
  31.1 2.0 %collective-permute-start.13 = (bf16[32,768]{1,0:T(8,128)(2,1)S(1)}, bf16[32,768]{1,0:T(8,128)(2,1)S(1)}, u32[]{:S(2)}, u32[]{:S(2)}) collective-permute-start(bf16[32,768]{1,0:T(8,128)(2,1)S(1)} %get-tuple-element.42), channel_id=1, source_target_pairs={{0,3},{1,2},{2,5},{3,4},{4,7},{5,6},{6,1},{7,0},{8,11},{9,10},{10,... | collective-permute-start | bytes 147464 | tf_op jit(solution)/shard_map/ppermute | solution.py:280
  33.1 2.0 %collective-permute-start.14 = (bf16[32,768]{1,0:T(8,128)(2,1)S(1)}, bf16[32,768]{1,0:T(8,128)(2,1)S(1)}, u32[]{:S(2)}, u32[]{:S(2)}) collective-permute-start(bf16[32,768]{1,0:T(8,128)(2,1)S(1)} %get-tuple-element.43), channel_id=1, source_target_pairs={{0,4},{1,5},{2,6},{3,7},{4,0},{5,1},{6,2},{7,3},{8,12},{9,13},{10,... | collective-permute-start | bytes 147464 | tf_op jit(solution)/shard_map/ppermute | solution.py:280
  35.1 0.6 %collective-permute-start.15 = (bf16[32,768]{1,0:T(8,128)(2,1)S(1)}, bf16[32,768]{1,0:T(8,128)(2,1)S(1)}, u32[]{:S(2)}, u32[]{:S(2)}) collective-permute-start(bf16[32,768]{1,0:T(8,128)(2,1)S(1)} %get-tuple-element.44), channel_id=1, source_target_pairs={{0,5},{1,4},{2,7},{3,6},{4,1},{5,0},{6,3},{7,2},{8,13},{9,12},{10,... | collective-permute-start | bytes 147464 | tf_op jit(solution)/shard_map/ppermute | solution.py:280
  35.7 0.0 collective-permute-done.11.refs_1_
  35.7 1.6 %collective-permute-start.16 = (bf16[32,768]{1,0:T(8,128)(2,1)S(1)}, bf16[32,768]{1,0:T(8,128)(2,1)S(1)}, u32[]{:S(2)}, u32[]{:S(2)}) collective-permute-start(bf16[32,768]{1,0:T(8,128)(2,1)S(1)} %get-tuple-element.45), channel_id=1, source_target_pairs={{0,6},{1,7},{2,0},{3,1},{4,2},{5,3},{6,4},{7,5},{8,14},{9,15},{10,... | collective-permute-start | bytes 147464 | tf_op jit(solution)/shard_map/ppermute | solution.py:280
  37.3 0.1 collective-permute-done.12.refs_2_
  37.4 1.5 %collective-permute-start.17 = (bf16[32,768]{1,0:T(8,128)(2,1)S(1)}, bf16[32,768]{1,0:T(8,128)(2,1)S(1)}, u32[]{:S(2)}, u32[]{:S(2)}) collective-permute-start(bf16[32,768]{1,0:T(8,128)(2,1)S(1)} %get-tuple-element.46), channel_id=1, source_target_pairs={{0,7},{1,6},{2,1},{3,0},{4,3},{5,2},{6,5},{7,4},{8,15},{9,14},{10,... | collective-permute-start | bytes 147464 | tf_op jit(solution)/shard_map/ppermute | solution.py:280
  38.9 0.0 collective-permute-done.13.refs_3_
  38.9 2.2 %collective-permute-done.14.refs_4_ = bf16[32,768]{1,0:T(8,128)(2,1)S(1)} collective-permute-done((bf16[32,768]{1,0:T(8,128)(2,1)S(1)}, bf16[32,768]{1,0:T(8,128)(2,1)S(1)}, u32[]{:S(2)}, u32[]{:S(2)}) %collective-permute-start.14) | collective-permute-done | bytes 49184 | tf_op jit(solution)/shard_map/ppermute | solution.py:280
  41.2 1.0 %collective-permute-done.15.refs_5_ = bf16[32,768]{1,0:T(8,128)(2,1)S(1)} collective-permute-done((bf16[32,768]{1,0:T(8,128)(2,1)S(1)}, bf16[32,768]{1,0:T(8,128)(2,1)S(1)}, u32[]{:S(2)}, u32[]{:S(2)}) %collective-permute-start.15) | collective-permute-done | bytes 49184 | tf_op jit(solution)/shard_map/ppermute | solution.py:280
  42.1 1.0 %collective-permute-done.17.refs_7_ = bf16[32,768]{1,0:T(8,128)(2,1)S(1)} collective-permute-done((bf16[32,768]{1,0:T(8,128)(2,1)S(1)}, bf16[32,768]{1,0:T(8,128)(2,1)S(1)}, u32[]{:S(2)}, u32[]{:S(2)}) %collective-permute-start.17) | collective-permute-done | bytes 49184 | tf_op jit(solution)/shard_map/ppermute | solution.py:280
  43.1 0.1 sum.1
  43.2 0.6 %collective-permute-start.18 = (bf16[32,768]{1,0:T(8,128)(2,1)S(1)}, bf16[32,768]{1,0:T(8,128)(2,1)S(1)}, u32[]{:S(2)}, u32[]{:S(2)}) collective-permute-start(bf16[32,768]{1,0:T(8,128)(2,1)S(1)} %get-tuple-element.48), channel_id=1, source_target_pairs={{0,8},{8,16},{16,24},{24,0},{1,9},{9,17},{17,25},{25,1},{2,10},{10... | collective-permute-start | bytes 147464 | tf_op jit(solution)/shard_map/ppermute | solution.py:275
  43.9 0.7 %collective-permute-start.19 = (bf16[32,768]{1,0:T(8,128)(2,1)S(1)}, bf16[32,768]{1,0:T(8,128)(2,1)S(1)}, u32[]{:S(2)}, u32[]{:S(2)}) collective-permute-start(bf16[32,768]{1,0:T(8,128)(2,1)S(1)} %get-tuple-element.49), channel_id=1, source_target_pairs={{0,16},{8,24},{16,0},{24,8},{1,17},{9,25},{17,1},{25,9},{2,18},{10... | collective-permute-start | bytes 147464 | tf_op jit(solution)/shard_map/ppermute | solution.py:275
  44.6 2.1 %collective-permute-start.20 = (bf16[32,768]{1,0:T(8,128)(2,1)S(1)}, bf16[32,768]{1,0:T(8,128)(2,1)S(1)}, u32[]{:S(2)}, u32[]{:S(2)}) collective-permute-start(bf16[32,768]{1,0:T(8,128)(2,1)S(1)} %get-tuple-element.50), channel_id=1, source_target_pairs={{0,24},{8,0},{16,8},{24,16},{1,25},{9,1},{17,9},{25,17},{2,26},{10... | collective-permute-start | bytes 147464 | tf_op jit(solution)/shard_map/ppermute | solution.py:275
  46.7 1.8 %collective-permute-done.18.refs_1_ = bf16[32,768]{1,0:T(8,128)(2,1)S(1)} collective-permute-done((bf16[32,768]{1,0:T(8,128)(2,1)S(1)}, bf16[32,768]{1,0:T(8,128)(2,1)S(1)}, u32[]{:S(2)}, u32[]{:S(2)}) %collective-permute-start.18) | collective-permute-done | bytes 49184 | tf_op jit(solution)/shard_map/ppermute | solution.py:275
  48.5 0.0 collective-permute-done.19.refs_2_
  48.5 0.3 collective-permute-done.20.refs_3_
  48.8 1.4 %deal.1 = bf16[16,8,768]{2,1,0:T(8,128)(2,1)} custom-call(s32[1]{0:T(128)} %bitcast.me_ref, s32[8]{0:T(128)S(1)} %copy-done.4, f32[8]{0:T(128)S(1)} %copy-done.5, f32[8,128]{1,0:T(8,128)S(1)} %get-tuple-element.33.total_ref, bf16[32,768]{1,0:T(8,128)(2,1)S(1)} %get-tuple-element.47.refs_0_, bf16[32,768]{1,0:T(8,128)(2,1)S(1)} %collective-permute-done.18.refs_1_, ...), custom_call_target="tpu_custom_call" | custom-call | bytes 397312 | tf_op jit(solution)/shard_map/deal/pallas_call | solution.py:249
  (12 shorter events, 0.0 us)
Async XLA Ops:
  0.0 26.8 %collective-permute-start.3 = (bf16[12,128,768]{2,1,0:T(8,128)(2,1)}, bf16[12,128,768]{2,1,0:T(8,128)(2,1)S(1)}, u32[]{:S(2)}, u32[]{:S(2)}) collective-permute-start(bf16[12,128,768]{2,1,0:T(8,128)(2,1)} %refs_0_.1), channel_id=1, source_target_pairs={{0,1},{1,0},{2,3},{3,2},{4,5},{5,4},{6,7},{7,6},{8,9},{9,8},{10,11... | collective-permute-start | bytes 7077896 | tf_op jit(solution)/shard_map/ppermute | solution.py:280
  2.3 9.7 %collective-permute-start = (bf16[32,896]{1,0:T(8,128)(2,1)}, bf16[32,896]{1,0:T(8,128)(2,1)S(1)}, u32[]{:S(2)}, u32[]{:S(2)}) collective-permute-start(bf16[32,896]{1,0:T(8,128)(2,1)} %get-tuple-element.30), channel_id=1, source_target_pairs={{0,8},{8,16},{16,24},{24,0},{1,9},{9,17},{17,25},{25,1},{2,10},{10... | collective-permute-start | bytes 172040 | tf_op jit(solution)/shard_map/ppermute | solution.py:275
  4.8 7.2 %collective-permute-start.1 = (bf16[32,896]{1,0:T(8,128)(2,1)}, bf16[32,896]{1,0:T(8,128)(2,1)S(1)}, u32[]{:S(2)}, u32[]{:S(2)}) collective-permute-start(bf16[32,896]{1,0:T(8,128)(2,1)} %get-tuple-element.31), channel_id=1, source_target_pairs={{0,16},{8,24},{16,0},{24,8},{1,17},{9,25},{17,1},{25,9},{2,18},{10... | collective-permute-start | bytes 172040 | tf_op jit(solution)/shard_map/ppermute | solution.py:275
  6.3 5.7 %collective-permute-start.2 = (bf16[32,896]{1,0:T(8,128)(2,1)}, bf16[32,896]{1,0:T(8,128)(2,1)S(1)}, u32[]{:S(2)}, u32[]{:S(2)}) collective-permute-start(bf16[32,896]{1,0:T(8,128)(2,1)} %get-tuple-element.32), channel_id=1, source_target_pairs={{0,24},{8,0},{16,8},{24,16},{1,25},{9,1},{17,9},{25,17},{2,26},{10... | collective-permute-start | bytes 172040 | tf_op jit(solution)/shard_map/ppermute | solution.py:275
  7.8 1.7 %copy-start = (bf16[12,128,768]{2,1,0:T(8,128)(2,1)S(1)}, bf16[12,128,768]{2,1,0:T(8,128)(2,1)}, u32[]{:S(2)}) copy-start(bf16[12,128,768]{2,1,0:T(8,128)(2,1)} %refs_0_.1) | copy-start | bytes 7077892
  9.4 1.3 %copy-start.1 = (bf16[768,768]{1,0:T(8,128)(2,1)S(1)}, bf16[768,768]{1,0:T(8,128)(2,1)}, u32[]{:S(2)}) copy-start(bf16[768,768]{1,0:T(8,128)(2,1)} %refs_1_.1) | copy-start | bytes 3538948
  10.7 0.8 %copy-start.3 = (f32[12,768]{1,0:T(8,128)S(1)}, f32[12,768]{1,0:T(8,128)}, u32[]{:S(2)}) copy-start(f32[12,768]{1,0:T(8,128)} %refs_2_.1) | copy-start | bytes 110596
  11.5 0.8 %copy-start.2 = (bf16[32,896]{1,0:T(8,128)(2,1)S(1)}, bf16[32,896]{1,0:T(8,128)(2,1)}, u32[]{:S(2)}) copy-start(bf16[32,896]{1,0:T(8,128)(2,1)} %get-tuple-element.29.refs_0_) | copy-start | bytes 172036
  12.6 6.2 %collective-permute-start.9 = (bf16[32,896]{1,0:T(8,128)(2,1)S(1)}, bf16[32,896]{1,0:T(8,128)(2,1)S(1)}, u32[]{:S(2)}, u32[]{:S(2)}) collective-permute-start(bf16[32,896]{1,0:T(8,128)(2,1)S(1)} %get-tuple-element.37.refs_0_), channel_id=1, source_target_pairs={{0,6},{1,7},{2,0},{3,1},{4,2},{5,3},{6,4},{7,5},{8,14},{9,15},{10,... | collective-permute-start | bytes 172040 | tf_op jit(solution)/shard_map/ppermute | solution.py:280
  16.2 5.2 %collective-permute-start.7 = (bf16[32,896]{1,0:T(8,128)(2,1)S(1)}, bf16[32,896]{1,0:T(8,128)(2,1)S(1)}, u32[]{:S(2)}, u32[]{:S(2)}) collective-permute-start(bf16[32,896]{1,0:T(8,128)(2,1)S(1)} %get-tuple-element.37.refs_0_), channel_id=1, source_target_pairs={{0,4},{1,5},{2,6},{3,7},{4,0},{5,1},{6,2},{7,3},{8,12},{9,13},{10,... | collective-permute-start | bytes 172040 | tf_op jit(solution)/shard_map/ppermute | solution.py:280
  16.2 6.8 %collective-permute-start.5 = (bf16[32,896]{1,0:T(8,128)(2,1)S(1)}, bf16[32,896]{1,0:T(8,128)(2,1)S(1)}, u32[]{:S(2)}, u32[]{:S(2)}) collective-permute-start(bf16[32,896]{1,0:T(8,128)(2,1)S(1)} %get-tuple-element.37.refs_0_), channel_id=1, source_target_pairs={{0,2},{1,3},{2,4},{3,5},{4,6},{5,7},{6,0},{7,1},{8,10},{9,11},{10,... | collective-permute-start | bytes 172040 | tf_op jit(solution)/shard_map/ppermute | solution.py:280
  17.3 5.8 %collective-permute-start.10 = (bf16[32,896]{1,0:T(8,128)(2,1)S(1)}, bf16[32,896]{1,0:T(8,128)(2,1)S(1)}, u32[]{:S(2)}, u32[]{:S(2)}) collective-permute-start(bf16[32,896]{1,0:T(8,128)(2,1)S(1)} %get-tuple-element.38), channel_id=1, source_target_pairs={{0,7},{1,6},{2,1},{3,0},{4,3},{5,2},{6,5},{7,4},{8,15},{9,14},{10,... | collective-permute-start | bytes 172040 | tf_op jit(solution)/shard_map/ppermute | solution.py:280
  18.8 6.3 %collective-permute-start.8 = (bf16[32,896]{1,0:T(8,128)(2,1)S(1)}, bf16[32,896]{1,0:T(8,128)(2,1)S(1)}, u32[]{:S(2)}, u32[]{:S(2)}) collective-permute-start(bf16[32,896]{1,0:T(8,128)(2,1)S(1)} %get-tuple-element.38), channel_id=1, source_target_pairs={{0,5},{1,4},{2,7},{3,6},{4,1},{5,0},{6,3},{7,2},{8,13},{9,12},{10,... | collective-permute-start | bytes 172040 | tf_op jit(solution)/shard_map/ppermute | solution.py:280
  21.4 5.4 %collective-permute-start.6 = (bf16[32,896]{1,0:T(8,128)(2,1)S(1)}, bf16[32,896]{1,0:T(8,128)(2,1)S(1)}, u32[]{:S(2)}, u32[]{:S(2)}) collective-permute-start(bf16[32,896]{1,0:T(8,128)(2,1)S(1)} %get-tuple-element.38), channel_id=1, source_target_pairs={{0,3},{1,2},{2,5},{3,4},{4,7},{5,6},{6,1},{7,0},{8,11},{9,10},{10,... | collective-permute-start | bytes 172040 | tf_op jit(solution)/shard_map/ppermute | solution.py:280
  23.1 3.7 %collective-permute-start.4 = (bf16[32,896]{1,0:T(8,128)(2,1)S(1)}, bf16[32,896]{1,0:T(8,128)(2,1)S(1)}, u32[]{:S(2)}, u32[]{:S(2)}) collective-permute-start(bf16[32,896]{1,0:T(8,128)(2,1)S(1)} %get-tuple-element.38), channel_id=1, source_target_pairs={{0,1},{1,0},{2,3},{3,2},{4,5},{5,4},{6,7},{7,6},{8,9},{9,8},{10,11... | collective-permute-start | bytes 172040 | tf_op jit(solution)/shard_map/ppermute | solution.py:280
  26.8 22.0 %copy-start.4 = (s32[8]{0:T(128)S(1)}, s32[8]{0:T(128)}, u32[]{:S(2)}) copy-start(s32[8]{0:T(128)} %target_ref.1) | copy-start | bytes 100
  26.8 22.0 %copy-start.5 = (f32[8]{0:T(128)S(1)}, f32[8]{0:T(128)}, u32[]{:S(2)}) copy-start(f32[8]{0:T(128)} %weights_ref.1) | copy-start | bytes 100
  30.8 4.9 %collective-permute-start.11 = (bf16[32,768]{1,0:T(8,128)(2,1)S(1)}, bf16[32,768]{1,0:T(8,128)(2,1)S(1)}, u32[]{:S(2)}, u32[]{:S(2)}) collective-permute-start(bf16[32,768]{1,0:T(8,128)(2,1)S(1)} %get-tuple-element.40), channel_id=1, source_target_pairs={{0,1},{1,0},{2,3},{3,2},{4,5},{5,4},{6,7},{7,6},{8,9},{9,8},{10,11... | collective-permute-start | bytes 147464 | tf_op jit(solution)/shard_map/ppermute | solution.py:280
  31.0 6.5 %collective-permute-start.12 = (bf16[32,768]{1,0:T(8,128)(2,1)S(1)}, bf16[32,768]{1,0:T(8,128)(2,1)S(1)}, u32[]{:S(2)}, u32[]{:S(2)}) collective-permute-start(bf16[32,768]{1,0:T(8,128)(2,1)S(1)} %get-tuple-element.41), channel_id=1, source_target_pairs={{0,2},{1,3},{2,4},{3,5},{4,6},{5,7},{6,0},{7,1},{8,10},{9,11},{10,... | collective-permute-start | bytes 147464 | tf_op jit(solution)/shard_map/ppermute | solution.py:280
  31.1 7.8 %collective-permute-start.13 = (bf16[32,768]{1,0:T(8,128)(2,1)S(1)}, bf16[32,768]{1,0:T(8,128)(2,1)S(1)}, u32[]{:S(2)}, u32[]{:S(2)}) collective-permute-start(bf16[32,768]{1,0:T(8,128)(2,1)S(1)} %get-tuple-element.42), channel_id=1, source_target_pairs={{0,3},{1,2},{2,5},{3,4},{4,7},{5,6},{6,1},{7,0},{8,11},{9,10},{10,... | collective-permute-start | bytes 147464 | tf_op jit(solution)/shard_map/ppermute | solution.py:280
  33.1 8.1 %collective-permute-start.14 = (bf16[32,768]{1,0:T(8,128)(2,1)S(1)}, bf16[32,768]{1,0:T(8,128)(2,1)S(1)}, u32[]{:S(2)}, u32[]{:S(2)}) collective-permute-start(bf16[32,768]{1,0:T(8,128)(2,1)S(1)} %get-tuple-element.43), channel_id=1, source_target_pairs={{0,4},{1,5},{2,6},{3,7},{4,0},{5,1},{6,2},{7,3},{8,12},{9,13},{10,... | collective-permute-start | bytes 147464 | tf_op jit(solution)/shard_map/ppermute | solution.py:280
  35.1 7.0 %collective-permute-start.15 = (bf16[32,768]{1,0:T(8,128)(2,1)S(1)}, bf16[32,768]{1,0:T(8,128)(2,1)S(1)}, u32[]{:S(2)}, u32[]{:S(2)}) collective-permute-start(bf16[32,768]{1,0:T(8,128)(2,1)S(1)} %get-tuple-element.44), channel_id=1, source_target_pairs={{0,5},{1,4},{2,7},{3,6},{4,1},{5,0},{6,3},{7,2},{8,13},{9,12},{10,... | collective-permute-start | bytes 147464 | tf_op jit(solution)/shard_map/ppermute | solution.py:280
  35.7 6.5 %collective-permute-start.16 = (bf16[32,768]{1,0:T(8,128)(2,1)S(1)}, bf16[32,768]{1,0:T(8,128)(2,1)S(1)}, u32[]{:S(2)}, u32[]{:S(2)}) collective-permute-start(bf16[32,768]{1,0:T(8,128)(2,1)S(1)} %get-tuple-element.45), channel_id=1, source_target_pairs={{0,6},{1,7},{2,0},{3,1},{4,2},{5,3},{6,4},{7,5},{8,14},{9,15},{10,... | collective-permute-start | bytes 147464 | tf_op jit(solution)/shard_map/ppermute | solution.py:280
  37.4 5.7 %collective-permute-start.17 = (bf16[32,768]{1,0:T(8,128)(2,1)S(1)}, bf16[32,768]{1,0:T(8,128)(2,1)S(1)}, u32[]{:S(2)}, u32[]{:S(2)}) collective-permute-start(bf16[32,768]{1,0:T(8,128)(2,1)S(1)} %get-tuple-element.46), channel_id=1, source_target_pairs={{0,7},{1,6},{2,1},{3,0},{4,3},{5,2},{6,5},{7,4},{8,15},{9,14},{10,... | collective-permute-start | bytes 147464 | tf_op jit(solution)/shard_map/ppermute | solution.py:280
  43.2 5.3 %collective-permute-start.18 = (bf16[32,768]{1,0:T(8,128)(2,1)S(1)}, bf16[32,768]{1,0:T(8,128)(2,1)S(1)}, u32[]{:S(2)}, u32[]{:S(2)}) collective-permute-start(bf16[32,768]{1,0:T(8,128)(2,1)S(1)} %get-tuple-element.48), channel_id=1, source_target_pairs={{0,8},{8,16},{16,24},{24,0},{1,9},{9,17},{17,25},{25,1},{2,10},{10... | collective-permute-start | bytes 147464 | tf_op jit(solution)/shard_map/ppermute | solution.py:275
  43.9 4.7 %collective-permute-start.19 = (bf16[32,768]{1,0:T(8,128)(2,1)S(1)}, bf16[32,768]{1,0:T(8,128)(2,1)S(1)}, u32[]{:S(2)}, u32[]{:S(2)}) collective-permute-start(bf16[32,768]{1,0:T(8,128)(2,1)S(1)} %get-tuple-element.49), channel_id=1, source_target_pairs={{0,16},{8,24},{16,0},{24,8},{1,17},{9,25},{17,1},{25,9},{2,18},{10... | collective-permute-start | bytes 147464 | tf_op jit(solution)/shard_map/ppermute | solution.py:275
  44.6 4.2 %collective-permute-start.20 = (bf16[32,768]{1,0:T(8,128)(2,1)S(1)}, bf16[32,768]{1,0:T(8,128)(2,1)S(1)}, u32[]{:S(2)}, u32[]{:S(2)}) collective-permute-start(bf16[32,768]{1,0:T(8,128)(2,1)S(1)} %get-tuple-element.50), channel_id=1, source_target_pairs={{0,24},{8,0},{16,8},{24,16},{1,25},{9,1},{17,9},{25,17},{2,26},{10... | collective-permute-start | bytes 147464 | tf_op jit(solution)/shard_map/ppermute | solution.py:275

commit v4 on v3

--- a/solution.py
+++ b/solution.py
@@ -1,4 +1,5 @@
 import functools
+import math
 import jax
 import jax.numpy as jnp
 from jax import lax
@@ -44,28 +45,30 @@
 
 
 def stage_kernel(*refs):
-    count = (len(refs) - 1) // 2
+    count = (len(refs) - 2) // 2
     sems = refs[-1]
-    copies = [pltpu.make_async_copy(refs[i], refs[count + i], sems.at[i]) for i in range(count)]
+    copies = [pltpu.make_async_copy(refs[i], refs[count + 1 + i], sems.at[i]) for i in range(count)]
     for copy in copies:
         copy.start()
     for copy in copies:
         copy.wait()
 
 
-def route_kernel(keep, cap, me_ref, target_any, weights_any, walkers_any, fields_any, *refs):
-    *outs, target_ref, weights_ref, walkers_ref, fields_ref, wide, blocks, lines, sems = refs
+def route_kernel(keep, cap, me_ref, target_any, weights_any, walkers_any, fields_any, diag_any, *refs):
+    *outs, target_ref, weights_ref, walkers_ref, fields_ref, diag_ref, wide, blocks, parts, lines, sems = refs
     pairs = (
         (walkers_any, walkers_ref),
         (target_any, target_ref),
         (weights_any, weights_ref),
         (fields_any, fields_ref),
+        (diag_any, diag_ref),
     )
     copies = [pltpu.make_async_copy(a, b, sems.at[i]) for i, (a, b) in enumerate(pairs)]
     for copy in copies:
         copy.start()
     rows, slots, orbitals = walkers_ref.shape
     vec_count = fields_ref.shape[1]
+    chunks = orbitals // LANES
     groups = len(outs)
     live = groups * keep
     blocks[...] = jnp.zeros(blocks.shape, F32)
@@ -73,8 +76,13 @@
     for copy in copies:
         copy.wait()
     wide[...] = walkers_ref[...].astype(F32)
+    exponent = fields_ref[:, 0:1] * diag_ref[0:1, :]
+    for g in range(1, vec_count):
+        exponent = exponent + fields_ref[:, g : g + 1] * diag_ref[g : g + 1, :]
+    for i, term in enumerate(terms(exponent, 2)):
+        for c in range(chunks):
+            parts[:, i * chunks + c, :] = term[:, c * LANES : (c + 1) * LANES]
     weight = F32(0.0)
-    lane = lax.broadcasted_iota(jnp.int32, (1, LANES), 1)
     for slot in range(slots):
         t = target_ref[slot]
         alive = t < live
@@ -82,55 +90,51 @@
         turn = lax.div(t, groups)
         at = jnp.where(alive, lax.rem(t, groups) * cap + lax.rem(turn, cap), groups * cap)
         blocks[at] = wide[:, slot, :]
-        lines[at] = jnp.where(lane == LANES - 1, (turn + 1).astype(F32), F32(0.0))
-        lines[at, :, 0:vec_count] = fields_ref[slot : slot + 1, :]
+        parts[slot, 2 * chunks : 2 * chunks + 1, :] = jnp.full((1, LANES), (turn + 1).astype(F32), F32)
+        lines[at] = parts[slot]
     sums = terms(jnp.full((1, LANES), weight, F32), 3)
     for s, out in enumerate(outs):
         base = lax.rem(me_ref[0] + s, groups) * cap
         out[:, 0:orbitals] = jnp.concatenate([blocks[base + k] for k in range(cap)], axis=0).astype(BF16)
-        line = jnp.concatenate([lines[base + k] for k in range(cap)], axis=0)
-        write_tail(out, orbitals, jnp.concatenate(terms(line, 3) + sums, axis=0))
-
-
-def merge_kernel(keep, cap, groups, core_ref, diag_ref, *refs):
+        tail = [lines[base + k][0 : 2 * chunks + 1] for k in range(cap)]
+        write_tail(out, orbitals, jnp.concatenate(tail + sums, axis=0))
+
+
+def merge_kernel(keep, cap, groups, orbitals, core_ref, *refs):
     ins, (same_ref, other_ref, weight_ref, pick_ref) = refs[:groups], refs[groups:]
-    vec_count, orbitals = diag_ref.shape
     half = keep // 2
     rows = ins[0].shape[0] // cap
     slab = half * rows
+    chunks = orbitals // LANES
+    each = 2 * chunks + 1
     weight = jnp.zeros((1, LANES), F32)
     walker = [jnp.zeros((rows, orbitals), F32)] * keep
-    line = [jnp.zeros((1, LANES), F32)] * keep
+    line = [jnp.zeros((2 * chunks, LANES), F32)] * keep
     for s, ref in enumerate(ins):
-        tail = read_tail(ref, orbitals, 3 * cap + 3)
-        weight = weight + (tail[3 * cap : 3 * cap + 1] + tail[3 * cap + 1 : 3 * cap + 2] + tail[3 * cap + 2 :])
+        tail = read_tail(ref, orbitals, cap * each + 3)
+        weight = weight + (tail[cap * each : cap * each + 1] + tail[cap * each + 1 : cap * each + 2] + tail[cap * each + 2 :])
         for k in range(cap):
-            fields = tail[k : k + 1] + tail[cap + k : cap + k + 1] + tail[2 * cap + k : 2 * cap + k + 1]
-            flag = jnp.broadcast_to(fields[:, LANES - 1 : LANES], (1, LANES))
+            flag = tail[(k + 1) * each - 1 : (k + 1) * each]
             block = ref[k * rows : (k + 1) * rows, 0:orbitals].astype(F32)
+            part = tail[k * each : (k + 1) * each - 1]
             for m in range(k, keep, cap):
                 mine = jnp.where(flag == m + 1, F32(1.0), F32(0.0))
                 pick_ref[s * keep + m : s * keep + m + 1, :] = mine
                 walker[m] = jnp.where(wide_mask(mine, orbitals), block, walker[m])
-                line[m] = jnp.where(mine > 0, fields, line[m])
+                line[m] = jnp.where(mine > 0, part, line[m])
     weight_ref[...] = jnp.broadcast_to(weight, weight_ref.shape)
-    fields = jnp.concatenate(line, axis=0)
-    exponent = fields[:, 0:1] * diag_ref[0:1, :]
-    for g in range(1, vec_count):
-        exponent = exponent + fields[:, g : g + 1] * diag_ref[g : g + 1, :]
     first = core_ref[0] == 0
-    high, low = terms(exponent, 2)
     for out, order in ((same_ref, (0, 1)), (other_ref, (1, 0))):
+        picked = []
         for k in range(half):
-            picked = jnp.where(first, walker[order[0] * half + k], walker[order[1] * half + k])
-            out[k * rows : (k + 1) * rows, 0:orbitals] = picked.astype(BF16)
-        pieces = []
-        for term in (high, low):
-            for k in range(half):
-                a, b = order[0] * half + k, order[1] * half + k
-                picked = jnp.where(first, term[a : a + 1], term[b : b + 1])
-                pieces += [picked[:, c : c + LANES] for c in range(0, orbitals, LANES)]
-        write_tail(out, orbitals, jnp.concatenate(pieces, axis=0))
+            a, b = order[0] * half + k, order[1] * half + k
+            picked.append(jnp.where(first, line[a], line[b]))
+            block = jnp.where(first, walker[a], walker[b])
+            for c in range(chunks):
+                at = c * slab + k * rows
+                out[at : at + rows, :] = block[:, c * LANES : (c + 1) * LANES].astype(BF16)
+        tail = [p[i * chunks : (i + 1) * chunks] for i in range(2) for p in picked]
+        out[chunks * slab :, :] = jnp.concatenate(tail, axis=0).astype(BF16)
 
 
 def hops(n):
@@ -149,28 +153,27 @@
     vec_count, occupied, orbitals = own_ref.shape
     slab = outs[0].shape[0]
     rows = slab // half
-    blocks = orbitals // LANES
+    chunks = orbitals // LANES
     blk = blk_ref[0]
-    exponent = jnp.zeros((2 * half * blocks, LANES), F32)
+    exponent = jnp.zeros((2 * half * chunks, LANES), F32)
     for ref in ins:
-        exponent = exponent + read_tail(ref, orbitals, 2 * half * blocks)
-    growth = jnp.exp(exponent[0 : half * blocks] + exponent[half * blocks :])
+        exponent = exponent + ref[chunks * slab :, :].astype(F32)
+    growth = jnp.exp(exponent[0 : half * chunks] + exponent[half * chunks :])
     for ref, (s, e) in zip(ins, hops(n)):
         source = partner(blk, s, e, n, -1)
         for w in range(half):
-            for c in range(blocks):
-                piece = ref[w * rows : (w + 1) * rows, c * LANES : (c + 1) * LANES].astype(F32)
-                prop[w, source, :, c * LANES : (c + 1) * LANES] = piece * growth[w * blocks + c : w * blocks + c + 1]
-    for w in range(half):
-        piece = jnp.concatenate([prop[w, i] for i in range(n)], axis=0).astype(BF16)
-        done = jnp.dot(piece, body_ref[...], preferred_element_type=F32)
-        turned[:, w * occupied : (w + 1) * occupied] = done.T.astype(BF16)
-    pair = 2 if vec_count % 2 == 0 else 1
+            for c in range(chunks):
+                piece = ref[c * slab + w * rows : c * slab + (w + 1) * rows, :].astype(F32)
+                piece = piece * growth[w * chunks + c : w * chunks + c + 1]
+                prop[w, source, :, c * LANES : (c + 1) * LANES] = piece.astype(prop.dtype)
+    scaled = jnp.concatenate([prop[w, i] for w in range(half) for i in range(n)], axis=0).astype(BF16)
+    turned[...] = jnp.dot(scaled, body_ref[...], preferred_element_type=F32).T.astype(BF16)
+    batch = math.gcd(vec_count, 4)
     for c, ref in enumerate((own_ref, sib_ref)):
-        for g in range(0, vec_count, pair):
-            left = ref[g : g + pair].reshape(pair * occupied, orbitals)
+        for g in range(0, vec_count, batch):
+            left = ref[g : g + batch].reshape(batch * occupied, orbitals)
             s = jnp.dot(left, turned[...], preferred_element_type=F32).astype(BF16)
-            for k in range(pair):
+            for k in range(batch):
                 at = (c * vec_count + g + k) * occupied
                 for w in range(half):
                     coup[w * occupied : (w + 1) * occupied, at : at + occupied] = s[
@@ -192,7 +195,7 @@
         for w in range(half):
             for i in range(n):
                 at = w * occupied + i * rows
-                result[w, i, :, t : t + tile] = total[at : at + rows]
+                result[w, i, :, t : t + tile] = total[at : at + rows].astype(result.dtype)
     for out, (s, e) in zip(outs, hops(n)):
         to = partner(blk, s, e, n, 1)
         for w in range(half):
@@ -279,48 +282,53 @@
             return x
         return lax.ppermute(x, "blk", [(i, (2 * (i // 2 + s) + (i % 2 ^ e)) % n) for i in range(n)])
 
+    chunks = orbitals // LANES
     sibling = to_block(chol, 0, 1)
-    own, held_body, diag = call(
-        stage_kernel,
-        [shape(x.shape, x.dtype) for x in (chol, one_body, field_diag)],
-        [],
-        [chol, one_body, field_diag],
-        [],
-        [pltpu.SemaphoreType.DMA((3,))],
-        "stage",
-    )
-    width = orbitals + tail_blocks(3 * cap + 3, cap * rows) * LANES
+    width = orbitals + tail_blocks(cap * (2 * chunks + 1) + 3, cap * rows) * LANES
     routed = call(
         functools.partial(route_kernel, keep, cap),
         [shape((cap * rows, width), BF16)] * groups,
         [grp],
-        [target, weights, walkers, fields],
+        [target, weights, walkers, fields, field_diag],
         [],
         [
             pltpu.SMEM(target.shape, target.dtype),
             pltpu.SMEM(weights.shape, weights.dtype),
             pltpu.VMEM(walkers.shape, walkers.dtype),
             pltpu.VMEM(fields.shape, fields.dtype),
+            pltpu.VMEM(field_diag.shape, field_diag.dtype),
             pltpu.VMEM((rows, slots, orbitals), F32),
             pltpu.VMEM((groups * cap + 1, rows, orbitals), F32),
-            pltpu.VMEM((groups * cap + 1, 1, LANES), F32),
-            pltpu.SemaphoreType.DMA((4,)),
+            pltpu.VMEM((slots, 2 * chunks + 4, LANES), F32),
+            pltpu.VMEM((groups * cap + 1, 2 * chunks + 4, LANES), F32),
+            pltpu.SemaphoreType.DMA((5,)),
         ],
         "route",
         vmem=56,
     )
     routed = [to_list(x, s) for s, x in enumerate(routed)]
-    payload = shape((slab, orbitals + tail_blocks(2 * half * (orbitals // LANES), slab) * LANES), BF16)
+    payload = shape((chunks * slab + 2 * half * chunks, LANES), BF16)
     same, other, weight_sum, pick = call(
-        functools.partial(merge_kernel, keep, cap, groups),
+        functools.partial(merge_kernel, keep, cap, groups, orbitals),
         [payload, payload, shape((8, LANES), F32), shape((groups * keep, LANES), F32)],
         [core],
         [],
-        [diag] + routed,
+        routed,
         [],
         "merge",
     )
+    own, held_body = call(
+        stage_kernel,
+        [shape(x.shape, x.dtype) for x in (chol, one_body)],
+        [],
+        [chol, one_body, weight_sum],
+        [],
+        [pltpu.SemaphoreType.DMA((2,))],
+        "stage",
+        vmem=48,
+    )
     gathered = [to_block(other if e else same, s, e) for s, e in hops(n)]
+    held = F32 if rows % 16 else BF16
     parts = call(
         functools.partial(fock_kernel, n, half),
         [shape((slab, orbitals), BF16)] * n,
@@ -328,10 +336,10 @@
         [],
         [held_body, own, sibling] + gathered,
         [
-            pltpu.VMEM((half, n, rows, orbitals), F32),
+            pltpu.VMEM((half, n, rows, orbitals), held),
             pltpu.VMEM((orbitals, half * occupied), BF16),
             pltpu.VMEM((half * occupied, 2 * vec_count * occupied), BF16),
-            pltpu.VMEM((half, n, rows, orbitals), F32),
+            pltpu.VMEM((half, n, rows, orbitals), held),
         ],
         "fock",
         flops=2 * n * slab * orbitals * (orbitals + 4 * vec_count * occupied),

time: 50.6 us -> 50.8 us (level)
  local copies, waits for them, and re-layouts: 4.03 us -> 2.1 us
  waiting for transfers between devices: 10.7 us -> 11.6 us
  Pallas kernels: 8.06 us -> 8.92 us
    ppermute x6, waiting for transfers between devices: 2.14 us -> 5.85 us  [to_list(): lax.ppermute(x, 'grp', [(i, (i + s) % groups) for i in range(groups)])]
    ppermute x15, waiting for transfers between devices: 8.55 us -> 5.77 us  [to_block(): lax.ppermute(x, 'blk', [(i, (2 * (i // 2 + s) + (i % 2 ^ e)) % n) for i i...]
    unnamed x12 -> x8, local copies, waits for them, and re-layouts: 4.03 us -> 2.1 us
    pallas_call x6, Pallas kernels: 8.06 us -> 8.92 us  [call(): pl.pallas_call(kernel, out_shape=outs, in_specs=[smem] * len(scalars) + [...]
    ppermute x6, starting transfers between devices: 8.97 us -> 9.68 us  [to_list(): lax.ppermute(x, 'grp', [(i, (i + s) % groups) for i in range(groups)])]
  transfers between devices with their start and end apart: 21 -> 21, of which waited for: 9 -> 13; matrix products, arithmetic and copies ran while one was open for 0% -> 0% of each run, Pallas kernels for 5% -> 7%
where the time goes in v4:
time: 50.8 us; the launch traced here: 50.6 us
  starting transfers between devices  27.8 us (55%)
  waiting for transfers between devices  11.6 us (23%)
  Pallas kernels  8.92 us (18%)
  local copies, waits for them, and re-layouts  2.1 us (4%)
    ppermute x15, starting transfers between devices, to_block(): lax.ppermute(x, 'blk', [(i, (2 * (i // 2 + s) + (i % 2 ^ e)) % n) for i i...  18.1 us
    ppermute x6, starting transfers between devices, to_list(): lax.ppermute(x, 'grp', [(i, (i + s) % groups) for i in range(groups)])  9.68 us
    pallas_call x6, Pallas kernels, call(): pl.pallas_call(kernel, out_shape=outs, in_specs=[smem] * len(scalars) + [...  8.92 us
    ppermute x6, waiting for transfers between devices, to_list(): lax.ppermute(x, 'grp', [(i, (i + s) % groups) for i in range(groups)])  5.85 us
    ppermute x15, waiting for transfers between devices, to_block(): lax.ppermute(x, 'blk', [(i, (2 * (i // 2 + s) + (i % 2 ^ e)) % n) for i i...  5.77 us
    unnamed x8, local copies, waits for them, and re-layouts  2.1 us
  transfers between devices with their start and end apart: 21, of which 13 were waited for; matrix products, arithmetic and copies ran while one was open for 0% of the time, Pallas kernels for 7%

profile of v4, /device:TPU:0, one launch (start us, length us, event | category | flops | bytes accessed | tf_op | source)
XLA Modules:
  0.0 50.6 jit_solution(6188761483585960253)
XLA Ops:
  0.0 0.5 collective-permute-start.3
  0.5 1.9 %route.1 = (bf16[32,896]{1,0:T(8,128)(2,1)}, bf16[32,896]{1,0:T(8,128)(2,1)}, bf16[32,896]{1,0:T(8,128)(2,1)}, bf16[32,896]{1,0:T(8,128)(2,1)}) custom-call(s32[1]{0:T(128)} %bitcast.me_ref, s32[8]{0:T(128)} %target_ref.1, f32[8]{0:T(128)} %weights_ref.1, bf16[16,8,768]{2,1,0:T(8,128)(2,1)} %walkers_any.1, f32[8,12]{1,0:T(8,128)} %fields_any.1, ...), custom_call_target="tpu_custom_call" | custom-call | bytes 229376 | tf_op jit(solution)/shard_map/route/pallas_call | solution.py:252
  2.4 2.5 %collective-permute-start = (bf16[32,896]{1,0:T(8,128)(2,1)}, bf16[32,896]{1,0:T(8,128)(2,1)S(1)}, u32[]{:S(2)}, u32[]{:S(2)}) collective-permute-start(bf16[32,896]{1,0:T(8,128)(2,1)} %get-tuple-element.28), channel_id=1, source_target_pairs={{0,8},{8,16},{16,24},{24,0},{1,9},{9,17},{17,25},{25,1},{2,10},{10... | collective-permute-start | bytes 172040 | tf_op jit(solution)/shard_map/ppermute | solution.py:278
  4.9 1.5 %collective-permute-start.1 = (bf16[32,896]{1,0:T(8,128)(2,1)}, bf16[32,896]{1,0:T(8,128)(2,1)S(1)}, u32[]{:S(2)}, u32[]{:S(2)}) collective-permute-start(bf16[32,896]{1,0:T(8,128)(2,1)} %get-tuple-element.29), channel_id=1, source_target_pairs={{0,16},{8,24},{16,0},{24,8},{1,17},{9,25},{17,1},{25,9},{2,18},{10... | collective-permute-start | bytes 172040 | tf_op jit(solution)/shard_map/ppermute | solution.py:278
  6.4 1.4 %collective-permute-start.2 = (bf16[32,896]{1,0:T(8,128)(2,1)}, bf16[32,896]{1,0:T(8,128)(2,1)S(1)}, u32[]{:S(2)}, u32[]{:S(2)}) collective-permute-start(bf16[32,896]{1,0:T(8,128)(2,1)} %get-tuple-element.30), channel_id=1, source_target_pairs={{0,24},{8,0},{16,8},{24,16},{1,25},{9,1},{17,9},{25,17},{2,26},{10... | collective-permute-start | bytes 172040 | tf_op jit(solution)/shard_map/ppermute | solution.py:278
  7.9 0.9 %collective-permute-done.refs_1_ = bf16[32,896]{1,0:T(8,128)(2,1)S(1)} collective-permute-done((bf16[32,896]{1,0:T(8,128)(2,1)}, bf16[32,896]{1,0:T(8,128)(2,1)S(1)}, u32[]{:S(2)}, u32[]{:S(2)}) %collective-permute-start) | collective-permute-done | bytes 57376 | tf_op jit(solution)/shard_map/ppermute | solution.py:278
  8.7 1.2 %collective-permute-done.1.refs_2_ = bf16[32,896]{1,0:T(8,128)(2,1)S(1)} collective-permute-done((bf16[32,896]{1,0:T(8,128)(2,1)}, bf16[32,896]{1,0:T(8,128)(2,1)S(1)}, u32[]{:S(2)}, u32[]{:S(2)}) %collective-permute-start.1) | collective-permute-done | bytes 57376 | tf_op jit(solution)/shard_map/ppermute | solution.py:278
  9.9 0.9 %collective-permute-done.2.refs_3_ = bf16[32,896]{1,0:T(8,128)(2,1)S(1)} collective-permute-done((bf16[32,896]{1,0:T(8,128)(2,1)}, bf16[32,896]{1,0:T(8,128)(2,1)S(1)}, u32[]{:S(2)}, u32[]{:S(2)}) %collective-permute-start.2) | collective-permute-done | bytes 57376 | tf_op jit(solution)/shard_map/ppermute | solution.py:278
  10.8 0.8 %copy-done.1 = bf16[32,896]{1,0:T(8,128)(2,1)S(1)} copy-done((bf16[32,896]{1,0:T(8,128)(2,1)S(1)}, bf16[32,896]{1,0:T(8,128)(2,1)}, u32[]{:S(2)}) %copy-start.1) | copy-done | bytes 57368
  11.6 0.1 merge.1
  11.7 3.7 %collective-permute-start.9 = (bf16[216,128]{1,0:T(8,128)(2,1)S(1)}, bf16[216,128]{1,0:T(8,128)(2,1)S(1)}, u32[]{:S(2)}, u32[]{:S(2)}) collective-permute-start(bf16[216,128]{1,0:T(8,128)(2,1)S(1)} %get-tuple-element.35.refs_0_), channel_id=1, source_target_pairs={{0,6},{1,7},{2,0},{3,1},{4,2},{5,3},{6,4},{7,5},{8,14},{9,15},{10,... | collective-permute-start | bytes 165896 | tf_op jit(solution)/shard_map/ppermute | solution.py:283
  15.4 0.0 collective-permute-start.7
  15.4 1.0 %collective-permute-start.5 = (bf16[216,128]{1,0:T(8,128)(2,1)S(1)}, bf16[216,128]{1,0:T(8,128)(2,1)S(1)}, u32[]{:S(2)}, u32[]{:S(2)}) collective-permute-start(bf16[216,128]{1,0:T(8,128)(2,1)S(1)} %get-tuple-element.35.refs_0_), channel_id=1, source_target_pairs={{0,2},{1,3},{2,4},{3,5},{4,6},{5,7},{6,0},{7,1},{8,10},{9,11},{10,... | collective-permute-start | bytes 165896 | tf_op jit(solution)/shard_map/ppermute | solution.py:283
  16.4 1.2 %collective-permute-start.10 = (bf16[216,128]{1,0:T(8,128)(2,1)S(1)}, bf16[216,128]{1,0:T(8,128)(2,1)S(1)}, u32[]{:S(2)}, u32[]{:S(2)}) collective-permute-start(bf16[216,128]{1,0:T(8,128)(2,1)S(1)} %get-tuple-element.36), channel_id=1, source_target_pairs={{0,7},{1,6},{2,1},{3,0},{4,3},{5,2},{6,5},{7,4},{8,15},{9,14},{10,... | collective-permute-start | bytes 165896 | tf_op jit(solution)/shard_map/ppermute | solution.py:283
  17.6 0.0 collective-permute-done.9.refs_6_
  17.6 2.5 %collective-permute-start.8 = (bf16[216,128]{1,0:T(8,128)(2,1)S(1)}, bf16[216,128]{1,0:T(8,128)(2,1)S(1)}, u32[]{:S(2)}, u32[]{:S(2)}) collective-permute-start(bf16[216,128]{1,0:T(8,128)(2,1)S(1)} %get-tuple-element.36), channel_id=1, source_target_pairs={{0,5},{1,4},{2,7},{3,6},{4,1},{5,0},{6,3},{7,2},{8,13},{9,12},{10,... | collective-permute-start | bytes 165896 | tf_op jit(solution)/shard_map/ppermute | solution.py:283
  20.1 0.4 collective-permute-done.7.refs_4_
  20.5 1.4 %collective-permute-start.6 = (bf16[216,128]{1,0:T(8,128)(2,1)S(1)}, bf16[216,128]{1,0:T(8,128)(2,1)S(1)}, u32[]{:S(2)}, u32[]{:S(2)}) collective-permute-start(bf16[216,128]{1,0:T(8,128)(2,1)S(1)} %get-tuple-element.36), channel_id=1, source_target_pairs={{0,3},{1,2},{2,5},{3,4},{4,7},{5,6},{6,1},{7,0},{8,11},{9,10},{10,... | collective-permute-start | bytes 165896 | tf_op jit(solution)/shard_map/ppermute | solution.py:283
  21.9 0.2 collective-permute-done.5.refs_2_
  22.0 1.3 %copy-done = bf16[768,768]{1,0:T(8,128)(2,1)S(1)} copy-done((bf16[768,768]{1,0:T(8,128)(2,1)S(1)}, bf16[768,768]{1,0:T(8,128)(2,1)}, u32[]{:S(2)}) %copy-start) | copy-done | bytes 1179672
  23.3 1.7 %stage.1 = (bf16[12,128,768]{2,1,0:T(8,128)(2,1)S(1)}, bf16[768,768]{1,0:T(8,128)(2,1)S(1)}) custom-call(bf16[12,128,768]{2,1,0:T(8,128)(2,1)} %refs_0_.1, bf16[768,768]{1,0:T(8,128)(2,1)S(1)} %copy-done, f32[8,128]{1,0:T(8,128)S(1)} %get-tuple-element.31.refs_2_.total_ref), custom_call_target="tpu_custom_call" | custom-call | bytes 3538944 | tf_op jit(solution)/shard_map/stage/pallas_call | solution.py:252
  25.0 0.0 collective-permute-done.8.refs_5_
  25.0 0.9 %collective-permute-done.6.refs_3_ = bf16[216,128]{1,0:T(8,128)(2,1)S(1)} collective-permute-done((bf16[216,128]{1,0:T(8,128)(2,1)S(1)}, bf16[216,128]{1,0:T(8,128)(2,1)S(1)}, u32[]{:S(2)}, u32[]{:S(2)}) %collective-permute-start.6) | collective-permute-done | bytes 55328 | tf_op jit(solution)/shard_map/ppermute | solution.py:283
  25.9 0.0 collective-permute-done.4.refs_1_
  25.9 0.0 collective-permute-done.3.sib_ref
  25.9 0.0 copy-start.3
  25.9 3.7 %fock.1 = (bf16[32,768]{1,0:T(8,128)(2,1)S(1)}, bf16[32,768]{1,0:T(8,128)(2,1)S(1)}, bf16[32,768]{1,0:T(8,128)(2,1)S(1)}, bf16[32,768]{1,0:T(8,128)(2,1)S(1)}, b...) custom-call(s32[1]{0:T(128)} %bitcast.1.blk_ref, ...), custom_call_target="tpu_custom_call" | custom-call | flops 2717908992 | bytes 6733824 | tf_op jit(solution)/shard_map/fock/pallas_call | solution.py:252
  29.6 0.1 collective-permute-start.11
  29.7 0.1 collective-permute-start.12
  29.8 1.7 %collective-permute-start.13 = (bf16[32,768]{1,0:T(8,128)(2,1)S(1)}, bf16[32,768]{1,0:T(8,128)(2,1)S(1)}, u32[]{:S(2)}, u32[]{:S(2)}) collective-permute-start(bf16[32,768]{1,0:T(8,128)(2,1)S(1)} %get-tuple-element.40), channel_id=1, source_target_pairs={{0,3},{1,2},{2,5},{3,4},{4,7},{5,6},{6,1},{7,0},{8,11},{9,10},{10,... | collective-permute-start | bytes 147464 | tf_op jit(solution)/shard_map/ppermute | solution.py:283
  31.4 2.5 %collective-permute-start.14 = (bf16[32,768]{1,0:T(8,128)(2,1)S(1)}, bf16[32,768]{1,0:T(8,128)(2,1)S(1)}, u32[]{:S(2)}, u32[]{:S(2)}) collective-permute-start(bf16[32,768]{1,0:T(8,128)(2,1)S(1)} %get-tuple-element.41), channel_id=1, source_target_pairs={{0,4},{1,5},{2,6},{3,7},{4,0},{5,1},{6,2},{7,3},{8,12},{9,13},{10,... | collective-permute-start | bytes 147464 | tf_op jit(solution)/shard_map/ppermute | solution.py:283
  33.9 0.1 collective-permute-start.15
  34.0 0.0 collective-permute-done.11.refs_1_
  34.0 2.0 %collective-permute-start.16 = (bf16[32,768]{1,0:T(8,128)(2,1)S(1)}, bf16[32,768]{1,0:T(8,128)(2,1)S(1)}, u32[]{:S(2)}, u32[]{:S(2)}) collective-permute-start(bf16[32,768]{1,0:T(8,128)(2,1)S(1)} %get-tuple-element.43), channel_id=1, source_target_pairs={{0,6},{1,7},{2,0},{3,1},{4,2},{5,3},{6,4},{7,5},{8,14},{9,15},{10,... | collective-permute-start | bytes 147464 | tf_op jit(solution)/shard_map/ppermute | solution.py:283
  36.0 0.1 collective-permute-done.12.refs_2_
  36.2 1.6 %collective-permute-start.17 = (bf16[32,768]{1,0:T(8,128)(2,1)S(1)}, bf16[32,768]{1,0:T(8,128)(2,1)S(1)}, u32[]{:S(2)}, u32[]{:S(2)}) collective-permute-start(bf16[32,768]{1,0:T(8,128)(2,1)S(1)} %get-tuple-element.44), channel_id=1, source_target_pairs={{0,7},{1,6},{2,1},{3,0},{4,3},{5,2},{6,5},{7,4},{8,15},{9,14},{10,... | collective-permute-start | bytes 147464 | tf_op jit(solution)/shard_map/ppermute | solution.py:283
  37.7 0.0 collective-permute-done.13.refs_3_
  37.7 2.2 %collective-permute-done.14.refs_4_ = bf16[32,768]{1,0:T(8,128)(2,1)S(1)} collective-permute-done((bf16[32,768]{1,0:T(8,128)(2,1)S(1)}, bf16[32,768]{1,0:T(8,128)(2,1)S(1)}, u32[]{:S(2)}, u32[]{:S(2)}) %collective-permute-start.14) | collective-permute-done | bytes 49184 | tf_op jit(solution)/shard_map/ppermute | solution.py:283
  40.0 1.0 %collective-permute-done.15.refs_5_ = bf16[32,768]{1,0:T(8,128)(2,1)S(1)} collective-permute-done((bf16[32,768]{1,0:T(8,128)(2,1)S(1)}, bf16[32,768]{1,0:T(8,128)(2,1)S(1)}, u32[]{:S(2)}, u32[]{:S(2)}) %collective-permute-start.15) | collective-permute-done | bytes 49184 | tf_op jit(solution)/shard_map/ppermute | solution.py:283
  40.9 1.0 %collective-permute-done.17.refs_7_ = bf16[32,768]{1,0:T(8,128)(2,1)S(1)} collective-permute-done((bf16[32,768]{1,0:T(8,128)(2,1)S(1)}, bf16[32,768]{1,0:T(8,128)(2,1)S(1)}, u32[]{:S(2)}, u32[]{:S(2)}) %collective-permute-start.17) | collective-permute-done | bytes 49184 | tf_op jit(solution)/shard_map/ppermute | solution.py:283
  41.9 0.1 sum.1
  42.0 1.5 %collective-permute-start.18 = (bf16[32,768]{1,0:T(8,128)(2,1)S(1)}, bf16[32,768]{1,0:T(8,128)(2,1)S(1)}, u32[]{:S(2)}, u32[]{:S(2)}) collective-permute-start(bf16[32,768]{1,0:T(8,128)(2,1)S(1)} %get-tuple-element.46), channel_id=1, source_target_pairs={{0,8},{8,16},{16,24},{24,0},{1,9},{9,17},{17,25},{25,1},{2,10},{10... | collective-permute-start | bytes 147464 | tf_op jit(solution)/shard_map/ppermute | solution.py:278
  43.5 1.5 %collective-permute-start.19 = (bf16[32,768]{1,0:T(8,128)(2,1)S(1)}, bf16[32,768]{1,0:T(8,128)(2,1)S(1)}, u32[]{:S(2)}, u32[]{:S(2)}) collective-permute-start(bf16[32,768]{1,0:T(8,128)(2,1)S(1)} %get-tuple-element.47), channel_id=1, source_target_pairs={{0,16},{8,24},{16,0},{24,8},{1,17},{9,25},{17,1},{25,9},{2,18},{10... | collective-permute-start | bytes 147464 | tf_op jit(solution)/shard_map/ppermute | solution.py:278
  45.0 1.2 %collective-permute-start.20 = (bf16[32,768]{1,0:T(8,128)(2,1)S(1)}, bf16[32,768]{1,0:T(8,128)(2,1)S(1)}, u32[]{:S(2)}, u32[]{:S(2)}) collective-permute-start(bf16[32,768]{1,0:T(8,128)(2,1)S(1)} %get-tuple-element.48), channel_id=1, source_target_pairs={{0,24},{8,0},{16,8},{24,16},{1,25},{9,1},{17,9},{25,17},{2,26},{10... | collective-permute-start | bytes 147464 | tf_op jit(solution)/shard_map/ppermute | solution.py:278
  46.2 0.9 %collective-permute-done.18.refs_1_ = bf16[32,768]{1,0:T(8,128)(2,1)S(1)} collective-permute-done((bf16[32,768]{1,0:T(8,128)(2,1)S(1)}, bf16[32,768]{1,0:T(8,128)(2,1)S(1)}, u32[]{:S(2)}, u32[]{:S(2)}) %collective-permute-start.18) | collective-permute-done | bytes 49184 | tf_op jit(solution)/shard_map/ppermute | solution.py:278
  47.1 0.7 %collective-permute-done.19.refs_2_ = bf16[32,768]{1,0:T(8,128)(2,1)S(1)} collective-permute-done((bf16[32,768]{1,0:T(8,128)(2,1)S(1)}, bf16[32,768]{1,0:T(8,128)(2,1)S(1)}, u32[]{:S(2)}, u32[]{:S(2)}) %collective-permute-start.19) | collective-permute-done | bytes 49184 | tf_op jit(solution)/shard_map/ppermute | solution.py:278
  47.8 1.3 %collective-permute-done.20.refs_3_ = bf16[32,768]{1,0:T(8,128)(2,1)S(1)} collective-permute-done((bf16[32,768]{1,0:T(8,128)(2,1)S(1)}, bf16[32,768]{1,0:T(8,128)(2,1)S(1)}, u32[]{:S(2)}, u32[]{:S(2)}) %collective-permute-start.20) | collective-permute-done | bytes 49184 | tf_op jit(solution)/shard_map/ppermute | solution.py:278
  49.1 1.4 %deal.1 = bf16[16,8,768]{2,1,0:T(8,128)(2,1)} custom-call(s32[1]{0:T(128)} %bitcast.me_ref, s32[8]{0:T(128)S(1)} %copy-done.2, f32[8]{0:T(128)S(1)} %copy-done.3, f32[8,128]{1,0:T(8,128)S(1)} %get-tuple-element.31.refs_2_.total_ref, bf16[32,768]{1,0:T(8,128)(2,1)S(1)} %get-tuple-element.45.refs_0_, bf16[32,768]{1,0:T(8,128)(2,1)S(1)} %collective-permute-done.18.refs_1_, ...), custom_call_target="tpu_custom_call" | custom-call | bytes 397312 | tf_op jit(solution)/shard_map/deal/pallas_call | solution.py:252
  (8 shorter events, 0.0 us)
Async XLA Ops:
  0.0 25.9 %collective-permute-start.3 = (bf16[12,128,768]{2,1,0:T(8,128)(2,1)}, bf16[12,128,768]{2,1,0:T(8,128)(2,1)S(1)}, u32[]{:S(2)}, u32[]{:S(2)}) collective-permute-start(bf16[12,128,768]{2,1,0:T(8,128)(2,1)} %refs_0_.1), channel_id=1, source_target_pairs={{0,1},{1,0},{2,3},{3,2},{4,5},{5,4},{6,7},{7,6},{8,9},{9,8},{10,11... | collective-permute-start | bytes 7077896 | tf_op jit(solution)/shard_map/ppermute | solution.py:283
  2.4 6.4 %collective-permute-start = (bf16[32,896]{1,0:T(8,128)(2,1)}, bf16[32,896]{1,0:T(8,128)(2,1)S(1)}, u32[]{:S(2)}, u32[]{:S(2)}) collective-permute-start(bf16[32,896]{1,0:T(8,128)(2,1)} %get-tuple-element.28), channel_id=1, source_target_pairs={{0,8},{8,16},{16,24},{24,0},{1,9},{9,17},{17,25},{25,1},{2,10},{10... | collective-permute-start | bytes 172040 | tf_op jit(solution)/shard_map/ppermute | solution.py:278
  4.9 5.0 %collective-permute-start.1 = (bf16[32,896]{1,0:T(8,128)(2,1)}, bf16[32,896]{1,0:T(8,128)(2,1)S(1)}, u32[]{:S(2)}, u32[]{:S(2)}) collective-permute-start(bf16[32,896]{1,0:T(8,128)(2,1)} %get-tuple-element.29), channel_id=1, source_target_pairs={{0,16},{8,24},{16,0},{24,8},{1,17},{9,25},{17,1},{25,9},{2,18},{10... | collective-permute-start | bytes 172040 | tf_op jit(solution)/shard_map/ppermute | solution.py:278
  6.4 4.4 %collective-permute-start.2 = (bf16[32,896]{1,0:T(8,128)(2,1)}, bf16[32,896]{1,0:T(8,128)(2,1)S(1)}, u32[]{:S(2)}, u32[]{:S(2)}) collective-permute-start(bf16[32,896]{1,0:T(8,128)(2,1)} %get-tuple-element.30), channel_id=1, source_target_pairs={{0,24},{8,0},{16,8},{24,16},{1,25},{9,1},{17,9},{25,17},{2,26},{10... | collective-permute-start | bytes 172040 | tf_op jit(solution)/shard_map/ppermute | solution.py:278
  10.8 0.8 %copy-start.1 = (bf16[32,896]{1,0:T(8,128)(2,1)S(1)}, bf16[32,896]{1,0:T(8,128)(2,1)}, u32[]{:S(2)}) copy-start(bf16[32,896]{1,0:T(8,128)(2,1)} %get-tuple-element.27.refs_0_) | copy-start | bytes 172036
  11.7 5.8 %collective-permute-start.9 = (bf16[216,128]{1,0:T(8,128)(2,1)S(1)}, bf16[216,128]{1,0:T(8,128)(2,1)S(1)}, u32[]{:S(2)}, u32[]{:S(2)}) collective-permute-start(bf16[216,128]{1,0:T(8,128)(2,1)S(1)} %get-tuple-element.35.refs_0_), channel_id=1, source_target_pairs={{0,6},{1,7},{2,0},{3,1},{4,2},{5,3},{6,4},{7,5},{8,14},{9,15},{10,... | collective-permute-start | bytes 165896 | tf_op jit(solution)/shard_map/ppermute | solution.py:283
  15.4 5.1 %collective-permute-start.7 = (bf16[216,128]{1,0:T(8,128)(2,1)S(1)}, bf16[216,128]{1,0:T(8,128)(2,1)S(1)}, u32[]{:S(2)}, u32[]{:S(2)}) collective-permute-start(bf16[216,128]{1,0:T(8,128)(2,1)S(1)} %get-tuple-element.35.refs_0_), channel_id=1, source_target_pairs={{0,4},{1,5},{2,6},{3,7},{4,0},{5,1},{6,2},{7,3},{8,12},{9,13},{10,... | collective-permute-start | bytes 165896 | tf_op jit(solution)/shard_map/ppermute | solution.py:283
  15.4 6.6 %collective-permute-start.5 = (bf16[216,128]{1,0:T(8,128)(2,1)S(1)}, bf16[216,128]{1,0:T(8,128)(2,1)S(1)}, u32[]{:S(2)}, u32[]{:S(2)}) collective-permute-start(bf16[216,128]{1,0:T(8,128)(2,1)S(1)} %get-tuple-element.35.refs_0_), channel_id=1, source_target_pairs={{0,2},{1,3},{2,4},{3,5},{4,6},{5,7},{6,0},{7,1},{8,10},{9,11},{10,... | collective-permute-start | bytes 165896 | tf_op jit(solution)/shard_map/ppermute | solution.py:283
  16.4 8.6 %collective-permute-start.10 = (bf16[216,128]{1,0:T(8,128)(2,1)S(1)}, bf16[216,128]{1,0:T(8,128)(2,1)S(1)}, u32[]{:S(2)}, u32[]{:S(2)}) collective-permute-start(bf16[216,128]{1,0:T(8,128)(2,1)S(1)} %get-tuple-element.36), channel_id=1, source_target_pairs={{0,7},{1,6},{2,1},{3,0},{4,3},{5,2},{6,5},{7,4},{8,15},{9,14},{10,... | collective-permute-start | bytes 165896 | tf_op jit(solution)/shard_map/ppermute | solution.py:283
  17.6 7.4 %collective-permute-start.8 = (bf16[216,128]{1,0:T(8,128)(2,1)S(1)}, bf16[216,128]{1,0:T(8,128)(2,1)S(1)}, u32[]{:S(2)}, u32[]{:S(2)}) collective-permute-start(bf16[216,128]{1,0:T(8,128)(2,1)S(1)} %get-tuple-element.36), channel_id=1, source_target_pairs={{0,5},{1,4},{2,7},{3,6},{4,1},{5,0},{6,3},{7,2},{8,13},{9,12},{10,... | collective-permute-start | bytes 165896 | tf_op jit(solution)/shard_map/ppermute | solution.py:283
  20.5 5.4 %collective-permute-start.6 = (bf16[216,128]{1,0:T(8,128)(2,1)S(1)}, bf16[216,128]{1,0:T(8,128)(2,1)S(1)}, u32[]{:S(2)}, u32[]{:S(2)}) collective-permute-start(bf16[216,128]{1,0:T(8,128)(2,1)S(1)} %get-tuple-element.36), channel_id=1, source_target_pairs={{0,3},{1,2},{2,5},{3,4},{4,7},{5,6},{6,1},{7,0},{8,11},{9,10},{10,... | collective-permute-start | bytes 165896 | tf_op jit(solution)/shard_map/ppermute | solution.py:283
  22.0 3.9 %collective-permute-start.4 = (bf16[216,128]{1,0:T(8,128)(2,1)S(1)}, bf16[216,128]{1,0:T(8,128)(2,1)S(1)}, u32[]{:S(2)}, u32[]{:S(2)}) collective-permute-start(bf16[216,128]{1,0:T(8,128)(2,1)S(1)} %get-tuple-element.36), channel_id=1, source_target_pairs={{0,1},{1,0},{2,3},{3,2},{4,5},{5,4},{6,7},{7,6},{8,9},{9,8},{10,11... | collective-permute-start | bytes 165896 | tf_op jit(solution)/shard_map/ppermute | solution.py:283
  22.0 1.3 %copy-start = (bf16[768,768]{1,0:T(8,128)(2,1)S(1)}, bf16[768,768]{1,0:T(8,128)(2,1)}, u32[]{:S(2)}) copy-start(bf16[768,768]{1,0:T(8,128)(2,1)} %refs_1_.1) | copy-start | bytes 3538948
  25.9 23.2 %copy-start.2 = (s32[8]{0:T(128)S(1)}, s32[8]{0:T(128)}, u32[]{:S(2)}) copy-start(s32[8]{0:T(128)} %target_ref.1) | copy-start | bytes 100
  25.9 23.2 %copy-start.3 = (f32[8]{0:T(128)S(1)}, f32[8]{0:T(128)}, u32[]{:S(2)}) copy-start(f32[8]{0:T(128)} %weights_ref.1) | copy-start | bytes 100
  29.6 4.4 %collective-permute-start.11 = (bf16[32,768]{1,0:T(8,128)(2,1)S(1)}, bf16[32,768]{1,0:T(8,128)(2,1)S(1)}, u32[]{:S(2)}, u32[]{:S(2)}) collective-permute-start(bf16[32,768]{1,0:T(8,128)(2,1)S(1)} %get-tuple-element.38), channel_id=1, source_target_pairs={{0,1},{1,0},{2,3},{3,2},{4,5},{5,4},{6,7},{7,6},{8,9},{9,8},{10,11... | collective-permute-start | bytes 147464 | tf_op jit(solution)/shard_map/ppermute | solution.py:283
  29.7 6.5 %collective-permute-start.12 = (bf16[32,768]{1,0:T(8,128)(2,1)S(1)}, bf16[32,768]{1,0:T(8,128)(2,1)S(1)}, u32[]{:S(2)}, u32[]{:S(2)}) collective-permute-start(bf16[32,768]{1,0:T(8,128)(2,1)S(1)} %get-tuple-element.39), channel_id=1, source_target_pairs={{0,2},{1,3},{2,4},{3,5},{4,6},{5,7},{6,0},{7,1},{8,10},{9,11},{10,... | collective-permute-start | bytes 147464 | tf_op jit(solution)/shard_map/ppermute | solution.py:283
  29.8 8.0 %collective-permute-start.13 = (bf16[32,768]{1,0:T(8,128)(2,1)S(1)}, bf16[32,768]{1,0:T(8,128)(2,1)S(1)}, u32[]{:S(2)}, u32[]{:S(2)}) collective-permute-start(bf16[32,768]{1,0:T(8,128)(2,1)S(1)} %get-tuple-element.40), channel_id=1, source_target_pairs={{0,3},{1,2},{2,5},{3,4},{4,7},{5,6},{6,1},{7,0},{8,11},{9,10},{10,... | collective-permute-start | bytes 147464 | tf_op jit(solution)/shard_map/ppermute | solution.py:283
  31.4 8.6 %collective-permute-start.14 = (bf16[32,768]{1,0:T(8,128)(2,1)S(1)}, bf16[32,768]{1,0:T(8,128)(2,1)S(1)}, u32[]{:S(2)}, u32[]{:S(2)}) collective-permute-start(bf16[32,768]{1,0:T(8,128)(2,1)S(1)} %get-tuple-element.41), channel_id=1, source_target_pairs={{0,4},{1,5},{2,6},{3,7},{4,0},{5,1},{6,2},{7,3},{8,12},{9,13},{10,... | collective-permute-start | bytes 147464 | tf_op jit(solution)/shard_map/ppermute | solution.py:283
  33.9 7.0 %collective-permute-start.15 = (bf16[32,768]{1,0:T(8,128)(2,1)S(1)}, bf16[32,768]{1,0:T(8,128)(2,1)S(1)}, u32[]{:S(2)}, u32[]{:S(2)}) collective-permute-start(bf16[32,768]{1,0:T(8,128)(2,1)S(1)} %get-tuple-element.42), channel_id=1, source_target_pairs={{0,5},{1,4},{2,7},{3,6},{4,1},{5,0},{6,3},{7,2},{8,13},{9,12},{10,... | collective-permute-start | bytes 147464 | tf_op jit(solution)/shard_map/ppermute | solution.py:283
  34.0 6.9 %collective-permute-start.16 = (bf16[32,768]{1,0:T(8,128)(2,1)S(1)}, bf16[32,768]{1,0:T(8,128)(2,1)S(1)}, u32[]{:S(2)}, u32[]{:S(2)}) collective-permute-start(bf16[32,768]{1,0:T(8,128)(2,1)S(1)} %get-tuple-element.43), channel_id=1, source_target_pairs={{0,6},{1,7},{2,0},{3,1},{4,2},{5,3},{6,4},{7,5},{8,14},{9,15},{10,... | collective-permute-start | bytes 147464 | tf_op jit(solution)/shard_map/ppermute | solution.py:283
  36.2 5.7 %collective-permute-start.17 = (bf16[32,768]{1,0:T(8,128)(2,1)S(1)}, bf16[32,768]{1,0:T(8,128)(2,1)S(1)}, u32[]{:S(2)}, u32[]{:S(2)}) collective-permute-start(bf16[32,768]{1,0:T(8,128)(2,1)S(1)} %get-tuple-element.44), channel_id=1, source_target_pairs={{0,7},{1,6},{2,1},{3,0},{4,3},{5,2},{6,5},{7,4},{8,15},{9,14},{10,... | collective-permute-start | bytes 147464 | tf_op jit(solution)/shard_map/ppermute | solution.py:283
  42.0 5.1 %collective-permute-start.18 = (bf16[32,768]{1,0:T(8,128)(2,1)S(1)}, bf16[32,768]{1,0:T(8,128)(2,1)S(1)}, u32[]{:S(2)}, u32[]{:S(2)}) collective-permute-start(bf16[32,768]{1,0:T(8,128)(2,1)S(1)} %get-tuple-element.46), channel_id=1, source_target_pairs={{0,8},{8,16},{16,24},{24,0},{1,9},{9,17},{17,25},{25,1},{2,10},{10... | collective-permute-start | bytes 147464 | tf_op jit(solution)/shard_map/ppermute | solution.py:278
  43.5 4.3 %collective-permute-start.19 = (bf16[32,768]{1,0:T(8,128)(2,1)S(1)}, bf16[32,768]{1,0:T(8,128)(2,1)S(1)}, u32[]{:S(2)}, u32[]{:S(2)}) collective-permute-start(bf16[32,768]{1,0:T(8,128)(2,1)S(1)} %get-tuple-element.47), channel_id=1, source_target_pairs={{0,16},{8,24},{16,0},{24,8},{1,17},{9,25},{17,1},{25,9},{2,18},{10... | collective-permute-start | bytes 147464 | tf_op jit(solution)/shard_map/ppermute | solution.py:278
  45.0 4.1 %collective-permute-start.20 = (bf16[32,768]{1,0:T(8,128)(2,1)S(1)}, bf16[32,768]{1,0:T(8,128)(2,1)S(1)}, u32[]{:S(2)}, u32[]{:S(2)}) collective-permute-start(bf16[32,768]{1,0:T(8,128)(2,1)S(1)} %get-tuple-element.48), channel_id=1, source_target_pairs={{0,24},{8,0},{16,8},{24,16},{1,25},{9,1},{17,9},{25,17},{2,26},{10... | collective-permute-start | bytes 147464 | tf_op jit(solution)/shard_map/ppermute | solution.py:278

commit v5 on v4

v5 whole, which is shorter than its diff:
```python
import functools
import math
import jax
import jax.numpy as jnp
from jax import lax
from jax.experimental import pallas as pl
from jax.experimental.pallas import tpu as pltpu
from jax.sharding import PartitionSpec as P

F32 = jnp.float32
BF16 = jnp.bfloat16
LANES = 128
PARTS = 1
ROUTE_VMEM = 56
STAGE_VMEM = 48


def power(size):
    return size & (size - 1) == 0


def target_of(me, s, size):
    return lax.bitwise_xor(me, jnp.int32(s)) if power(size) else lax.rem(me + s, size)


def source_of(me, s, size):
    return lax.bitwise_xor(me, jnp.int32(s)) if power(size) else lax.rem(me + size - s, size)


def back_of(s, size):
    return s if power(size) else (size - s) % size


def terms(value, count):
    out = []
    for _ in range(count):
        term = value.astype(BF16).astype(F32)
        out.append(term)
        value = value - term
    return out


def round_up(x, unit):
    return -(-x // unit) * unit


def write_lines(out, start, pieces):
    have = sum(p.shape[0] for p in pieces)
    rest = out.shape[0] - start - have
    if rest:
        pieces = list(pieces) + [jnp.zeros((rest, LANES), F32)]
    out[start:, :] = jnp.concatenate(pieces, axis=0).astype(BF16)


def wide_mask(line, width):
    return jnp.concatenate([line] * (width // LANES), axis=1) > 0


def stage_kernel(*refs):
    sems = refs[-1]
    count = sems.shape[0]
    copies = [pltpu.make_async_copy(refs[i], refs[i - count - 1], sems.at[i]) for i in range(count)]
    for copy in copies:
        copy.start()
    for copy in copies:
        copy.wait()


def route_kernel(keep, cap, core_ref, grp_ref, *refs):
    anys, refs = refs[:5], refs[5:]
    mine_ref, twin_ref, target_ref, weights_ref, own_ref, fields_ref, diag_ref, wide, blocks, parts, lines, sems = refs
    held = (target_ref, weights_ref, own_ref, fields_ref, diag_ref)
    copies = [pltpu.make_async_copy(a, b, sems.at[i]) for i, (a, b) in enumerate(zip(anys, held))]
    for copy in copies:
        copy.start()
    grp, core = grp_ref[0], core_ref[0]
    rows, slots, orbitals = own_ref.shape
    vec_count = fields_ref.shape[1]
    chunks = orbitals // LANES
    spots = (blocks.shape[0] - 1) // 2
    groups = spots // cap
    live = groups * keep
    blocks[...] = jnp.zeros(blocks.shape, F32)
    lines[...] = jnp.zeros(lines.shape, F32)
    for copy in copies:
        copy.wait()
    wide[...] = own_ref[...].astype(F32)
    exponent = fields_ref[:, 0:1] * diag_ref[0:1, :]
    for g in range(1, vec_count):
        exponent = exponent + fields_ref[:, g : g + 1] * diag_ref[g : g + 1, :]
    for i, term in enumerate(terms(exponent, 2)):
        for c in range(chunks):
            parts[:, i * chunks + c, :] = term[:, c * LANES : (c + 1) * LANES]
    weight = F32(0.0)
    for slot in range(slots):
        t = target_ref[slot]
        alive = t < live
        weight = weight + jnp.where(alive, weights_ref[slot], F32(0.0))
        turn = lax.div(t, groups)
        other = jnp.where(lax.rem(turn, 2) == core, 0, 1)
        turn = lax.div(turn, 2)
        at = (other * groups + lax.rem(t, groups)) * cap + lax.rem(turn, cap)
        at = jnp.where(alive, at, 2 * spots)
        blocks[at] = wide[:, slot, :]
        parts[slot, 2 * chunks : 2 * chunks + 1, :] = jnp.full((1, LANES), (turn + 1).astype(F32), F32)
        lines[at] = parts[slot]
    sums = terms(jnp.full((1, LANES), weight, F32), 3)
    for other, out in enumerate((mine_ref, twin_ref)):
        tail = []
        for s in range(groups):
            base = (other * groups + target_of(grp, s, groups)) * cap
            for k in range(cap):
                block = blocks[base + k]
                for c in range(chunks):
                    at = ((s * cap + k) * chunks + c) * rows
                    out[at : at + rows, :] = block[:, c * LANES : (c + 1) * LANES].astype(BF16)
                tail.append(lines[base + k][0 : 2 * chunks + 1])
        write_lines(out, spots * chunks * rows, tail + sums)


def pair_kernel(cap, chunks, rows, core_ref, mine_ref, twin_ref, *outs):
    spots = len(outs) * cap
    each = 2 * chunks + 1
    first = core_ref[0] == 0
    start = spots * chunks * rows
    tail_mine, tail_twin = mine_ref[start:, :].astype(F32), twin_ref[start:, :].astype(F32)
    sums = [tail_mine[spots * each : spots * each + 3]]
    for s, out in enumerate(outs):
        tail = []
        for k in range(cap):
            spot = s * cap + k
            for c in range(chunks):
                at = (spot * chunks + c) * rows
                a, b = mine_ref[at : at + rows, :].astype(F32), twin_ref[at : at + rows, :].astype(F32)
                both = jnp.concatenate([jnp.where(first, a, b), jnp.where(first, b, a)], axis=0)
                to = (k * chunks + c) * 2 * rows
                out[to : to + 2 * rows, :] = both.astype(BF16)
            at = spot * each
            a, b = tail_mine[at : at + 2 * chunks], tail_twin[at : at + 2 * chunks]
            total = (a[0:chunks] + b[0:chunks]) + (a[chunks:] + b[chunks:])
            tail += terms(total, 2) + [tail_mine[at + 2 * chunks : at + each]]
        write_lines(out, cap * chunks * 2 * rows, tail + sums)


def merge_kernel(order, half, cap, rows, chunks, *refs):
    ins, (*outs, weight_ref, pick_ref) = refs[: len(order)], refs[len(order) :]
    each = 2 * chunks + 1
    start = cap * chunks * rows
    weight = jnp.zeros((1, LANES), F32)
    walker = [[jnp.zeros((rows, LANES), F32)] * chunks for _ in range(half)]
    line = [jnp.zeros((2 * chunks, LANES), F32)] * half
    for s, ref in zip(order, ins):
        tail = ref[start:, :].astype(F32)
        total = tail[cap * each : cap * each + 1] + tail[cap * each + 1 : cap * each + 2]
        weight = weight + (total + tail[cap * each + 2 : cap * each + 3])
        for k in range(cap):
            flag = tail[(k + 1) * each - 1 : (k + 1) * each]
            part = tail[k * each : (k + 1) * each - 1]
            for u in range(k, half, cap):
                mine = jnp.where(flag == u + 1, F32(1.0), F32(0.0))
                pick_ref[s * half + u : s * half + u + 1, :] = mine
                line[u] = jnp.where(mine > 0, part, line[u])
                for c in range(chunks):
                    at = (k * chunks + c) * rows
                    block = ref[at : at + rows, :].astype(F32)
                    walker[u][c] = jnp.where(mine > 0, block, walker[u][c])
    weight_ref[...] = jnp.broadcast_to(weight, weight_ref.shape)
    count = half // len(outs)
    for p, out in enumerate(outs):
        for w in range(count):
            for c in range(chunks):
                at = (w * chunks + c) * rows
                out[at : at + rows, :] = walker[p * count + w][c].astype(BF16)
        write_lines(out, count * chunks * rows, line[p * count : (p + 1) * count])


def fock_kernel(order, send_order, count, rows, chip_ref, body_ref, own_ref, twin_ref, *refs):
    n = len(order)
    ins, outs = refs[:n], refs[n : 2 * n]
    prop, turned, coup, result = refs[2 * n :]
    vec_count, occupied, orbitals = own_ref.shape
    chunks = orbitals // LANES
    chip = chip_ref[0]
    start = count * chunks * rows
    exponent = jnp.zeros((2 * count * chunks, LANES), F32)
    for ref in ins:
        exponent = exponent + ref[start : start + 2 * count * chunks, :].astype(F32)
    growth = []
    for w in range(count):
        at = 2 * w * chunks
        growth.append(jnp.exp(exponent[at : at + chunks] + exponent[at + chunks : at + 2 * chunks]))
    for ref, s in zip(ins, order):
        source = source_of(chip, s, n)
        for w in range(count):
            for c in range(chunks):
                at = (w * chunks + c) * rows
                piece = ref[at : at + rows, :].astype(F32) * growth[w][c : c + 1]
                prop[w, source, :, c * LANES : (c + 1) * LANES] = piece.astype(prop.dtype)
    scaled = jnp.concatenate([prop[w, i] for w in range(count) for i in range(n)], axis=0).astype(BF16)
    turned[...] = jnp.dot(scaled, body_ref[...], preferred_element_type=F32).T.astype(BF16)
    batch = math.gcd(vec_count, 4)
    for c, ref in enumerate((own_ref, twin_ref)):
        for g in range(0, vec_count, batch):
            left = ref[g : g + batch].reshape(batch * occupied, orbitals)
            s = jnp.dot(left, turned[...], preferred_element_type=F32).astype(BF16)
            for k in range(batch):
                at = (c * vec_count + g + k) * occupied
                for w in range(count):
                    coup[w * occupied : (w + 1) * occupied, at : at + occupied] = s[
                        k * occupied : (k + 1) * occupied, w * occupied : (w + 1) * occupied
                    ]
    tile = 256 if orbitals % 256 == 0 else orbitals
    depth = vec_count * occupied
    for t in range(0, orbitals, tile):
        total = jnp.dot(
            coup[:, :depth],
            own_ref[:, :, t : t + tile].reshape(depth, tile),
            preferred_element_type=F32,
        )
        total = total + jnp.dot(
            coup[:, depth:],
            twin_ref[:, :, t : t + tile].reshape(depth, tile),
            preferred_element_type=F32,
        )
        for w in range(count):
            for i in range(n):
                at = w * occupied + i * rows
                result[w, i, :, t : t + tile] = total[at : at + rows].astype(result.dtype)
    for out, s in zip(outs, send_order):
        to = target_of(chip, s, n)
        for w in range(count):
            out[w * rows : (w + 1) * rows, :] = result[w, to].astype(BF16)


def sum_kernel(n, first, half, cap, groups, core_ref, pick_ref, *refs):
    ins, (mine_ref, twin_ref) = refs[:n], refs[n:]
    orbitals = mine_ref.shape[1]
    rows = mine_ref.shape[0] // (groups * cap)
    total = ins[0][...].astype(F32)
    for ref in ins[1:]:
        total = total + ref[...].astype(F32)
    count = total.shape[0] // (2 * rows)
    core = core_ref[0]
    for s in range(groups):
        source = back_of(s, groups)
        for k in range(cap):
            value = jnp.zeros((2 * rows, orbitals), F32)
            for w in range(count):
                u = first + w
                if u % cap == k:
                    mine = pick_ref[source * half + u : source * half + u + 1, :]
                    value = jnp.where(wide_mask(mine, orbitals), total[2 * w * rows : 2 * (w + 1) * rows], value)
            at = (s * cap + k) * rows
            low, high = value[0:rows], value[rows:]
            mine_ref[at : at + rows, :] = jnp.where(core == 0, low, high).astype(BF16)
            twin_ref[at : at + rows, :] = jnp.where(core == 0, high, low).astype(BF16)


def join_kernel(parts, core_ref, *refs):
    mine, twin, outs = refs[:parts], refs[parts : 2 * parts], refs[2 * parts :]
    block = outs[0].shape[0] // 2
    core = core_ref[0]
    for s, out in enumerate(outs):
        at = slice(s * block, (s + 1) * block)
        a, b = mine[0][at, :].astype(F32), twin[0][at, :].astype(F32)
        for p in range(1, parts):
            a, b = a + mine[p][at, :].astype(F32), b + twin[p][at, :].astype(F32)
        out[0:block, :] = jnp.where(core == 0, a, b).astype(BF16)
        out[block:, :] = jnp.where(core == 0, b, a).astype(BF16)


def deal_kernel(keep, cap, order, grp_ref, target_ref, weights_ref, total_ref, *refs):
    groups = len(order)
    ins, (out_ref, blocks, wide) = refs[:groups], refs[groups:]
    rows, slots, orbitals = out_ref.shape
    live = groups * keep
    for s, ref in zip(order, ins):
        base = source_of(grp_ref[0], s, groups) * 2 * cap
        for k in range(2 * cap):
            blocks[base + k] = ref[k * rows : (k + 1) * rows, :].astype(F32)
    blocks[groups * 2 * cap] = jnp.zeros((rows, orbitals), F32)
    for slot in range(slots):
        t = target_ref[slot]
        alive = t < live
        turn = lax.div(t, groups)
        at = (lax.rem(t, groups) * 2 + lax.rem(turn, 2)) * cap + lax.rem(lax.div(turn, 2), cap)
        at = jnp.where(alive, at, groups * 2 * cap)
        weight = jnp.where(alive, weights_ref[slot], F32(0.0))
        factor = jnp.full((1, LANES), weight * live, F32) / total_ref[0:1, :]
        wide[:, slot, :] = blocks[at] * factor[:, 0:1]
    out_ref[...] = wide[...].astype(BF16)


def call(kernel, outs, scalars, held, arrays, scratch, name, flops=0, vmem=40):
    smem = pl.BlockSpec(memory_space=pltpu.SMEM)
    full = pl.BlockSpec(memory_space=pltpu.VMEM)
    size = sum(x.size * x.dtype.itemsize for x in list(arrays) + list(outs))
    return pl.pallas_call(
        kernel,
        out_shape=outs,
        in_specs=[smem] * len(scalars) + [pl.BlockSpec(memory_space=pl.ANY)] * len(held) + [full] * len(arrays),
        out_specs=[full] * len(outs),
        scratch_shapes=scratch,
        compiler_params=pltpu.CompilerParams(vmem_limit_bytes=vmem * 2**20),
        cost_estimate=pl.CostEstimate(flops=flops, bytes_accessed=size, transcendentals=0),
        name=name,
    )(*scalars, *held, *arrays)


def body(walkers, one_body, fields, field_diag, chol, weights, target):
    rows, slots, orbitals = walkers.shape
    vec_count, occupied, _ = chol.shape
    n, groups = lax.axis_size("blk"), lax.axis_size("grp")
    chips = n // 2
    keep = slots // 2
    half = keep // 2
    count = half // PARTS
    cap = -(-slots // (2 * groups))
    chunks = orbitals // LANES
    shape = jax.ShapeDtypeStruct
    blk = lax.axis_index("blk")
    grp = lax.axis_index("grp").reshape(1)
    core, chip = lax.rem(blk, 2).reshape(1), lax.div(blk, 2).reshape(1)

    def to_twin(x):
        return lax.ppermute(x, "blk", [(i, i ^ 1) for i in range(n)])

    def to_list(x, s):
        to = [(i, i ^ s if power(groups) else (i + s) % groups) for i in range(groups)]
        return lax.ppermute(x, "grp", to) if s else x

    def to_chip(x, s):
        to = [(i, 2 * (i // 2 ^ s if power(chips) else (i // 2 + s) % chips) + i % 2) for i in range(n)]
        return lax.ppermute(x, "blk", to) if s else x

    send_order = [0] + list(range(chips // 2, chips)) + list(range(1, chips // 2))
    chip_order = [0] + send_order[:0:-1]
    list_order = [0] + sorted(range(1, groups), key=lambda s: -bin(s).count("1"))

    chol_twin = to_twin(chol)
    lines = groups * cap * (chunks * rows + 2 * chunks + 1) + 3
    scalars = [pltpu.SMEM(x.shape, x.dtype) for x in (target, weights)]
    mine, twin = call(
        functools.partial(route_kernel, keep, cap),
        [shape((round_up(lines, 16), LANES), BF16)] * 2,
        [core, grp],
        [target, weights, walkers, fields, field_diag],
        [],
        scalars
        + [pltpu.VMEM(x.shape, x.dtype) for x in (walkers, fields, field_diag)]
        + [
            pltpu.VMEM((rows, slots, orbitals), F32),
            pltpu.VMEM((2 * groups * cap + 1, rows, orbitals), F32),
            pltpu.VMEM((slots, 2 * chunks + 4, LANES), F32),
            pltpu.VMEM((2 * groups * cap + 1, 2 * chunks + 4, LANES), F32),
            pltpu.SemaphoreType.DMA((5,)),
        ],
        "route",
        vmem=ROUTE_VMEM,
    )
    lines = cap * (chunks * 2 * rows + 2 * chunks + 1) + 3
    twin = to_twin(twin)
    (mine,) = call(
        stage_kernel,
        [shape(mine.shape, mine.dtype)],
        [],
        [mine],
        [],
        [pltpu.SemaphoreType.DMA((1,))],
        "hold",
    )
    routed = call(
        functools.partial(pair_kernel, cap, chunks, rows),
        [shape((round_up(lines, 16), LANES), BF16)] * groups,
        [core],
        [],
        [mine, twin],
        [],
        "pair",
    )
    routed = [to_list(routed[s], s) for s in list_order]
    payload = shape((count * chunks * 2 * rows + round_up(2 * count * chunks, 8), LANES), BF16)
    *payloads, weight_sum, pick = call(
        functools.partial(merge_kernel, list_order, half, cap, 2 * rows, chunks),
        [payload] * PARTS + [shape((8, LANES), F32), shape((groups * half, LANES), F32)],
        [],
        [],
        routed,
        [],
        "merge",
    )
    own, held_body = call(
        stage_kernel,
        [shape(x.shape, x.dtype) for x in (chol, one_body)],
        [],
        [chol, one_body, weight_sum],
        [],
        [pltpu.SemaphoreType.DMA((2,))],
        "stage",
        vmem=STAGE_VMEM,
    )
    gathered = [[to_chip(x, s) for s in chip_order] for x in payloads]
    held = F32 if rows % 8 else BF16
    mine, twin = [], []
    for p in range(PARTS):
        out = call(
            functools.partial(fock_kernel, chip_order, send_order, count, 2 * rows),
            [shape((count * 2 * rows, orbitals), BF16)] * chips,
            [chip],
            [],
            [held_body, own, chol_twin] + gathered[p],
            [
                pltpu.VMEM((count, chips, 2 * rows, orbitals), held),
                pltpu.VMEM((orbitals, count * occupied), BF16),
                pltpu.VMEM((count * occupied, 2 * vec_count * occupied), BF16),
                pltpu.VMEM((count, chips, 2 * rows, orbitals), held),
            ],
            "fock",
            flops=2 * count * occupied * orbitals * (orbitals + 4 * vec_count * occupied),
        )
        out = [to_chip(x, s) for s, x in zip(send_order, out)]
        a, b = call(
            functools.partial(sum_kernel, chips, p * count, half, cap, groups),
            [shape((groups * cap * rows, orbitals), BF16)] * 2,
            [core],
            [],
            [pick] + out,
            [],
            "sum",
        )
        mine.append(a)
        twin.append(to_twin(b))
    back = call(
        functools.partial(join_kernel, PARTS),
        [shape((2 * cap * rows, orbitals), BF16)] * groups,
        [core],
        [],
        mine + twin,
        [],
        "join",
    )
    back = [to_list(back[s], s) for s in list_order]
    (out,) = call(
        functools.partial(deal_kernel, keep, cap, list_order),
        [shape(walkers.shape, BF16)],
        [grp, target, weights],
        [],
        [weight_sum] + back,
        [pltpu.VMEM((groups * 2 * cap + 1, rows, orbitals), F32), pltpu.VMEM(walkers.shape, F32)],
        "deal",
    )
    return out


def solution(mesh):
    in_specs = (
        P("blk", "grp", None),
        P(),
        P("grp", "blk"),
        P("blk", None),
        P("blk", None, None),
        P("grp"),
        P("grp"),
    )
    out_specs = P("blk", "grp", None)
    return jax.shard_map(body, mesh=mesh, in_specs=in_specs, out_specs=out_specs, check_vma=False)
```

time: 50.8 us -> 49.8 us (0.980)
  starting transfers between devices: 27.8 us -> 17 us
  waiting for transfers between devices: 11.6 us -> 21.2 us
    ppermute x21 -> x15, starting transfers between devices: 27.8 us -> 17 us  [the longest x6 8.25 us: to_list(): return lax.ppermute(x, 'grp', to) if s else x]
    ppermute x21 -> x15, waiting for transfers between devices: 11.6 us -> 21.2 us  [the longest x6 10.9 us: to_chip(): return lax.ppermute(x, 'blk', to) if s else x]
    pallas_call x6 -> x9, Pallas kernels: 8.92 us -> 9.09 us  [call(): pl.pallas_call(kernel, out_shape=outs, in_specs=[smem] * len(scalars) + [...]
  transfers between devices with their start and end apart: 21 -> 15, of which waited for: 13 -> 12; matrix products, arithmetic and copies ran while one was open for 0% -> 0% of each run, Pallas kernels for 7% -> 8%
where the time goes in v5:
time: 49.8 us; the launch traced here: 49.6 us
  waiting for transfers between devices  21.2 us (43%)
  starting transfers between devices  17 us (34%)
  Pallas kernels  9.09 us (18%)
  local copies, waits for them, and re-layouts  2.18 us (4%)
    ppermute x6, waiting for transfers between devices, to_chip(): return lax.ppermute(x, 'blk', to) if s else x  10.9 us
    pallas_call x9, Pallas kernels, call(): pl.pallas_call(kernel, out_shape=outs, in_specs=[smem] * len(scalars) + [...  9.09 us
    ppermute x6, starting transfers between devices, to_list(): return lax.ppermute(x, 'grp', to) if s else x  8.25 us
    ppermute x6, starting transfers between devices, to_chip(): return lax.ppermute(x, 'blk', to) if s else x  8.12 us
    ppermute x6, waiting for transfers between devices, to_list(): return lax.ppermute(x, 'grp', to) if s else x  7.57 us
    ppermute x3, waiting for transfers between devices, to_twin(): return lax.ppermute(x, 'blk', [(i, i ^ 1) for i in range(n)])  2.78 us
    unnamed x8, local copies, waits for them, and re-layouts  2.18 us
  transfers between devices with their start and end apart: 15, of which 12 were waited for; matrix products, arithmetic and copies ran while one was open for 0% of the time, Pallas kernels for 8%

profile of v5, /device:TPU:0, one launch (start us, length us, event | category | flops | bytes accessed | tf_op | source)
XLA Modules:
  0.0 49.6 jit_solution(18000394850006876863)
XLA Ops:
  0.0 0.5 collective-permute-start.4
  0.5 1.9 %route.1 = (bf16[448,128]{1,0:T(8,128)(2,1)}, bf16[448,128]{1,0:T(8,128)(2,1)}) custom-call(s32[1]{0:T(128)} %bitcast.1.core_ref, s32[1]{0:T(128)} %bitcast.grp_ref, s32[8]{0:T(128)} %target_ref.1, f32[8]{0:T(128)} %weights_ref.1, bf16[16,8,768]{2,1,0:T(8,128)(2,1)} %refs_2_.1, f32[8,12]{1,0:T(8,128)} %refs_3_.1, f32[12,768]{1,0:T(8,128)} %refs_4_.1), custom_call_target="tpu_custom_call" | custom-call | bytes 229376 | tf_op jit(solution)/shard_map/route/pallas_call | solution.py:298
  2.3 0.1 collective-permute-start
  2.5 0.0 copy-start.1
  2.5 0.9 %copy-done.1 = bf16[448,128]{1,0:T(8,128)(2,1)S(1)} copy-done((bf16[448,128]{1,0:T(8,128)(2,1)S(1)}, bf16[448,128]{1,0:T(8,128)(2,1)}, u32[]{:S(2)}) %copy-start.1) | copy-done | bytes 114712
  3.4 0.1 hold.1.mine_ref
  3.5 1.5 %collective-permute-done.twin_ref = bf16[448,128]{1,0:T(8,128)(2,1)S(1)} collective-permute-done((bf16[448,128]{1,0:T(8,128)(2,1)}, bf16[448,128]{1,0:T(8,128)(2,1)S(1)}, u32[]{:S(2)}, u32[]{:S(2)}) %collective-permute-start) | collective-permute-done | bytes 114720 | tf_op jit(solution)/shard_map/ppermute | solution.py:326
  5.0 0.1 pair.1
  5.0 3.9 %collective-permute-start.1 = (bf16[208,128]{1,0:T(8,128)(2,1)S(1)}, bf16[208,128]{1,0:T(8,128)(2,1)S(1)}, u32[]{:S(2)}, u32[]{:S(2)}) collective-permute-start(bf16[208,128]{1,0:T(8,128)(2,1)S(1)} %get-tuple-element.29), channel_id=1, source_target_pairs={{0,24},{8,16},{16,8},{24,0},{1,25},{9,17},{17,9},{25,1},{2,26},{10... | collective-permute-start | bytes 159752 | tf_op jit(solution)/shard_map/ppermute | solution.py:330
  8.9 0.5 %collective-permute-start.2 = (bf16[208,128]{1,0:T(8,128)(2,1)S(1)}, bf16[208,128]{1,0:T(8,128)(2,1)S(1)}, u32[]{:S(2)}, u32[]{:S(2)}) collective-permute-start(bf16[208,128]{1,0:T(8,128)(2,1)S(1)} %get-tuple-element.30), channel_id=1, source_target_pairs={{0,8},{8,0},{16,24},{24,16},{1,9},{9,1},{17,25},{25,17},{2,10},{10... | collective-permute-start | bytes 159752 | tf_op jit(solution)/shard_map/ppermute | solution.py:330
  9.5 0.1 collective-permute-start.3
  9.6 1.5 %collective-permute-done.1.refs_1_ = bf16[208,128]{1,0:T(8,128)(2,1)S(1)} collective-permute-done((bf16[208,128]{1,0:T(8,128)(2,1)S(1)}, bf16[208,128]{1,0:T(8,128)(2,1)S(1)}, u32[]{:S(2)}, u32[]{:S(2)}) %collective-permute-start.1) | collective-permute-done | bytes 53280 | tf_op jit(solution)/shard_map/ppermute | solution.py:330
  11.1 2.0 %collective-permute-done.2.refs_2_ = bf16[208,128]{1,0:T(8,128)(2,1)S(1)} collective-permute-done((bf16[208,128]{1,0:T(8,128)(2,1)S(1)}, bf16[208,128]{1,0:T(8,128)(2,1)S(1)}, u32[]{:S(2)}, u32[]{:S(2)}) %collective-permute-start.2) | collective-permute-done | bytes 53280 | tf_op jit(solution)/shard_map/ppermute | solution.py:330
  13.1 0.5 %collective-permute-done.3.refs_3_ = bf16[208,128]{1,0:T(8,128)(2,1)S(1)} collective-permute-done((bf16[208,128]{1,0:T(8,128)(2,1)S(1)}, bf16[208,128]{1,0:T(8,128)(2,1)S(1)}, u32[]{:S(2)}, u32[]{:S(2)}) %collective-permute-start.3) | collective-permute-done | bytes 53280 | tf_op jit(solution)/shard_map/ppermute | solution.py:330
  13.6 0.1 merge.1
  13.7 2.7 %collective-permute-start.7 = (bf16[408,128]{1,0:T(8,128)(2,1)S(1)}, bf16[408,128]{1,0:T(8,128)(2,1)S(1)}, u32[]{:S(2)}, u32[]{:S(2)}) collective-permute-start(bf16[408,128]{1,0:T(8,128)(2,1)S(1)} %get-tuple-element.36.refs_0_), channel_id=1, source_target_pairs={{0,4},{1,5},{2,6},{3,7},{4,0},{5,1},{6,2},{7,3},{8,12},{9,13},{10,... | collective-permute-start | bytes 313352 | tf_op jit(solution)/shard_map/ppermute | solution.py:334
  16.3 1.3 %collective-permute-start.6 = (bf16[408,128]{1,0:T(8,128)(2,1)S(1)}, bf16[408,128]{1,0:T(8,128)(2,1)S(1)}, u32[]{:S(2)}, u32[]{:S(2)}) collective-permute-start(bf16[408,128]{1,0:T(8,128)(2,1)S(1)} %get-tuple-element.36.refs_0_), channel_id=1, source_target_pairs={{0,6},{1,7},{2,4},{3,5},{4,2},{5,3},{6,0},{7,1},{8,14},{9,15},{10,... | collective-permute-start | bytes 313352 | tf_op jit(solution)/shard_map/ppermute | solution.py:334
  17.7 0.2 collective-permute-start.5
  17.9 0.0 copy-start
  17.9 1.3 %copy-done = bf16[768,768]{1,0:T(8,128)(2,1)S(1)} copy-done((bf16[768,768]{1,0:T(8,128)(2,1)S(1)}, bf16[768,768]{1,0:T(8,128)(2,1)}, u32[]{:S(2)}) %copy-start) | copy-done | bytes 1179672
  19.2 1.7 %stage.1 = (bf16[12,128,768]{2,1,0:T(8,128)(2,1)S(1)}, bf16[768,768]{1,0:T(8,128)(2,1)S(1)}) custom-call(bf16[12,128,768]{2,1,0:T(8,128)(2,1)} %refs_0_.3, bf16[768,768]{1,0:T(8,128)(2,1)S(1)} %copy-done, f32[8,128]{1,0:T(8,128)S(1)} %get-tuple-element.32.refs_2_.total_ref), custom_call_target="tpu_custom_call" | custom-call | bytes 3538944 | tf_op jit(solution)/shard_map/stage/pallas_call | solution.py:298
  20.9 2.9 %collective-permute-done.7.refs_3_ = bf16[408,128]{1,0:T(8,128)(2,1)S(1)} collective-permute-done((bf16[408,128]{1,0:T(8,128)(2,1)S(1)}, bf16[408,128]{1,0:T(8,128)(2,1)S(1)}, u32[]{:S(2)}, u32[]{:S(2)}) %collective-permute-start.7) | collective-permute-done | bytes 104480 | tf_op jit(solution)/shard_map/ppermute | solution.py:334
  23.8 0.0 collective-permute-done.6.refs_2_
  23.8 0.4 collective-permute-done.5.refs_1_
  24.1 0.0 collective-permute-done.4.twin_ref
  24.1 0.0 copy-start.2
  24.1 0.0 copy-start.3
  24.1 3.7 %fock.1 = (bf16[64,768]{1,0:T(8,128)(2,1)S(1)}, bf16[64,768]{1,0:T(8,128)(2,1)S(1)}, bf16[64,768]{1,0:T(8,128)(2,1)S(1)}, bf16[64,768]{1,0:T(8,128)(2,1)S(1)}) custom-call(s32[1]{0:T(128)} %bitcast.2.chip_ref, bf16[768,768]{1,0:T(8,128)(2,1)S(1)} %get-tuple-element.34.body_ref, bf16[12,128,768]{2,1,0:T(8,128)(2,1)S(1)} %get-tuple-element.35.own_ref, ...), custom_call_target="tpu_custom_call" | custom-call | flops 2717908992 | bytes 6709248 | tf_op jit(solution)/shard_map/fock/pallas_call | solution.py:298
  27.8 3.2 %collective-permute-start.8 = (bf16[64,768]{1,0:T(8,128)(2,1)S(1)}, bf16[64,768]{1,0:T(8,128)(2,1)S(1)}, u32[]{:S(2)}, u32[]{:S(2)}) collective-permute-start(bf16[64,768]{1,0:T(8,128)(2,1)S(1)} %get-tuple-element.38), channel_id=1, source_target_pairs={{0,4},{1,5},{2,6},{3,7},{4,0},{5,1},{6,2},{7,3},{8,12},{9,13},{10,... | collective-permute-start | bytes 294920 | tf_op jit(solution)/shard_map/ppermute | solution.py:334
  31.1 0.5 %collective-permute-start.9 = (bf16[64,768]{1,0:T(8,128)(2,1)S(1)}, bf16[64,768]{1,0:T(8,128)(2,1)S(1)}, u32[]{:S(2)}, u32[]{:S(2)}) collective-permute-start(bf16[64,768]{1,0:T(8,128)(2,1)S(1)} %get-tuple-element.39), channel_id=1, source_target_pairs={{0,6},{1,7},{2,4},{3,5},{4,2},{5,3},{6,0},{7,1},{8,14},{9,15},{10,... | collective-permute-start | bytes 294920 | tf_op jit(solution)/shard_map/ppermute | solution.py:334
  31.6 0.1 collective-permute-start.10
  31.7 6.6 %collective-permute-done.8.refs_1_ = bf16[64,768]{1,0:T(8,128)(2,1)S(1)} collective-permute-done((bf16[64,768]{1,0:T(8,128)(2,1)S(1)}, bf16[64,768]{1,0:T(8,128)(2,1)S(1)}, u32[]{:S(2)}, u32[]{:S(2)}) %collective-permute-start.8) | collective-permute-done | bytes 98336 | tf_op jit(solution)/shard_map/ppermute | solution.py:334
  38.3 0.0 collective-permute-done.9.refs_2_
  38.3 1.0 %collective-permute-done.10.refs_3_ = bf16[64,768]{1,0:T(8,128)(2,1)S(1)} collective-permute-done((bf16[64,768]{1,0:T(8,128)(2,1)S(1)}, bf16[64,768]{1,0:T(8,128)(2,1)S(1)}, u32[]{:S(2)}, u32[]{:S(2)}) %collective-permute-start.10) | collective-permute-done | bytes 98336 | tf_op jit(solution)/shard_map/ppermute | solution.py:334
  39.3 0.1 sum.1
  39.4 0.1 collective-permute-start.11
  39.5 1.3 %collective-permute-done.11.refs_1_ = bf16[64,768]{1,0:T(8,128)(2,1)S(1)} collective-permute-done((bf16[64,768]{1,0:T(8,128)(2,1)S(1)}, bf16[64,768]{1,0:T(8,128)(2,1)S(1)}, u32[]{:S(2)}, u32[]{:S(2)}) %collective-permute-start.11) | collective-permute-done | bytes 98336 | tf_op jit(solution)/shard_map/ppermute | solution.py:326
  40.8 2.4 %collective-permute-start.12 = (bf16[32,768]{1,0:T(8,128)(2,1)S(1)}, bf16[32,768]{1,0:T(8,128)(2,1)S(1)}, u32[]{:S(2)}, u32[]{:S(2)}) collective-permute-start(bf16[32,768]{1,0:T(8,128)(2,1)S(1)} %get-tuple-element.44), channel_id=1, source_target_pairs={{0,24},{8,16},{16,8},{24,0},{1,25},{9,17},{17,9},{25,1},{2,26},{10... | collective-permute-start | bytes 147464 | tf_op jit(solution)/shard_map/ppermute | solution.py:330
  43.2 0.8 %collective-permute-start.13 = (bf16[32,768]{1,0:T(8,128)(2,1)S(1)}, bf16[32,768]{1,0:T(8,128)(2,1)S(1)}, u32[]{:S(2)}, u32[]{:S(2)}) collective-permute-start(bf16[32,768]{1,0:T(8,128)(2,1)S(1)} %get-tuple-element.45), channel_id=1, source_target_pairs={{0,8},{8,0},{16,24},{24,16},{1,9},{9,1},{17,25},{25,17},{2,10},{10... | collective-permute-start | bytes 147464 | tf_op jit(solution)/shard_map/ppermute | solution.py:330
  44.0 0.5 %collective-permute-start.14 = (bf16[32,768]{1,0:T(8,128)(2,1)S(1)}, bf16[32,768]{1,0:T(8,128)(2,1)S(1)}, u32[]{:S(2)}, u32[]{:S(2)}) collective-permute-start(bf16[32,768]{1,0:T(8,128)(2,1)S(1)} %get-tuple-element.46), channel_id=1, source_target_pairs={{0,16},{8,24},{16,0},{24,8},{1,17},{9,25},{17,1},{25,9},{2,18},{10... | collective-permute-start | bytes 147464 | tf_op jit(solution)/shard_map/ppermute | solution.py:330
  44.6 1.3 %collective-permute-done.12.refs_1_ = bf16[32,768]{1,0:T(8,128)(2,1)S(1)} collective-permute-done((bf16[32,768]{1,0:T(8,128)(2,1)S(1)}, bf16[32,768]{1,0:T(8,128)(2,1)S(1)}, u32[]{:S(2)}, u32[]{:S(2)}) %collective-permute-start.12) | collective-permute-done | bytes 49184 | tf_op jit(solution)/shard_map/ppermute | solution.py:330
  45.9 1.5 %collective-permute-done.13.refs_2_ = bf16[32,768]{1,0:T(8,128)(2,1)S(1)} collective-permute-done((bf16[32,768]{1,0:T(8,128)(2,1)S(1)}, bf16[32,768]{1,0:T(8,128)(2,1)S(1)}, u32[]{:S(2)}, u32[]{:S(2)}) %collective-permute-start.13) | collective-permute-done | bytes 49184 | tf_op jit(solution)/shard_map/ppermute | solution.py:330
  47.3 0.8 %collective-permute-done.14.refs_3_ = bf16[32,768]{1,0:T(8,128)(2,1)S(1)} collective-permute-done((bf16[32,768]{1,0:T(8,128)(2,1)S(1)}, bf16[32,768]{1,0:T(8,128)(2,1)S(1)}, u32[]{:S(2)}, u32[]{:S(2)}) %collective-permute-start.14) | collective-permute-done | bytes 49184 | tf_op jit(solution)/shard_map/ppermute | solution.py:330
  48.1 0.0 copy-done.2
  48.1 0.0 copy-done.3
  48.1 1.4 %deal.1 = bf16[16,8,768]{2,1,0:T(8,128)(2,1)} custom-call(s32[1]{0:T(128)} %bitcast.grp_ref, s32[8]{0:T(128)S(1)} %copy-done.2, f32[8]{0:T(128)S(1)} %copy-done.3, f32[8,128]{1,0:T(8,128)S(1)} %get-tuple-element.32.refs_2_.total_ref, bf16[32,768]{1,0:T(8,128)(2,1)S(1)} %get-tuple-element.43.refs_0_, bf16[32,768]{1,0:T(8,128)(2,1)S(1)} %collective-permute-done.12.refs_1_, ...), custom_call_target="tpu_custom_call" | custom-call | bytes 397312 | tf_op jit(solution)/shard_map/deal/pallas_call | solution.py:298
  (1 shorter events, 0.0 us)
Async XLA Ops:
  0.0 24.1 %collective-permute-start.4 = (bf16[12,128,768]{2,1,0:T(8,128)(2,1)}, bf16[12,128,768]{2,1,0:T(8,128)(2,1)S(1)}, u32[]{:S(2)}, u32[]{:S(2)}) collective-permute-start(bf16[12,128,768]{2,1,0:T(8,128)(2,1)} %refs_0_.3), channel_id=1, source_target_pairs={{0,1},{1,0},{2,3},{3,2},{4,5},{5,4},{6,7},{7,6},{8,9},{9,8},{10,11... | collective-permute-start | bytes 7077896 | tf_op jit(solution)/shard_map/ppermute | solution.py:326
  2.3 2.6 %collective-permute-start = (bf16[448,128]{1,0:T(8,128)(2,1)}, bf16[448,128]{1,0:T(8,128)(2,1)S(1)}, u32[]{:S(2)}, u32[]{:S(2)}) collective-permute-start(bf16[448,128]{1,0:T(8,128)(2,1)} %get-tuple-element.27), channel_id=1, source_target_pairs={{0,1},{1,0},{2,3},{3,2},{4,5},{5,4},{6,7},{7,6},{8,9},{9,8},{10,11... | collective-permute-start | bytes 344072 | tf_op jit(solution)/shard_map/ppermute | solution.py:326
  2.5 0.9 %copy-start.1 = (bf16[448,128]{1,0:T(8,128)(2,1)S(1)}, bf16[448,128]{1,0:T(8,128)(2,1)}, u32[]{:S(2)}) copy-start(bf16[448,128]{1,0:T(8,128)(2,1)} %get-tuple-element.26.refs_0_) | copy-start | bytes 344068
  5.0 6.0 %collective-permute-start.1 = (bf16[208,128]{1,0:T(8,128)(2,1)S(1)}, bf16[208,128]{1,0:T(8,128)(2,1)S(1)}, u32[]{:S(2)}, u32[]{:S(2)}) collective-permute-start(bf16[208,128]{1,0:T(8,128)(2,1)S(1)} %get-tuple-element.29), channel_id=1, source_target_pairs={{0,24},{8,16},{16,8},{24,0},{1,25},{9,17},{17,9},{25,1},{2,26},{10... | collective-permute-start | bytes 159752 | tf_op jit(solution)/shard_map/ppermute | solution.py:330
  8.9 4.1 %collective-permute-start.2 = (bf16[208,128]{1,0:T(8,128)(2,1)S(1)}, bf16[208,128]{1,0:T(8,128)(2,1)S(1)}, u32[]{:S(2)}, u32[]{:S(2)}) collective-permute-start(bf16[208,128]{1,0:T(8,128)(2,1)S(1)} %get-tuple-element.30), channel_id=1, source_target_pairs={{0,8},{8,0},{16,24},{24,16},{1,9},{9,1},{17,25},{25,17},{2,10},{10... | collective-permute-start | bytes 159752 | tf_op jit(solution)/shard_map/ppermute | solution.py:330
  9.5 4.1 %collective-permute-start.3 = (bf16[208,128]{1,0:T(8,128)(2,1)S(1)}, bf16[208,128]{1,0:T(8,128)(2,1)S(1)}, u32[]{:S(2)}, u32[]{:S(2)}) collective-permute-start(bf16[208,128]{1,0:T(8,128)(2,1)S(1)} %get-tuple-element.31), channel_id=1, source_target_pairs={{0,16},{8,24},{16,0},{24,8},{1,17},{9,25},{17,1},{25,9},{2,18},{10... | collective-permute-start | bytes 159752 | tf_op jit(solution)/shard_map/ppermute | solution.py:330
  13.7 10.1 %collective-permute-start.7 = (bf16[408,128]{1,0:T(8,128)(2,1)S(1)}, bf16[408,128]{1,0:T(8,128)(2,1)S(1)}, u32[]{:S(2)}, u32[]{:S(2)}) collective-permute-start(bf16[408,128]{1,0:T(8,128)(2,1)S(1)} %get-tuple-element.36.refs_0_), channel_id=1, source_target_pairs={{0,4},{1,5},{2,6},{3,7},{4,0},{5,1},{6,2},{7,3},{8,12},{9,13},{10,... | collective-permute-start | bytes 313352 | tf_op jit(solution)/shard_map/ppermute | solution.py:334
  16.3 7.4 %collective-permute-start.6 = (bf16[408,128]{1,0:T(8,128)(2,1)S(1)}, bf16[408,128]{1,0:T(8,128)(2,1)S(1)}, u32[]{:S(2)}, u32[]{:S(2)}) collective-permute-start(bf16[408,128]{1,0:T(8,128)(2,1)S(1)} %get-tuple-element.36.refs_0_), channel_id=1, source_target_pairs={{0,6},{1,7},{2,4},{3,5},{4,2},{5,3},{6,0},{7,1},{8,14},{9,15},{10,... | collective-permute-start | bytes 313352 | tf_op jit(solution)/shard_map/ppermute | solution.py:334
  17.7 6.5 %collective-permute-start.5 = (bf16[408,128]{1,0:T(8,128)(2,1)S(1)}, bf16[408,128]{1,0:T(8,128)(2,1)S(1)}, u32[]{:S(2)}, u32[]{:S(2)}) collective-permute-start(bf16[408,128]{1,0:T(8,128)(2,1)S(1)} %get-tuple-element.36.refs_0_), channel_id=1, source_target_pairs={{0,2},{1,3},{2,0},{3,1},{4,6},{5,7},{6,4},{7,5},{8,10},{9,11},{10,... | collective-permute-start | bytes 313352 | tf_op jit(solution)/shard_map/ppermute | solution.py:334
  17.9 1.3 %copy-start = (bf16[768,768]{1,0:T(8,128)(2,1)S(1)}, bf16[768,768]{1,0:T(8,128)(2,1)}, u32[]{:S(2)}) copy-start(bf16[768,768]{1,0:T(8,128)(2,1)} %refs_1_.3) | copy-start | bytes 3538948
  24.1 24.0 %copy-start.2 = (s32[8]{0:T(128)S(1)}, s32[8]{0:T(128)}, u32[]{:S(2)}) copy-start(s32[8]{0:T(128)} %target_ref.1) | copy-start | bytes 100
  24.1 24.0 %copy-start.3 = (f32[8]{0:T(128)S(1)}, f32[8]{0:T(128)}, u32[]{:S(2)}) copy-start(f32[8]{0:T(128)} %weights_ref.1) | copy-start | bytes 100
  27.8 10.5 %collective-permute-start.8 = (bf16[64,768]{1,0:T(8,128)(2,1)S(1)}, bf16[64,768]{1,0:T(8,128)(2,1)S(1)}, u32[]{:S(2)}, u32[]{:S(2)}) collective-permute-start(bf16[64,768]{1,0:T(8,128)(2,1)S(1)} %get-tuple-element.38), channel_id=1, source_target_pairs={{0,4},{1,5},{2,6},{3,7},{4,0},{5,1},{6,2},{7,3},{8,12},{9,13},{10,... | collective-permute-start | bytes 294920 | tf_op jit(solution)/shard_map/ppermute | solution.py:334
  31.1 7.3 %collective-permute-start.9 = (bf16[64,768]{1,0:T(8,128)(2,1)S(1)}, bf16[64,768]{1,0:T(8,128)(2,1)S(1)}, u32[]{:S(2)}, u32[]{:S(2)}) collective-permute-start(bf16[64,768]{1,0:T(8,128)(2,1)S(1)} %get-tuple-element.39), channel_id=1, source_target_pairs={{0,6},{1,7},{2,4},{3,5},{4,2},{5,3},{6,0},{7,1},{8,14},{9,15},{10,... | collective-permute-start | bytes 294920 | tf_op jit(solution)/shard_map/ppermute | solution.py:334
  31.6 7.7 %collective-permute-start.10 = (bf16[64,768]{1,0:T(8,128)(2,1)S(1)}, bf16[64,768]{1,0:T(8,128)(2,1)S(1)}, u32[]{:S(2)}, u32[]{:S(2)}) collective-permute-start(bf16[64,768]{1,0:T(8,128)(2,1)S(1)} %get-tuple-element.40), channel_id=1, source_target_pairs={{0,2},{1,3},{2,0},{3,1},{4,6},{5,7},{6,4},{7,5},{8,10},{9,11},{10,... | collective-permute-start | bytes 294920 | tf_op jit(solution)/shard_map/ppermute | solution.py:334
  39.4 1.4 %collective-permute-start.11 = (bf16[64,768]{1,0:T(8,128)(2,1)S(1)}, bf16[64,768]{1,0:T(8,128)(2,1)S(1)}, u32[]{:S(2)}, u32[]{:S(2)}) collective-permute-start(bf16[64,768]{1,0:T(8,128)(2,1)S(1)} %get-tuple-element.42), channel_id=1, source_target_pairs={{0,1},{1,0},{2,3},{3,2},{4,5},{5,4},{6,7},{7,6},{8,9},{9,8},{10,11... | collective-permute-start | bytes 294920 | tf_op jit(solution)/shard_map/ppermute | solution.py:326
  40.8 5.1 %collective-permute-start.12 = (bf16[32,768]{1,0:T(8,128)(2,1)S(1)}, bf16[32,768]{1,0:T(8,128)(2,1)S(1)}, u32[]{:S(2)}, u32[]{:S(2)}) collective-permute-start(bf16[32,768]{1,0:T(8,128)(2,1)S(1)} %get-tuple-element.44), channel_id=1, source_target_pairs={{0,24},{8,16},{16,8},{24,0},{1,25},{9,17},{17,9},{25,1},{2,26},{10... | collective-permute-start | bytes 147464 | tf_op jit(solution)/shard_map/ppermute | solution.py:330
  43.2 4.1 %collective-permute-start.13 = (bf16[32,768]{1,0:T(8,128)(2,1)S(1)}, bf16[32,768]{1,0:T(8,128)(2,1)S(1)}, u32[]{:S(2)}, u32[]{:S(2)}) collective-permute-start(bf16[32,768]{1,0:T(8,128)(2,1)S(1)} %get-tuple-element.45), channel_id=1, source_target_pairs={{0,8},{8,0},{16,24},{24,16},{1,9},{9,1},{17,25},{25,17},{2,10},{10... | collective-permute-start | bytes 147464 | tf_op jit(solution)/shard_map/ppermute | solution.py:330
  44.0 4.1 %collective-permute-start.14 = (bf16[32,768]{1,0:T(8,128)(2,1)S(1)}, bf16[32,768]{1,0:T(8,128)(2,1)S(1)}, u32[]{:S(2)}, u32[]{:S(2)}) collective-permute-start(bf16[32,768]{1,0:T(8,128)(2,1)S(1)} %get-tuple-element.46), channel_id=1, source_target_pairs={{0,16},{8,24},{16,0},{24,8},{1,17},{9,25},{17,1},{25,9},{2,18},{10... | collective-permute-start | bytes 147464 | tf_op jit(solution)/shard_map/ppermute | solution.py:330

commit v6 on v5

--- a/solution.py
+++ b/solution.py
@@ -10,7 +10,7 @@
 F32 = jnp.float32
 BF16 = jnp.bfloat16
 LANES = 128
-PARTS = 1
+PARTS = 2
 ROUTE_VMEM = 56
 STAGE_VMEM = 48
 
@@ -142,7 +142,7 @@
         write_lines(out, cap * chunks * 2 * rows, tail + sums)
 
 
-def merge_kernel(order, half, cap, rows, chunks, *refs):
+def merge_kernel(order, half, cap, rows, chunks, when, *refs):
     ins, (*outs, weight_ref, pick_ref) = refs[: len(order)], refs[len(order) :]
     each = 2 * chunks + 1
     start = cap * chunks * rows
@@ -378,26 +378,26 @@
         [],
         "pair",
     )
+    own, held_body = call(
+        stage_kernel,
+        [shape(x.shape, x.dtype) for x in (chol, one_body)],
+        [],
+        [chol, one_body, routed[0]],
+        [],
+        [pltpu.SemaphoreType.DMA((2,))],
+        "stage",
+        vmem=STAGE_VMEM,
+    )
     routed = [to_list(routed[s], s) for s in list_order]
     payload = shape((count * chunks * 2 * rows + round_up(2 * count * chunks, 8), LANES), BF16)
     *payloads, weight_sum, pick = call(
         functools.partial(merge_kernel, list_order, half, cap, 2 * rows, chunks),
         [payload] * PARTS + [shape((8, LANES), F32), shape((groups * half, LANES), F32)],
         [],
-        [],
+        [own],
         routed,
         [],
         "merge",
-    )
-    own, held_body = call(
-        stage_kernel,
-        [shape(x.shape, x.dtype) for x in (chol, one_body)],
-        [],
-        [chol, one_body, weight_sum],
-        [],
-        [pltpu.SemaphoreType.DMA((2,))],
-        "stage",
-        vmem=STAGE_VMEM,
     )
     gathered = [[to_chip(x, s) for s in chip_order] for x in payloads]
     held = F32 if rows % 8 else BF16

time: 49.8 us -> 57.7 us (1.16)
  starting transfers between devices: 17 us -> 28.8 us
  waiting for transfers between devices: 21.2 us -> 10.8 us
  Pallas kernels: 9.09 us -> 14.8 us
  local copies, waits for them, and re-layouts: 2.18 us -> 2.79 us
    ppermute x6 -> x12, starting transfers between devices: 8.12 us -> 20.1 us  [to_chip(): return lax.ppermute(x, 'blk', to) if s else x]
    ppermute x6 -> x12, waiting for transfers between devices: 10.9 us -> 3.94 us  [to_chip(): return lax.ppermute(x, 'blk', to) if s else x]
    pallas_call x9 -> x11, Pallas kernels: 9.09 us -> 14.8 us  [call(): pl.pallas_call(kernel, out_shape=outs, in_specs=[smem] * len(scalars) + [...]
    ppermute x6, waiting for transfers between devices: 7.57 us -> 4.07 us  [to_list(): return lax.ppermute(x, 'grp', to) if s else x]
    unnamed x8 -> x12, local copies, waits for them, and re-layouts: 2.18 us -> 2.79 us
    ppermute x3 -> x4, waiting for transfers between devices: 2.78 us -> 2.76 us  [to_twin(): return lax.ppermute(x, 'blk', [(i, i ^ 1) for i in range(n)])]
  transfers between devices with their start and end apart: 15 -> 22, of which waited for: 12 -> 10; matrix products, arithmetic and copies ran while one was open for 0% -> 0% of each run, Pallas kernels for 8% -> 23%
where the time goes in v6:
time: 57.7 us; the launch traced here: 57.4 us
  starting transfers between devices  28.8 us (50%)
  Pallas kernels  14.8 us (26%)
  waiting for transfers between devices  10.8 us (19%)
  local copies, waits for them, and re-layouts  2.79 us (5%)
    ppermute x12, starting transfers between devices, to_chip(): return lax.ppermute(x, 'blk', to) if s else x  20.1 us
    pallas_call x11, Pallas kernels, call(): pl.pallas_call(kernel, out_shape=outs, in_specs=[smem] * len(scalars) + [...  14.8 us
    ppermute x6, starting transfers between devices, to_list(): return lax.ppermute(x, 'grp', to) if s else x  8.07 us
    ppermute x6, waiting for transfers between devices, to_list(): return lax.ppermute(x, 'grp', to) if s else x  4.07 us
    ppermute x12, waiting for transfers between devices, to_chip(): return lax.ppermute(x, 'blk', to) if s else x  3.94 us
    unnamed x12, local copies, waits for them, and re-layouts  2.79 us
    ppermute x4, waiting for transfers between devices, to_twin(): return lax.ppermute(x, 'blk', [(i, i ^ 1) for i in range(n)])  2.76 us
  transfers between devices with their start and end apart: 22, of which 10 were waited for; matrix products, arithmetic and copies ran while one was open for 0% of the time, Pallas kernels for 23%

profile of v6, /device:TPU:0, one launch (start us, length us, event | category | flops | bytes accessed | tf_op | source)
XLA Modules:
  0.0 57.4 jit_solution(10426170805689094182)
XLA Ops:
  0.0 0.5 collective-permute-start.4
  0.5 1.9 %route.1 = (bf16[448,128]{1,0:T(8,128)(2,1)}, bf16[448,128]{1,0:T(8,128)(2,1)}) custom-call(s32[1]{0:T(128)} %bitcast.1.core_ref, s32[1]{0:T(128)} %bitcast.grp_ref, s32[8]{0:T(128)} %target_ref.1, f32[8]{0:T(128)} %weights_ref.1, bf16[16,8,768]{2,1,0:T(8,128)(2,1)} %refs_2_.1, f32[8,12]{1,0:T(8,128)} %refs_3_.1, f32[12,768]{1,0:T(8,128)} %refs_4_.1), custom_call_target="tpu_custom_call" | custom-call | bytes 229376 | tf_op jit(solution)/shard_map/route/pallas_call | solution.py:298
  2.4 0.1 collective-permute-start
  2.5 0.9 %copy-done.1 = bf16[448,128]{1,0:T(8,128)(2,1)S(1)} copy-done((bf16[448,128]{1,0:T(8,128)(2,1)S(1)}, bf16[448,128]{1,0:T(8,128)(2,1)}, u32[]{:S(2)}) %copy-start.1) | copy-done | bytes 114712
  3.4 0.1 hold.1.mine_ref
  3.5 1.5 %collective-permute-done.twin_ref = bf16[448,128]{1,0:T(8,128)(2,1)S(1)} collective-permute-done((bf16[448,128]{1,0:T(8,128)(2,1)}, bf16[448,128]{1,0:T(8,128)(2,1)S(1)}, u32[]{:S(2)}, u32[]{:S(2)}) %collective-permute-start) | collective-permute-done | bytes 114720 | tf_op jit(solution)/shard_map/ppermute | solution.py:326
  5.0 0.1 pair.1
  5.0 3.9 %collective-permute-start.1 = (bf16[208,128]{1,0:T(8,128)(2,1)S(1)}, bf16[208,128]{1,0:T(8,128)(2,1)S(1)}, u32[]{:S(2)}, u32[]{:S(2)}) collective-permute-start(bf16[208,128]{1,0:T(8,128)(2,1)S(1)} %get-tuple-element.37), channel_id=1, source_target_pairs={{0,24},{8,16},{16,8},{24,0},{1,25},{9,17},{17,9},{25,1},{2,26},{10... | collective-permute-start | bytes 159752 | tf_op jit(solution)/shard_map/ppermute | solution.py:330
  8.9 0.5 collective-permute-start.2
  9.5 0.1 collective-permute-start.3
  9.6 1.3 %copy-done = bf16[768,768]{1,0:T(8,128)(2,1)S(1)} copy-done((bf16[768,768]{1,0:T(8,128)(2,1)S(1)}, bf16[768,768]{1,0:T(8,128)(2,1)}, u32[]{:S(2)}) %copy-start) | copy-done | bytes 1179672
  10.8 1.7 %stage.1 = (bf16[12,128,768]{2,1,0:T(8,128)(2,1)S(1)}, bf16[768,768]{1,0:T(8,128)(2,1)S(1)}) custom-call(bf16[12,128,768]{2,1,0:T(8,128)(2,1)} %refs_0_.3, bf16[768,768]{1,0:T(8,128)(2,1)S(1)} %copy-done, bf16[208,128]{1,0:T(8,128)(2,1)S(1)} %get-tuple-element.35.refs_2_.refs_0_), custom_call_target="tpu_custom_call" | custom-call | bytes 3538944 | tf_op jit(solution)/shard_map/stage/pallas_call | solution.py:298
  12.5 0.5 collective-permute-done.2.refs_2_
  13.1 0.5 collective-permute-done.3.refs_3_
  13.6 0.7 %merge.1 = (bf16[208,128]{1,0:T(8,128)(2,1)S(1)}, bf16[208,128]{1,0:T(8,128)(2,1)}, f32[8,128]{1,0:T(8,128)S(1)}, f32[8,128]{1,0:T(8,128)S(1)}) custom-call(bf16[12,128,768]{2,1,0:T(8,128)(2,1)S(1)} %get-tuple-element.36.when.own_ref, bf16[208,128]{1,0:T(8,128)(2,1)S(1)} %get-tuple-element.35.refs_2_.refs_0_, ...), custom_call_target="tpu_custom_call" | custom-call | bytes 327680 | tf_op jit(solution)/shard_map/merge/pallas_call | solution.py:298
  14.3 0.6 %copy-done.2 = bf16[208,128]{1,0:T(8,128)(2,1)} copy-done((bf16[208,128]{1,0:T(8,128)(2,1)}, bf16[208,128]{1,0:T(8,128)(2,1)S(1)}, u32[]{:S(2)}) %copy-start.2) | copy-done | bytes 53272
  14.9 2.6 %collective-permute-start.13 = (bf16[208,128]{1,0:T(8,128)(2,1)}, bf16[208,128]{1,0:T(8,128)(2,1)}, u32[]{:S(2)}, u32[]{:S(2)}) collective-permute-start(bf16[208,128]{1,0:T(8,128)(2,1)} %get-tuple-element.49.refs_0_), channel_id=1, source_target_pairs={{0,4},{1,5},{2,6},{3,7},{4,0},{5,1},{6,2},{7,3},{8,12},{9,13},{10,... | collective-permute-start | bytes 159752 | tf_op jit(solution)/shard_map/ppermute | solution.py:334
  17.5 1.3 %collective-permute-start.12 = (bf16[208,128]{1,0:T(8,128)(2,1)}, bf16[208,128]{1,0:T(8,128)(2,1)}, u32[]{:S(2)}, u32[]{:S(2)}) collective-permute-start(bf16[208,128]{1,0:T(8,128)(2,1)} %get-tuple-element.49.refs_0_), channel_id=1, source_target_pairs={{0,6},{1,7},{2,4},{3,5},{4,2},{5,3},{6,0},{7,1},{8,14},{9,15},{10,... | collective-permute-start | bytes 159752 | tf_op jit(solution)/shard_map/ppermute | solution.py:334
  18.8 0.2 collective-permute-start.11
  19.0 2.8 %collective-permute-start.7 = (bf16[208,128]{1,0:T(8,128)(2,1)}, bf16[208,128]{1,0:T(8,128)(2,1)S(1)}, u32[]{:S(2)}, u32[]{:S(2)}) collective-permute-start(bf16[208,128]{1,0:T(8,128)(2,1)} %copy-done.2), channel_id=1, source_target_pairs={{0,4},{1,5},{2,6},{3,7},{4,0},{5,1},{6,2},{7,3},{8,12},{9,13},{10,... | collective-permute-start | bytes 159752 | tf_op jit(solution)/shard_map/ppermute | solution.py:334
  21.9 4.2 %collective-permute-start.6 = (bf16[208,128]{1,0:T(8,128)(2,1)}, bf16[208,128]{1,0:T(8,128)(2,1)S(1)}, u32[]{:S(2)}, u32[]{:S(2)}) collective-permute-start(bf16[208,128]{1,0:T(8,128)(2,1)} %copy-done.2), channel_id=1, source_target_pairs={{0,6},{1,7},{2,4},{3,5},{4,2},{5,3},{6,0},{7,1},{8,14},{9,15},{10,... | collective-permute-start | bytes 159752 | tf_op jit(solution)/shard_map/ppermute | solution.py:334
  26.1 0.0 collective-permute-done.12.refs_2_
  26.1 0.0 collective-permute-start.5
  26.1 0.0 collective-permute-done.4.twin_ref
  26.1 4.4 %fock.3 = (bf16[32,768]{1,0:T(8,128)(2,1)S(1)}, bf16[32,768]{1,0:T(8,128)(2,1)S(1)}, bf16[32,768]{1,0:T(8,128)(2,1)S(1)}, bf16[32,768]{1,0:T(8,128)(2,1)S(1)}) custom-call(s32[1]{0:T(128)} %bitcast.2.chip_ref, bf16[768,768]{1,0:T(8,128)(2,1)S(1)} %get-tuple-element.42.body_ref, bf16[12,128,768]{2,1,0:T(8,128)(2,1)S(1)} %get-tuple-element.36.when.own_ref, ...), custom_call_target="tpu_custom_call" | custom-call | flops 1358954496 | bytes 6307840 | tf_op jit(solution)/shard_map/fock/pallas_call | solution.py:298
  30.5 0.9 %collective-permute-start.14 = (bf16[32,768]{1,0:T(8,128)(2,1)S(1)}, bf16[32,768]{1,0:T(8,128)(2,1)S(1)}, u32[]{:S(2)}, u32[]{:S(2)}) collective-permute-start(bf16[32,768]{1,0:T(8,128)(2,1)S(1)} %get-tuple-element.51), channel_id=1, source_target_pairs={{0,4},{1,5},{2,6},{3,7},{4,0},{5,1},{6,2},{7,3},{8,12},{9,13},{10,... | collective-permute-start | bytes 147464 | tf_op jit(solution)/shard_map/ppermute | solution.py:334
  31.4 3.5 %collective-permute-start.15 = (bf16[32,768]{1,0:T(8,128)(2,1)S(1)}, bf16[32,768]{1,0:T(8,128)(2,1)S(1)}, u32[]{:S(2)}, u32[]{:S(2)}) collective-permute-start(bf16[32,768]{1,0:T(8,128)(2,1)S(1)} %get-tuple-element.52), channel_id=1, source_target_pairs={{0,6},{1,7},{2,4},{3,5},{4,2},{5,3},{6,0},{7,1},{8,14},{9,15},{10,... | collective-permute-start | bytes 147464 | tf_op jit(solution)/shard_map/ppermute | solution.py:334
  35.0 0.0 collective-permute-start.16
  35.0 0.0 collective-permute-done.5.refs_1_
  35.0 4.4 %fock.2 = (bf16[32,768]{1,0:T(8,128)(2,1)S(1)}, bf16[32,768]{1,0:T(8,128)(2,1)S(1)}, bf16[32,768]{1,0:T(8,128)(2,1)S(1)}, bf16[32,768]{1,0:T(8,128)(2,1)S(1)}) custom-call(s32[1]{0:T(128)} %bitcast.2.chip_ref, bf16[768,768]{1,0:T(8,128)(2,1)S(1)} %get-tuple-element.42.body_ref, bf16[12,128,768]{2,1,0:T(8,128)(2,1)S(1)} %get-tuple-element.36.when.own_ref, ...), custom_call_target="tpu_custom_call" | custom-call | flops 1358954496 | bytes 6307840 | tf_op jit(solution)/shard_map/fock/pallas_call | solution.py:298
  39.4 0.9 %collective-permute-start.8 = (bf16[32,768]{1,0:T(8,128)(2,1)S(1)}, bf16[32,768]{1,0:T(8,128)(2,1)S(1)}, u32[]{:S(2)}, u32[]{:S(2)}) collective-permute-start(bf16[32,768]{1,0:T(8,128)(2,1)S(1)} %get-tuple-element.45), channel_id=1, source_target_pairs={{0,4},{1,5},{2,6},{3,7},{4,0},{5,1},{6,2},{7,3},{8,12},{9,13},{10,... | collective-permute-start | bytes 147464 | tf_op jit(solution)/shard_map/ppermute | solution.py:334
  40.3 3.5 %collective-permute-start.9 = (bf16[32,768]{1,0:T(8,128)(2,1)S(1)}, bf16[32,768]{1,0:T(8,128)(2,1)S(1)}, u32[]{:S(2)}, u32[]{:S(2)}) collective-permute-start(bf16[32,768]{1,0:T(8,128)(2,1)S(1)} %get-tuple-element.46), channel_id=1, source_target_pairs={{0,6},{1,7},{2,4},{3,5},{4,2},{5,3},{6,0},{7,1},{8,14},{9,15},{10,... | collective-permute-start | bytes 147464 | tf_op jit(solution)/shard_map/ppermute | solution.py:334
  43.8 0.1 sum.3
  43.9 0.1 collective-permute-start.18
  44.0 0.5 collective-permute-done.8.refs_1_
  44.4 2.0 %collective-permute-done.9.refs_2_ = bf16[32,768]{1,0:T(8,128)(2,1)S(1)} collective-permute-done((bf16[32,768]{1,0:T(8,128)(2,1)S(1)}, bf16[32,768]{1,0:T(8,128)(2,1)S(1)}, u32[]{:S(2)}, u32[]{:S(2)}) %collective-permute-start.9) | collective-permute-done | bytes 49184 | tf_op jit(solution)/shard_map/ppermute | solution.py:334
  46.4 1.5 %collective-permute-done.10.refs_3_ = bf16[32,768]{1,0:T(8,128)(2,1)S(1)} collective-permute-done((bf16[32,768]{1,0:T(8,128)(2,1)S(1)}, bf16[32,768]{1,0:T(8,128)(2,1)S(1)}, u32[]{:S(2)}, u32[]{:S(2)}) %collective-permute-start.10) | collective-permute-done | bytes 49184 | tf_op jit(solution)/shard_map/ppermute | solution.py:334
  47.9 0.1 sum.2
  48.0 0.1 collective-permute-start.17
  48.0 1.3 %collective-permute-done.17.refs_2_ = bf16[64,768]{1,0:T(8,128)(2,1)S(1)} collective-permute-done((bf16[64,768]{1,0:T(8,128)(2,1)S(1)}, bf16[64,768]{1,0:T(8,128)(2,1)S(1)}, u32[]{:S(2)}, u32[]{:S(2)}) %collective-permute-start.17) | collective-permute-done | bytes 98336 | tf_op jit(solution)/shard_map/ppermute | solution.py:326
  49.3 0.1 join.1
  49.4 1.9 %collective-permute-start.19 = (bf16[32,768]{1,0:T(8,128)(2,1)S(1)}, bf16[32,768]{1,0:T(8,128)(2,1)S(1)}, u32[]{:S(2)}, u32[]{:S(2)}) collective-permute-start(bf16[32,768]{1,0:T(8,128)(2,1)S(1)} %get-tuple-element.58), channel_id=1, source_target_pairs={{0,24},{8,16},{16,8},{24,0},{1,25},{9,17},{17,9},{25,1},{2,26},{10... | collective-permute-start | bytes 147464 | tf_op jit(solution)/shard_map/ppermute | solution.py:330
  51.3 0.5 collective-permute-start.20
  51.9 1.1 %collective-permute-start.21 = (bf16[32,768]{1,0:T(8,128)(2,1)S(1)}, bf16[32,768]{1,0:T(8,128)(2,1)S(1)}, u32[]{:S(2)}, u32[]{:S(2)}) collective-permute-start(bf16[32,768]{1,0:T(8,128)(2,1)S(1)} %get-tuple-element.60), channel_id=1, source_target_pairs={{0,16},{8,24},{16,0},{24,8},{1,17},{9,25},{17,1},{25,9},{2,18},{10... | collective-permute-start | bytes 147464 | tf_op jit(solution)/shard_map/ppermute | solution.py:330
  52.9 1.5 %collective-permute-done.19.refs_1_ = bf16[32,768]{1,0:T(8,128)(2,1)S(1)} collective-permute-done((bf16[32,768]{1,0:T(8,128)(2,1)S(1)}, bf16[32,768]{1,0:T(8,128)(2,1)S(1)}, u32[]{:S(2)}, u32[]{:S(2)}) %collective-permute-start.19) | collective-permute-done | bytes 49184 | tf_op jit(solution)/shard_map/ppermute | solution.py:330
  54.5 0.9 %collective-permute-done.20.refs_2_ = bf16[32,768]{1,0:T(8,128)(2,1)S(1)} collective-permute-done((bf16[32,768]{1,0:T(8,128)(2,1)S(1)}, bf16[32,768]{1,0:T(8,128)(2,1)S(1)}, u32[]{:S(2)}, u32[]{:S(2)}) %collective-permute-start.20) | collective-permute-done | bytes 49184 | tf_op jit(solution)/shard_map/ppermute | solution.py:330
  55.4 0.5 collective-permute-done.21.refs_3_
  56.0 1.4 %deal.1 = bf16[16,8,768]{2,1,0:T(8,128)(2,1)} custom-call(s32[1]{0:T(128)} %bitcast.grp_ref, s32[8]{0:T(128)S(1)} %copy-done.4, f32[8]{0:T(128)S(1)} %copy-done.5, f32[8,128]{1,0:T(8,128)S(1)} %get-tuple-element.40.total_ref, bf16[32,768]{1,0:T(8,128)(2,1)S(1)} %get-tuple-element.57.refs_0_, bf16[32,768]{1,0:T(8,128)(2,1)S(1)} %collective-permute-done.19.refs_1_, ...), custom_call_target="tpu_custom_call" | custom-call | bytes 397312 | tf_op jit(solution)/shard_map/deal/pallas_call | solution.py:298
  (19 shorter events, 0.0 us)
Async XLA Ops:
  0.0 26.1 %collective-permute-start.4 = (bf16[12,128,768]{2,1,0:T(8,128)(2,1)}, bf16[12,128,768]{2,1,0:T(8,128)(2,1)}, u32[]{:S(2)}, u32[]{:S(2)}) collective-permute-start(bf16[12,128,768]{2,1,0:T(8,128)(2,1)} %refs_0_.3), channel_id=1, source_target_pairs={{0,1},{1,0},{2,3},{3,2},{4,5},{5,4},{6,7},{7,6},{8,9},{9,8},{10,11... | collective-permute-start | bytes 7077896 | tf_op jit(solution)/shard_map/ppermute | solution.py:326
  2.4 2.6 %collective-permute-start = (bf16[448,128]{1,0:T(8,128)(2,1)}, bf16[448,128]{1,0:T(8,128)(2,1)S(1)}, u32[]{:S(2)}, u32[]{:S(2)}) collective-permute-start(bf16[448,128]{1,0:T(8,128)(2,1)} %get-tuple-element.34), channel_id=1, source_target_pairs={{0,1},{1,0},{2,3},{3,2},{4,5},{5,4},{6,7},{7,6},{8,9},{9,8},{10,11... | collective-permute-start | bytes 344072 | tf_op jit(solution)/shard_map/ppermute | solution.py:326
  2.5 0.9 %copy-start.1 = (bf16[448,128]{1,0:T(8,128)(2,1)S(1)}, bf16[448,128]{1,0:T(8,128)(2,1)}, u32[]{:S(2)}) copy-start(bf16[448,128]{1,0:T(8,128)(2,1)} %get-tuple-element.33.refs_0_) | copy-start | bytes 344068
  5.0 7.5 %collective-permute-start.1 = (bf16[208,128]{1,0:T(8,128)(2,1)S(1)}, bf16[208,128]{1,0:T(8,128)(2,1)S(1)}, u32[]{:S(2)}, u32[]{:S(2)}) collective-permute-start(bf16[208,128]{1,0:T(8,128)(2,1)S(1)} %get-tuple-element.37), channel_id=1, source_target_pairs={{0,24},{8,16},{16,8},{24,0},{1,25},{9,17},{17,9},{25,1},{2,26},{10... | collective-permute-start | bytes 159752 | tf_op jit(solution)/shard_map/ppermute | solution.py:330
  8.9 4.1 %collective-permute-start.2 = (bf16[208,128]{1,0:T(8,128)(2,1)S(1)}, bf16[208,128]{1,0:T(8,128)(2,1)S(1)}, u32[]{:S(2)}, u32[]{:S(2)}) collective-permute-start(bf16[208,128]{1,0:T(8,128)(2,1)S(1)} %get-tuple-element.38), channel_id=1, source_target_pairs={{0,8},{8,0},{16,24},{24,16},{1,9},{9,1},{17,25},{25,17},{2,10},{10... | collective-permute-start | bytes 159752 | tf_op jit(solution)/shard_map/ppermute | solution.py:330
  9.5 4.1 %collective-permute-start.3 = (bf16[208,128]{1,0:T(8,128)(2,1)S(1)}, bf16[208,128]{1,0:T(8,128)(2,1)S(1)}, u32[]{:S(2)}, u32[]{:S(2)}) collective-permute-start(bf16[208,128]{1,0:T(8,128)(2,1)S(1)} %get-tuple-element.39), channel_id=1, source_target_pairs={{0,16},{8,24},{16,0},{24,8},{1,17},{9,25},{17,1},{25,9},{2,18},{10... | collective-permute-start | bytes 159752 | tf_op jit(solution)/shard_map/ppermute | solution.py:330
  9.6 1.3 %copy-start = (bf16[768,768]{1,0:T(8,128)(2,1)S(1)}, bf16[768,768]{1,0:T(8,128)(2,1)}, u32[]{:S(2)}) copy-start(bf16[768,768]{1,0:T(8,128)(2,1)} %refs_1_.3) | copy-start | bytes 3538948
  14.3 0.6 %copy-start.2 = (bf16[208,128]{1,0:T(8,128)(2,1)}, bf16[208,128]{1,0:T(8,128)(2,1)S(1)}, u32[]{:S(2)}) copy-start(bf16[208,128]{1,0:T(8,128)(2,1)S(1)} %get-tuple-element.43.refs_0_) | copy-start | bytes 159748
  14.9 7.0 %collective-permute-start.13 = (bf16[208,128]{1,0:T(8,128)(2,1)}, bf16[208,128]{1,0:T(8,128)(2,1)}, u32[]{:S(2)}, u32[]{:S(2)}) collective-permute-start(bf16[208,128]{1,0:T(8,128)(2,1)} %get-tuple-element.49.refs_0_), channel_id=1, source_target_pairs={{0,4},{1,5},{2,6},{3,7},{4,0},{5,1},{6,2},{7,3},{8,12},{9,13},{10,... | collective-permute-start | bytes 159752 | tf_op jit(solution)/shard_map/ppermute | solution.py:334
  17.5 8.6 %collective-permute-start.12 = (bf16[208,128]{1,0:T(8,128)(2,1)}, bf16[208,128]{1,0:T(8,128)(2,1)}, u32[]{:S(2)}, u32[]{:S(2)}) collective-permute-start(bf16[208,128]{1,0:T(8,128)(2,1)} %get-tuple-element.49.refs_0_), channel_id=1, source_target_pairs={{0,6},{1,7},{2,4},{3,5},{4,2},{5,3},{6,0},{7,1},{8,14},{9,15},{10,... | collective-permute-start | bytes 159752 | tf_op jit(solution)/shard_map/ppermute | solution.py:334
  18.8 7.3 %collective-permute-start.11 = (bf16[208,128]{1,0:T(8,128)(2,1)}, bf16[208,128]{1,0:T(8,128)(2,1)}, u32[]{:S(2)}, u32[]{:S(2)}) collective-permute-start(bf16[208,128]{1,0:T(8,128)(2,1)} %get-tuple-element.49.refs_0_), channel_id=1, source_target_pairs={{0,2},{1,3},{2,0},{3,1},{4,6},{5,7},{6,4},{7,5},{8,10},{9,11},{10,... | collective-permute-start | bytes 159752 | tf_op jit(solution)/shard_map/ppermute | solution.py:334
  19.0 15.9 %collective-permute-start.7 = (bf16[208,128]{1,0:T(8,128)(2,1)}, bf16[208,128]{1,0:T(8,128)(2,1)S(1)}, u32[]{:S(2)}, u32[]{:S(2)}) collective-permute-start(bf16[208,128]{1,0:T(8,128)(2,1)} %copy-done.2), channel_id=1, source_target_pairs={{0,4},{1,5},{2,6},{3,7},{4,0},{5,1},{6,2},{7,3},{8,12},{9,13},{10,... | collective-permute-start | bytes 159752 | tf_op jit(solution)/shard_map/ppermute | solution.py:334
  21.9 13.1 %collective-permute-start.6 = (bf16[208,128]{1,0:T(8,128)(2,1)}, bf16[208,128]{1,0:T(8,128)(2,1)S(1)}, u32[]{:S(2)}, u32[]{:S(2)}) collective-permute-start(bf16[208,128]{1,0:T(8,128)(2,1)} %copy-done.2), channel_id=1, source_target_pairs={{0,6},{1,7},{2,4},{3,5},{4,2},{5,3},{6,0},{7,1},{8,14},{9,15},{10,... | collective-permute-start | bytes 159752 | tf_op jit(solution)/shard_map/ppermute | solution.py:334
  26.1 8.9 %collective-permute-start.5 = (bf16[208,128]{1,0:T(8,128)(2,1)}, bf16[208,128]{1,0:T(8,128)(2,1)S(1)}, u32[]{:S(2)}, u32[]{:S(2)}) collective-permute-start(bf16[208,128]{1,0:T(8,128)(2,1)} %copy-done.2), channel_id=1, source_target_pairs={{0,2},{1,3},{2,0},{3,1},{4,6},{5,7},{6,4},{7,5},{8,10},{9,11},{10,... | collective-permute-start | bytes 159752 | tf_op jit(solution)/shard_map/ppermute | solution.py:334
  26.1 8.9 %copy-start.3 = (bf16[208,128]{1,0:T(8,128)(2,1)S(1)}, bf16[208,128]{1,0:T(8,128)(2,1)}, u32[]{:S(2)}) copy-start(bf16[208,128]{1,0:T(8,128)(2,1)} %copy-done.2) | copy-start | bytes 159748
  30.5 13.3 %collective-permute-start.14 = (bf16[32,768]{1,0:T(8,128)(2,1)S(1)}, bf16[32,768]{1,0:T(8,128)(2,1)S(1)}, u32[]{:S(2)}, u32[]{:S(2)}) collective-permute-start(bf16[32,768]{1,0:T(8,128)(2,1)S(1)} %get-tuple-element.51), channel_id=1, source_target_pairs={{0,4},{1,5},{2,6},{3,7},{4,0},{5,1},{6,2},{7,3},{8,12},{9,13},{10,... | collective-permute-start | bytes 147464 | tf_op jit(solution)/shard_map/ppermute | solution.py:334
  31.4 12.4 %collective-permute-start.15 = (bf16[32,768]{1,0:T(8,128)(2,1)S(1)}, bf16[32,768]{1,0:T(8,128)(2,1)S(1)}, u32[]{:S(2)}, u32[]{:S(2)}) collective-permute-start(bf16[32,768]{1,0:T(8,128)(2,1)S(1)} %get-tuple-element.52), channel_id=1, source_target_pairs={{0,6},{1,7},{2,4},{3,5},{4,2},{5,3},{6,0},{7,1},{8,14},{9,15},{10,... | collective-permute-start | bytes 147464 | tf_op jit(solution)/shard_map/ppermute | solution.py:334
  35.0 21.0 %copy-start.4 = (s32[8]{0:T(128)S(1)}, s32[8]{0:T(128)}, u32[]{:S(2)}) copy-start(s32[8]{0:T(128)} %target_ref.1) | copy-start | bytes 100
  35.0 21.0 %copy-start.5 = (f32[8]{0:T(128)S(1)}, f32[8]{0:T(128)}, u32[]{:S(2)}) copy-start(f32[8]{0:T(128)} %weights_ref.1) | copy-start | bytes 100
  35.0 8.8 %collective-permute-start.16 = (bf16[32,768]{1,0:T(8,128)(2,1)S(1)}, bf16[32,768]{1,0:T(8,128)(2,1)S(1)}, u32[]{:S(2)}, u32[]{:S(2)}) collective-permute-start(bf16[32,768]{1,0:T(8,128)(2,1)S(1)} %get-tuple-element.53), channel_id=1, source_target_pairs={{0,2},{1,3},{2,0},{3,1},{4,6},{5,7},{6,4},{7,5},{8,10},{9,11},{10,... | collective-permute-start | bytes 147464 | tf_op jit(solution)/shard_map/ppermute | solution.py:334
  39.4 5.1 %collective-permute-start.8 = (bf16[32,768]{1,0:T(8,128)(2,1)S(1)}, bf16[32,768]{1,0:T(8,128)(2,1)S(1)}, u32[]{:S(2)}, u32[]{:S(2)}) collective-permute-start(bf16[32,768]{1,0:T(8,128)(2,1)S(1)} %get-tuple-element.45), channel_id=1, source_target_pairs={{0,4},{1,5},{2,6},{3,7},{4,0},{5,1},{6,2},{7,3},{8,12},{9,13},{10,... | collective-permute-start | bytes 147464 | tf_op jit(solution)/shard_map/ppermute | solution.py:334
  40.3 6.1 %collective-permute-start.9 = (bf16[32,768]{1,0:T(8,128)(2,1)S(1)}, bf16[32,768]{1,0:T(8,128)(2,1)S(1)}, u32[]{:S(2)}, u32[]{:S(2)}) collective-permute-start(bf16[32,768]{1,0:T(8,128)(2,1)S(1)} %get-tuple-element.46), channel_id=1, source_target_pairs={{0,6},{1,7},{2,4},{3,5},{4,2},{5,3},{6,0},{7,1},{8,14},{9,15},{10,... | collective-permute-start | bytes 147464 | tf_op jit(solution)/shard_map/ppermute | solution.py:334
  43.8 4.1 %collective-permute-start.10 = (bf16[32,768]{1,0:T(8,128)(2,1)S(1)}, bf16[32,768]{1,0:T(8,128)(2,1)S(1)}, u32[]{:S(2)}, u32[]{:S(2)}) collective-permute-start(bf16[32,768]{1,0:T(8,128)(2,1)S(1)} %get-tuple-element.47), channel_id=1, source_target_pairs={{0,2},{1,3},{2,0},{3,1},{4,6},{5,7},{6,4},{7,5},{8,10},{9,11},{10,... | collective-permute-start | bytes 147464 | tf_op jit(solution)/shard_map/ppermute | solution.py:334
  43.9 4.1 %collective-permute-start.18 = (bf16[64,768]{1,0:T(8,128)(2,1)S(1)}, bf16[64,768]{1,0:T(8,128)(2,1)S(1)}, u32[]{:S(2)}, u32[]{:S(2)}) collective-permute-start(bf16[64,768]{1,0:T(8,128)(2,1)S(1)} %get-tuple-element.56), channel_id=1, source_target_pairs={{0,1},{1,0},{2,3},{3,2},{4,5},{5,4},{6,7},{7,6},{8,9},{9,8},{10,11... | collective-permute-start | bytes 294920 | tf_op jit(solution)/shard_map/ppermute | solution.py:326
  48.0 1.4 %collective-permute-start.17 = (bf16[64,768]{1,0:T(8,128)(2,1)S(1)}, bf16[64,768]{1,0:T(8,128)(2,1)S(1)}, u32[]{:S(2)}, u32[]{:S(2)}) collective-permute-start(bf16[64,768]{1,0:T(8,128)(2,1)S(1)} %get-tuple-element.55), channel_id=1, source_target_pairs={{0,1},{1,0},{2,3},{3,2},{4,5},{5,4},{6,7},{7,6},{8,9},{9,8},{10,11... | collective-permute-start | bytes 294920 | tf_op jit(solution)/shard_map/ppermute | solution.py:326
  49.4 5.1 %collective-permute-start.19 = (bf16[32,768]{1,0:T(8,128)(2,1)S(1)}, bf16[32,768]{1,0:T(8,128)(2,1)S(1)}, u32[]{:S(2)}, u32[]{:S(2)}) collective-permute-start(bf16[32,768]{1,0:T(8,128)(2,1)S(1)} %get-tuple-element.58), channel_id=1, source_target_pairs={{0,24},{8,16},{16,8},{24,0},{1,25},{9,17},{17,9},{25,1},{2,26},{10... | collective-permute-start | bytes 147464 | tf_op jit(solution)/shard_map/ppermute | solution.py:330
  51.3 4.1 %collective-permute-start.20 = (bf16[32,768]{1,0:T(8,128)(2,1)S(1)}, bf16[32,768]{1,0:T(8,128)(2,1)S(1)}, u32[]{:S(2)}, u32[]{:S(2)}) collective-permute-start(bf16[32,768]{1,0:T(8,128)(2,1)S(1)} %get-tuple-element.59), channel_id=1, source_target_pairs={{0,8},{8,0},{16,24},{24,16},{1,9},{9,1},{17,25},{25,17},{2,10},{10... | collective-permute-start | bytes 147464 | tf_op jit(solution)/shard_map/ppermute | solution.py:330
  51.9 4.1 %collective-permute-start.21 = (bf16[32,768]{1,0:T(8,128)(2,1)S(1)}, bf16[32,768]{1,0:T(8,128)(2,1)S(1)}, u32[]{:S(2)}, u32[]{:S(2)}) collective-permute-start(bf16[32,768]{1,0:T(8,128)(2,1)S(1)} %get-tuple-element.60), channel_id=1, source_target_pairs={{0,16},{8,24},{16,0},{24,8},{1,17},{9,25},{17,1},{25,9},{2,18},{10... | collective-permute-start | bytes 147464 | tf_op jit(solution)/shard_map/ppermute | solution.py:330

commit v7 on v6

--- a/solution.py
+++ b/solution.py
@@ -10,7 +10,8 @@
 F32 = jnp.float32
 BF16 = jnp.bfloat16
 LANES = 128
-PARTS = 2
+PARTS = 1
+VMEM = 24
 ROUTE_VMEM = 56
 STAGE_VMEM = 48
 
@@ -142,8 +143,32 @@
         write_lines(out, cap * chunks * 2 * rows, tail + sums)
 
 
-def merge_kernel(order, half, cap, rows, chunks, when, *refs):
-    ins, (*outs, weight_ref, pick_ref) = refs[: len(order)], refs[len(order) :]
+def fold(body_ref, own_ref, twin_ref, out_ref):
+    vec_count, occupied, orbitals = own_ref.shape
+    batch = math.gcd(vec_count, 2)
+    for c, ref in enumerate((own_ref, twin_ref)):
+
+        @pl.loop(0, vec_count // batch)
+        def _(i):
+            left = ref[pl.ds(i * batch, batch)].reshape(batch * occupied, orbitals)
+            done = lax.dot_general(left, body_ref[...], (((1,), (1,)), ((), ())), preferred_element_type=F32)
+            out_ref[pl.ds(c * vec_count + i * batch, batch)] = done.astype(BF16).reshape(batch, occupied, orbitals)
+
+
+def fold_kernel(core_ref, body_ref, own_ref, twin_ref, early_ref, out_ref):
+    core = core_ref[0]
+
+    @pl.when(core == 0)
+    def _():
+        out_ref[...] = early_ref[...]
+
+    @pl.when(core != 0)
+    def _():
+        fold(body_ref, own_ref, twin_ref, out_ref)
+
+
+def merge_kernel(order, half, cap, rows, chunks, core_ref, body_ref, own_ref, chol_ref, *refs):
+    ins, (*outs, weight_ref, pick_ref, early_ref) = refs[: len(order)], refs[len(order) :]
     each = 2 * chunks + 1
     start = cap * chunks * rows
     weight = jnp.zeros((1, LANES), F32)
@@ -173,8 +198,12 @@
                 out[at : at + rows, :] = walker[p * count + w][c].astype(BF16)
         write_lines(out, count * chunks * rows, line[p * count : (p + 1) * count])
 
-
-def fock_kernel(order, send_order, count, rows, chip_ref, body_ref, own_ref, twin_ref, *refs):
+    @pl.when(core_ref[0] == 0)
+    def _():
+        fold(body_ref, own_ref, chol_ref, early_ref)
+
+
+def fock_kernel(order, send_order, count, rows, chip_ref, folded_ref, own_ref, twin_ref, *refs):
     n = len(order)
     ins, outs = refs[:n], refs[n : 2 * n]
     prop, turned, coup, result = refs[2 * n :]
@@ -197,18 +226,17 @@
                 piece = ref[at : at + rows, :].astype(F32) * growth[w][c : c + 1]
                 prop[w, source, :, c * LANES : (c + 1) * LANES] = piece.astype(prop.dtype)
     scaled = jnp.concatenate([prop[w, i] for w in range(count) for i in range(n)], axis=0).astype(BF16)
-    turned[...] = jnp.dot(scaled, body_ref[...], preferred_element_type=F32).T.astype(BF16)
+    turned[...] = scaled.astype(F32).T.astype(BF16)
     batch = math.gcd(vec_count, 4)
-    for c, ref in enumerate((own_ref, twin_ref)):
-        for g in range(0, vec_count, batch):
-            left = ref[g : g + batch].reshape(batch * occupied, orbitals)
-            s = jnp.dot(left, turned[...], preferred_element_type=F32).astype(BF16)
-            for k in range(batch):
-                at = (c * vec_count + g + k) * occupied
-                for w in range(count):
-                    coup[w * occupied : (w + 1) * occupied, at : at + occupied] = s[
-                        k * occupied : (k + 1) * occupied, w * occupied : (w + 1) * occupied
-                    ]
+    for g in range(0, 2 * vec_count, batch):
+        left = folded_ref[g : g + batch].reshape(batch * occupied, orbitals)
+        s = jnp.dot(left, turned[...], preferred_element_type=F32).astype(BF16)
+        for k in range(batch):
+            at = (g + k) * occupied
+            for w in range(count):
+                coup[w * occupied : (w + 1) * occupied, at : at + occupied] = s[
+                    k * occupied : (k + 1) * occupied, w * occupied : (w + 1) * occupied
+                ]
     tile = 256 if orbitals % 256 == 0 else orbitals
     depth = vec_count * occupied
     for t in range(0, orbitals, tile):
@@ -291,7 +319,7 @@
     out_ref[...] = wide[...].astype(BF16)
 
 
-def call(kernel, outs, scalars, held, arrays, scratch, name, flops=0, vmem=40):
+def call(kernel, outs, scalars, held, arrays, scratch, name, flops=0, vmem=VMEM):
     smem = pl.BlockSpec(memory_space=pltpu.SMEM)
     full = pl.BlockSpec(memory_space=pltpu.VMEM)
     size = sum(x.size * x.dtype.itemsize for x in list(arrays) + list(outs))
@@ -334,7 +362,7 @@
         return lax.ppermute(x, "blk", to) if s else x
 
     send_order = [0] + list(range(chips // 2, chips)) + list(range(1, chips // 2))
-    chip_order = [0] + send_order[:0:-1]
+    chip_order = send_order
     list_order = [0] + sorted(range(1, groups), key=lambda s: -bin(s).count("1"))
 
     chol_twin = to_twin(chol)
@@ -389,15 +417,27 @@
         vmem=STAGE_VMEM,
     )
     routed = [to_list(routed[s], s) for s in list_order]
+    folded_shape = shape((2 * vec_count, occupied, orbitals), BF16)
     payload = shape((count * chunks * 2 * rows + round_up(2 * count * chunks, 8), LANES), BF16)
-    *payloads, weight_sum, pick = call(
+    *payloads, weight_sum, pick, early = call(
         functools.partial(merge_kernel, list_order, half, cap, 2 * rows, chunks),
-        [payload] * PARTS + [shape((8, LANES), F32), shape((groups * half, LANES), F32)],
-        [],
-        [own],
-        routed,
+        [payload] * PARTS + [shape((8, LANES), F32), shape((groups * half, LANES), F32), folded_shape],
+        [core],
+        [],
+        [held_body, own, chol_twin] + routed,
         [],
         "merge",
+        flops=4 * vec_count * occupied * orbitals * orbitals,
+    )
+    (folded,) = call(
+        fold_kernel,
+        [folded_shape],
+        [core],
+        [],
+        [held_body, own, chol_twin, early],
+        [],
+        "fold",
+        flops=4 * vec_count * occupied * orbitals * orbitals,
     )
     gathered = [[to_chip(x, s) for s in chip_order] for x in payloads]
     held = F32 if rows % 8 else BF16
@@ -408,7 +448,7 @@
             [shape((count * 2 * rows, orbitals), BF16)] * chips,
             [chip],
             [],
-            [held_body, own, chol_twin] + gathered[p],
+            [folded, own, chol_twin] + gathered[p],
             [
                 pltpu.VMEM((count, chips, 2 * rows, orbitals), held),
                 pltpu.VMEM((orbitals, count * occupied), BF16),
@@ -416,7 +456,7 @@
                 pltpu.VMEM((count, chips, 2 * rows, orbitals), held),
             ],
             "fock",
-            flops=2 * count * occupied * orbitals * (orbitals + 4 * vec_count * occupied),
+            flops=2 * count * occupied * orbitals * 4 * vec_count * occupied,
         )
         out = [to_chip(x, s) for s, x in zip(send_order, out)]
         a, b = call(

time: 57.7 us -> 51.2 us (0.89)
  starting transfers between devices: 28.8 us -> 16.5 us
  waiting for transfers between devices: 10.8 us -> 17 us
  local copies, waits for them, and re-layouts: 2.79 us -> 2.18 us
    ppermute x12 -> x6, starting transfers between devices: 20.1 us -> 7.78 us  [to_chip(): return lax.ppermute(x, 'blk', to) if s else x]
    ppermute x12 -> x6, waiting for transfers between devices: 3.94 us -> 10.6 us  [to_chip(): return lax.ppermute(x, 'blk', to) if s else x]
    unnamed x12 -> x8, local copies, waits for them, and re-layouts: 2.79 us -> 2.18 us
    pallas_call x11 -> x10, Pallas kernels: 14.8 us -> 15.2 us  [call(): pl.pallas_call(kernel, out_shape=outs, in_specs=[smem] * len(scalars) + [...]
    ppermute x4 -> x3, waiting for transfers between devices: 2.76 us -> 2.78 us  [to_twin(): return lax.ppermute(x, 'blk', [(i, i ^ 1) for i in range(n)])]
  transfers between devices with their start and end apart: 22 -> 15, of which waited for: 10 -> 13; matrix products, arithmetic and copies ran while one was open for 0% -> 0% of each run, Pallas kernels for 23% -> 8%
where the time goes in v7:
time: 51.2 us; the launch traced here: 51 us
  waiting for transfers between devices  17 us (33%)
  starting transfers between devices  16.5 us (32%)
  Pallas kernels  15.2 us (30%)
  local copies, waits for them, and re-layouts  2.18 us (4%)
    pallas_call x10, Pallas kernels, call(): pl.pallas_call(kernel, out_shape=outs, in_specs=[smem] * len(scalars) + [...  15.2 us
    ppermute x6, waiting for transfers between devices, to_chip(): return lax.ppermute(x, 'blk', to) if s else x  10.6 us
    ppermute x6, starting transfers between devices, to_list(): return lax.ppermute(x, 'grp', to) if s else x  8.07 us
    ppermute x6, starting transfers between devices, to_chip(): return lax.ppermute(x, 'blk', to) if s else x  7.78 us
    ppermute x6, waiting for transfers between devices, to_list(): return lax.ppermute(x, 'grp', to) if s else x  3.68 us
    ppermute x3, waiting for transfers between devices, to_twin(): return lax.ppermute(x, 'blk', [(i, i ^ 1) for i in range(n)])  2.78 us
    unnamed x8, local copies, waits for them, and re-layouts  2.18 us
  transfers between devices with their start and end apart: 15, of which 13 were waited for; matrix products, arithmetic and copies ran while one was open for 0% of the time, Pallas kernels for 8%

profile of v7, /device:TPU:0, one launch (start us, length us, event | category | flops | bytes accessed | tf_op | source)
XLA Modules:
  0.0 51.0 jit_solution(12462087877011345364)
XLA Ops:
  0.0 0.5 collective-permute-start.1
  0.5 1.9 %route.1 = (bf16[448,128]{1,0:T(8,128)(2,1)}, bf16[448,128]{1,0:T(8,128)(2,1)}) custom-call(s32[1]{0:T(128)} %bitcast.1.core_ref, s32[1]{0:T(128)} %bitcast.grp_ref, s32[8]{0:T(128)} %target_ref.1, f32[8]{0:T(128)} %weights_ref.1, bf16[16,8,768]{2,1,0:T(8,128)(2,1)} %refs_2_.1, f32[8,12]{1,0:T(8,128)} %refs_3_.1, f32[12,768]{1,0:T(8,128)} %refs_4_.1), custom_call_target="tpu_custom_call" | custom-call | bytes 229376 | tf_op jit(solution)/shard_map/route/pallas_call | solution.py:326
  2.3 0.1 collective-permute-start
  2.5 0.0 copy-start.1
  2.5 0.9 %copy-done.1 = bf16[448,128]{1,0:T(8,128)(2,1)S(1)} copy-done((bf16[448,128]{1,0:T(8,128)(2,1)S(1)}, bf16[448,128]{1,0:T(8,128)(2,1)}, u32[]{:S(2)}) %copy-start.1) | copy-done | bytes 114712
  3.4 0.1 hold.1.mine_ref
  3.5 1.5 %collective-permute-done.twin_ref = bf16[448,128]{1,0:T(8,128)(2,1)S(1)} collective-permute-done((bf16[448,128]{1,0:T(8,128)(2,1)}, bf16[448,128]{1,0:T(8,128)(2,1)S(1)}, u32[]{:S(2)}, u32[]{:S(2)}) %collective-permute-start) | collective-permute-done | bytes 114720 | tf_op jit(solution)/shard_map/ppermute | solution.py:354
  5.0 0.1 pair.1
  5.0 3.9 %collective-permute-start.2 = (bf16[208,128]{1,0:T(8,128)(2,1)S(1)}, bf16[208,128]{1,0:T(8,128)(2,1)S(1)}, u32[]{:S(2)}, u32[]{:S(2)}) collective-permute-start(bf16[208,128]{1,0:T(8,128)(2,1)S(1)} %get-tuple-element.32), channel_id=1, source_target_pairs={{0,24},{8,16},{16,8},{24,0},{1,25},{9,17},{17,9},{25,1},{2,26},{10... | collective-permute-start | bytes 159752 | tf_op jit(solution)/shard_map/ppermute | solution.py:358
  8.9 0.5 %collective-permute-start.3 = (bf16[208,128]{1,0:T(8,128)(2,1)S(1)}, bf16[208,128]{1,0:T(8,128)(2,1)S(1)}, u32[]{:S(2)}, u32[]{:S(2)}) collective-permute-start(bf16[208,128]{1,0:T(8,128)(2,1)S(1)} %get-tuple-element.33), channel_id=1, source_target_pairs={{0,8},{8,0},{16,24},{24,16},{1,9},{9,1},{17,25},{25,17},{2,10},{10... | collective-permute-start | bytes 159752 | tf_op jit(solution)/shard_map/ppermute | solution.py:358
  9.5 0.1 collective-permute-start.4
  9.6 0.0 copy-start
  9.6 1.3 %copy-done = bf16[768,768]{1,0:T(8,128)(2,1)S(1)} copy-done((bf16[768,768]{1,0:T(8,128)(2,1)S(1)}, bf16[768,768]{1,0:T(8,128)(2,1)}, u32[]{:S(2)}) %copy-start) | copy-done | bytes 1179672
  10.8 1.7 %stage.1 = (bf16[12,128,768]{2,1,0:T(8,128)(2,1)S(1)}, bf16[768,768]{1,0:T(8,128)(2,1)S(1)}) custom-call(bf16[12,128,768]{2,1,0:T(8,128)(2,1)} %refs_0_.3, bf16[768,768]{1,0:T(8,128)(2,1)S(1)} %copy-done, bf16[208,128]{1,0:T(8,128)(2,1)S(1)} %get-tuple-element.29.refs_2_.refs_0_), custom_call_target="tpu_custom_call" | custom-call | bytes 3538944 | tf_op jit(solution)/shard_map/stage/pallas_call | solution.py:326
  12.5 0.0 collective-permute-done.2.refs_1_
  12.5 0.5 %collective-permute-done.3.refs_2_ = bf16[208,128]{1,0:T(8,128)(2,1)S(1)} collective-permute-done((bf16[208,128]{1,0:T(8,128)(2,1)S(1)}, bf16[208,128]{1,0:T(8,128)(2,1)S(1)}, u32[]{:S(2)}, u32[]{:S(2)}) %collective-permute-start.3) | collective-permute-done | bytes 53280 | tf_op jit(solution)/shard_map/ppermute | solution.py:358
  13.1 0.5 %collective-permute-done.4.refs_3_ = bf16[208,128]{1,0:T(8,128)(2,1)S(1)} collective-permute-done((bf16[208,128]{1,0:T(8,128)(2,1)S(1)}, bf16[208,128]{1,0:T(8,128)(2,1)S(1)}, u32[]{:S(2)}, u32[]{:S(2)}) %collective-permute-start.4) | collective-permute-done | bytes 53280 | tf_op jit(solution)/shard_map/ppermute | solution.py:358
  13.6 0.0 collective-permute-done.1.chol_ref.twin_ref
  13.6 6.1 %merge.1 = (bf16[408,128]{1,0:T(8,128)(2,1)S(1)}, f32[8,128]{1,0:T(8,128)S(1)}, f32[8,128]{1,0:T(8,128)S(1)}, bf16[24,128,768]{2,1,0:T(8,128)(2,1)S(1)}) custom-call(s32[1]{0:T(128)} %bitcast.1.core_ref, bf16[768,768]{1,0:T(8,128)(2,1)S(1)} %get-tuple-element.30.body_ref, bf16[12,128,768]{2,1,0:T(8,128)(2,1)S(1)} %get-tuple-element.31.own_ref, ...), custom_call_target="tpu_custom_call" | custom-call | flops 3623878656 | bytes 10942464 | tf_op jit(solution)/shard_map/merge/pallas_call | solution.py:326
  19.8 2.6 %collective-permute-start.5 = (bf16[408,128]{1,0:T(8,128)(2,1)S(1)}, bf16[408,128]{1,0:T(8,128)(2,1)S(1)}, u32[]{:S(2)}, u32[]{:S(2)}) collective-permute-start(bf16[408,128]{1,0:T(8,128)(2,1)S(1)} %get-tuple-element.38.refs_0_), channel_id=1, source_target_pairs={{0,4},{1,5},{2,6},{3,7},{4,0},{5,1},{6,2},{7,3},{8,12},{9,13},{10,... | collective-permute-start | bytes 313352 | tf_op jit(solution)/shard_map/ppermute | solution.py:362
  22.4 1.4 %collective-permute-start.6 = (bf16[408,128]{1,0:T(8,128)(2,1)S(1)}, bf16[408,128]{1,0:T(8,128)(2,1)S(1)}, u32[]{:S(2)}, u32[]{:S(2)}) collective-permute-start(bf16[408,128]{1,0:T(8,128)(2,1)S(1)} %get-tuple-element.38.refs_0_), channel_id=1, source_target_pairs={{0,6},{1,7},{2,4},{3,5},{4,2},{5,3},{6,0},{7,1},{8,14},{9,15},{10,... | collective-permute-start | bytes 313352 | tf_op jit(solution)/shard_map/ppermute | solution.py:362
  23.8 0.2 collective-permute-start.7
  24.0 0.3 fold.1.folded_ref
  24.3 2.2 %collective-permute-done.5.refs_1_ = bf16[408,128]{1,0:T(8,128)(2,1)S(1)} collective-permute-done((bf16[408,128]{1,0:T(8,128)(2,1)S(1)}, bf16[408,128]{1,0:T(8,128)(2,1)S(1)}, u32[]{:S(2)}, u32[]{:S(2)}) %collective-permute-start.5) | collective-permute-done | bytes 104480 | tf_op jit(solution)/shard_map/ppermute | solution.py:362
  26.5 2.5 %collective-permute-done.6.refs_2_ = bf16[408,128]{1,0:T(8,128)(2,1)S(1)} collective-permute-done((bf16[408,128]{1,0:T(8,128)(2,1)S(1)}, bf16[408,128]{1,0:T(8,128)(2,1)S(1)}, u32[]{:S(2)}, u32[]{:S(2)}) %collective-permute-start.6) | collective-permute-done | bytes 104480 | tf_op jit(solution)/shard_map/ppermute | solution.py:362
  29.0 1.6 %collective-permute-done.7.refs_3_ = bf16[408,128]{1,0:T(8,128)(2,1)S(1)} collective-permute-done((bf16[408,128]{1,0:T(8,128)(2,1)S(1)}, bf16[408,128]{1,0:T(8,128)(2,1)S(1)}, u32[]{:S(2)}, u32[]{:S(2)}) %collective-permute-start.7) | collective-permute-done | bytes 104480 | tf_op jit(solution)/shard_map/ppermute | solution.py:362
  30.6 0.0 copy-start.2
  30.6 0.0 copy-start.3
  30.6 3.5 %fock.1 = (bf16[64,768]{1,0:T(8,128)(2,1)S(1)}, bf16[64,768]{1,0:T(8,128)(2,1)S(1)}, bf16[64,768]{1,0:T(8,128)(2,1)S(1)}, bf16[64,768]{1,0:T(8,128)(2,1)S(1)}) custom-call(s32[1]{0:T(128)} %bitcast.2.chip_ref, bf16[24,128,768]{2,1,0:T(8,128)(2,1)S(1)} %fold.1.folded_ref, bf16[12,128,768]{2,1,0:T(8,128)(2,1)S(1)} %get-tuple-element.31.own_ref, ...), custom_call_target="tpu_custom_call" | custom-call | flops 2415919104 | bytes 10248192 | tf_op jit(solution)/shard_map/fock/pallas_call | solution.py:326
  34.1 1.2 %collective-permute-start.8 = (bf16[64,768]{1,0:T(8,128)(2,1)S(1)}, bf16[64,768]{1,0:T(8,128)(2,1)S(1)}, u32[]{:S(2)}, u32[]{:S(2)}) collective-permute-start(bf16[64,768]{1,0:T(8,128)(2,1)S(1)} %get-tuple-element.40), channel_id=1, source_target_pairs={{0,4},{1,5},{2,6},{3,7},{4,0},{5,1},{6,2},{7,3},{8,12},{9,13},{10,... | collective-permute-start | bytes 294920 | tf_op jit(solution)/shard_map/ppermute | solution.py:362
  35.2 1.0 %collective-permute-start.9 = (bf16[64,768]{1,0:T(8,128)(2,1)S(1)}, bf16[64,768]{1,0:T(8,128)(2,1)S(1)}, u32[]{:S(2)}, u32[]{:S(2)}) collective-permute-start(bf16[64,768]{1,0:T(8,128)(2,1)S(1)} %get-tuple-element.41), channel_id=1, source_target_pairs={{0,6},{1,7},{2,4},{3,5},{4,2},{5,3},{6,0},{7,1},{8,14},{9,15},{10,... | collective-permute-start | bytes 294920 | tf_op jit(solution)/shard_map/ppermute | solution.py:362
  36.2 1.4 %collective-permute-start.10 = (bf16[64,768]{1,0:T(8,128)(2,1)S(1)}, bf16[64,768]{1,0:T(8,128)(2,1)S(1)}, u32[]{:S(2)}, u32[]{:S(2)}) collective-permute-start(bf16[64,768]{1,0:T(8,128)(2,1)S(1)} %get-tuple-element.42), channel_id=1, source_target_pairs={{0,2},{1,3},{2,0},{3,1},{4,6},{5,7},{6,4},{7,5},{8,10},{9,11},{10,... | collective-permute-start | bytes 294920 | tf_op jit(solution)/shard_map/ppermute | solution.py:362
  37.6 2.1 %collective-permute-done.8.refs_1_ = bf16[64,768]{1,0:T(8,128)(2,1)S(1)} collective-permute-done((bf16[64,768]{1,0:T(8,128)(2,1)S(1)}, bf16[64,768]{1,0:T(8,128)(2,1)S(1)}, u32[]{:S(2)}, u32[]{:S(2)}) %collective-permute-start.8) | collective-permute-done | bytes 98336 | tf_op jit(solution)/shard_map/ppermute | solution.py:362
  39.8 2.0 %collective-permute-done.9.refs_2_ = bf16[64,768]{1,0:T(8,128)(2,1)S(1)} collective-permute-done((bf16[64,768]{1,0:T(8,128)(2,1)S(1)}, bf16[64,768]{1,0:T(8,128)(2,1)S(1)}, u32[]{:S(2)}, u32[]{:S(2)}) %collective-permute-start.9) | collective-permute-done | bytes 98336 | tf_op jit(solution)/shard_map/ppermute | solution.py:362
  41.8 0.1 collective-permute-done.10.refs_3_
  41.9 0.1 sum.1
  42.0 0.1 collective-permute-start.11
  42.1 1.3 %collective-permute-done.11.refs_1_ = bf16[64,768]{1,0:T(8,128)(2,1)S(1)} collective-permute-done((bf16[64,768]{1,0:T(8,128)(2,1)S(1)}, bf16[64,768]{1,0:T(8,128)(2,1)S(1)}, u32[]{:S(2)}, u32[]{:S(2)}) %collective-permute-start.11) | collective-permute-done | bytes 98336 | tf_op jit(solution)/shard_map/ppermute | solution.py:354
  43.4 1.5 %collective-permute-start.12 = (bf16[32,768]{1,0:T(8,128)(2,1)S(1)}, bf16[32,768]{1,0:T(8,128)(2,1)S(1)}, u32[]{:S(2)}, u32[]{:S(2)}) collective-permute-start(bf16[32,768]{1,0:T(8,128)(2,1)S(1)} %get-tuple-element.46), channel_id=1, source_target_pairs={{0,24},{8,16},{16,8},{24,0},{1,25},{9,17},{17,9},{25,1},{2,26},{10... | collective-permute-start | bytes 147464 | tf_op jit(solution)/shard_map/ppermute | solution.py:358
  44.9 0.5 %collective-permute-start.13 = (bf16[32,768]{1,0:T(8,128)(2,1)S(1)}, bf16[32,768]{1,0:T(8,128)(2,1)S(1)}, u32[]{:S(2)}, u32[]{:S(2)}) collective-permute-start(bf16[32,768]{1,0:T(8,128)(2,1)S(1)} %get-tuple-element.47), channel_id=1, source_target_pairs={{0,8},{8,0},{16,24},{24,16},{1,9},{9,1},{17,25},{25,17},{2,10},{10... | collective-permute-start | bytes 147464 | tf_op jit(solution)/shard_map/ppermute | solution.py:358
  45.5 1.5 %collective-permute-start.14 = (bf16[32,768]{1,0:T(8,128)(2,1)S(1)}, bf16[32,768]{1,0:T(8,128)(2,1)S(1)}, u32[]{:S(2)}, u32[]{:S(2)}) collective-permute-start(bf16[32,768]{1,0:T(8,128)(2,1)S(1)} %get-tuple-element.48), channel_id=1, source_target_pairs={{0,16},{8,24},{16,0},{24,8},{1,17},{9,25},{17,1},{25,9},{2,18},{10... | collective-permute-start | bytes 147464 | tf_op jit(solution)/shard_map/ppermute | solution.py:358
  46.9 1.7 %collective-permute-done.12.refs_1_ = bf16[32,768]{1,0:T(8,128)(2,1)S(1)} collective-permute-done((bf16[32,768]{1,0:T(8,128)(2,1)S(1)}, bf16[32,768]{1,0:T(8,128)(2,1)S(1)}, u32[]{:S(2)}, u32[]{:S(2)}) %collective-permute-start.12) | collective-permute-done | bytes 49184 | tf_op jit(solution)/shard_map/ppermute | solution.py:358
  48.7 0.3 collective-permute-done.13.refs_2_
  49.0 0.5 %collective-permute-done.14.refs_3_ = bf16[32,768]{1,0:T(8,128)(2,1)S(1)} collective-permute-done((bf16[32,768]{1,0:T(8,128)(2,1)S(1)}, bf16[32,768]{1,0:T(8,128)(2,1)S(1)}, u32[]{:S(2)}, u32[]{:S(2)}) %collective-permute-start.14) | collective-permute-done | bytes 49184 | tf_op jit(solution)/shard_map/ppermute | solution.py:358
  49.6 0.0 copy-done.2
  49.6 0.0 copy-done.3
  49.6 1.4 %deal.1 = bf16[16,8,768]{2,1,0:T(8,128)(2,1)} custom-call(s32[1]{0:T(128)} %bitcast.grp_ref, s32[8]{0:T(128)S(1)} %copy-done.2, f32[8]{0:T(128)S(1)} %copy-done.3, f32[8,128]{1,0:T(8,128)S(1)} %get-tuple-element.35.total_ref, bf16[32,768]{1,0:T(8,128)(2,1)S(1)} %get-tuple-element.45.refs_0_, bf16[32,768]{1,0:T(8,128)(2,1)S(1)} %collective-permute-done.12.refs_1_, ...), custom_call_target="tpu_custom_call" | custom-call | bytes 397312 | tf_op jit(solution)/shard_map/deal/pallas_call | solution.py:326
  (1 shorter events, 0.0 us)
Async XLA Ops:
  0.0 13.6 %collective-permute-start.1 = (bf16[12,128,768]{2,1,0:T(8,128)(2,1)}, bf16[12,128,768]{2,1,0:T(8,128)(2,1)S(1)}, u32[]{:S(2)}, u32[]{:S(2)}) collective-permute-start(bf16[12,128,768]{2,1,0:T(8,128)(2,1)} %refs_0_.3), channel_id=1, source_target_pairs={{0,1},{1,0},{2,3},{3,2},{4,5},{5,4},{6,7},{7,6},{8,9},{9,8},{10,11... | collective-permute-start | bytes 7077896 | tf_op jit(solution)/shard_map/ppermute | solution.py:354
  2.3 2.6 %collective-permute-start = (bf16[448,128]{1,0:T(8,128)(2,1)}, bf16[448,128]{1,0:T(8,128)(2,1)S(1)}, u32[]{:S(2)}, u32[]{:S(2)}) collective-permute-start(bf16[448,128]{1,0:T(8,128)(2,1)} %get-tuple-element.28), channel_id=1, source_target_pairs={{0,1},{1,0},{2,3},{3,2},{4,5},{5,4},{6,7},{7,6},{8,9},{9,8},{10,11... | collective-permute-start | bytes 344072 | tf_op jit(solution)/shard_map/ppermute | solution.py:354
  2.5 0.9 %copy-start.1 = (bf16[448,128]{1,0:T(8,128)(2,1)S(1)}, bf16[448,128]{1,0:T(8,128)(2,1)}, u32[]{:S(2)}) copy-start(bf16[448,128]{1,0:T(8,128)(2,1)} %get-tuple-element.27.refs_0_) | copy-start | bytes 344068
  5.0 7.5 %collective-permute-start.2 = (bf16[208,128]{1,0:T(8,128)(2,1)S(1)}, bf16[208,128]{1,0:T(8,128)(2,1)S(1)}, u32[]{:S(2)}, u32[]{:S(2)}) collective-permute-start(bf16[208,128]{1,0:T(8,128)(2,1)S(1)} %get-tuple-element.32), channel_id=1, source_target_pairs={{0,24},{8,16},{16,8},{24,0},{1,25},{9,17},{17,9},{25,1},{2,26},{10... | collective-permute-start | bytes 159752 | tf_op jit(solution)/shard_map/ppermute | solution.py:358
  8.9 4.1 %collective-permute-start.3 = (bf16[208,128]{1,0:T(8,128)(2,1)S(1)}, bf16[208,128]{1,0:T(8,128)(2,1)S(1)}, u32[]{:S(2)}, u32[]{:S(2)}) collective-permute-start(bf16[208,128]{1,0:T(8,128)(2,1)S(1)} %get-tuple-element.33), channel_id=1, source_target_pairs={{0,8},{8,0},{16,24},{24,16},{1,9},{9,1},{17,25},{25,17},{2,10},{10... | collective-permute-start | bytes 159752 | tf_op jit(solution)/shard_map/ppermute | solution.py:358
  9.5 4.1 %collective-permute-start.4 = (bf16[208,128]{1,0:T(8,128)(2,1)S(1)}, bf16[208,128]{1,0:T(8,128)(2,1)S(1)}, u32[]{:S(2)}, u32[]{:S(2)}) collective-permute-start(bf16[208,128]{1,0:T(8,128)(2,1)S(1)} %get-tuple-element.34), channel_id=1, source_target_pairs={{0,16},{8,24},{16,0},{24,8},{1,17},{9,25},{17,1},{25,9},{2,18},{10... | collective-permute-start | bytes 159752 | tf_op jit(solution)/shard_map/ppermute | solution.py:358
  9.6 1.3 %copy-start = (bf16[768,768]{1,0:T(8,128)(2,1)S(1)}, bf16[768,768]{1,0:T(8,128)(2,1)}, u32[]{:S(2)}) copy-start(bf16[768,768]{1,0:T(8,128)(2,1)} %refs_1_.3) | copy-start | bytes 3538948
  19.8 6.8 %collective-permute-start.5 = (bf16[408,128]{1,0:T(8,128)(2,1)S(1)}, bf16[408,128]{1,0:T(8,128)(2,1)S(1)}, u32[]{:S(2)}, u32[]{:S(2)}) collective-permute-start(bf16[408,128]{1,0:T(8,128)(2,1)S(1)} %get-tuple-element.38.refs_0_), channel_id=1, source_target_pairs={{0,4},{1,5},{2,6},{3,7},{4,0},{5,1},{6,2},{7,3},{8,12},{9,13},{10,... | collective-permute-start | bytes 313352 | tf_op jit(solution)/shard_map/ppermute | solution.py:362
  22.4 6.6 %collective-permute-start.6 = (bf16[408,128]{1,0:T(8,128)(2,1)S(1)}, bf16[408,128]{1,0:T(8,128)(2,1)S(1)}, u32[]{:S(2)}, u32[]{:S(2)}) collective-permute-start(bf16[408,128]{1,0:T(8,128)(2,1)S(1)} %get-tuple-element.38.refs_0_), channel_id=1, source_target_pairs={{0,6},{1,7},{2,4},{3,5},{4,2},{5,3},{6,0},{7,1},{8,14},{9,15},{10,... | collective-permute-start | bytes 313352 | tf_op jit(solution)/shard_map/ppermute | solution.py:362
  23.8 6.8 %collective-permute-start.7 = (bf16[408,128]{1,0:T(8,128)(2,1)S(1)}, bf16[408,128]{1,0:T(8,128)(2,1)S(1)}, u32[]{:S(2)}, u32[]{:S(2)}) collective-permute-start(bf16[408,128]{1,0:T(8,128)(2,1)S(1)} %get-tuple-element.38.refs_0_), channel_id=1, source_target_pairs={{0,2},{1,3},{2,0},{3,1},{4,6},{5,7},{6,4},{7,5},{8,10},{9,11},{10,... | collective-permute-start | bytes 313352 | tf_op jit(solution)/shard_map/ppermute | solution.py:362
  30.6 19.0 %copy-start.2 = (s32[8]{0:T(128)S(1)}, s32[8]{0:T(128)}, u32[]{:S(2)}) copy-start(s32[8]{0:T(128)} %target_ref.1) | copy-start | bytes 100
  30.6 19.0 %copy-start.3 = (f32[8]{0:T(128)S(1)}, f32[8]{0:T(128)}, u32[]{:S(2)}) copy-start(f32[8]{0:T(128)} %weights_ref.1) | copy-start | bytes 100
  34.1 5.7 %collective-permute-start.8 = (bf16[64,768]{1,0:T(8,128)(2,1)S(1)}, bf16[64,768]{1,0:T(8,128)(2,1)S(1)}, u32[]{:S(2)}, u32[]{:S(2)}) collective-permute-start(bf16[64,768]{1,0:T(8,128)(2,1)S(1)} %get-tuple-element.40), channel_id=1, source_target_pairs={{0,4},{1,5},{2,6},{3,7},{4,0},{5,1},{6,2},{7,3},{8,12},{9,13},{10,... | collective-permute-start | bytes 294920 | tf_op jit(solution)/shard_map/ppermute | solution.py:362
  35.2 6.6 %collective-permute-start.9 = (bf16[64,768]{1,0:T(8,128)(2,1)S(1)}, bf16[64,768]{1,0:T(8,128)(2,1)S(1)}, u32[]{:S(2)}, u32[]{:S(2)}) collective-permute-start(bf16[64,768]{1,0:T(8,128)(2,1)S(1)} %get-tuple-element.41), channel_id=1, source_target_pairs={{0,6},{1,7},{2,4},{3,5},{4,2},{5,3},{6,0},{7,1},{8,14},{9,15},{10,... | collective-permute-start | bytes 294920 | tf_op jit(solution)/shard_map/ppermute | solution.py:362
  36.2 5.7 %collective-permute-start.10 = (bf16[64,768]{1,0:T(8,128)(2,1)S(1)}, bf16[64,768]{1,0:T(8,128)(2,1)S(1)}, u32[]{:S(2)}, u32[]{:S(2)}) collective-permute-start(bf16[64,768]{1,0:T(8,128)(2,1)S(1)} %get-tuple-element.42), channel_id=1, source_target_pairs={{0,2},{1,3},{2,0},{3,1},{4,6},{5,7},{6,4},{7,5},{8,10},{9,11},{10,... | collective-permute-start | bytes 294920 | tf_op jit(solution)/shard_map/ppermute | solution.py:362
  42.0 1.4 %collective-permute-start.11 = (bf16[64,768]{1,0:T(8,128)(2,1)S(1)}, bf16[64,768]{1,0:T(8,128)(2,1)S(1)}, u32[]{:S(2)}, u32[]{:S(2)}) collective-permute-start(bf16[64,768]{1,0:T(8,128)(2,1)S(1)} %get-tuple-element.44), channel_id=1, source_target_pairs={{0,1},{1,0},{2,3},{3,2},{4,5},{5,4},{6,7},{7,6},{8,9},{9,8},{10,11... | collective-permute-start | bytes 294920 | tf_op jit(solution)/shard_map/ppermute | solution.py:354
  43.4 5.3 %collective-permute-start.12 = (bf16[32,768]{1,0:T(8,128)(2,1)S(1)}, bf16[32,768]{1,0:T(8,128)(2,1)S(1)}, u32[]{:S(2)}, u32[]{:S(2)}) collective-permute-start(bf16[32,768]{1,0:T(8,128)(2,1)S(1)} %get-tuple-element.46), channel_id=1, source_target_pairs={{0,24},{8,16},{16,8},{24,0},{1,25},{9,17},{17,9},{25,1},{2,26},{10... | collective-permute-start | bytes 147464 | tf_op jit(solution)/shard_map/ppermute | solution.py:358
  44.9 4.1 %collective-permute-start.13 = (bf16[32,768]{1,0:T(8,128)(2,1)S(1)}, bf16[32,768]{1,0:T(8,128)(2,1)S(1)}, u32[]{:S(2)}, u32[]{:S(2)}) collective-permute-start(bf16[32,768]{1,0:T(8,128)(2,1)S(1)} %get-tuple-element.47), channel_id=1, source_target_pairs={{0,8},{8,0},{16,24},{24,16},{1,9},{9,1},{17,25},{25,17},{2,10},{10... | collective-permute-start | bytes 147464 | tf_op jit(solution)/shard_map/ppermute | solution.py:358
  45.5 4.1 %collective-permute-start.14 = (bf16[32,768]{1,0:T(8,128)(2,1)S(1)}, bf16[32,768]{1,0:T(8,128)(2,1)S(1)}, u32[]{:S(2)}, u32[]{:S(2)}) collective-permute-start(bf16[32,768]{1,0:T(8,128)(2,1)S(1)} %get-tuple-element.48), channel_id=1, source_target_pairs={{0,16},{8,24},{16,0},{24,8},{1,17},{9,25},{17,1},{25,9},{2,18},{10... | collective-permute-start | bytes 147464 | tf_op jit(solution)/shard_map/ppermute | solution.py:358

commit v8 on v5

v8 whole, which is shorter than its diff:
```python
import functools
import math
import jax
import jax.numpy as jnp
from jax import lax
from jax.experimental import pallas as pl
from jax.experimental.pallas import tpu as pltpu
from jax.sharding import PartitionSpec as P

F32 = jnp.float32
BF16 = jnp.bfloat16
LANES = 128
ROUTE_VMEM = 56
STAGE_VMEM = 48


def power(size):
    return size & (size - 1) == 0


def target_of(me, s, size):
    return lax.bitwise_xor(me, jnp.int32(s)) if power(size) else lax.rem(me + s, size)


def source_of(me, s, size):
    return lax.bitwise_xor(me, jnp.int32(s)) if power(size) else lax.rem(me + size - s, size)


def terms(value, count):
    out = []
    for _ in range(count):
        term = value.astype(BF16).astype(F32)
        out.append(term)
        value = value - term
    return out


def round_up(x, unit):
    return -(-x // unit) * unit


def write_lines(out, start, pieces):
    have = sum(p.shape[0] for p in pieces)
    rest = out.shape[0] - start - have
    if rest:
        pieces = list(pieces) + [jnp.zeros((rest, LANES), F32)]
    out[start:, :] = jnp.concatenate(pieces, axis=0).astype(BF16)


def wide_mask(line, width):
    return jnp.concatenate([line] * (width // LANES), axis=1) > 0


def stage_kernel(*refs):
    sems = refs[-1]
    count = sems.shape[0]
    copies = [pltpu.make_async_copy(refs[i], refs[i - count - 1], sems.at[i]) for i in range(count)]
    for copy in copies:
        copy.start()
    for copy in copies:
        copy.wait()


def route_kernel(keep, cap, *refs):
    anys, refs = refs[:5], refs[5:]
    out, target_ref, weights_ref, own_ref, fields_ref, diag_ref, wide, blocks, parts, lines, sems = refs
    held = (target_ref, weights_ref, own_ref, fields_ref, diag_ref)
    copies = [pltpu.make_async_copy(a, b, sems.at[i]) for i, (a, b) in enumerate(zip(anys, held))]
    for copy in copies:
        copy.start()
    rows, slots, orbitals = own_ref.shape
    vec_count = fields_ref.shape[1]
    chunks = orbitals // LANES
    spots = blocks.shape[0] - 1
    groups = spots // cap // 2
    live = groups * keep
    blocks[...] = jnp.zeros(blocks.shape, F32)
    lines[...] = jnp.zeros(lines.shape, F32)
    for copy in copies:
        copy.wait()
    wide[...] = own_ref[...].astype(F32)
    exponent = fields_ref[:, 0:1] * diag_ref[0:1, :]
    for g in range(1, vec_count):
        exponent = exponent + fields_ref[:, g : g + 1] * diag_ref[g : g + 1, :]
    for i, term in enumerate(terms(exponent, 2)):
        for c in range(chunks):
            parts[:, i * chunks + c, :] = term[:, c * LANES : (c + 1) * LANES]
    weight = F32(0.0)
    for slot in range(slots):
        t = target_ref[slot]
        alive = t < live
        weight = weight + jnp.where(alive, weights_ref[slot], F32(0.0))
        turn = lax.div(t, groups)
        at = (lax.rem(t, groups) * 2 + lax.rem(turn, 2)) * cap
        turn = lax.div(turn, 2)
        at = jnp.where(alive, at + lax.rem(turn, cap), spots)
        blocks[at] = wide[:, slot, :]
        parts[slot, 2 * chunks : 2 * chunks + 1, :] = jnp.full((1, LANES), (turn + 1).astype(F32), F32)
        lines[at] = parts[slot]
    sums = terms(jnp.full((1, LANES), weight, F32), 3)
    for d in range(2 * groups):
        for k in range(cap):
            block = blocks[d * cap + k]
            for c in range(chunks):
                at = (k * chunks + c) * rows
                out[d, at : at + rows, :] = block[:, c * LANES : (c + 1) * LANES].astype(BF16)
        tail = [lines[d * cap + k][0 : 2 * chunks + 1] for k in range(cap)]
        write_lines(out.at[d], cap * chunks * rows, tail + sums)


def merge_kernel(half, cap, rows, chunks, routed_ref, out, weight_ref, pick_ref):
    each = 2 * chunks + 1
    start = cap * chunks * rows
    weight = jnp.zeros((1, LANES), F32)
    walker = [[jnp.zeros((2 * rows, LANES), F32)] * chunks for _ in range(half)]
    line = [jnp.zeros((2 * chunks, LANES), F32)] * half
    for q in range(routed_ref.shape[0] // 2):
        tails = [routed_ref[2 * q + e, start:, :].astype(F32) for e in range(2)]
        total = tails[0][cap * each : cap * each + 1] + tails[0][cap * each + 1 : cap * each + 2]
        weight = weight + (total + tails[0][cap * each + 2 : cap * each + 3])
        for k in range(cap):
            flag = tails[0][(k + 1) * each - 1 : (k + 1) * each]
            a, b = [tail[k * each : (k + 1) * each - 1] for tail in tails]
            both = (a[0:chunks] + b[0:chunks]) + (a[chunks:] + b[chunks:])
            part = jnp.concatenate(terms(both, 2), axis=0)
            for u in range(k, half, cap):
                mine = jnp.where(flag == u + 1, F32(1.0), F32(0.0))
                pick_ref[q * half + u : q * half + u + 1, :] = mine
                line[u] = jnp.where(mine > 0, part, line[u])
                for c in range(chunks):
                    at = (k * chunks + c) * rows
                    block = [routed_ref[2 * q + e, at : at + rows, :].astype(F32) for e in range(2)]
                    walker[u][c] = jnp.where(mine > 0, jnp.concatenate(block, axis=0), walker[u][c])
    weight_ref[...] = jnp.broadcast_to(weight, weight_ref.shape)
    for u in range(half):
        for c in range(chunks):
            at = (u * chunks + c) * 2 * rows
            out[at : at + 2 * rows, :] = walker[u][c].astype(BF16)
    write_lines(out, half * chunks * 2 * rows, line)


def fock_kernel(order, send_order, count, rows, chip_ref, body_ref, own_ref, twin_ref, *refs):
    n = len(order)
    ins, outs = refs[:n], refs[n : 2 * n]
    prop, turned, coup, result = refs[2 * n :]
    vec_count, occupied, orbitals = own_ref.shape
    chunks = orbitals // LANES
    chip = chip_ref[0]
    start = count * chunks * rows
    exponent = jnp.zeros((2 * count * chunks, LANES), F32)
    for ref in ins:
        exponent = exponent + ref[start : start + 2 * count * chunks, :].astype(F32)
    growth = []
    for w in range(count):
        at = 2 * w * chunks
        growth.append(jnp.exp(exponent[at : at + chunks] + exponent[at + chunks : at + 2 * chunks]))
    for ref, s in zip(ins, order):
        source = source_of(chip, s, n)
        for w in range(count):
            for c in range(chunks):
                at = (w * chunks + c) * rows
                piece = ref[at : at + rows, :].astype(F32) * growth[w][c : c + 1]
                prop[w, source, :, c * LANES : (c + 1) * LANES] = piece.astype(prop.dtype)
    scaled = jnp.concatenate([prop[w, i] for w in range(count) for i in range(n)], axis=0).astype(BF16)
    turned[...] = jnp.dot(scaled, body_ref[...], preferred_element_type=F32).T.astype(BF16)
    batch = math.gcd(vec_count, 4)
    for c, ref in enumerate((own_ref, twin_ref)):
        for g in range(0, vec_count, batch):
            left = ref[g : g + batch].reshape(batch * occupied, orbitals)
            s = jnp.dot(left, turned[...], preferred_element_type=F32).astype(BF16)
            for k in range(batch):
                at = (c * vec_count + g + k) * occupied
                for w in range(count):
                    coup[w * occupied : (w + 1) * occupied, at : at + occupied] = s[
                        k * occupied : (k + 1) * occupied, w * occupied : (w + 1) * occupied
                    ]
    tile = 256 if orbitals % 256 == 0 else orbitals
    depth = vec_count * occupied
    for t in range(0, orbitals, tile):
        total = jnp.dot(
            coup[:, :depth],
            own_ref[:, :, t : t + tile].reshape(depth, tile),
            preferred_element_type=F32,
        )
        total = total + jnp.dot(
            coup[:, depth:],
            twin_ref[:, :, t : t + tile].reshape(depth, tile),
            preferred_element_type=F32,
        )
        for w in range(count):
            for i in range(n):
                at = w * occupied + i * rows
                result[w, i, :, t : t + tile] = total[at : at + rows].astype(result.dtype)
    for out, s in zip(outs, send_order):
        to = target_of(chip, s, n)
        for w in range(count):
            out[w * rows : (w + 1) * rows, :] = result[w, to].astype(BF16)


def sum_kernel(half, cap, rows, pick_ref, *refs):
    ins, out = refs[:-1], refs[-1]
    orbitals = out.shape[2]
    total = ins[0][...].astype(F32)
    for ref in ins[1:]:
        total = total + ref[...].astype(F32)
    for q in range(out.shape[0] // cap // 2):
        for k in range(cap):
            value = jnp.zeros((2 * rows, orbitals), F32)
            for u in range(k, half, cap):
                mine = pick_ref[q * half + u : q * half + u + 1, :]
                value = jnp.where(wide_mask(mine, orbitals), total[2 * u * rows : 2 * (u + 1) * rows], value)
            for e in range(2):
                out[(2 * q + e) * cap + k] = value[e * rows : (e + 1) * rows].astype(BF16)


def deal_kernel(keep, cap, target_ref, weights_ref, total_ref, back_ref, out_ref, wide):
    rows, slots, orbitals = out_ref.shape
    groups = back_ref.shape[0] // cap // 2
    live = groups * keep
    for slot in range(slots):
        t = target_ref[slot]
        alive = t < live
        turn = lax.div(t, groups)
        at = (lax.rem(t, groups) * 2 + lax.rem(turn, 2)) * cap + lax.rem(lax.div(turn, 2), cap)
        block = back_ref[jnp.where(alive, at, 0)].astype(F32)
        weight = jnp.where(alive, weights_ref[slot], F32(0.0))
        factor = jnp.full((1, LANES), weight * live, F32) / total_ref[0:1, :]
        wide[:, slot, :] = jnp.where(alive, block * factor[:, 0:1], F32(0.0))
    out_ref[...] = wide[...].astype(BF16)


def call(kernel, outs, scalars, held, arrays, scratch, name, flops=0, vmem=40):
    smem = pl.BlockSpec(memory_space=pltpu.SMEM)
    full = pl.BlockSpec(memory_space=pltpu.VMEM)
    size = sum(x.size * x.dtype.itemsize for x in list(arrays) + list(outs))
    return pl.pallas_call(
        kernel,
        out_shape=outs,
        in_specs=[smem] * len(scalars) + [pl.BlockSpec(memory_space=pl.ANY)] * len(held) + [full] * len(arrays),
        out_specs=[full] * len(outs),
        scratch_shapes=scratch,
        compiler_params=pltpu.CompilerParams(vmem_limit_bytes=vmem * 2**20),
        cost_estimate=pl.CostEstimate(flops=flops, bytes_accessed=size, transcendentals=0),
        name=name,
    )(*scalars, *held, *arrays)


def body(walkers, one_body, fields, field_diag, chol, weights, target):
    rows, slots, orbitals = walkers.shape
    vec_count, occupied, _ = chol.shape
    chips, groups = lax.axis_size("chip"), lax.axis_size("grp")
    keep = slots // 2
    half = keep // 2
    cap = -(-slots // (2 * groups))
    chunks = orbitals // LANES
    shape = jax.ShapeDtypeStruct
    chip = lax.axis_index("chip").reshape(1)

    def to_chip(x, s):
        to = [(i, i ^ s if power(chips) else (i + s) % chips) for i in range(chips)]
        return lax.ppermute(x, "chip", to) if s else x

    def exchange(x):
        return lax.all_to_all(x, ("grp", "core"), 0, 0, tiled=True)

    send_order = [0] + list(range(chips // 2, chips)) + list(range(1, chips // 2))
    chip_order = [0] + send_order[:0:-1]
    chol_twin = lax.ppermute(chol, "core", [(0, 1), (1, 0)])
    lines = cap * (chunks * rows + 2 * chunks + 1) + 3
    routed = call(
        functools.partial(route_kernel, keep, cap),
        [shape((2 * groups, round_up(lines, 16), LANES), BF16)],
        [],
        [target, weights, walkers, fields, field_diag],
        [],
        [pltpu.SMEM(x.shape, x.dtype) for x in (target, weights)]
        + [pltpu.VMEM(x.shape, x.dtype) for x in (walkers, fields, field_diag)]
        + [
            pltpu.VMEM((rows, slots, orbitals), F32),
            pltpu.VMEM((2 * groups * cap + 1, rows, orbitals), F32),
            pltpu.VMEM((slots, 2 * chunks + 4, LANES), F32),
            pltpu.VMEM((2 * groups * cap + 1, 2 * chunks + 4, LANES), F32),
            pltpu.SemaphoreType.DMA((5,)),
        ],
        "route",
        vmem=ROUTE_VMEM,
    )
    routed = [exchange(routed[0])]
    payload = shape((half * chunks * 2 * rows + round_up(2 * half * chunks, 8), LANES), BF16)
    payload, weight_sum, pick = call(
        functools.partial(merge_kernel, half, cap, rows, chunks),
        [payload, shape((8, LANES), F32), shape((groups * half, LANES), F32)],
        [],
        [],
        routed,
        [],
        "merge",
    )
    own, held_body = call(
        stage_kernel,
        [shape(x.shape, x.dtype) for x in (chol, one_body)],
        [],
        [chol, one_body, weight_sum],
        [],
        [pltpu.SemaphoreType.DMA((2,))],
        "stage",
        vmem=STAGE_VMEM,
    )
    gathered = [to_chip(payload, s) for s in chip_order]
    held = F32 if rows % 8 else BF16
    parts = call(
        functools.partial(fock_kernel, chip_order, send_order, half, 2 * rows),
        [shape((half * 2 * rows, orbitals), BF16)] * chips,
        [chip],
        [],
        [held_body, own, chol_twin] + gathered,
        [
            pltpu.VMEM((half, chips, 2 * rows, orbitals), held),
            pltpu.VMEM((orbitals, half * occupied), BF16),
            pltpu.VMEM((half * occupied, 2 * vec_count * occupied), BF16),
            pltpu.VMEM((half, chips, 2 * rows, orbitals), held),
        ],
        "fock",
        flops=2 * half * occupied * orbitals * (orbitals + 4 * vec_count * occupied),
    )
    parts = [to_chip(x, s) for s, x in zip(send_order, parts)]
    (back,) = call(
        functools.partial(sum_kernel, half, cap, rows),
        [shape((2 * groups * cap, rows, orbitals), BF16)],
        [],
        [],
        [pick] + parts,
        [],
        "sum",
    )
    (out,) = call(
        functools.partial(deal_kernel, keep, cap),
        [shape(walkers.shape, BF16)],
        [target, weights],
        [],
        [weight_sum, exchange(back)],
        [pltpu.VMEM(walkers.shape, F32)],
        "deal",
    )
    return out


def solution(mesh):
    groups, n = mesh.shape["grp"], mesh.shape["blk"]
    split = jax.sharding.Mesh(mesh.devices.reshape(groups, n // 2, 2), ("grp", "chip", "core"))
    blk = ("chip", "core")
    in_specs = (
        P(blk, "grp", None),
        P(),
        P("grp", blk),
        P(blk, None),
        P(blk, None, None),
        P("grp"),
        P("grp"),
    )
    out_specs = P(blk, "grp", None)
    return jax.shard_map(body, mesh=split, in_specs=in_specs, out_specs=out_specs, check_vma=False)
```

time: 49.8 us -> 51.3 us (1.030)
  blocking collectives: 0 us -> 20.1 us
  waiting for transfers between devices: 21.2 us -> 11.6 us
  starting transfers between devices: 17 us -> 9.02 us
  local copies, waits for them, and re-layouts: 2.18 us -> 1.28 us
    all_to_all x0 -> x2, blocking collectives: none -> 20.1 us  [exchange(): return lax.all_to_all(x, ('grp', 'core'), 0, 0, tiled=True)]
    ppermute x15 -> x7, waiting for transfers between devices: 21.2 us -> 11.6 us  [the longest x6 11.6 us: to_chip(): return lax.ppermute(x, 'chip', to) if s else x]
    ppermute x15 -> x7, starting transfers between devices: 17 us -> 9.02 us  [the longest x6 8.56 us: to_chip(): return lax.ppermute(x, 'chip', to) if s else x]
    unnamed x8 -> x6, local copies, waits for them, and re-layouts: 2.18 us -> 1.28 us
    pallas_call x9 -> x6, Pallas kernels: 9.09 us -> 8.97 us  [call(): pl.pallas_call(kernel, out_shape=outs, in_specs=[smem] * len(scalars) + [...]
  transfers between devices with their start and end apart: 15 -> 7, of which waited for: 12 -> 4; matrix products, arithmetic and copies ran while one was open for 0% -> 0% of each run, Pallas kernels for 8% -> 7%
where the time goes in v8:
time: 51.3 us; the launch traced here: 50.9 us
  blocking collectives  20.1 us (39%)
  waiting for transfers between devices  11.6 us (23%)
  starting transfers between devices  9.02 us (18%)
  Pallas kernels  8.97 us (17%)
  local copies, waits for them, and re-layouts  1.28 us (2%)
    all_to_all x2, blocking collectives, exchange(): return lax.all_to_all(x, ('grp', 'core'), 0, 0, tiled=True)  20.1 us
    ppermute x6, waiting for transfers between devices, to_chip(): return lax.ppermute(x, 'chip', to) if s else x  11.6 us
    pallas_call x6, Pallas kernels, call(): pl.pallas_call(kernel, out_shape=outs, in_specs=[smem] * len(scalars) + [...  8.97 us
    ppermute x6, starting transfers between devices, to_chip(): return lax.ppermute(x, 'chip', to) if s else x  8.56 us
    unnamed x6, local copies, waits for them, and re-layouts  1.28 us
  transfers between devices with their start and end apart: 7, of which 4 were waited for; matrix products, arithmetic and copies ran while one was open for 0% of the time, Pallas kernels for 7%

profile of v8, /device:TPU:0, one launch (start us, length us, event | category | flops | bytes accessed | tf_op | source)
XLA Modules:
  0.0 50.9 jit_solution(13106890630271959106)
XLA Ops:
  0.0 0.5 collective-permute-start
  0.5 1.9 %route.1 = bf16[8,112,128]{2,1,0:T(8,128)(2,1)} custom-call(s32[8]{0:T(128)} %target_ref.1, f32[8]{0:T(128)} %weights_ref.1, bf16[16,8,768]{2,1,0:T(8,128)(2,1)} %refs_2_.1, f32[8,12]{1,0:T(8,128)} %refs_3_.1, f32[12,768]{1,0:T(8,128)} %refs_4_.1), custom_call_target="tpu_custom_call" | custom-call | bytes 229376 | tf_op jit(solution)/shard_map/route/pallas_call | solution.py:236
  2.4 11.4 %all_to_all.10.routed_ref = bf16[8,112,128]{2,1,0:T(8,128)(2,1)S(1)} all-to-all(bf16[8,112,128]{2,1,0:T(8,128)(2,1)} %route.1), channel_id=1, replica_groups=mesh['grp'=4,'chip'=4,'core'=2] {'grp','core'}, dimensions={0} | all-to-all | bytes 458752 | tf_op jit(solution)/shard_map/all_to_all | solution.py:264
  13.8 0.1 merge.1
  13.9 2.7 %collective-permute-start.3 = (bf16[408,128]{1,0:T(8,128)(2,1)S(1)}, bf16[408,128]{1,0:T(8,128)(2,1)S(1)}, u32[]{:S(2)}, u32[]{:S(2)}) collective-permute-start(bf16[408,128]{1,0:T(8,128)(2,1)S(1)} %get-tuple-element.18.refs_0_), channel_id=1, source_target_pairs={{0,4},{2,6},{4,0},{6,2},{1,5},{3,7},{5,1},{7,3},{8,12},{10,14},{12... | collective-permute-start | bytes 313352 | tf_op jit(solution)/shard_map/ppermute | solution.py:261
  16.5 1.3 %collective-permute-start.2 = (bf16[408,128]{1,0:T(8,128)(2,1)S(1)}, bf16[408,128]{1,0:T(8,128)(2,1)S(1)}, u32[]{:S(2)}, u32[]{:S(2)}) collective-permute-start(bf16[408,128]{1,0:T(8,128)(2,1)S(1)} %get-tuple-element.18.refs_0_), channel_id=1, source_target_pairs={{0,6},{2,4},{4,2},{6,0},{1,7},{3,5},{5,3},{7,1},{8,14},{10,12},{12... | collective-permute-start | bytes 313352 | tf_op jit(solution)/shard_map/ppermute | solution.py:261
  17.9 0.2 collective-permute-start.1
  18.1 0.0 copy-start
  18.1 1.3 %copy-done = bf16[768,768]{1,0:T(8,128)(2,1)S(1)} copy-done((bf16[768,768]{1,0:T(8,128)(2,1)S(1)}, bf16[768,768]{1,0:T(8,128)(2,1)}, u32[]{:S(2)}) %copy-start) | copy-done | bytes 1179672
  19.4 1.7 %stage.1 = (bf16[12,128,768]{2,1,0:T(8,128)(2,1)S(1)}, bf16[768,768]{1,0:T(8,128)(2,1)S(1)}) custom-call(bf16[12,128,768]{2,1,0:T(8,128)(2,1)} %refs_0_.3, bf16[768,768]{1,0:T(8,128)(2,1)S(1)} %copy-done, f32[8,128]{1,0:T(8,128)S(1)} %get-tuple-element.14.refs_2_.total_ref), custom_call_target="tpu_custom_call" | custom-call | bytes 3538944 | tf_op jit(solution)/shard_map/stage/pallas_call | solution.py:236
  21.1 3.4 %collective-permute-done.3.refs_3_ = bf16[408,128]{1,0:T(8,128)(2,1)S(1)} collective-permute-done((bf16[408,128]{1,0:T(8,128)(2,1)S(1)}, bf16[408,128]{1,0:T(8,128)(2,1)S(1)}, u32[]{:S(2)}, u32[]{:S(2)}) %collective-permute-start.3) | collective-permute-done | bytes 104480 | tf_op jit(solution)/shard_map/ppermute | solution.py:261
  24.5 0.0 collective-permute-done.2.refs_2_
  24.5 0.3 collective-permute-done.1.refs_1_
  24.7 0.0 collective-permute-done.twin_ref
  24.8 0.0 copy-start.1
  24.8 0.0 copy-start.2
  24.8 3.7 %fock.1 = (bf16[64,768]{1,0:T(8,128)(2,1)S(1)}, bf16[64,768]{1,0:T(8,128)(2,1)S(1)}, bf16[64,768]{1,0:T(8,128)(2,1)S(1)}, bf16[64,768]{1,0:T(8,128)(2,1)S(1)}) custom-call(s32[1]{0:T(128)} %bitcast.chip_ref, bf16[768,768]{1,0:T(8,128)(2,1)S(1)} %get-tuple-element.16.body_ref, bf16[12,128,768]{2,1,0:T(8,128)(2,1)S(1)} %get-tuple-element.17.own_ref, ...), custom_call_target="tpu_custom_call" | custom-call | flops 2717908992 | bytes 6709248 | tf_op jit(solution)/shard_map/fock/pallas_call | solution.py:236
  28.5 3.7 %collective-permute-start.4 = (bf16[64,768]{1,0:T(8,128)(2,1)S(1)}, bf16[64,768]{1,0:T(8,128)(2,1)S(1)}, u32[]{:S(2)}, u32[]{:S(2)}) collective-permute-start(bf16[64,768]{1,0:T(8,128)(2,1)S(1)} %get-tuple-element.20), channel_id=1, source_target_pairs={{0,4},{2,6},{4,0},{6,2},{1,5},{3,7},{5,1},{7,3},{8,12},{10,14},{12... | collective-permute-start | bytes 294920 | tf_op jit(solution)/shard_map/ppermute | solution.py:261
  32.2 0.4 collective-permute-start.5
  32.6 0.2 collective-permute-start.6
  32.8 6.8 %collective-permute-done.4.refs_1_ = bf16[64,768]{1,0:T(8,128)(2,1)S(1)} collective-permute-done((bf16[64,768]{1,0:T(8,128)(2,1)S(1)}, bf16[64,768]{1,0:T(8,128)(2,1)S(1)}, u32[]{:S(2)}, u32[]{:S(2)}) %collective-permute-start.4) | collective-permute-done | bytes 98336 | tf_op jit(solution)/shard_map/ppermute | solution.py:261
  39.7 0.0 collective-permute-done.5.refs_2_
  39.7 1.1 %collective-permute-done.6.refs_3_ = bf16[64,768]{1,0:T(8,128)(2,1)S(1)} collective-permute-done((bf16[64,768]{1,0:T(8,128)(2,1)S(1)}, bf16[64,768]{1,0:T(8,128)(2,1)S(1)}, u32[]{:S(2)}, u32[]{:S(2)}) %collective-permute-start.6) | collective-permute-done | bytes 98336 | tf_op jit(solution)/shard_map/ppermute | solution.py:261
  40.7 0.1 sum.1
  40.8 8.6 %all_to_all.11.back_ref = bf16[8,16,768]{2,1,0:T(8,128)(2,1)S(1)} all-to-all(bf16[8,16,768]{2,1,0:T(8,128)(2,1)S(1)} %sum.1), channel_id=1, replica_groups=mesh['grp'=4,'chip'=4,'core'=2] {'grp','core'}, dimensions={0} | all-to-all | bytes 393216 | tf_op jit(solution)/shard_map/all_to_all | solution.py:264
  49.5 0.0 copy-done.1
  49.5 0.0 copy-done.2
  49.5 1.5 %deal.1 = bf16[16,8,768]{2,1,0:T(8,128)(2,1)} custom-call(s32[8]{0:T(128)S(1)} %copy-done.1, f32[8]{0:T(128)S(1)} %copy-done.2, f32[8,128]{1,0:T(8,128)S(1)} %get-tuple-element.14.refs_2_.total_ref, bf16[8,16,768]{2,1,0:T(8,128)(2,1)S(1)} %all_to_all.11.back_ref), custom_call_target="tpu_custom_call" | custom-call | bytes 397312 | tf_op jit(solution)/shard_map/deal/pallas_call | solution.py:236
Async XLA Ops:
  0.0 24.8 %collective-permute-start = (bf16[12,128,768]{2,1,0:T(8,128)(2,1)}, bf16[12,128,768]{2,1,0:T(8,128)(2,1)S(1)}, u32[]{:S(2)}, u32[]{:S(2)}) collective-permute-start(bf16[12,128,768]{2,1,0:T(8,128)(2,1)} %refs_0_.3), channel_id=1, source_target_pairs={{0,1},{1,0},{2,3},{3,2},{4,5},{5,4},{6,7},{7,6},{8,9},{9,8},{10,11... | collective-permute-start | bytes 7077896 | tf_op jit(solution)/shard_map/ppermute | solution.py:268
  13.9 10.6 %collective-permute-start.3 = (bf16[408,128]{1,0:T(8,128)(2,1)S(1)}, bf16[408,128]{1,0:T(8,128)(2,1)S(1)}, u32[]{:S(2)}, u32[]{:S(2)}) collective-permute-start(bf16[408,128]{1,0:T(8,128)(2,1)S(1)} %get-tuple-element.18.refs_0_), channel_id=1, source_target_pairs={{0,4},{2,6},{4,0},{6,2},{1,5},{3,7},{5,1},{7,3},{8,12},{10,14},{12... | collective-permute-start | bytes 313352 | tf_op jit(solution)/shard_map/ppermute | solution.py:261
  16.5 7.9 %collective-permute-start.2 = (bf16[408,128]{1,0:T(8,128)(2,1)S(1)}, bf16[408,128]{1,0:T(8,128)(2,1)S(1)}, u32[]{:S(2)}, u32[]{:S(2)}) collective-permute-start(bf16[408,128]{1,0:T(8,128)(2,1)S(1)} %get-tuple-element.18.refs_0_), channel_id=1, source_target_pairs={{0,6},{2,4},{4,2},{6,0},{1,7},{3,5},{5,3},{7,1},{8,14},{10,12},{12... | collective-permute-start | bytes 313352 | tf_op jit(solution)/shard_map/ppermute | solution.py:261
  17.9 6.9 %collective-permute-start.1 = (bf16[408,128]{1,0:T(8,128)(2,1)S(1)}, bf16[408,128]{1,0:T(8,128)(2,1)S(1)}, u32[]{:S(2)}, u32[]{:S(2)}) collective-permute-start(bf16[408,128]{1,0:T(8,128)(2,1)S(1)} %get-tuple-element.18.refs_0_), channel_id=1, source_target_pairs={{0,2},{2,0},{4,6},{6,4},{1,3},{3,1},{5,7},{7,5},{8,10},{10,8},{12,... | collective-permute-start | bytes 313352 | tf_op jit(solution)/shard_map/ppermute | solution.py:261
  18.1 1.3 %copy-start = (bf16[768,768]{1,0:T(8,128)(2,1)S(1)}, bf16[768,768]{1,0:T(8,128)(2,1)}, u32[]{:S(2)}) copy-start(bf16[768,768]{1,0:T(8,128)(2,1)} %refs_1_.3) | copy-start | bytes 3538948
  24.8 24.7 %copy-start.1 = (s32[8]{0:T(128)S(1)}, s32[8]{0:T(128)}, u32[]{:S(2)}) copy-start(s32[8]{0:T(128)} %target_ref.1) | copy-start | bytes 100
  24.8 24.7 %copy-start.2 = (f32[8]{0:T(128)S(1)}, f32[8]{0:T(128)}, u32[]{:S(2)}) copy-start(f32[8]{0:T(128)} %weights_ref.1) | copy-start | bytes 100
  28.5 11.2 %collective-permute-start.4 = (bf16[64,768]{1,0:T(8,128)(2,1)S(1)}, bf16[64,768]{1,0:T(8,128)(2,1)S(1)}, u32[]{:S(2)}, u32[]{:S(2)}) collective-permute-start(bf16[64,768]{1,0:T(8,128)(2,1)S(1)} %get-tuple-element.20), channel_id=1, source_target_pairs={{0,4},{2,6},{4,0},{6,2},{1,5},{3,7},{5,1},{7,3},{8,12},{10,14},{12... | collective-permute-start | bytes 294920 | tf_op jit(solution)/shard_map/ppermute | solution.py:261
  32.2 7.5 %collective-permute-start.5 = (bf16[64,768]{1,0:T(8,128)(2,1)S(1)}, bf16[64,768]{1,0:T(8,128)(2,1)S(1)}, u32[]{:S(2)}, u32[]{:S(2)}) collective-permute-start(bf16[64,768]{1,0:T(8,128)(2,1)S(1)} %get-tuple-element.21), channel_id=1, source_target_pairs={{0,6},{2,4},{4,2},{6,0},{1,7},{3,5},{5,3},{7,1},{8,14},{10,12},{12... | collective-permute-start | bytes 294920 | tf_op jit(solution)/shard_map/ppermute | solution.py:261
  32.6 8.1 %collective-permute-start.6 = (bf16[64,768]{1,0:T(8,128)(2,1)S(1)}, bf16[64,768]{1,0:T(8,128)(2,1)S(1)}, u32[]{:S(2)}, u32[]{:S(2)}) collective-permute-start(bf16[64,768]{1,0:T(8,128)(2,1)S(1)} %get-tuple-element.22), channel_id=1, source_target_pairs={{0,2},{2,0},{4,6},{6,4},{1,3},{3,1},{5,7},{7,5},{8,10},{10,8},{12,... | collective-permute-start | bytes 294920 | tf_op jit(solution)/shard_map/ppermute | solution.py:261

commit v9 on v4

--- a/solution.py
+++ b/solution.py
@@ -10,6 +10,9 @@
 F32 = jnp.float32
 BF16 = jnp.bfloat16
 LANES = 128
+VMEM = 24
+ROUTE_VMEM = 56
+STAGE_VMEM = 48
 
 
 def terms(value, count):
@@ -45,9 +48,9 @@
 
 
 def stage_kernel(*refs):
-    count = (len(refs) - 2) // 2
     sems = refs[-1]
-    copies = [pltpu.make_async_copy(refs[i], refs[count + 1 + i], sems.at[i]) for i in range(count)]
+    count = sems.shape[0]
+    copies = [pltpu.make_async_copy(refs[i], refs[i - count - 1], sems.at[i]) for i in range(count)]
     for copy in copies:
         copy.start()
     for copy in copies:
@@ -94,14 +97,14 @@
         lines[at] = parts[slot]
     sums = terms(jnp.full((1, LANES), weight, F32), 3)
     for s, out in enumerate(outs):
-        base = lax.rem(me_ref[0] + s, groups) * cap
+        base = moved(me_ref[0], s, groups, 1) * cap
         out[:, 0:orbitals] = jnp.concatenate([blocks[base + k] for k in range(cap)], axis=0).astype(BF16)
         tail = [lines[base + k][0 : 2 * chunks + 1] for k in range(cap)]
         write_tail(out, orbitals, jnp.concatenate(tail + sums, axis=0))
 
 
-def merge_kernel(keep, cap, groups, orbitals, core_ref, *refs):
-    ins, (same_ref, other_ref, weight_ref, pick_ref) = refs[:groups], refs[groups:]
+def merge_kernel(order, keep, cap, orbitals, core_ref, when, *refs):
+    ins, (same_ref, other_ref, weight_ref, pick_ref) = refs[: len(order)], refs[len(order) :]
     half = keep // 2
     rows = ins[0].shape[0] // cap
     slab = half * rows
@@ -110,7 +113,7 @@
     weight = jnp.zeros((1, LANES), F32)
     walker = [jnp.zeros((rows, orbitals), F32)] * keep
     line = [jnp.zeros((2 * chunks, LANES), F32)] * keep
-    for s, ref in enumerate(ins):
+    for s, ref in zip(order, ins):
         tail = read_tail(ref, orbitals, cap * each + 3)
         weight = weight + (tail[cap * each : cap * each + 1] + tail[cap * each + 1 : cap * each + 2] + tail[cap * each + 2 :])
         for k in range(cap):
@@ -137,12 +140,29 @@
         out[chunks * slab :, :] = jnp.concatenate(tail, axis=0).astype(BF16)
 
 
+def power(size):
+    return size & (size - 1) == 0
+
+
+def moved(me, s, size, sign):
+    if power(size):
+        return me ^ s if isinstance(me, int) else lax.bitwise_xor(me, jnp.int32(s))
+    at = me + (s if sign > 0 else size - s)
+    return at % size if isinstance(me, int) else lax.rem(at, size)
+
+
 def hops(n):
-    return [(s, e) for s in range(n // 2) for e in range(2)]
+    chips = n // 2
+    far = list(range(chips // 2, chips)) + list(range(1, chips // 2))
+    return [(0, 0)] + [(s, e) for s in far for e in range(2)] + [(0, 1)]
+
+
+def arrivals(n):
+    return hops(n)[:1] + hops(n)[:0:-1]
 
 
 def partner(blk, s, e, n, sign):
-    chip = lax.rem(lax.div(blk, 2) + (s if sign > 0 else n // 2 - s), n // 2)
+    chip = moved(lax.div(blk, 2), s, n // 2, sign)
     core = lax.rem(blk, 2)
     return 2 * chip + (core if e == 0 else 1 - core)
 
@@ -159,7 +179,7 @@
     for ref in ins:
         exponent = exponent + ref[chunks * slab :, :].astype(F32)
     growth = jnp.exp(exponent[0 : half * chunks] + exponent[half * chunks :])
-    for ref, (s, e) in zip(ins, hops(n)):
+    for ref, (s, e) in zip(ins, arrivals(n)):
         source = partner(blk, s, e, n, -1)
         for w in range(half):
             for c in range(chunks):
@@ -209,15 +229,16 @@
     rows = slab // half
     halves = []
     for e in range(2):
-        total = ins[e][...].astype(F32)
-        for ref in ins[e + 2 :: 2]:
+        same = [ref for ref, (_, other) in zip(ins, hops(n)) if other == e]
+        total = same[0][...].astype(F32)
+        for ref in same[1:]:
             total = total + ref[...].astype(F32)
         halves.append(total)
     first = core_ref[0] == 0
     whole = [jnp.where(first, halves[0], halves[1]), jnp.where(first, halves[1], halves[0])]
     walker = [whole[m // half][(m % half) * rows : (m % half + 1) * rows] for m in range(keep)]
     for s, out in enumerate(outs):
-        source = (groups - s) % groups
+        source = s if power(groups) else (groups - s) % groups
         for k in range(cap):
             value = jnp.zeros((rows, orbitals), F32)
             for m in range(k, keep, cap):
@@ -226,12 +247,13 @@
             out[k * rows : (k + 1) * rows, :] = value.astype(BF16)
 
 
-def deal_kernel(keep, cap, groups, me_ref, target_ref, weights_ref, total_ref, *refs):
+def deal_kernel(order, keep, cap, me_ref, target_ref, weights_ref, total_ref, *refs):
+    groups = len(order)
     ins, (out_ref, blocks, wide) = refs[:groups], refs[groups:]
     rows, slots, orbitals = out_ref.shape
     live = groups * keep
-    for s, ref in enumerate(ins):
-        base = lax.rem(me_ref[0] + groups - s, groups) * cap
+    for s, ref in zip(order, ins):
+        base = moved(me_ref[0], s, groups, -1) * cap
         for k in range(cap):
             blocks[base + k] = ref[k * rows : (k + 1) * rows, :].astype(F32)
     blocks[groups * cap] = jnp.zeros((rows, orbitals), F32)
@@ -245,7 +267,7 @@
     out_ref[...] = wide[...].astype(BF16)
 
 
-def call(kernel, outs, scalars, held, arrays, scratch, name, flops=0, vmem=40):
+def call(kernel, outs, scalars, held, arrays, scratch, name, flops=0, vmem=VMEM):
     smem = pl.BlockSpec(memory_space=pltpu.SMEM)
     full = pl.BlockSpec(memory_space=pltpu.VMEM)
     size = sum(x.size * x.dtype.itemsize for x in list(arrays) + list(outs))
@@ -275,13 +297,14 @@
     core = lax.rem(blk, 2)
 
     def to_list(x, s):
-        return lax.ppermute(x, "grp", [(i, (i + s) % groups) for i in range(groups)]) if s else x
+        return lax.ppermute(x, "grp", [(i, moved(i, s, groups, 1)) for i in range(groups)]) if s else x
 
     def to_block(x, s, e):
         if not s and not e:
             return x
-        return lax.ppermute(x, "blk", [(i, (2 * (i // 2 + s) + (i % 2 ^ e)) % n) for i in range(n)])
-
+        return lax.ppermute(x, "blk", [(i, 2 * moved(i // 2, s, n // 2, 1) + (i % 2 ^ e)) for i in range(n)])
+
+    order = [0] + sorted(range(1, groups), key=lambda s: -bin(s).count("1"))
     chunks = orbitals // LANES
     sibling = to_block(chol, 0, 1)
     width = orbitals + tail_blocks(cap * (2 * chunks + 1) + 3, cap * rows) * LANES
@@ -304,30 +327,48 @@
             pltpu.SemaphoreType.DMA((5,)),
         ],
         "route",
-        vmem=56,
-    )
-    routed = [to_list(x, s) for s, x in enumerate(routed)]
+        vmem=ROUTE_VMEM,
+    )
+    (kept,) = call(
+        stage_kernel,
+        [shape(routed[0].shape, BF16)],
+        [],
+        [routed[0]],
+        [],
+        [pltpu.SemaphoreType.DMA((1,))],
+        "keep",
+    )
+    (own,) = call(
+        stage_kernel,
+        [shape(chol.shape, chol.dtype)],
+        [],
+        [chol, kept],
+        [],
+        [pltpu.SemaphoreType.DMA((1,))],
+        "stage",
+        vmem=STAGE_VMEM,
+    )
+    routed = [to_list(routed[s], s) if s else kept for s in order]
     payload = shape((chunks * slab + 2 * half * chunks, LANES), BF16)
     same, other, weight_sum, pick = call(
-        functools.partial(merge_kernel, keep, cap, groups, orbitals),
+        functools.partial(merge_kernel, order, keep, cap, orbitals),
         [payload, payload, shape((8, LANES), F32), shape((groups * keep, LANES), F32)],
         [core],
-        [],
+        [own],
         routed,
         [],
         "merge",
     )
-    own, held_body = call(
+    (held_body,) = call(
         stage_kernel,
-        [shape(x.shape, x.dtype) for x in (chol, one_body)],
-        [],
-        [chol, one_body, weight_sum],
-        [],
-        [pltpu.SemaphoreType.DMA((2,))],
-        "stage",
-        vmem=48,
-    )
-    gathered = [to_block(other if e else same, s, e) for s, e in hops(n)]
+        [shape(one_body.shape, one_body.dtype)],
+        [],
+        [one_body, weight_sum],
+        [],
+        [pltpu.SemaphoreType.DMA((1,))],
+        "hold",
+    )
+    gathered = [to_block(other if e else same, s, e) for s, e in arrivals(n)]
     held = F32 if rows % 16 else BF16
     parts = call(
         functools.partial(fock_kernel, n, half),
@@ -354,9 +395,9 @@
         [],
         "sum",
     )
-    back = [to_list(x, s) for s, x in enumerate(back)]
+    back = [to_list(back[s], s) for s in order]
     (out,) = call(
-        functools.partial(deal_kernel, keep, cap, groups),
+        functools.partial(deal_kernel, order, keep, cap),
         [shape(walkers.shape, BF16)],
         [grp, target, weights],
         [],

time: 50.8 us -> 49 us (0.965)
  starting transfers between devices: 27.8 us -> 25.7 us
  Pallas kernels: 8.92 us -> 7.71 us
  waiting for transfers between devices: 11.6 us -> 12.7 us
    ppermute x21, starting transfers between devices: 27.8 us -> 25.7 us  [the longest x15 18 us: to_block(): lax.ppermute(x, 'blk', [(i, 2 * moved(i // 2, s, n // 2, 1) + (i % 2 ^ e)...]
    pallas_call x6 -> x8, Pallas kernels: 8.92 us -> 7.71 us  [call(): pl.pallas_call(kernel, out_shape=outs, in_specs=[smem] * len(scalars) + [...]
    ppermute x21, waiting for transfers between devices: 11.6 us -> 12.7 us  [the longest x15 8.04 us: to_block(): lax.ppermute(x, 'blk', [(i, 2 * moved(i // 2, s, n // 2, 1) + (i % 2 ^ e)...]
    unnamed x8 -> x10, local copies, waits for them, and re-layouts: 2.1 us -> 2.5 us
  transfers between devices with their start and end apart: 21 -> 21, of which waited for: 13 -> 14; matrix products, arithmetic and copies ran while one was open for 0% -> 0% of each run, Pallas kernels for 7% -> 5%
where the time goes in v9:
time: 49 us; the launch traced here: 48.8 us
  starting transfers between devices  25.7 us (52%)
  waiting for transfers between devices  12.7 us (26%)
  Pallas kernels  7.71 us (16%)
  local copies, waits for them, and re-layouts  2.5 us (5%)
    ppermute x15, starting transfers between devices, to_block(): lax.ppermute(x, 'blk', [(i, 2 * moved(i // 2, s, n // 2, 1) + (i % 2 ^ e)...  18 us
    ppermute x15, waiting for transfers between devices, to_block(): lax.ppermute(x, 'blk', [(i, 2 * moved(i // 2, s, n // 2, 1) + (i % 2 ^ e)...  8.04 us
    pallas_call x8, Pallas kernels, call(): pl.pallas_call(kernel, out_shape=outs, in_specs=[smem] * len(scalars) + [...  7.71 us
    ppermute x6, starting transfers between devices, to_list(): lax.ppermute(x, 'grp', [(i, moved(i, s, groups, 1)) for i in range(groups)])  7.71 us
    ppermute x6, waiting for transfers between devices, to_list(): lax.ppermute(x, 'grp', [(i, moved(i, s, groups, 1)) for i in range(groups)])  4.71 us
    unnamed x10, local copies, waits for them, and re-layouts  2.5 us
  transfers between devices with their start and end apart: 21, of which 14 were waited for; matrix products, arithmetic and copies ran while one was open for 0% of the time, Pallas kernels for 5%

profile of v9, /device:TPU:0, one launch (start us, length us, event | category | flops | bytes accessed | tf_op | source)
XLA Modules:
  0.0 48.8 jit_solution(15459712036888902619)
XLA Ops:
  0.0 0.5 collective-permute-start.3
  0.5 1.9 %route.1 = (bf16[32,896]{1,0:T(8,128)(2,1)}, bf16[32,896]{1,0:T(8,128)(2,1)}, bf16[32,896]{1,0:T(8,128)(2,1)}, bf16[32,896]{1,0:T(8,128)(2,1)}) custom-call(s32[1]{0:T(128)} %bitcast.me_ref, s32[8]{0:T(128)} %target_ref.1, f32[8]{0:T(128)} %weights_ref.1, bf16[16,8,768]{2,1,0:T(8,128)(2,1)} %walkers_any.1, f32[8,12]{1,0:T(8,128)} %fields_any.1, ...), custom_call_target="tpu_custom_call" | custom-call | bytes 229376 | tf_op jit(solution)/shard_map/route/pallas_call | solution.py:274
  2.4 3.5 %collective-permute-start = (bf16[32,896]{1,0:T(8,128)(2,1)}, bf16[32,896]{1,0:T(8,128)(2,1)S(1)}, u32[]{:S(2)}, u32[]{:S(2)}) collective-permute-start(bf16[32,896]{1,0:T(8,128)(2,1)} %get-tuple-element.26), channel_id=1, source_target_pairs={{0,24},{8,16},{16,8},{24,0},{1,25},{9,17},{17,9},{25,1},{2,26},{10... | collective-permute-start | bytes 172040 | tf_op jit(solution)/shard_map/ppermute | solution.py:300
  5.9 0.5 %collective-permute-start.1 = (bf16[32,896]{1,0:T(8,128)(2,1)}, bf16[32,896]{1,0:T(8,128)(2,1)S(1)}, u32[]{:S(2)}, u32[]{:S(2)}) collective-permute-start(bf16[32,896]{1,0:T(8,128)(2,1)} %get-tuple-element.27), channel_id=1, source_target_pairs={{0,8},{8,0},{16,24},{24,16},{1,9},{9,1},{17,25},{25,17},{2,10},{10... | collective-permute-start | bytes 172040 | tf_op jit(solution)/shard_map/ppermute | solution.py:300
  6.4 0.1 collective-permute-start.2
  6.5 0.8 %copy-done.2 = bf16[32,896]{1,0:T(8,128)(2,1)S(1)} copy-done((bf16[32,896]{1,0:T(8,128)(2,1)S(1)}, bf16[32,896]{1,0:T(8,128)(2,1)}, u32[]{:S(2)}) %copy-start.2) | copy-done | bytes 57368
  7.4 0.0 copy-start
  7.4 1.7 %copy-done = bf16[12,128,768]{2,1,0:T(8,128)(2,1)S(1)} copy-done((bf16[12,128,768]{2,1,0:T(8,128)(2,1)S(1)}, bf16[12,128,768]{2,1,0:T(8,128)(2,1)}, u32[]{:S(2)}) %copy-start) | copy-done | bytes 2359320
  9.1 0.2 stage.1.when.own_ref
  9.2 0.0 copy-start.1
  9.3 0.0 collective-permute-done.refs_1_
  9.3 1.0 %collective-permute-done.1.refs_2_ = bf16[32,896]{1,0:T(8,128)(2,1)S(1)} collective-permute-done((bf16[32,896]{1,0:T(8,128)(2,1)}, bf16[32,896]{1,0:T(8,128)(2,1)S(1)}, u32[]{:S(2)}, u32[]{:S(2)}) %collective-permute-start.1) | collective-permute-done | bytes 57376 | tf_op jit(solution)/shard_map/ppermute | solution.py:300
  10.3 0.5 %collective-permute-done.2.refs_3_ = bf16[32,896]{1,0:T(8,128)(2,1)S(1)} collective-permute-done((bf16[32,896]{1,0:T(8,128)(2,1)}, bf16[32,896]{1,0:T(8,128)(2,1)S(1)}, u32[]{:S(2)}, u32[]{:S(2)}) %collective-permute-start.2) | collective-permute-done | bytes 57376 | tf_op jit(solution)/shard_map/ppermute | solution.py:300
  10.8 0.1 merge.1
  10.9 2.7 %collective-permute-start.10 = (bf16[216,128]{1,0:T(8,128)(2,1)S(1)}, bf16[216,128]{1,0:T(8,128)(2,1)S(1)}, u32[]{:S(2)}, u32[]{:S(2)}) collective-permute-start(bf16[216,128]{1,0:T(8,128)(2,1)S(1)} %get-tuple-element.31.refs_0_), channel_id=1, source_target_pairs={{0,4},{1,5},{2,6},{3,7},{4,0},{5,1},{6,2},{7,3},{8,12},{9,13},{10,... | collective-permute-start | bytes 165896 | tf_op jit(solution)/shard_map/ppermute | solution.py:305
  13.5 1.3 %collective-permute-start.8 = (bf16[216,128]{1,0:T(8,128)(2,1)S(1)}, bf16[216,128]{1,0:T(8,128)(2,1)S(1)}, u32[]{:S(2)}, u32[]{:S(2)}) collective-permute-start(bf16[216,128]{1,0:T(8,128)(2,1)S(1)} %get-tuple-element.31.refs_0_), channel_id=1, source_target_pairs={{0,6},{1,7},{2,4},{3,5},{4,2},{5,3},{6,0},{7,1},{8,14},{9,15},{10,... | collective-permute-start | bytes 165896 | tf_op jit(solution)/shard_map/ppermute | solution.py:305
  14.9 0.2 collective-permute-start.6
  15.1 0.7 %collective-permute-start.9 = (bf16[216,128]{1,0:T(8,128)(2,1)S(1)}, bf16[216,128]{1,0:T(8,128)(2,1)S(1)}, u32[]{:S(2)}, u32[]{:S(2)}) collective-permute-start(bf16[216,128]{1,0:T(8,128)(2,1)S(1)} %get-tuple-element.32), channel_id=1, source_target_pairs={{0,5},{1,4},{2,7},{3,6},{4,1},{5,0},{6,3},{7,2},{8,13},{9,12},{10,... | collective-permute-start | bytes 165896 | tf_op jit(solution)/shard_map/ppermute | solution.py:305
  15.8 0.3 collective-permute-done.10.refs_7_
  16.1 2.9 %collective-permute-start.7 = (bf16[216,128]{1,0:T(8,128)(2,1)S(1)}, bf16[216,128]{1,0:T(8,128)(2,1)S(1)}, u32[]{:S(2)}, u32[]{:S(2)}) collective-permute-start(bf16[216,128]{1,0:T(8,128)(2,1)S(1)} %get-tuple-element.32), channel_id=1, source_target_pairs={{0,7},{1,6},{2,5},{3,4},{4,3},{5,2},{6,1},{7,0},{8,15},{9,14},{10,... | collective-permute-start | bytes 165896 | tf_op jit(solution)/shard_map/ppermute | solution.py:305
  19.0 0.6 %collective-permute-done.8.refs_5_ = bf16[216,128]{1,0:T(8,128)(2,1)S(1)} collective-permute-done((bf16[216,128]{1,0:T(8,128)(2,1)S(1)}, bf16[216,128]{1,0:T(8,128)(2,1)S(1)}, u32[]{:S(2)}, u32[]{:S(2)}) %collective-permute-start.8) | collective-permute-done | bytes 55328 | tf_op jit(solution)/shard_map/ppermute | solution.py:305
  19.6 0.0 collective-permute-start.5
  19.6 0.7 %collective-permute-done.6.refs_3_ = bf16[216,128]{1,0:T(8,128)(2,1)S(1)} collective-permute-done((bf16[216,128]{1,0:T(8,128)(2,1)S(1)}, bf16[216,128]{1,0:T(8,128)(2,1)S(1)}, u32[]{:S(2)}, u32[]{:S(2)}) %collective-permute-start.6) | collective-permute-done | bytes 55328 | tf_op jit(solution)/shard_map/ppermute | solution.py:305
  20.4 1.0 %collective-permute-start.4 = (bf16[216,128]{1,0:T(8,128)(2,1)S(1)}, bf16[216,128]{1,0:T(8,128)(2,1)S(1)}, u32[]{:S(2)}, u32[]{:S(2)}) collective-permute-start(bf16[216,128]{1,0:T(8,128)(2,1)S(1)} %get-tuple-element.32), channel_id=1, source_target_pairs={{0,1},{1,0},{2,3},{3,2},{4,5},{5,4},{6,7},{7,6},{8,9},{9,8},{10,11... | collective-permute-start | bytes 165896 | tf_op jit(solution)/shard_map/ppermute | solution.py:305
  21.4 0.2 hold.1.body_ref
  21.6 0.0 copy-start.3
  21.7 0.0 copy-start.4
  21.7 0.8 %collective-permute-done.9.refs_6_ = bf16[216,128]{1,0:T(8,128)(2,1)S(1)} collective-permute-done((bf16[216,128]{1,0:T(8,128)(2,1)S(1)}, bf16[216,128]{1,0:T(8,128)(2,1)S(1)}, u32[]{:S(2)}, u32[]{:S(2)}) %collective-permute-start.9) | collective-permute-done | bytes 55328 | tf_op jit(solution)/shard_map/ppermute | solution.py:305
  22.5 1.4 %collective-permute-done.5.refs_2_ = bf16[216,128]{1,0:T(8,128)(2,1)S(1)} collective-permute-done((bf16[216,128]{1,0:T(8,128)(2,1)S(1)}, bf16[216,128]{1,0:T(8,128)(2,1)S(1)}, u32[]{:S(2)}, u32[]{:S(2)}) %collective-permute-start.5) | collective-permute-done | bytes 55328 | tf_op jit(solution)/shard_map/ppermute | solution.py:305
  23.8 3.7 %fock.1 = (bf16[32,768]{1,0:T(8,128)(2,1)S(1)}, bf16[32,768]{1,0:T(8,128)(2,1)S(1)}, bf16[32,768]{1,0:T(8,128)(2,1)S(1)}, bf16[32,768]{1,0:T(8,128)(2,1)S(1)}, b...) custom-call(s32[1]{0:T(128)} %bitcast.1.blk_ref, ...), custom_call_target="tpu_custom_call" | custom-call | flops 2717908992 | bytes 6733824 | tf_op jit(solution)/shard_map/fock/pallas_call | solution.py:274
  27.6 1.6 %collective-permute-start.11 = (bf16[32,768]{1,0:T(8,128)(2,1)S(1)}, bf16[32,768]{1,0:T(8,128)(2,1)S(1)}, u32[]{:S(2)}, u32[]{:S(2)}) collective-permute-start(bf16[32,768]{1,0:T(8,128)(2,1)S(1)} %get-tuple-element.34), channel_id=1, source_target_pairs={{0,4},{1,5},{2,6},{3,7},{4,0},{5,1},{6,2},{7,3},{8,12},{9,13},{10,... | collective-permute-start | bytes 147464 | tf_op jit(solution)/shard_map/ppermute | solution.py:305
  29.2 1.8 %collective-permute-start.12 = (bf16[32,768]{1,0:T(8,128)(2,1)S(1)}, bf16[32,768]{1,0:T(8,128)(2,1)S(1)}, u32[]{:S(2)}, u32[]{:S(2)}) collective-permute-start(bf16[32,768]{1,0:T(8,128)(2,1)S(1)} %get-tuple-element.35), channel_id=1, source_target_pairs={{0,5},{1,4},{2,7},{3,6},{4,1},{5,0},{6,3},{7,2},{8,13},{9,12},{10,... | collective-permute-start | bytes 147464 | tf_op jit(solution)/shard_map/ppermute | solution.py:305
  31.0 1.9 %collective-permute-start.13 = (bf16[32,768]{1,0:T(8,128)(2,1)S(1)}, bf16[32,768]{1,0:T(8,128)(2,1)S(1)}, u32[]{:S(2)}, u32[]{:S(2)}) collective-permute-start(bf16[32,768]{1,0:T(8,128)(2,1)S(1)} %get-tuple-element.36), channel_id=1, source_target_pairs={{0,6},{1,7},{2,4},{3,5},{4,2},{5,3},{6,0},{7,1},{8,14},{9,15},{10,... | collective-permute-start | bytes 147464 | tf_op jit(solution)/shard_map/ppermute | solution.py:305
  32.9 0.9 %collective-permute-start.14 = (bf16[32,768]{1,0:T(8,128)(2,1)S(1)}, bf16[32,768]{1,0:T(8,128)(2,1)S(1)}, u32[]{:S(2)}, u32[]{:S(2)}) collective-permute-start(bf16[32,768]{1,0:T(8,128)(2,1)S(1)} %get-tuple-element.37), channel_id=1, source_target_pairs={{0,7},{1,6},{2,5},{3,4},{4,3},{5,2},{6,1},{7,0},{8,15},{9,14},{10,... | collective-permute-start | bytes 147464 | tf_op jit(solution)/shard_map/ppermute | solution.py:305
  33.8 2.4 %collective-permute-start.16 = (bf16[32,768]{1,0:T(8,128)(2,1)S(1)}, bf16[32,768]{1,0:T(8,128)(2,1)S(1)}, u32[]{:S(2)}, u32[]{:S(2)}) collective-permute-start(bf16[32,768]{1,0:T(8,128)(2,1)S(1)} %get-tuple-element.39), channel_id=1, source_target_pairs={{0,3},{1,2},{2,1},{3,0},{4,7},{5,6},{6,5},{7,4},{8,11},{9,10},{10,... | collective-permute-start | bytes 147464 | tf_op jit(solution)/shard_map/ppermute | solution.py:305
  36.3 0.7 %collective-permute-done.12.refs_2_ = bf16[32,768]{1,0:T(8,128)(2,1)S(1)} collective-permute-done((bf16[32,768]{1,0:T(8,128)(2,1)S(1)}, bf16[32,768]{1,0:T(8,128)(2,1)S(1)}, u32[]{:S(2)}, u32[]{:S(2)}) %collective-permute-start.12) | collective-permute-done | bytes 49184 | tf_op jit(solution)/shard_map/ppermute | solution.py:305
  37.0 0.1 collective-permute-start.17
  37.1 1.3 %collective-permute-done.14.refs_4_ = bf16[32,768]{1,0:T(8,128)(2,1)S(1)} collective-permute-done((bf16[32,768]{1,0:T(8,128)(2,1)S(1)}, bf16[32,768]{1,0:T(8,128)(2,1)S(1)}, u32[]{:S(2)}, u32[]{:S(2)}) %collective-permute-start.14) | collective-permute-done | bytes 49184 | tf_op jit(solution)/shard_map/ppermute | solution.py:305
  38.4 1.0 %collective-permute-done.15.refs_5_ = bf16[32,768]{1,0:T(8,128)(2,1)S(1)} collective-permute-done((bf16[32,768]{1,0:T(8,128)(2,1)S(1)}, bf16[32,768]{1,0:T(8,128)(2,1)S(1)}, u32[]{:S(2)}, u32[]{:S(2)}) %collective-permute-start.15) | collective-permute-done | bytes 49184 | tf_op jit(solution)/shard_map/ppermute | solution.py:305
  39.4 1.2 %collective-permute-done.16.refs_6_ = bf16[32,768]{1,0:T(8,128)(2,1)S(1)} collective-permute-done((bf16[32,768]{1,0:T(8,128)(2,1)S(1)}, bf16[32,768]{1,0:T(8,128)(2,1)S(1)}, u32[]{:S(2)}, u32[]{:S(2)}) %collective-permute-start.16) | collective-permute-done | bytes 49184 | tf_op jit(solution)/shard_map/ppermute | solution.py:305
  40.5 0.1 sum.1
  40.6 2.1 %collective-permute-start.18 = (bf16[32,768]{1,0:T(8,128)(2,1)S(1)}, bf16[32,768]{1,0:T(8,128)(2,1)S(1)}, u32[]{:S(2)}, u32[]{:S(2)}) collective-permute-start(bf16[32,768]{1,0:T(8,128)(2,1)S(1)} %get-tuple-element.42), channel_id=1, source_target_pairs={{0,24},{8,16},{16,8},{24,0},{1,25},{9,17},{17,9},{25,1},{2,26},{10... | collective-permute-start | bytes 147464 | tf_op jit(solution)/shard_map/ppermute | solution.py:300
  42.7 0.6 %collective-permute-start.19 = (bf16[32,768]{1,0:T(8,128)(2,1)S(1)}, bf16[32,768]{1,0:T(8,128)(2,1)S(1)}, u32[]{:S(2)}, u32[]{:S(2)}) collective-permute-start(bf16[32,768]{1,0:T(8,128)(2,1)S(1)} %get-tuple-element.43), channel_id=1, source_target_pairs={{0,8},{8,0},{16,24},{24,16},{1,9},{9,1},{17,25},{25,17},{2,10},{10... | collective-permute-start | bytes 147464 | tf_op jit(solution)/shard_map/ppermute | solution.py:300
  43.3 0.9 %collective-permute-start.20 = (bf16[32,768]{1,0:T(8,128)(2,1)S(1)}, bf16[32,768]{1,0:T(8,128)(2,1)S(1)}, u32[]{:S(2)}, u32[]{:S(2)}) collective-permute-start(bf16[32,768]{1,0:T(8,128)(2,1)S(1)} %get-tuple-element.44), channel_id=1, source_target_pairs={{0,16},{8,24},{16,0},{24,8},{1,17},{9,25},{17,1},{25,9},{2,18},{10... | collective-permute-start | bytes 147464 | tf_op jit(solution)/shard_map/ppermute | solution.py:300
  44.2 1.8 %collective-permute-done.18.refs_1_ = bf16[32,768]{1,0:T(8,128)(2,1)S(1)} collective-permute-done((bf16[32,768]{1,0:T(8,128)(2,1)S(1)}, bf16[32,768]{1,0:T(8,128)(2,1)S(1)}, u32[]{:S(2)}, u32[]{:S(2)}) %collective-permute-start.18) | collective-permute-done | bytes 49184 | tf_op jit(solution)/shard_map/ppermute | solution.py:300
  46.0 0.8 %collective-permute-done.19.refs_2_ = bf16[32,768]{1,0:T(8,128)(2,1)S(1)} collective-permute-done((bf16[32,768]{1,0:T(8,128)(2,1)S(1)}, bf16[32,768]{1,0:T(8,128)(2,1)S(1)}, u32[]{:S(2)}, u32[]{:S(2)}) %collective-permute-start.19) | collective-permute-done | bytes 49184 | tf_op jit(solution)/shard_map/ppermute | solution.py:300
  46.8 0.6 %collective-permute-done.20.refs_3_ = bf16[32,768]{1,0:T(8,128)(2,1)S(1)} collective-permute-done((bf16[32,768]{1,0:T(8,128)(2,1)S(1)}, bf16[32,768]{1,0:T(8,128)(2,1)S(1)}, u32[]{:S(2)}, u32[]{:S(2)}) %collective-permute-start.20) | collective-permute-done | bytes 49184 | tf_op jit(solution)/shard_map/ppermute | solution.py:300
  47.4 1.4 %deal.1 = bf16[16,8,768]{2,1,0:T(8,128)(2,1)} custom-call(s32[1]{0:T(128)} %bitcast.me_ref, s32[8]{0:T(128)S(1)} %copy-done.3, f32[8]{0:T(128)S(1)} %copy-done.4, f32[8,128]{1,0:T(8,128)S(1)} %get-tuple-element.29.refs_1_.total_ref, bf16[32,768]{1,0:T(8,128)(2,1)S(1)} %get-tuple-element.41.refs_0_, bf16[32,768]{1,0:T(8,128)(2,1)S(1)} %collective-permute-done.18.refs_1_, ...), custom_call_target="tpu_custom_call" | custom-call | bytes 397312 | tf_op jit(solution)/shard_map/deal/pallas_call | solution.py:274
  (12 shorter events, 0.1 us)
Async XLA Ops:
  0.0 23.8 %collective-permute-start.3 = (bf16[12,128,768]{2,1,0:T(8,128)(2,1)}, bf16[12,128,768]{2,1,0:T(8,128)(2,1)S(1)}, u32[]{:S(2)}, u32[]{:S(2)}) collective-permute-start(bf16[12,128,768]{2,1,0:T(8,128)(2,1)} %refs_0_.2), channel_id=1, source_target_pairs={{0,1},{1,0},{2,3},{3,2},{4,5},{5,4},{6,7},{7,6},{8,9},{9,8},{10,11... | collective-permute-start | bytes 7077896 | tf_op jit(solution)/shard_map/ppermute | solution.py:305
  2.4 6.9 %collective-permute-start = (bf16[32,896]{1,0:T(8,128)(2,1)}, bf16[32,896]{1,0:T(8,128)(2,1)S(1)}, u32[]{:S(2)}, u32[]{:S(2)}) collective-permute-start(bf16[32,896]{1,0:T(8,128)(2,1)} %get-tuple-element.26), channel_id=1, source_target_pairs={{0,24},{8,16},{16,8},{24,0},{1,25},{9,17},{17,9},{25,1},{2,26},{10... | collective-permute-start | bytes 172040 | tf_op jit(solution)/shard_map/ppermute | solution.py:300
  5.9 4.4 %collective-permute-start.1 = (bf16[32,896]{1,0:T(8,128)(2,1)}, bf16[32,896]{1,0:T(8,128)(2,1)S(1)}, u32[]{:S(2)}, u32[]{:S(2)}) collective-permute-start(bf16[32,896]{1,0:T(8,128)(2,1)} %get-tuple-element.27), channel_id=1, source_target_pairs={{0,8},{8,0},{16,24},{24,16},{1,9},{9,1},{17,25},{25,17},{2,10},{10... | collective-permute-start | bytes 172040 | tf_op jit(solution)/shard_map/ppermute | solution.py:300
  6.4 4.4 %collective-permute-start.2 = (bf16[32,896]{1,0:T(8,128)(2,1)}, bf16[32,896]{1,0:T(8,128)(2,1)S(1)}, u32[]{:S(2)}, u32[]{:S(2)}) collective-permute-start(bf16[32,896]{1,0:T(8,128)(2,1)} %get-tuple-element.28), channel_id=1, source_target_pairs={{0,16},{8,24},{16,0},{24,8},{1,17},{9,25},{17,1},{25,9},{2,18},{10... | collective-permute-start | bytes 172040 | tf_op jit(solution)/shard_map/ppermute | solution.py:300
  6.5 0.8 %copy-start.2 = (bf16[32,896]{1,0:T(8,128)(2,1)S(1)}, bf16[32,896]{1,0:T(8,128)(2,1)}, u32[]{:S(2)}) copy-start(bf16[32,896]{1,0:T(8,128)(2,1)} %get-tuple-element.25.refs_0_) | copy-start | bytes 172036
  7.4 1.7 %copy-start = (bf16[12,128,768]{2,1,0:T(8,128)(2,1)S(1)}, bf16[12,128,768]{2,1,0:T(8,128)(2,1)}, u32[]{:S(2)}) copy-start(bf16[12,128,768]{2,1,0:T(8,128)(2,1)} %refs_0_.2) | copy-start | bytes 7077892
  9.2 12.2 %copy-start.1 = (bf16[768,768]{1,0:T(8,128)(2,1)S(1)}, bf16[768,768]{1,0:T(8,128)(2,1)}, u32[]{:S(2)}) copy-start(bf16[768,768]{1,0:T(8,128)(2,1)} %refs_0_.3) | copy-start | bytes 3538948
  10.9 5.2 %collective-permute-start.10 = (bf16[216,128]{1,0:T(8,128)(2,1)S(1)}, bf16[216,128]{1,0:T(8,128)(2,1)S(1)}, u32[]{:S(2)}, u32[]{:S(2)}) collective-permute-start(bf16[216,128]{1,0:T(8,128)(2,1)S(1)} %get-tuple-element.31.refs_0_), channel_id=1, source_target_pairs={{0,4},{1,5},{2,6},{3,7},{4,0},{5,1},{6,2},{7,3},{8,12},{9,13},{10,... | collective-permute-start | bytes 165896 | tf_op jit(solution)/shard_map/ppermute | solution.py:305
  13.5 6.1 %collective-permute-start.8 = (bf16[216,128]{1,0:T(8,128)(2,1)S(1)}, bf16[216,128]{1,0:T(8,128)(2,1)S(1)}, u32[]{:S(2)}, u32[]{:S(2)}) collective-permute-start(bf16[216,128]{1,0:T(8,128)(2,1)S(1)} %get-tuple-element.31.refs_0_), channel_id=1, source_target_pairs={{0,6},{1,7},{2,4},{3,5},{4,2},{5,3},{6,0},{7,1},{8,14},{9,15},{10,... | collective-permute-start | bytes 165896 | tf_op jit(solution)/shard_map/ppermute | solution.py:305
  14.9 5.5 %collective-permute-start.6 = (bf16[216,128]{1,0:T(8,128)(2,1)S(1)}, bf16[216,128]{1,0:T(8,128)(2,1)S(1)}, u32[]{:S(2)}, u32[]{:S(2)}) collective-permute-start(bf16[216,128]{1,0:T(8,128)(2,1)S(1)} %get-tuple-element.31.refs_0_), channel_id=1, source_target_pairs={{0,2},{1,3},{2,0},{3,1},{4,6},{5,7},{6,4},{7,5},{8,10},{9,11},{10,... | collective-permute-start | bytes 165896 | tf_op jit(solution)/shard_map/ppermute | solution.py:305
  15.1 7.3 %collective-permute-start.9 = (bf16[216,128]{1,0:T(8,128)(2,1)S(1)}, bf16[216,128]{1,0:T(8,128)(2,1)S(1)}, u32[]{:S(2)}, u32[]{:S(2)}) collective-permute-start(bf16[216,128]{1,0:T(8,128)(2,1)S(1)} %get-tuple-element.32), channel_id=1, source_target_pairs={{0,5},{1,4},{2,7},{3,6},{4,1},{5,0},{6,3},{7,2},{8,13},{9,12},{10,... | collective-permute-start | bytes 165896 | tf_op jit(solution)/shard_map/ppermute | solution.py:305
  16.1 6.3 %collective-permute-start.7 = (bf16[216,128]{1,0:T(8,128)(2,1)S(1)}, bf16[216,128]{1,0:T(8,128)(2,1)S(1)}, u32[]{:S(2)}, u32[]{:S(2)}) collective-permute-start(bf16[216,128]{1,0:T(8,128)(2,1)S(1)} %get-tuple-element.32), channel_id=1, source_target_pairs={{0,7},{1,6},{2,5},{3,4},{4,3},{5,2},{6,1},{7,0},{8,15},{9,14},{10,... | collective-permute-start | bytes 165896 | tf_op jit(solution)/shard_map/ppermute | solution.py:305
  19.6 4.2 %collective-permute-start.5 = (bf16[216,128]{1,0:T(8,128)(2,1)S(1)}, bf16[216,128]{1,0:T(8,128)(2,1)S(1)}, u32[]{:S(2)}, u32[]{:S(2)}) collective-permute-start(bf16[216,128]{1,0:T(8,128)(2,1)S(1)} %get-tuple-element.32), channel_id=1, source_target_pairs={{0,3},{1,2},{2,1},{3,0},{4,7},{5,6},{6,5},{7,4},{8,11},{9,10},{10,... | collective-permute-start | bytes 165896 | tf_op jit(solution)/shard_map/ppermute | solution.py:305
  20.4 3.4 %collective-permute-start.4 = (bf16[216,128]{1,0:T(8,128)(2,1)S(1)}, bf16[216,128]{1,0:T(8,128)(2,1)S(1)}, u32[]{:S(2)}, u32[]{:S(2)}) collective-permute-start(bf16[216,128]{1,0:T(8,128)(2,1)S(1)} %get-tuple-element.32), channel_id=1, source_target_pairs={{0,1},{1,0},{2,3},{3,2},{4,5},{5,4},{6,7},{7,6},{8,9},{9,8},{10,11... | collective-permute-start | bytes 165896 | tf_op jit(solution)/shard_map/ppermute | solution.py:305
  21.6 25.7 %copy-start.3 = (s32[8]{0:T(128)S(1)}, s32[8]{0:T(128)}, u32[]{:S(2)}) copy-start(s32[8]{0:T(128)} %target_ref.1) | copy-start | bytes 100
  21.7 25.7 %copy-start.4 = (f32[8]{0:T(128)S(1)}, f32[8]{0:T(128)}, u32[]{:S(2)}) copy-start(f32[8]{0:T(128)} %weights_ref.1) | copy-start | bytes 100
  27.6 6.3 %collective-permute-start.11 = (bf16[32,768]{1,0:T(8,128)(2,1)S(1)}, bf16[32,768]{1,0:T(8,128)(2,1)S(1)}, u32[]{:S(2)}, u32[]{:S(2)}) collective-permute-start(bf16[32,768]{1,0:T(8,128)(2,1)S(1)} %get-tuple-element.34), channel_id=1, source_target_pairs={{0,4},{1,5},{2,6},{3,7},{4,0},{5,1},{6,2},{7,3},{8,12},{9,13},{10,... | collective-permute-start | bytes 147464 | tf_op jit(solution)/shard_map/ppermute | solution.py:305
  29.2 7.8 %collective-permute-start.12 = (bf16[32,768]{1,0:T(8,128)(2,1)S(1)}, bf16[32,768]{1,0:T(8,128)(2,1)S(1)}, u32[]{:S(2)}, u32[]{:S(2)}) collective-permute-start(bf16[32,768]{1,0:T(8,128)(2,1)S(1)} %get-tuple-element.35), channel_id=1, source_target_pairs={{0,5},{1,4},{2,7},{3,6},{4,1},{5,0},{6,3},{7,2},{8,13},{9,12},{10,... | collective-permute-start | bytes 147464 | tf_op jit(solution)/shard_map/ppermute | solution.py:305
  31.0 6.1 %collective-permute-start.13 = (bf16[32,768]{1,0:T(8,128)(2,1)S(1)}, bf16[32,768]{1,0:T(8,128)(2,1)S(1)}, u32[]{:S(2)}, u32[]{:S(2)}) collective-permute-start(bf16[32,768]{1,0:T(8,128)(2,1)S(1)} %get-tuple-element.36), channel_id=1, source_target_pairs={{0,6},{1,7},{2,4},{3,5},{4,2},{5,3},{6,0},{7,1},{8,14},{9,15},{10,... | collective-permute-start | bytes 147464 | tf_op jit(solution)/shard_map/ppermute | solution.py:305
  32.9 5.5 %collective-permute-start.14 = (bf16[32,768]{1,0:T(8,128)(2,1)S(1)}, bf16[32,768]{1,0:T(8,128)(2,1)S(1)}, u32[]{:S(2)}, u32[]{:S(2)}) collective-permute-start(bf16[32,768]{1,0:T(8,128)(2,1)S(1)} %get-tuple-element.37), channel_id=1, source_target_pairs={{0,7},{1,6},{2,5},{3,4},{4,3},{5,2},{6,1},{7,0},{8,15},{9,14},{10,... | collective-permute-start | bytes 147464 | tf_op jit(solution)/shard_map/ppermute | solution.py:305
  33.8 5.6 %collective-permute-start.15 = (bf16[32,768]{1,0:T(8,128)(2,1)S(1)}, bf16[32,768]{1,0:T(8,128)(2,1)S(1)}, u32[]{:S(2)}, u32[]{:S(2)}) collective-permute-start(bf16[32,768]{1,0:T(8,128)(2,1)S(1)} %get-tuple-element.38), channel_id=1, source_target_pairs={{0,2},{1,3},{2,0},{3,1},{4,6},{5,7},{6,4},{7,5},{8,10},{9,11},{10,... | collective-permute-start | bytes 147464 | tf_op jit(solution)/shard_map/ppermute | solution.py:305
  33.8 6.7 %collective-permute-start.16 = (bf16[32,768]{1,0:T(8,128)(2,1)S(1)}, bf16[32,768]{1,0:T(8,128)(2,1)S(1)}, u32[]{:S(2)}, u32[]{:S(2)}) collective-permute-start(bf16[32,768]{1,0:T(8,128)(2,1)S(1)} %get-tuple-element.39), channel_id=1, source_target_pairs={{0,3},{1,2},{2,1},{3,0},{4,7},{5,6},{6,5},{7,4},{8,11},{9,10},{10,... | collective-permute-start | bytes 147464 | tf_op jit(solution)/shard_map/ppermute | solution.py:305
  37.0 3.6 %collective-permute-start.17 = (bf16[32,768]{1,0:T(8,128)(2,1)S(1)}, bf16[32,768]{1,0:T(8,128)(2,1)S(1)}, u32[]{:S(2)}, u32[]{:S(2)}) collective-permute-start(bf16[32,768]{1,0:T(8,128)(2,1)S(1)} %get-tuple-element.40), channel_id=1, source_target_pairs={{0,1},{1,0},{2,3},{3,2},{4,5},{5,4},{6,7},{7,6},{8,9},{9,8},{10,11... | collective-permute-start | bytes 147464 | tf_op jit(solution)/shard_map/ppermute | solution.py:305
  40.6 5.4 %collective-permute-start.18 = (bf16[32,768]{1,0:T(8,128)(2,1)S(1)}, bf16[32,768]{1,0:T(8,128)(2,1)S(1)}, u32[]{:S(2)}, u32[]{:S(2)}) collective-permute-start(bf16[32,768]{1,0:T(8,128)(2,1)S(1)} %get-tuple-element.42), channel_id=1, source_target_pairs={{0,24},{8,16},{16,8},{24,0},{1,25},{9,17},{17,9},{25,1},{2,26},{10... | collective-permute-start | bytes 147464 | tf_op jit(solution)/shard_map/ppermute | solution.py:300
  42.7 4.1 %collective-permute-start.19 = (bf16[32,768]{1,0:T(8,128)(2,1)S(1)}, bf16[32,768]{1,0:T(8,128)(2,1)S(1)}, u32[]{:S(2)}, u32[]{:S(2)}) collective-permute-start(bf16[32,768]{1,0:T(8,128)(2,1)S(1)} %get-tuple-element.43), channel_id=1, source_target_pairs={{0,8},{8,0},{16,24},{24,16},{1,9},{9,1},{17,25},{25,17},{2,10},{10... | collective-permute-start | bytes 147464 | tf_op jit(solution)/shard_map/ppermute | solution.py:300
  43.3 4.1 %collective-permute-start.20 = (bf16[32,768]{1,0:T(8,128)(2,1)S(1)}, bf16[32,768]{1,0:T(8,128)(2,1)S(1)}, u32[]{:S(2)}, u32[]{:S(2)}) collective-permute-start(bf16[32,768]{1,0:T(8,128)(2,1)S(1)} %get-tuple-element.44), channel_id=1, source_target_pairs={{0,16},{8,24},{16,0},{24,8},{1,17},{9,25},{17,1},{25,9},{2,18},{10... | collective-permute-start | bytes 147464 | tf_op jit(solution)/shard_map/ppermute | solution.py:300

commit v10 on v9

--- a/solution.py
+++ b/solution.py
@@ -159,6 +159,26 @@
 
 def arrivals(n):
     return hops(n)[:1] + hops(n)[:0:-1]
+
+
+def leading(s, chips):
+    top = 1 << (s.bit_length() - 1) if s else 0
+    return top if power(chips) else s
+
+
+def returns(n):
+    return [(s, e) for s, e in hops(n) if leading(s, n // 2) == s]
+
+
+def add_kernel(count, *refs):
+    outs = refs[len(refs) - 1 - count :]
+    ins = refs[: len(refs) - 1 - count]
+    total = ins[count][...].astype(F32)
+    for ref in ins[count + 1 :]:
+        total = total + ref[...].astype(F32)
+    outs[0][...] = total.astype(BF16)
+    for i in range(count):
+        outs[1 + i][...] = ins[i][...]
 
 
 def partner(blk, s, e, n, sign):
@@ -223,13 +243,14 @@
 
 
 def sum_kernel(n, keep, cap, groups, core_ref, pick_ref, *refs):
-    ins, outs = refs[:n], refs[n:]
+    known = returns(n)
+    ins, outs = refs[: len(known)], refs[len(known) :]
     slab, orbitals = ins[0].shape
     half = keep // 2
     rows = slab // half
     halves = []
     for e in range(2):
-        same = [ref for ref, (_, other) in zip(ins, hops(n)) if other == e]
+        same = [ref for ref, (_, other) in zip(ins, known) if other == e]
         total = same[0][...].astype(F32)
         for ref in same[1:]:
             total = total + ref[...].astype(F32)
@@ -368,7 +389,15 @@
         [pltpu.SemaphoreType.DMA((1,))],
         "hold",
     )
-    gathered = [to_block(other if e else same, s, e) for s, e in arrivals(n)]
+    gathered = {}
+    for s, e in arrivals(n):
+        if leading(s, n // 2) == s:
+            gathered[s, e] = to_block(other if e else same, s, e)
+    for s, e in arrivals(n):
+        top = leading(s, n // 2)
+        if top != s:
+            gathered[s, e] = to_block(gathered[top, e], s ^ top, 0)
+    gathered = [gathered[hop] for hop in arrivals(n)]
     held = F32 if rows % 16 else BF16
     parts = call(
         functools.partial(fock_kernel, n, half),
@@ -385,13 +414,29 @@
         "fock",
         flops=2 * n * slab * orbitals * (orbitals + 4 * vec_count * occupied),
     )
-    parts = [to_block(x, s, e) for x, (s, e) in zip(parts, hops(n))]
+    parts = dict(zip(hops(n), parts))
+    for s, e in returns(n):
+        via = [hop for hop in hops(n) if hop[1] == e and hop[0] != s and leading(hop[0], n // 2) == s]
+        if via:
+            later = [hop for hop in returns(n) if 0 < hop[0] < s and hop[1] == e] + [(0, 1)] * e
+            terms_in = [parts[s, e]] + [to_block(parts[hop], hop[0] ^ s, 0) for hop in via]
+            out = call(
+                functools.partial(add_kernel, len(later)),
+                [shape((slab, orbitals), BF16)] * (1 + len(later)),
+                [],
+                [],
+                [parts[hop] for hop in later] + terms_in,
+                [],
+                "add",
+            )
+            parts.update(zip([(s, e)] + later, out))
+    backs = [to_block(parts[hop], *hop) for hop in returns(n)]
     back = call(
         functools.partial(sum_kernel, n, keep, cap, groups),
         [shape((cap * rows, orbitals), BF16)] * groups,
         [core],
         [],
-        [pick] + parts,
+        [pick] + backs,
         [],
         "sum",
     )

time: 49 us -> 49 us (level)
  waiting for transfers between devices: 12.7 us -> 16.5 us
  starting transfers between devices: 25.7 us -> 22 us
    ppermute x15, starting transfers between devices: 18 us -> 14.2 us  [to_block(): lax.ppermute(x, 'blk', [(i, 2 * moved(i // 2, s, n // 2, 1) + (i % 2 ^ e)...]
    ppermute x15, waiting for transfers between devices: 8.04 us -> 11.2 us  [to_block(): lax.ppermute(x, 'blk', [(i, 2 * moved(i // 2, s, n // 2, 1) + (i % 2 ^ e)...]
    ppermute x6, waiting for transfers between devices: 4.71 us -> 5.2 us  [to_list(): lax.ppermute(x, 'grp', [(i, moved(i, s, groups, 1)) for i in range(groups)])]
    pallas_call x8 -> x10, Pallas kernels: 7.71 us -> 7.74 us  [call(): pl.pallas_call(kernel, out_shape=outs, in_specs=[smem] * len(scalars) + [...]
where the time goes in v10:
time: 49 us; the launch traced here: 48.8 us
  starting transfers between devices  22 us (45%)
  waiting for transfers between devices  16.5 us (34%)
  Pallas kernels  7.74 us (16%)
  local copies, waits for them, and re-layouts  2.5 us (5%)
    ppermute x15, starting transfers between devices, to_block(): lax.ppermute(x, 'blk', [(i, 2 * moved(i // 2, s, n // 2, 1) + (i % 2 ^ e)...  14.2 us
    ppermute x15, waiting for transfers between devices, to_block(): lax.ppermute(x, 'blk', [(i, 2 * moved(i // 2, s, n // 2, 1) + (i % 2 ^ e)...  11.2 us
    pallas_call x10, Pallas kernels, call(): pl.pallas_call(kernel, out_shape=outs, in_specs=[smem] * len(scalars) + [...  7.74 us
    ppermute x6, starting transfers between devices, to_list(): lax.ppermute(x, 'grp', [(i, moved(i, s, groups, 1)) for i in range(groups)])  7.71 us
    ppermute x6, waiting for transfers between devices, to_list(): lax.ppermute(x, 'grp', [(i, moved(i, s, groups, 1)) for i in range(groups)])  5.2 us
    unnamed x10, local copies, waits for them, and re-layouts  2.5 us
  transfers between devices with their start and end apart: 21, of which 14 were waited for; matrix products, arithmetic and copies ran while one was open for 0% of the time, Pallas kernels for 5%

profile of v10, /device:TPU:0, one launch (start us, length us, event | category | flops | bytes accessed | tf_op | source)
XLA Modules:
  0.0 48.8 jit_solution(3452845780185301181)
XLA Ops:
  0.0 0.5 collective-permute-start.3
  0.5 1.9 %route.1 = (bf16[32,896]{1,0:T(8,128)(2,1)}, bf16[32,896]{1,0:T(8,128)(2,1)}, bf16[32,896]{1,0:T(8,128)(2,1)}, bf16[32,896]{1,0:T(8,128)(2,1)}) custom-call(s32[1]{0:T(128)} %bitcast.me_ref, s32[8]{0:T(128)} %target_ref.1, f32[8]{0:T(128)} %weights_ref.1, bf16[16,8,768]{2,1,0:T(8,128)(2,1)} %walkers_any.1, f32[8,12]{1,0:T(8,128)} %fields_any.1, ...), custom_call_target="tpu_custom_call" | custom-call | bytes 229376 | tf_op jit(solution)/shard_map/route/pallas_call | solution.py:295
  2.4 3.5 %collective-permute-start = (bf16[32,896]{1,0:T(8,128)(2,1)}, bf16[32,896]{1,0:T(8,128)(2,1)S(1)}, u32[]{:S(2)}, u32[]{:S(2)}) collective-permute-start(bf16[32,896]{1,0:T(8,128)(2,1)} %get-tuple-element.31), channel_id=1, source_target_pairs={{0,24},{8,16},{16,8},{24,0},{1,25},{9,17},{17,9},{25,1},{2,26},{10... | collective-permute-start | bytes 172040 | tf_op jit(solution)/shard_map/ppermute | solution.py:321
  5.9 0.5 %collective-permute-start.1 = (bf16[32,896]{1,0:T(8,128)(2,1)}, bf16[32,896]{1,0:T(8,128)(2,1)S(1)}, u32[]{:S(2)}, u32[]{:S(2)}) collective-permute-start(bf16[32,896]{1,0:T(8,128)(2,1)} %get-tuple-element.32), channel_id=1, source_target_pairs={{0,8},{8,0},{16,24},{24,16},{1,9},{9,1},{17,25},{25,17},{2,10},{10... | collective-permute-start | bytes 172040 | tf_op jit(solution)/shard_map/ppermute | solution.py:321
  6.4 0.1 collective-permute-start.2
  6.5 0.8 %copy-done.2 = bf16[32,896]{1,0:T(8,128)(2,1)S(1)} copy-done((bf16[32,896]{1,0:T(8,128)(2,1)S(1)}, bf16[32,896]{1,0:T(8,128)(2,1)}, u32[]{:S(2)}) %copy-start.2) | copy-done | bytes 57368
  7.4 0.0 copy-start
  7.4 1.7 %copy-done = bf16[12,128,768]{2,1,0:T(8,128)(2,1)S(1)} copy-done((bf16[12,128,768]{2,1,0:T(8,128)(2,1)S(1)}, bf16[12,128,768]{2,1,0:T(8,128)(2,1)}, u32[]{:S(2)}) %copy-start) | copy-done | bytes 2359320
  9.1 0.2 stage.1.when.own_ref
  9.2 0.0 copy-start.1
  9.3 0.0 collective-permute-done.refs_1_
  9.3 1.0 %collective-permute-done.1.refs_2_ = bf16[32,896]{1,0:T(8,128)(2,1)S(1)} collective-permute-done((bf16[32,896]{1,0:T(8,128)(2,1)}, bf16[32,896]{1,0:T(8,128)(2,1)S(1)}, u32[]{:S(2)}, u32[]{:S(2)}) %collective-permute-start.1) | collective-permute-done | bytes 57376 | tf_op jit(solution)/shard_map/ppermute | solution.py:321
  10.3 0.5 %collective-permute-done.2.refs_3_ = bf16[32,896]{1,0:T(8,128)(2,1)S(1)} collective-permute-done((bf16[32,896]{1,0:T(8,128)(2,1)}, bf16[32,896]{1,0:T(8,128)(2,1)S(1)}, u32[]{:S(2)}, u32[]{:S(2)}) %collective-permute-start.2) | collective-permute-done | bytes 57376 | tf_op jit(solution)/shard_map/ppermute | solution.py:321
  10.8 0.1 merge.1
  10.9 2.7 %collective-permute-start.9 = (bf16[216,128]{1,0:T(8,128)(2,1)S(1)}, bf16[216,128]{1,0:T(8,128)(2,1)S(1)}, u32[]{:S(2)}, u32[]{:S(2)}) collective-permute-start(bf16[216,128]{1,0:T(8,128)(2,1)S(1)} %get-tuple-element.36.refs_0_), channel_id=1, source_target_pairs={{0,4},{1,5},{2,6},{3,7},{4,0},{5,1},{6,2},{7,3},{8,12},{9,13},{10,... | collective-permute-start | bytes 165896 | tf_op jit(solution)/shard_map/ppermute | solution.py:326
  13.5 1.6 %collective-permute-start.6 = (bf16[216,128]{1,0:T(8,128)(2,1)S(1)}, bf16[216,128]{1,0:T(8,128)(2,1)S(1)}, u32[]{:S(2)}, u32[]{:S(2)}) collective-permute-start(bf16[216,128]{1,0:T(8,128)(2,1)S(1)} %get-tuple-element.36.refs_0_), channel_id=1, source_target_pairs={{0,2},{1,3},{2,0},{3,1},{4,6},{5,7},{6,4},{7,5},{8,10},{9,11},{10,... | collective-permute-start | bytes 165896 | tf_op jit(solution)/shard_map/ppermute | solution.py:326
  15.1 0.0 collective-permute-start.7
  15.1 0.5 %collective-permute-start.5 = (bf16[216,128]{1,0:T(8,128)(2,1)S(1)}, bf16[216,128]{1,0:T(8,128)(2,1)S(1)}, u32[]{:S(2)}, u32[]{:S(2)}) collective-permute-start(bf16[216,128]{1,0:T(8,128)(2,1)S(1)} %get-tuple-element.37), channel_id=1, source_target_pairs={{0,3},{1,2},{2,1},{3,0},{4,7},{5,6},{6,5},{7,4},{8,11},{9,10},{10,... | collective-permute-start | bytes 165896 | tf_op jit(solution)/shard_map/ppermute | solution.py:326
  15.6 0.5 %collective-permute-done.9.refs_7_ = bf16[216,128]{1,0:T(8,128)(2,1)S(1)} collective-permute-done((bf16[216,128]{1,0:T(8,128)(2,1)S(1)}, bf16[216,128]{1,0:T(8,128)(2,1)S(1)}, u32[]{:S(2)}, u32[]{:S(2)}) %collective-permute-start.9) | collective-permute-done | bytes 55328 | tf_op jit(solution)/shard_map/ppermute | solution.py:326
  16.1 0.0 collective-permute-start.4
  16.1 1.6 %collective-permute-done.6.refs_3_ = bf16[216,128]{1,0:T(8,128)(2,1)S(1)} collective-permute-done((bf16[216,128]{1,0:T(8,128)(2,1)S(1)}, bf16[216,128]{1,0:T(8,128)(2,1)S(1)}, u32[]{:S(2)}, u32[]{:S(2)}) %collective-permute-start.6) | collective-permute-done | bytes 55328 | tf_op jit(solution)/shard_map/ppermute | solution.py:326
  17.7 2.2 %collective-permute-start.10 = (bf16[216,128]{1,0:T(8,128)(2,1)S(1)}, bf16[216,128]{1,0:T(8,128)(2,1)S(1)}, u32[]{:S(2)}, u32[]{:S(2)}) collective-permute-start(bf16[216,128]{1,0:T(8,128)(2,1)S(1)} %collective-permute-done.9.refs_7_), channel_id=1, source_target_pairs={{0,2},{1,3},{2,0},{3,1},{4,6},{5,7},{6,4},{7,5},{8,10},{9,11},{10,... | collective-permute-start | bytes 165896 | tf_op jit(solution)/shard_map/ppermute | solution.py:326
  19.9 0.3 collective-permute-done.7.refs_6_
  20.1 0.2 hold.1.body_ref
  20.4 0.0 copy-start.3
  20.4 0.0 copy-start.4
  20.4 2.1 %collective-permute-done.10.refs_5_ = bf16[216,128]{1,0:T(8,128)(2,1)S(1)} collective-permute-done((bf16[216,128]{1,0:T(8,128)(2,1)S(1)}, bf16[216,128]{1,0:T(8,128)(2,1)S(1)}, u32[]{:S(2)}, u32[]{:S(2)}) %collective-permute-start.10) | collective-permute-done | bytes 55328 | tf_op jit(solution)/shard_map/ppermute | solution.py:326
  22.5 1.8 %collective-permute-done.8.refs_4_ = bf16[216,128]{1,0:T(8,128)(2,1)S(1)} collective-permute-done((bf16[216,128]{1,0:T(8,128)(2,1)S(1)}, bf16[216,128]{1,0:T(8,128)(2,1)S(1)}, u32[]{:S(2)}, u32[]{:S(2)}) %collective-permute-start.8) | collective-permute-done | bytes 55328 | tf_op jit(solution)/shard_map/ppermute | solution.py:326
  24.3 3.7 %fock.1 = (bf16[32,768]{1,0:T(8,128)(2,1)S(1)}, bf16[32,768]{1,0:T(8,128)(2,1)S(1)}, bf16[32,768]{1,0:T(8,128)(2,1)S(1)}, bf16[32,768]{1,0:T(8,128)(2,1)S(1)}, b...) custom-call(s32[1]{0:T(128)} %bitcast.1.blk_ref, ...), custom_call_target="tpu_custom_call" | custom-call | flops 2717908992 | bytes 6733824 | tf_op jit(solution)/shard_map/fock/pallas_call | solution.py:295
  28.0 0.4 collective-permute-start.11
  28.4 1.7 %collective-permute-start.13 = (bf16[32,768]{1,0:T(8,128)(2,1)S(1)}, bf16[32,768]{1,0:T(8,128)(2,1)S(1)}, u32[]{:S(2)}, u32[]{:S(2)}) collective-permute-start(bf16[32,768]{1,0:T(8,128)(2,1)S(1)} %get-tuple-element.46), channel_id=1, source_target_pairs={{0,2},{1,3},{2,0},{3,1},{4,6},{5,7},{6,4},{7,5},{8,10},{9,11},{10,... | collective-permute-start | bytes 147464 | tf_op jit(solution)/shard_map/ppermute | solution.py:326
  30.1 2.1 %collective-permute-done.11.refs_2_ = bf16[32,768]{1,0:T(8,128)(2,1)S(1)} collective-permute-done((bf16[32,768]{1,0:T(8,128)(2,1)S(1)}, bf16[32,768]{1,0:T(8,128)(2,1)S(1)}, u32[]{:S(2)}, u32[]{:S(2)}) %collective-permute-start.11) | collective-permute-done | bytes 49184 | tf_op jit(solution)/shard_map/ppermute | solution.py:326
  32.2 2.2 %collective-permute-start.12 = (bf16[32,768]{1,0:T(8,128)(2,1)S(1)}, bf16[32,768]{1,0:T(8,128)(2,1)S(1)}, u32[]{:S(2)}, u32[]{:S(2)}) collective-permute-start(bf16[32,768]{1,0:T(8,128)(2,1)S(1)} %get-tuple-element.42), channel_id=1, source_target_pairs={{0,4},{1,5},{2,6},{3,7},{4,0},{5,1},{6,2},{7,3},{8,12},{9,13},{10,... | collective-permute-start | bytes 147464 | tf_op jit(solution)/shard_map/ppermute | solution.py:326
  34.4 1.0 %collective-permute-start.15 = (bf16[32,768]{1,0:T(8,128)(2,1)S(1)}, bf16[32,768]{1,0:T(8,128)(2,1)S(1)}, u32[]{:S(2)}, u32[]{:S(2)}) collective-permute-start(bf16[32,768]{1,0:T(8,128)(2,1)S(1)} %get-tuple-element.48), channel_id=1, source_target_pairs={{0,2},{1,3},{2,0},{3,1},{4,6},{5,7},{6,4},{7,5},{8,10},{9,11},{10,... | collective-permute-start | bytes 147464 | tf_op jit(solution)/shard_map/ppermute | solution.py:326
  35.4 0.1 collective-permute-start.14
  35.5 1.5 %collective-permute-start.16 = (bf16[32,768]{1,0:T(8,128)(2,1)S(1)}, bf16[32,768]{1,0:T(8,128)(2,1)S(1)}, u32[]{:S(2)}, u32[]{:S(2)}) collective-permute-start(bf16[32,768]{1,0:T(8,128)(2,1)S(1)} %get-tuple-element.49), channel_id=1, source_target_pairs={{0,3},{1,2},{2,1},{3,0},{4,7},{5,6},{6,5},{7,4},{8,11},{9,10},{10,... | collective-permute-start | bytes 147464 | tf_op jit(solution)/shard_map/ppermute | solution.py:326
  37.0 0.0 collective-permute-start.17
  37.0 0.5 %collective-permute-done.12.refs_1_ = bf16[32,768]{1,0:T(8,128)(2,1)S(1)} collective-permute-done((bf16[32,768]{1,0:T(8,128)(2,1)S(1)}, bf16[32,768]{1,0:T(8,128)(2,1)S(1)}, u32[]{:S(2)}, u32[]{:S(2)}) %collective-permute-start.12) | collective-permute-done | bytes 49184 | tf_op jit(solution)/shard_map/ppermute | solution.py:326
  37.5 1.3 %collective-permute-done.15.refs_3_ = bf16[32,768]{1,0:T(8,128)(2,1)S(1)} collective-permute-done((bf16[32,768]{1,0:T(8,128)(2,1)S(1)}, bf16[32,768]{1,0:T(8,128)(2,1)S(1)}, u32[]{:S(2)}, u32[]{:S(2)}) %collective-permute-start.15) | collective-permute-done | bytes 49184 | tf_op jit(solution)/shard_map/ppermute | solution.py:326
  38.8 1.2 %collective-permute-done.14.refs_2_ = bf16[32,768]{1,0:T(8,128)(2,1)S(1)} collective-permute-done((bf16[32,768]{1,0:T(8,128)(2,1)S(1)}, bf16[32,768]{1,0:T(8,128)(2,1)S(1)}, u32[]{:S(2)}, u32[]{:S(2)}) %collective-permute-start.14) | collective-permute-done | bytes 49184 | tf_op jit(solution)/shard_map/ppermute | solution.py:326
  40.0 0.1 sum.1
  40.1 2.6 %collective-permute-start.18 = (bf16[32,768]{1,0:T(8,128)(2,1)S(1)}, bf16[32,768]{1,0:T(8,128)(2,1)S(1)}, u32[]{:S(2)}, u32[]{:S(2)}) collective-permute-start(bf16[32,768]{1,0:T(8,128)(2,1)S(1)} %get-tuple-element.52), channel_id=1, source_target_pairs={{0,24},{8,16},{16,8},{24,0},{1,25},{9,17},{17,9},{25,1},{2,26},{10... | collective-permute-start | bytes 147464 | tf_op jit(solution)/shard_map/ppermute | solution.py:321
  42.7 0.5 %collective-permute-start.19 = (bf16[32,768]{1,0:T(8,128)(2,1)S(1)}, bf16[32,768]{1,0:T(8,128)(2,1)S(1)}, u32[]{:S(2)}, u32[]{:S(2)}) collective-permute-start(bf16[32,768]{1,0:T(8,128)(2,1)S(1)} %get-tuple-element.53), channel_id=1, source_target_pairs={{0,8},{8,0},{16,24},{24,16},{1,9},{9,1},{17,25},{25,17},{2,10},{10... | collective-permute-start | bytes 147464 | tf_op jit(solution)/shard_map/ppermute | solution.py:321
  43.2 0.4 collective-permute-start.20
  43.7 1.7 %collective-permute-done.18.refs_1_ = bf16[32,768]{1,0:T(8,128)(2,1)S(1)} collective-permute-done((bf16[32,768]{1,0:T(8,128)(2,1)S(1)}, bf16[32,768]{1,0:T(8,128)(2,1)S(1)}, u32[]{:S(2)}, u32[]{:S(2)}) %collective-permute-start.18) | collective-permute-done | bytes 49184 | tf_op jit(solution)/shard_map/ppermute | solution.py:321
  45.4 1.4 %collective-permute-done.19.refs_2_ = bf16[32,768]{1,0:T(8,128)(2,1)S(1)} collective-permute-done((bf16[32,768]{1,0:T(8,128)(2,1)S(1)}, bf16[32,768]{1,0:T(8,128)(2,1)S(1)}, u32[]{:S(2)}, u32[]{:S(2)}) %collective-permute-start.19) | collective-permute-done | bytes 49184 | tf_op jit(solution)/shard_map/ppermute | solution.py:321
  46.8 0.5 %collective-permute-done.20.refs_3_ = bf16[32,768]{1,0:T(8,128)(2,1)S(1)} collective-permute-done((bf16[32,768]{1,0:T(8,128)(2,1)S(1)}, bf16[32,768]{1,0:T(8,128)(2,1)S(1)}, u32[]{:S(2)}, u32[]{:S(2)}) %collective-permute-start.20) | collective-permute-done | bytes 49184 | tf_op jit(solution)/shard_map/ppermute | solution.py:321
  47.3 1.4 %deal.1 = bf16[16,8,768]{2,1,0:T(8,128)(2,1)} custom-call(s32[1]{0:T(128)} %bitcast.me_ref, s32[8]{0:T(128)S(1)} %copy-done.3, f32[8]{0:T(128)S(1)} %copy-done.4, f32[8,128]{1,0:T(8,128)S(1)} %get-tuple-element.34.refs_1_.total_ref, bf16[32,768]{1,0:T(8,128)(2,1)S(1)} %get-tuple-element.51.refs_0_, bf16[32,768]{1,0:T(8,128)(2,1)S(1)} %collective-permute-done.18.refs_1_, ...), custom_call_target="tpu_custom_call" | custom-call | bytes 397312 | tf_op jit(solution)/shard_map/deal/pallas_call | solution.py:295
  (14 shorter events, 0.1 us)
Async XLA Ops:
  0.0 24.3 %collective-permute-start.3 = (bf16[12,128,768]{2,1,0:T(8,128)(2,1)}, bf16[12,128,768]{2,1,0:T(8,128)(2,1)S(1)}, u32[]{:S(2)}, u32[]{:S(2)}) collective-permute-start(bf16[12,128,768]{2,1,0:T(8,128)(2,1)} %refs_0_.2), channel_id=1, source_target_pairs={{0,1},{1,0},{2,3},{3,2},{4,5},{5,4},{6,7},{7,6},{8,9},{9,8},{10,11... | collective-permute-start | bytes 7077896 | tf_op jit(solution)/shard_map/ppermute | solution.py:326
  2.4 6.9 %collective-permute-start = (bf16[32,896]{1,0:T(8,128)(2,1)}, bf16[32,896]{1,0:T(8,128)(2,1)S(1)}, u32[]{:S(2)}, u32[]{:S(2)}) collective-permute-start(bf16[32,896]{1,0:T(8,128)(2,1)} %get-tuple-element.31), channel_id=1, source_target_pairs={{0,24},{8,16},{16,8},{24,0},{1,25},{9,17},{17,9},{25,1},{2,26},{10... | collective-permute-start | bytes 172040 | tf_op jit(solution)/shard_map/ppermute | solution.py:321
  5.9 4.4 %collective-permute-start.1 = (bf16[32,896]{1,0:T(8,128)(2,1)}, bf16[32,896]{1,0:T(8,128)(2,1)S(1)}, u32[]{:S(2)}, u32[]{:S(2)}) collective-permute-start(bf16[32,896]{1,0:T(8,128)(2,1)} %get-tuple-element.32), channel_id=1, source_target_pairs={{0,8},{8,0},{16,24},{24,16},{1,9},{9,1},{17,25},{25,17},{2,10},{10... | collective-permute-start | bytes 172040 | tf_op jit(solution)/shard_map/ppermute | solution.py:321
  6.4 4.4 %collective-permute-start.2 = (bf16[32,896]{1,0:T(8,128)(2,1)}, bf16[32,896]{1,0:T(8,128)(2,1)S(1)}, u32[]{:S(2)}, u32[]{:S(2)}) collective-permute-start(bf16[32,896]{1,0:T(8,128)(2,1)} %get-tuple-element.33), channel_id=1, source_target_pairs={{0,16},{8,24},{16,0},{24,8},{1,17},{9,25},{17,1},{25,9},{2,18},{10... | collective-permute-start | bytes 172040 | tf_op jit(solution)/shard_map/ppermute | solution.py:321
  6.5 0.8 %copy-start.2 = (bf16[32,896]{1,0:T(8,128)(2,1)S(1)}, bf16[32,896]{1,0:T(8,128)(2,1)}, u32[]{:S(2)}) copy-start(bf16[32,896]{1,0:T(8,128)(2,1)} %get-tuple-element.30.refs_0_) | copy-start | bytes 172036
  7.4 1.7 %copy-start = (bf16[12,128,768]{2,1,0:T(8,128)(2,1)S(1)}, bf16[12,128,768]{2,1,0:T(8,128)(2,1)}, u32[]{:S(2)}) copy-start(bf16[12,128,768]{2,1,0:T(8,128)(2,1)} %refs_0_.2) | copy-start | bytes 7077892
  9.2 10.9 %copy-start.1 = (bf16[768,768]{1,0:T(8,128)(2,1)S(1)}, bf16[768,768]{1,0:T(8,128)(2,1)}, u32[]{:S(2)}) copy-start(bf16[768,768]{1,0:T(8,128)(2,1)} %refs_0_.3) | copy-start | bytes 3538948
  10.9 5.2 %collective-permute-start.9 = (bf16[216,128]{1,0:T(8,128)(2,1)S(1)}, bf16[216,128]{1,0:T(8,128)(2,1)S(1)}, u32[]{:S(2)}, u32[]{:S(2)}) collective-permute-start(bf16[216,128]{1,0:T(8,128)(2,1)S(1)} %get-tuple-element.36.refs_0_), channel_id=1, source_target_pairs={{0,4},{1,5},{2,6},{3,7},{4,0},{5,1},{6,2},{7,3},{8,12},{9,13},{10,... | collective-permute-start | bytes 165896 | tf_op jit(solution)/shard_map/ppermute | solution.py:326
  13.5 4.2 %collective-permute-start.6 = (bf16[216,128]{1,0:T(8,128)(2,1)S(1)}, bf16[216,128]{1,0:T(8,128)(2,1)S(1)}, u32[]{:S(2)}, u32[]{:S(2)}) collective-permute-start(bf16[216,128]{1,0:T(8,128)(2,1)S(1)} %get-tuple-element.36.refs_0_), channel_id=1, source_target_pairs={{0,2},{1,3},{2,0},{3,1},{4,6},{5,7},{6,4},{7,5},{8,10},{9,11},{10,... | collective-permute-start | bytes 165896 | tf_op jit(solution)/shard_map/ppermute | solution.py:326
  15.1 5.0 %collective-permute-start.7 = (bf16[216,128]{1,0:T(8,128)(2,1)S(1)}, bf16[216,128]{1,0:T(8,128)(2,1)S(1)}, u32[]{:S(2)}, u32[]{:S(2)}) collective-permute-start(bf16[216,128]{1,0:T(8,128)(2,1)S(1)} %get-tuple-element.37), channel_id=1, source_target_pairs={{0,5},{1,4},{2,7},{3,6},{4,1},{5,0},{6,3},{7,2},{8,13},{9,12},{10,... | collective-permute-start | bytes 165896 | tf_op jit(solution)/shard_map/ppermute | solution.py:326
  15.1 5.3 %collective-permute-start.5 = (bf16[216,128]{1,0:T(8,128)(2,1)S(1)}, bf16[216,128]{1,0:T(8,128)(2,1)S(1)}, u32[]{:S(2)}, u32[]{:S(2)}) collective-permute-start(bf16[216,128]{1,0:T(8,128)(2,1)S(1)} %get-tuple-element.37), channel_id=1, source_target_pairs={{0,3},{1,2},{2,1},{3,0},{4,7},{5,6},{6,5},{7,4},{8,11},{9,10},{10,... | collective-permute-start | bytes 165896 | tf_op jit(solution)/shard_map/ppermute | solution.py:326
  16.1 4.3 %collective-permute-start.4 = (bf16[216,128]{1,0:T(8,128)(2,1)S(1)}, bf16[216,128]{1,0:T(8,128)(2,1)S(1)}, u32[]{:S(2)}, u32[]{:S(2)}) collective-permute-start(bf16[216,128]{1,0:T(8,128)(2,1)S(1)} %get-tuple-element.37), channel_id=1, source_target_pairs={{0,1},{1,0},{2,3},{3,2},{4,5},{5,4},{6,7},{7,6},{8,9},{9,8},{10,11... | collective-permute-start | bytes 165896 | tf_op jit(solution)/shard_map/ppermute | solution.py:326
  17.7 4.8 %collective-permute-start.10 = (bf16[216,128]{1,0:T(8,128)(2,1)S(1)}, bf16[216,128]{1,0:T(8,128)(2,1)S(1)}, u32[]{:S(2)}, u32[]{:S(2)}) collective-permute-start(bf16[216,128]{1,0:T(8,128)(2,1)S(1)} %collective-permute-done.9.refs_7_), channel_id=1, source_target_pairs={{0,2},{1,3},{2,0},{3,1},{4,6},{5,7},{6,4},{7,5},{8,10},{9,11},{10,... | collective-permute-start | bytes 165896 | tf_op jit(solution)/shard_map/ppermute | solution.py:326
  20.1 4.2 %collective-permute-start.8 = (bf16[216,128]{1,0:T(8,128)(2,1)S(1)}, bf16[216,128]{1,0:T(8,128)(2,1)S(1)}, u32[]{:S(2)}, u32[]{:S(2)}) collective-permute-start(bf16[216,128]{1,0:T(8,128)(2,1)S(1)} %collective-permute-done.7.refs_6_), channel_id=1, source_target_pairs={{0,2},{1,3},{2,0},{3,1},{4,6},{5,7},{6,4},{7,5},{8,10},{9,11},{10,... | collective-permute-start | bytes 165896 | tf_op jit(solution)/shard_map/ppermute | solution.py:326
  20.4 26.9 %copy-start.3 = (s32[8]{0:T(128)S(1)}, s32[8]{0:T(128)}, u32[]{:S(2)}) copy-start(s32[8]{0:T(128)} %target_ref.1) | copy-start | bytes 100
  20.4 26.9 %copy-start.4 = (f32[8]{0:T(128)S(1)}, f32[8]{0:T(128)}, u32[]{:S(2)}) copy-start(f32[8]{0:T(128)} %weights_ref.1) | copy-start | bytes 100
  28.0 4.2 %collective-permute-start.11 = (bf16[32,768]{1,0:T(8,128)(2,1)S(1)}, bf16[32,768]{1,0:T(8,128)(2,1)S(1)}, u32[]{:S(2)}, u32[]{:S(2)}) collective-permute-start(bf16[32,768]{1,0:T(8,128)(2,1)S(1)} %get-tuple-element.41), channel_id=1, source_target_pairs={{0,2},{1,3},{2,0},{3,1},{4,6},{5,7},{6,4},{7,5},{8,10},{9,11},{10,... | collective-permute-start | bytes 147464 | tf_op jit(solution)/shard_map/ppermute | solution.py:326
  28.4 7.0 %collective-permute-start.13 = (bf16[32,768]{1,0:T(8,128)(2,1)S(1)}, bf16[32,768]{1,0:T(8,128)(2,1)S(1)}, u32[]{:S(2)}, u32[]{:S(2)}) collective-permute-start(bf16[32,768]{1,0:T(8,128)(2,1)S(1)} %get-tuple-element.46), channel_id=1, source_target_pairs={{0,2},{1,3},{2,0},{3,1},{4,6},{5,7},{6,4},{7,5},{8,10},{9,11},{10,... | collective-permute-start | bytes 147464 | tf_op jit(solution)/shard_map/ppermute | solution.py:326
  32.2 5.3 %collective-permute-start.12 = (bf16[32,768]{1,0:T(8,128)(2,1)S(1)}, bf16[32,768]{1,0:T(8,128)(2,1)S(1)}, u32[]{:S(2)}, u32[]{:S(2)}) collective-permute-start(bf16[32,768]{1,0:T(8,128)(2,1)S(1)} %get-tuple-element.42), channel_id=1, source_target_pairs={{0,4},{1,5},{2,6},{3,7},{4,0},{5,1},{6,2},{7,3},{8,12},{9,13},{10,... | collective-permute-start | bytes 147464 | tf_op jit(solution)/shard_map/ppermute | solution.py:326
  34.4 4.4 %collective-permute-start.15 = (bf16[32,768]{1,0:T(8,128)(2,1)S(1)}, bf16[32,768]{1,0:T(8,128)(2,1)S(1)}, u32[]{:S(2)}, u32[]{:S(2)}) collective-permute-start(bf16[32,768]{1,0:T(8,128)(2,1)S(1)} %get-tuple-element.48), channel_id=1, source_target_pairs={{0,2},{1,3},{2,0},{3,1},{4,6},{5,7},{6,4},{7,5},{8,10},{9,11},{10,... | collective-permute-start | bytes 147464 | tf_op jit(solution)/shard_map/ppermute | solution.py:326
  35.4 4.6 %collective-permute-start.14 = (bf16[32,768]{1,0:T(8,128)(2,1)S(1)}, bf16[32,768]{1,0:T(8,128)(2,1)S(1)}, u32[]{:S(2)}, u32[]{:S(2)}) collective-permute-start(bf16[32,768]{1,0:T(8,128)(2,1)S(1)} %get-tuple-element.47), channel_id=1, source_target_pairs={{0,5},{1,4},{2,7},{3,6},{4,1},{5,0},{6,3},{7,2},{8,13},{9,12},{10,... | collective-permute-start | bytes 147464 | tf_op jit(solution)/shard_map/ppermute | solution.py:326
  35.5 4.5 %collective-permute-start.16 = (bf16[32,768]{1,0:T(8,128)(2,1)S(1)}, bf16[32,768]{1,0:T(8,128)(2,1)S(1)}, u32[]{:S(2)}, u32[]{:S(2)}) collective-permute-start(bf16[32,768]{1,0:T(8,128)(2,1)S(1)} %get-tuple-element.49), channel_id=1, source_target_pairs={{0,3},{1,2},{2,1},{3,0},{4,7},{5,6},{6,5},{7,4},{8,11},{9,10},{10,... | collective-permute-start | bytes 147464 | tf_op jit(solution)/shard_map/ppermute | solution.py:326
  37.0 3.0 %collective-permute-start.17 = (bf16[32,768]{1,0:T(8,128)(2,1)S(1)}, bf16[32,768]{1,0:T(8,128)(2,1)S(1)}, u32[]{:S(2)}, u32[]{:S(2)}) collective-permute-start(bf16[32,768]{1,0:T(8,128)(2,1)S(1)} %get-tuple-element.50), channel_id=1, source_target_pairs={{0,1},{1,0},{2,3},{3,2},{4,5},{5,4},{6,7},{7,6},{8,9},{9,8},{10,11... | collective-permute-start | bytes 147464 | tf_op jit(solution)/shard_map/ppermute | solution.py:326
  40.1 5.3 %collective-permute-start.18 = (bf16[32,768]{1,0:T(8,128)(2,1)S(1)}, bf16[32,768]{1,0:T(8,128)(2,1)S(1)}, u32[]{:S(2)}, u32[]{:S(2)}) collective-permute-start(bf16[32,768]{1,0:T(8,128)(2,1)S(1)} %get-tuple-element.52), channel_id=1, source_target_pairs={{0,24},{8,16},{16,8},{24,0},{1,25},{9,17},{17,9},{25,1},{2,26},{10... | collective-permute-start | bytes 147464 | tf_op jit(solution)/shard_map/ppermute | solution.py:321
  42.7 4.1 %collective-permute-start.19 = (bf16[32,768]{1,0:T(8,128)(2,1)S(1)}, bf16[32,768]{1,0:T(8,128)(2,1)S(1)}, u32[]{:S(2)}, u32[]{:S(2)}) collective-permute-start(bf16[32,768]{1,0:T(8,128)(2,1)S(1)} %get-tuple-element.53), channel_id=1, source_target_pairs={{0,8},{8,0},{16,24},{24,16},{1,9},{9,1},{17,25},{25,17},{2,10},{10... | collective-permute-start | bytes 147464 | tf_op jit(solution)/shard_map/ppermute | solution.py:321
  43.2 4.1 %collective-permute-start.20 = (bf16[32,768]{1,0:T(8,128)(2,1)S(1)}, bf16[32,768]{1,0:T(8,128)(2,1)S(1)}, u32[]{:S(2)}, u32[]{:S(2)}) collective-permute-start(bf16[32,768]{1,0:T(8,128)(2,1)S(1)} %get-tuple-element.54), channel_id=1, source_target_pairs={{0,16},{8,24},{16,0},{24,8},{1,17},{9,25},{17,1},{25,9},{2,18},{10... | collective-permute-start | bytes 147464 | tf_op jit(solution)/shard_map/ppermute | solution.py:321

commit v11 on v9

--- a/solution.py
+++ b/solution.py
@@ -161,6 +161,11 @@
     return hops(n)[:1] + hops(n)[:0:-1]
 
 
+def leading(s, chips):
+    top = 1 << (s.bit_length() - 1) if s else 0
+    return top if power(chips) else s
+
+
 def partner(blk, s, e, n, sign):
     chip = moved(lax.div(blk, 2), s, n // 2, sign)
     core = lax.rem(blk, 2)
@@ -169,7 +174,7 @@
 
 def fock_kernel(n, half, blk_ref, body_ref, own_ref, sib_ref, *refs):
     ins, outs = refs[:n], refs[n : 2 * n]
-    prop, turned, coup, result = refs[2 * n :]
+    prop, carried, coup, result = refs[2 * n :]
     vec_count, occupied, orbitals = own_ref.shape
     slab = outs[0].shape[0]
     rows = slab // half
@@ -187,12 +192,12 @@
                 piece = piece * growth[w * chunks + c : w * chunks + c + 1]
                 prop[w, source, :, c * LANES : (c + 1) * LANES] = piece.astype(prop.dtype)
     scaled = jnp.concatenate([prop[w, i] for w in range(half) for i in range(n)], axis=0).astype(BF16)
-    turned[...] = jnp.dot(scaled, body_ref[...], preferred_element_type=F32).T.astype(BF16)
+    carried[...] = jnp.dot(scaled, body_ref[...], preferred_element_type=F32).astype(BF16)
     batch = math.gcd(vec_count, 4)
     for c, ref in enumerate((own_ref, sib_ref)):
         for g in range(0, vec_count, batch):
             left = ref[g : g + batch].reshape(batch * occupied, orbitals)
-            s = jnp.dot(left, turned[...], preferred_element_type=F32).astype(BF16)
+            s = lax.dot_general(left, carried[...], (((1,), (1,)), ((), ())), preferred_element_type=F32).astype(BF16)
             for k in range(batch):
                 at = (c * vec_count + g + k) * occupied
                 for w in range(half):
@@ -249,25 +254,36 @@
 
 def deal_kernel(order, keep, cap, me_ref, target_ref, weights_ref, total_ref, *refs):
     groups = len(order)
-    ins, (out_ref, blocks, wide) = refs[:groups], refs[groups:]
-    rows, slots, orbitals = out_ref.shape
+    ins, (out_any, blocks, wide, held, sems) = refs[:groups], refs[groups:]
+    rows, slots, orbitals = wide.shape
     live = groups * keep
     for s, ref in zip(order, ins):
         base = moved(me_ref[0], s, groups, -1) * cap
         for k in range(cap):
             blocks[base + k] = ref[k * rows : (k + 1) * rows, :].astype(F32)
     blocks[groups * cap] = jnp.zeros((rows, orbitals), F32)
+    places = []
     for slot in range(slots):
         t = target_ref[slot]
         alive = t < live
         at = jnp.where(alive, lax.rem(t, groups) * cap + lax.rem(lax.div(t, groups), cap), groups * cap)
         weight = jnp.where(alive, weights_ref[slot], F32(0.0))
         factor = jnp.full((1, LANES), weight * live, F32) / total_ref[0:1, :]
-        wide[:, slot, :] = blocks[at] * factor[:, 0:1]
-    out_ref[...] = wide[...].astype(BF16)
-
-
-def call(kernel, outs, scalars, held, arrays, scratch, name, flops=0, vmem=VMEM):
+        places.append((at, factor[:, 0:1]))
+    step = rows // sems.shape[0]
+    copies = []
+    for h in range(sems.shape[0]):
+        band = slice(h * step, (h + 1) * step)
+        for slot, (at, factor) in enumerate(places):
+            wide[band, slot, :] = blocks[at, band, :] * factor
+        held[band] = wide[band].astype(BF16)
+        copies.append(pltpu.make_async_copy(held.at[band], out_any.at[band], sems.at[h]))
+        copies[-1].start()
+    for copy in copies:
+        copy.wait()
+
+
+def call(kernel, outs, scalars, held, arrays, scratch, name, flops=0, vmem=VMEM, place=pltpu.VMEM):
     smem = pl.BlockSpec(memory_space=pltpu.SMEM)
     full = pl.BlockSpec(memory_space=pltpu.VMEM)
     size = sum(x.size * x.dtype.itemsize for x in list(arrays) + list(outs))
@@ -275,7 +291,7 @@
         kernel,
         out_shape=outs,
         in_specs=[smem] * len(scalars) + [pl.BlockSpec(memory_space=pl.ANY)] * len(held) + [full] * len(arrays),
-        out_specs=[full] * len(outs),
+        out_specs=[pl.BlockSpec(memory_space=place)] * len(outs),
         scratch_shapes=scratch,
         compiler_params=pltpu.CompilerParams(vmem_limit_bytes=vmem * 2**20),
         cost_estimate=pl.CostEstimate(flops=flops, bytes_accessed=size, transcendentals=0),
@@ -304,7 +320,7 @@
             return x
         return lax.ppermute(x, "blk", [(i, 2 * moved(i // 2, s, n // 2, 1) + (i % 2 ^ e)) for i in range(n)])
 
-    order = [0] + sorted(range(1, groups), key=lambda s: -bin(s).count("1"))
+    order = [0] + sorted(range(1, groups), key=lambda s: (s & 1, -s))
     chunks = orbitals // LANES
     sibling = to_block(chol, 0, 1)
     width = orbitals + tail_blocks(cap * (2 * chunks + 1) + 3, cap * rows) * LANES
@@ -368,7 +384,15 @@
         [pltpu.SemaphoreType.DMA((1,))],
         "hold",
     )
-    gathered = [to_block(other if e else same, s, e) for s, e in arrivals(n)]
+    gathered = {}
+    for s, e in arrivals(n):
+        if leading(s, n // 2) == s:
+            gathered[s, e] = to_block(other if e else same, s, e)
+    for s, e in arrivals(n):
+        top = leading(s, n // 2)
+        if top != s:
+            gathered[s, e] = to_block(gathered[top, e], s ^ top, 0)
+    gathered = [gathered[hop] for hop in arrivals(n)]
     held = F32 if rows % 16 else BF16
     parts = call(
         functools.partial(fock_kernel, n, half),
@@ -378,20 +402,20 @@
         [held_body, own, sibling] + gathered,
         [
             pltpu.VMEM((half, n, rows, orbitals), held),
-            pltpu.VMEM((orbitals, half * occupied), BF16),
+            pltpu.VMEM((half * occupied, orbitals), BF16),
             pltpu.VMEM((half * occupied, 2 * vec_count * occupied), BF16),
             pltpu.VMEM((half, n, rows, orbitals), held),
         ],
         "fock",
         flops=2 * n * slab * orbitals * (orbitals + 4 * vec_count * occupied),
     )
-    parts = [to_block(x, s, e) for x, (s, e) in zip(parts, hops(n))]
+    backs = [to_block(x, s, e) for x, (s, e) in zip(parts, hops(n))]
     back = call(
         functools.partial(sum_kernel, n, keep, cap, groups),
         [shape((cap * rows, orbitals), BF16)] * groups,
         [core],
         [],
-        [pick] + parts,
+        [pick] + backs,
         [],
         "sum",
     )
@@ -402,8 +426,14 @@
         [grp, target, weights],
         [],
         [weight_sum] + back,
-        [pltpu.VMEM((groups * cap + 1, rows, orbitals), F32), pltpu.VMEM(walkers.shape, F32)],
+        [
+            pltpu.VMEM((groups * cap + 1, rows, orbitals), F32),
+            pltpu.VMEM(walkers.shape, F32),
+            pltpu.VMEM(walkers.shape, BF16),
+            pltpu.SemaphoreType.DMA((2,)),
+        ],
         "deal",
+        place=pl.ANY,
     )
     return out
 

time: 49 us -> 48.2 us (0.984)
  starting transfers between devices: 25.7 us -> 22 us
  waiting for transfers between devices: 12.7 us -> 15.7 us
    ppermute x15, starting transfers between devices: 18 us -> 14.3 us  [to_block(): lax.ppermute(x, 'blk', [(i, 2 * moved(i // 2, s, n // 2, 1) + (i % 2 ^ e)...]
    ppermute x15, waiting for transfers between devices: 8.04 us -> 10.7 us  [to_block(): lax.ppermute(x, 'blk', [(i, 2 * moved(i // 2, s, n // 2, 1) + (i % 2 ^ e)...]
  transfers between devices with their start and end apart: 21 -> 21, of which waited for: 14 -> 12; matrix products, arithmetic and copies ran while one was open for 0% -> 0% of each run, Pallas kernels for 5% -> 5%
where the time goes in v11:
time: 48.2 us; the launch traced here: 48 us
  starting transfers between devices  22 us (46%)
  waiting for transfers between devices  15.7 us (33%)
  Pallas kernels  7.68 us (16%)
  local copies, waits for them, and re-layouts  2.5 us (5%)
    ppermute x15, starting transfers between devices, to_block(): lax.ppermute(x, 'blk', [(i, 2 * moved(i // 2, s, n // 2, 1) + (i % 2 ^ e)...  14.3 us
    ppermute x15, waiting for transfers between devices, to_block(): lax.ppermute(x, 'blk', [(i, 2 * moved(i // 2, s, n // 2, 1) + (i % 2 ^ e)...  10.7 us
    pallas_call x8, Pallas kernels, call(): pl.pallas_call(kernel, out_shape=outs, in_specs=[smem] * len(scalars) + [...  7.68 us
    ppermute x6, starting transfers between devices, to_list(): lax.ppermute(x, 'grp', [(i, moved(i, s, groups, 1)) for i in range(groups)])  7.68 us
    ppermute x6, waiting for transfers between devices, to_list(): lax.ppermute(x, 'grp', [(i, moved(i, s, groups, 1)) for i in range(groups)])  5.04 us
    unnamed x10, local copies, waits for them, and re-layouts  2.5 us
  transfers between devices with their start and end apart: 21, of which 12 were waited for; matrix products, arithmetic and copies ran while one was open for 0% of the time, Pallas kernels for 5%

profile of v11, /device:TPU:0, one launch (start us, length us, event | category | flops | bytes accessed | tf_op | source)
XLA Modules:
  0.0 48.0 jit_solution(15304057833669436178)
XLA Ops:
  0.0 0.5 collective-permute-start.3
  0.5 1.9 %route.1 = (bf16[32,896]{1,0:T(8,128)(2,1)}, bf16[32,896]{1,0:T(8,128)(2,1)}, bf16[32,896]{1,0:T(8,128)(2,1)}, bf16[32,896]{1,0:T(8,128)(2,1)}) custom-call(s32[1]{0:T(128)} %bitcast.me_ref, s32[8]{0:T(128)} %target_ref.1, f32[8]{0:T(128)} %weights_ref.1, bf16[16,8,768]{2,1,0:T(8,128)(2,1)} %walkers_any.1, f32[8,12]{1,0:T(8,128)} %fields_any.1, ...), custom_call_target="tpu_custom_call" | custom-call | bytes 229376 | tf_op jit(solution)/shard_map/route/pallas_call | solution.py:290
  2.4 2.6 %collective-permute-start = (bf16[32,896]{1,0:T(8,128)(2,1)}, bf16[32,896]{1,0:T(8,128)(2,1)S(1)}, u32[]{:S(2)}, u32[]{:S(2)}) collective-permute-start(bf16[32,896]{1,0:T(8,128)(2,1)} %get-tuple-element.26), channel_id=1, source_target_pairs={{0,16},{8,24},{16,0},{24,8},{1,17},{9,25},{17,1},{25,9},{2,18},{10... | collective-permute-start | bytes 172040 | tf_op jit(solution)/shard_map/ppermute | solution.py:316
  4.9 1.4 %collective-permute-start.1 = (bf16[32,896]{1,0:T(8,128)(2,1)}, bf16[32,896]{1,0:T(8,128)(2,1)S(1)}, u32[]{:S(2)}, u32[]{:S(2)}) collective-permute-start(bf16[32,896]{1,0:T(8,128)(2,1)} %get-tuple-element.27), channel_id=1, source_target_pairs={{0,24},{8,16},{16,8},{24,0},{1,25},{9,17},{17,9},{25,1},{2,26},{10... | collective-permute-start | bytes 172040 | tf_op jit(solution)/shard_map/ppermute | solution.py:316
  6.4 0.1 collective-permute-start.2
  6.5 0.8 %copy-done.2 = bf16[32,896]{1,0:T(8,128)(2,1)S(1)} copy-done((bf16[32,896]{1,0:T(8,128)(2,1)S(1)}, bf16[32,896]{1,0:T(8,128)(2,1)}, u32[]{:S(2)}) %copy-start.2) | copy-done | bytes 57368
  7.4 0.0 copy-start
  7.4 1.7 %copy-done = bf16[12,128,768]{2,1,0:T(8,128)(2,1)S(1)} copy-done((bf16[12,128,768]{2,1,0:T(8,128)(2,1)S(1)}, bf16[12,128,768]{2,1,0:T(8,128)(2,1)}, u32[]{:S(2)}) %copy-start) | copy-done | bytes 2359320
  9.0 0.2 stage.1.when.own_ref
  9.2 0.0 copy-start.1
  9.2 1.2 %collective-permute-done.1.refs_2_ = bf16[32,896]{1,0:T(8,128)(2,1)S(1)} collective-permute-done((bf16[32,896]{1,0:T(8,128)(2,1)}, bf16[32,896]{1,0:T(8,128)(2,1)S(1)}, u32[]{:S(2)}, u32[]{:S(2)}) %collective-permute-start.1) | collective-permute-done | bytes 57376 | tf_op jit(solution)/shard_map/ppermute | solution.py:316
  10.5 0.3 collective-permute-done.2.refs_3_
  10.8 0.1 merge.1
  10.9 2.7 %collective-permute-start.9 = (bf16[216,128]{1,0:T(8,128)(2,1)S(1)}, bf16[216,128]{1,0:T(8,128)(2,1)S(1)}, u32[]{:S(2)}, u32[]{:S(2)}) collective-permute-start(bf16[216,128]{1,0:T(8,128)(2,1)S(1)} %get-tuple-element.31.refs_0_), channel_id=1, source_target_pairs={{0,4},{1,5},{2,6},{3,7},{4,0},{5,1},{6,2},{7,3},{8,12},{9,13},{10,... | collective-permute-start | bytes 165896 | tf_op jit(solution)/shard_map/ppermute | solution.py:321
  13.5 1.6 %collective-permute-start.6 = (bf16[216,128]{1,0:T(8,128)(2,1)S(1)}, bf16[216,128]{1,0:T(8,128)(2,1)S(1)}, u32[]{:S(2)}, u32[]{:S(2)}) collective-permute-start(bf16[216,128]{1,0:T(8,128)(2,1)S(1)} %get-tuple-element.31.refs_0_), channel_id=1, source_target_pairs={{0,2},{1,3},{2,0},{3,1},{4,6},{5,7},{6,4},{7,5},{8,10},{9,11},{10,... | collective-permute-start | bytes 165896 | tf_op jit(solution)/shard_map/ppermute | solution.py:321
  15.1 0.5 %collective-permute-start.5 = (bf16[216,128]{1,0:T(8,128)(2,1)S(1)}, bf16[216,128]{1,0:T(8,128)(2,1)S(1)}, u32[]{:S(2)}, u32[]{:S(2)}) collective-permute-start(bf16[216,128]{1,0:T(8,128)(2,1)S(1)} %get-tuple-element.32), channel_id=1, source_target_pairs={{0,3},{1,2},{2,1},{3,0},{4,7},{5,6},{6,5},{7,4},{8,11},{9,10},{10,... | collective-permute-start | bytes 165896 | tf_op jit(solution)/shard_map/ppermute | solution.py:321
  15.6 0.5 %collective-permute-done.9.refs_7_ = bf16[216,128]{1,0:T(8,128)(2,1)S(1)} collective-permute-done((bf16[216,128]{1,0:T(8,128)(2,1)S(1)}, bf16[216,128]{1,0:T(8,128)(2,1)S(1)}, u32[]{:S(2)}, u32[]{:S(2)}) %collective-permute-start.9) | collective-permute-done | bytes 55328 | tf_op jit(solution)/shard_map/ppermute | solution.py:321
  16.1 1.6 %collective-permute-done.6.refs_3_ = bf16[216,128]{1,0:T(8,128)(2,1)S(1)} collective-permute-done((bf16[216,128]{1,0:T(8,128)(2,1)S(1)}, bf16[216,128]{1,0:T(8,128)(2,1)S(1)}, u32[]{:S(2)}, u32[]{:S(2)}) %collective-permute-start.6) | collective-permute-done | bytes 55328 | tf_op jit(solution)/shard_map/ppermute | solution.py:321
  17.7 2.2 %collective-permute-start.10 = (bf16[216,128]{1,0:T(8,128)(2,1)S(1)}, bf16[216,128]{1,0:T(8,128)(2,1)S(1)}, u32[]{:S(2)}, u32[]{:S(2)}) collective-permute-start(bf16[216,128]{1,0:T(8,128)(2,1)S(1)} %collective-permute-done.9.refs_7_), channel_id=1, source_target_pairs={{0,2},{1,3},{2,0},{3,1},{4,6},{5,7},{6,4},{7,5},{8,10},{9,11},{10,... | collective-permute-start | bytes 165896 | tf_op jit(solution)/shard_map/ppermute | solution.py:321
  19.8 0.3 collective-permute-done.7.refs_6_
  20.2 0.2 hold.1.body_ref
  20.4 0.0 copy-start.3
  20.4 0.0 copy-start.4
  20.4 0.0 collective-permute-done.4.refs_1_
  20.5 2.1 %collective-permute-done.10.refs_5_ = bf16[216,128]{1,0:T(8,128)(2,1)S(1)} collective-permute-done((bf16[216,128]{1,0:T(8,128)(2,1)S(1)}, bf16[216,128]{1,0:T(8,128)(2,1)S(1)}, u32[]{:S(2)}, u32[]{:S(2)}) %collective-permute-start.10) | collective-permute-done | bytes 55328 | tf_op jit(solution)/shard_map/ppermute | solution.py:321
  22.5 1.8 %collective-permute-done.8.refs_4_ = bf16[216,128]{1,0:T(8,128)(2,1)S(1)} collective-permute-done((bf16[216,128]{1,0:T(8,128)(2,1)S(1)}, bf16[216,128]{1,0:T(8,128)(2,1)S(1)}, u32[]{:S(2)}, u32[]{:S(2)}) %collective-permute-start.8) | collective-permute-done | bytes 55328 | tf_op jit(solution)/shard_map/ppermute | solution.py:321
  24.3 3.7 %fock.1 = (bf16[32,768]{1,0:T(8,128)(2,1)S(1)}, bf16[32,768]{1,0:T(8,128)(2,1)S(1)}, bf16[32,768]{1,0:T(8,128)(2,1)S(1)}, bf16[32,768]{1,0:T(8,128)(2,1)S(1)}, b...) custom-call(s32[1]{0:T(128)} %bitcast.1.blk_ref, ...), custom_call_target="tpu_custom_call" | custom-call | flops 2717908992 | bytes 6733824 | tf_op jit(solution)/shard_map/fock/pallas_call | solution.py:290
  28.0 1.6 %collective-permute-start.11 = (bf16[32,768]{1,0:T(8,128)(2,1)S(1)}, bf16[32,768]{1,0:T(8,128)(2,1)S(1)}, u32[]{:S(2)}, u32[]{:S(2)}) collective-permute-start(bf16[32,768]{1,0:T(8,128)(2,1)S(1)} %get-tuple-element.34), channel_id=1, source_target_pairs={{0,4},{1,5},{2,6},{3,7},{4,0},{5,1},{6,2},{7,3},{8,12},{9,13},{10,... | collective-permute-start | bytes 147464 | tf_op jit(solution)/shard_map/ppermute | solution.py:321
  29.7 2.7 %collective-permute-start.13 = (bf16[32,768]{1,0:T(8,128)(2,1)S(1)}, bf16[32,768]{1,0:T(8,128)(2,1)S(1)}, u32[]{:S(2)}, u32[]{:S(2)}) collective-permute-start(bf16[32,768]{1,0:T(8,128)(2,1)S(1)} %get-tuple-element.36), channel_id=1, source_target_pairs={{0,6},{1,7},{2,4},{3,5},{4,2},{5,3},{6,0},{7,1},{8,14},{9,15},{10,... | collective-permute-start | bytes 147464 | tf_op jit(solution)/shard_map/ppermute | solution.py:321
  32.4 1.9 %collective-permute-start.14 = (bf16[32,768]{1,0:T(8,128)(2,1)S(1)}, bf16[32,768]{1,0:T(8,128)(2,1)S(1)}, u32[]{:S(2)}, u32[]{:S(2)}) collective-permute-start(bf16[32,768]{1,0:T(8,128)(2,1)S(1)} %get-tuple-element.37), channel_id=1, source_target_pairs={{0,7},{1,6},{2,5},{3,4},{4,3},{5,2},{6,1},{7,0},{8,15},{9,14},{10,... | collective-permute-start | bytes 147464 | tf_op jit(solution)/shard_map/ppermute | solution.py:321
  34.3 0.0 collective-permute-start.15
  34.3 0.0 collective-permute-done.11.refs_1_
  34.3 0.7 %collective-permute-start.16 = (bf16[32,768]{1,0:T(8,128)(2,1)S(1)}, bf16[32,768]{1,0:T(8,128)(2,1)S(1)}, u32[]{:S(2)}, u32[]{:S(2)}) collective-permute-start(bf16[32,768]{1,0:T(8,128)(2,1)S(1)} %get-tuple-element.39), channel_id=1, source_target_pairs={{0,3},{1,2},{2,1},{3,0},{4,7},{5,6},{6,5},{7,4},{8,11},{9,10},{10,... | collective-permute-start | bytes 147464 | tf_op jit(solution)/shard_map/ppermute | solution.py:321
  35.0 1.7 %collective-permute-done.12.refs_2_ = bf16[32,768]{1,0:T(8,128)(2,1)S(1)} collective-permute-done((bf16[32,768]{1,0:T(8,128)(2,1)S(1)}, bf16[32,768]{1,0:T(8,128)(2,1)S(1)}, u32[]{:S(2)}, u32[]{:S(2)}) %collective-permute-start.12) | collective-permute-done | bytes 49184 | tf_op jit(solution)/shard_map/ppermute | solution.py:321
  36.7 0.0 collective-permute-start.17
  36.7 0.0 collective-permute-done.13.refs_3_
  36.7 1.1 %collective-permute-done.14.refs_4_ = bf16[32,768]{1,0:T(8,128)(2,1)S(1)} collective-permute-done((bf16[32,768]{1,0:T(8,128)(2,1)S(1)}, bf16[32,768]{1,0:T(8,128)(2,1)S(1)}, u32[]{:S(2)}, u32[]{:S(2)}) %collective-permute-start.14) | collective-permute-done | bytes 49184 | tf_op jit(solution)/shard_map/ppermute | solution.py:321
  37.8 1.5 %collective-permute-done.15.refs_5_ = bf16[32,768]{1,0:T(8,128)(2,1)S(1)} collective-permute-done((bf16[32,768]{1,0:T(8,128)(2,1)S(1)}, bf16[32,768]{1,0:T(8,128)(2,1)S(1)}, u32[]{:S(2)}, u32[]{:S(2)}) %collective-permute-start.15) | collective-permute-done | bytes 49184 | tf_op jit(solution)/shard_map/ppermute | solution.py:321
  39.4 0.0 collective-permute-done.16.refs_6_
  39.4 0.0 collective-permute-done.17.refs_7_
  39.4 0.1 sum.1
  39.5 1.6 %collective-permute-start.18 = (bf16[32,768]{1,0:T(8,128)(2,1)S(1)}, bf16[32,768]{1,0:T(8,128)(2,1)S(1)}, u32[]{:S(2)}, u32[]{:S(2)}) collective-permute-start(bf16[32,768]{1,0:T(8,128)(2,1)S(1)} %get-tuple-element.42), channel_id=1, source_target_pairs={{0,16},{8,24},{16,0},{24,8},{1,17},{9,25},{17,1},{25,9},{2,18},{10... | collective-permute-start | bytes 147464 | tf_op jit(solution)/shard_map/ppermute | solution.py:316
  41.1 1.4 %collective-permute-start.19 = (bf16[32,768]{1,0:T(8,128)(2,1)S(1)}, bf16[32,768]{1,0:T(8,128)(2,1)S(1)}, u32[]{:S(2)}, u32[]{:S(2)}) collective-permute-start(bf16[32,768]{1,0:T(8,128)(2,1)S(1)} %get-tuple-element.43), channel_id=1, source_target_pairs={{0,24},{8,16},{16,8},{24,0},{1,25},{9,17},{17,9},{25,1},{2,26},{10... | collective-permute-start | bytes 147464 | tf_op jit(solution)/shard_map/ppermute | solution.py:316
  42.5 0.6 %collective-permute-start.20 = (bf16[32,768]{1,0:T(8,128)(2,1)S(1)}, bf16[32,768]{1,0:T(8,128)(2,1)S(1)}, u32[]{:S(2)}, u32[]{:S(2)}) collective-permute-start(bf16[32,768]{1,0:T(8,128)(2,1)S(1)} %get-tuple-element.44), channel_id=1, source_target_pairs={{0,8},{8,0},{16,24},{24,16},{1,9},{9,1},{17,25},{25,17},{2,10},{10... | collective-permute-start | bytes 147464 | tf_op jit(solution)/shard_map/ppermute | solution.py:316
  43.0 0.6 %collective-permute-done.18.refs_1_ = bf16[32,768]{1,0:T(8,128)(2,1)S(1)} collective-permute-done((bf16[32,768]{1,0:T(8,128)(2,1)S(1)}, bf16[32,768]{1,0:T(8,128)(2,1)S(1)}, u32[]{:S(2)}, u32[]{:S(2)}) %collective-permute-start.18) | collective-permute-done | bytes 49184 | tf_op jit(solution)/shard_map/ppermute | solution.py:316
  43.6 2.9 %collective-permute-done.19.refs_2_ = bf16[32,768]{1,0:T(8,128)(2,1)S(1)} collective-permute-done((bf16[32,768]{1,0:T(8,128)(2,1)S(1)}, bf16[32,768]{1,0:T(8,128)(2,1)S(1)}, u32[]{:S(2)}, u32[]{:S(2)}) %collective-permute-start.19) | collective-permute-done | bytes 49184 | tf_op jit(solution)/shard_map/ppermute | solution.py:316
  46.5 0.0 collective-permute-done.20.refs_3_
  46.5 1.4 %deal.1 = bf16[16,8,768]{2,1,0:T(8,128)(2,1)} custom-call(s32[1]{0:T(128)} %bitcast.me_ref, s32[8]{0:T(128)S(1)} %copy-done.3, f32[8]{0:T(128)S(1)} %copy-done.4, f32[8,128]{1,0:T(8,128)S(1)} %get-tuple-element.29.refs_1_.total_ref, bf16[32,768]{1,0:T(8,128)(2,1)S(1)} %get-tuple-element.41.refs_0_, bf16[32,768]{1,0:T(8,128)(2,1)S(1)} %collective-permute-done.18.refs_1_, ...), custom_call_target="tpu_custom_call" | custom-call | bytes 397312 | tf_op jit(solution)/shard_map/deal/pallas_call | solution.py:290
  (12 shorter events, 0.1 us)
Async XLA Ops:
  0.0 24.3 %collective-permute-start.3 = (bf16[12,128,768]{2,1,0:T(8,128)(2,1)}, bf16[12,128,768]{2,1,0:T(8,128)(2,1)S(1)}, u32[]{:S(2)}, u32[]{:S(2)}) collective-permute-start(bf16[12,128,768]{2,1,0:T(8,128)(2,1)} %refs_0_.2), channel_id=1, source_target_pairs={{0,1},{1,0},{2,3},{3,2},{4,5},{5,4},{6,7},{7,6},{8,9},{9,8},{10,11... | collective-permute-start | bytes 7077896 | tf_op jit(solution)/shard_map/ppermute | solution.py:321
  2.4 6.9 %collective-permute-start = (bf16[32,896]{1,0:T(8,128)(2,1)}, bf16[32,896]{1,0:T(8,128)(2,1)S(1)}, u32[]{:S(2)}, u32[]{:S(2)}) collective-permute-start(bf16[32,896]{1,0:T(8,128)(2,1)} %get-tuple-element.26), channel_id=1, source_target_pairs={{0,16},{8,24},{16,0},{24,8},{1,17},{9,25},{17,1},{25,9},{2,18},{10... | collective-permute-start | bytes 172040 | tf_op jit(solution)/shard_map/ppermute | solution.py:316
  4.9 5.5 %collective-permute-start.1 = (bf16[32,896]{1,0:T(8,128)(2,1)}, bf16[32,896]{1,0:T(8,128)(2,1)S(1)}, u32[]{:S(2)}, u32[]{:S(2)}) collective-permute-start(bf16[32,896]{1,0:T(8,128)(2,1)} %get-tuple-element.27), channel_id=1, source_target_pairs={{0,24},{8,16},{16,8},{24,0},{1,25},{9,17},{17,9},{25,1},{2,26},{10... | collective-permute-start | bytes 172040 | tf_op jit(solution)/shard_map/ppermute | solution.py:316
  6.4 4.4 %collective-permute-start.2 = (bf16[32,896]{1,0:T(8,128)(2,1)}, bf16[32,896]{1,0:T(8,128)(2,1)S(1)}, u32[]{:S(2)}, u32[]{:S(2)}) collective-permute-start(bf16[32,896]{1,0:T(8,128)(2,1)} %get-tuple-element.28), channel_id=1, source_target_pairs={{0,8},{8,0},{16,24},{24,16},{1,9},{9,1},{17,25},{25,17},{2,10},{10... | collective-permute-start | bytes 172040 | tf_op jit(solution)/shard_map/ppermute | solution.py:316
  6.5 0.8 %copy-start.2 = (bf16[32,896]{1,0:T(8,128)(2,1)S(1)}, bf16[32,896]{1,0:T(8,128)(2,1)}, u32[]{:S(2)}) copy-start(bf16[32,896]{1,0:T(8,128)(2,1)} %get-tuple-element.25.refs_0_) | copy-start | bytes 172036
  7.4 1.7 %copy-start = (bf16[12,128,768]{2,1,0:T(8,128)(2,1)S(1)}, bf16[12,128,768]{2,1,0:T(8,128)(2,1)}, u32[]{:S(2)}) copy-start(bf16[12,128,768]{2,1,0:T(8,128)(2,1)} %refs_0_.2) | copy-start | bytes 7077892
  9.2 10.9 %copy-start.1 = (bf16[768,768]{1,0:T(8,128)(2,1)S(1)}, bf16[768,768]{1,0:T(8,128)(2,1)}, u32[]{:S(2)}) copy-start(bf16[768,768]{1,0:T(8,128)(2,1)} %refs_0_.3) | copy-start | bytes 3538948
  10.9 5.2 %collective-permute-start.9 = (bf16[216,128]{1,0:T(8,128)(2,1)S(1)}, bf16[216,128]{1,0:T(8,128)(2,1)S(1)}, u32[]{:S(2)}, u32[]{:S(2)}) collective-permute-start(bf16[216,128]{1,0:T(8,128)(2,1)S(1)} %get-tuple-element.31.refs_0_), channel_id=1, source_target_pairs={{0,4},{1,5},{2,6},{3,7},{4,0},{5,1},{6,2},{7,3},{8,12},{9,13},{10,... | collective-permute-start | bytes 165896 | tf_op jit(solution)/shard_map/ppermute | solution.py:321
  13.5 4.2 %collective-permute-start.6 = (bf16[216,128]{1,0:T(8,128)(2,1)S(1)}, bf16[216,128]{1,0:T(8,128)(2,1)S(1)}, u32[]{:S(2)}, u32[]{:S(2)}) collective-permute-start(bf16[216,128]{1,0:T(8,128)(2,1)S(1)} %get-tuple-element.31.refs_0_), channel_id=1, source_target_pairs={{0,2},{1,3},{2,0},{3,1},{4,6},{5,7},{6,4},{7,5},{8,10},{9,11},{10,... | collective-permute-start | bytes 165896 | tf_op jit(solution)/shard_map/ppermute | solution.py:321
  15.1 5.1 %collective-permute-start.7 = (bf16[216,128]{1,0:T(8,128)(2,1)S(1)}, bf16[216,128]{1,0:T(8,128)(2,1)S(1)}, u32[]{:S(2)}, u32[]{:S(2)}) collective-permute-start(bf16[216,128]{1,0:T(8,128)(2,1)S(1)} %get-tuple-element.32), channel_id=1, source_target_pairs={{0,5},{1,4},{2,7},{3,6},{4,1},{5,0},{6,3},{7,2},{8,13},{9,12},{10,... | collective-permute-start | bytes 165896 | tf_op jit(solution)/shard_map/ppermute | solution.py:321
  15.1 5.3 %collective-permute-start.5 = (bf16[216,128]{1,0:T(8,128)(2,1)S(1)}, bf16[216,128]{1,0:T(8,128)(2,1)S(1)}, u32[]{:S(2)}, u32[]{:S(2)}) collective-permute-start(bf16[216,128]{1,0:T(8,128)(2,1)S(1)} %get-tuple-element.32), channel_id=1, source_target_pairs={{0,3},{1,2},{2,1},{3,0},{4,7},{5,6},{6,5},{7,4},{8,11},{9,10},{10,... | collective-permute-start | bytes 165896 | tf_op jit(solution)/shard_map/ppermute | solution.py:321
  16.1 4.4 %collective-permute-start.4 = (bf16[216,128]{1,0:T(8,128)(2,1)S(1)}, bf16[216,128]{1,0:T(8,128)(2,1)S(1)}, u32[]{:S(2)}, u32[]{:S(2)}) collective-permute-start(bf16[216,128]{1,0:T(8,128)(2,1)S(1)} %get-tuple-element.32), channel_id=1, source_target_pairs={{0,1},{1,0},{2,3},{3,2},{4,5},{5,4},{6,7},{7,6},{8,9},{9,8},{10,11... | collective-permute-start | bytes 165896 | tf_op jit(solution)/shard_map/ppermute | solution.py:321
  17.7 4.8 %collective-permute-start.10 = (bf16[216,128]{1,0:T(8,128)(2,1)S(1)}, bf16[216,128]{1,0:T(8,128)(2,1)S(1)}, u32[]{:S(2)}, u32[]{:S(2)}) collective-permute-start(bf16[216,128]{1,0:T(8,128)(2,1)S(1)} %collective-permute-done.9.refs_7_), channel_id=1, source_target_pairs={{0,2},{1,3},{2,0},{3,1},{4,6},{5,7},{6,4},{7,5},{8,10},{9,11},{10,... | collective-permute-start | bytes 165896 | tf_op jit(solution)/shard_map/ppermute | solution.py:321
  20.1 4.2 %collective-permute-start.8 = (bf16[216,128]{1,0:T(8,128)(2,1)S(1)}, bf16[216,128]{1,0:T(8,128)(2,1)S(1)}, u32[]{:S(2)}, u32[]{:S(2)}) collective-permute-start(bf16[216,128]{1,0:T(8,128)(2,1)S(1)} %collective-permute-done.7.refs_6_), channel_id=1, source_target_pairs={{0,2},{1,3},{2,0},{3,1},{4,6},{5,7},{6,4},{7,5},{8,10},{9,11},{10,... | collective-permute-start | bytes 165896 | tf_op jit(solution)/shard_map/ppermute | solution.py:321
  20.4 26.1 %copy-start.3 = (s32[8]{0:T(128)S(1)}, s32[8]{0:T(128)}, u32[]{:S(2)}) copy-start(s32[8]{0:T(128)} %target_ref.1) | copy-start | bytes 100
  20.4 26.1 %copy-start.4 = (f32[8]{0:T(128)S(1)}, f32[8]{0:T(128)}, u32[]{:S(2)}) copy-start(f32[8]{0:T(128)} %weights_ref.1) | copy-start | bytes 100
  28.0 6.3 %collective-permute-start.11 = (bf16[32,768]{1,0:T(8,128)(2,1)S(1)}, bf16[32,768]{1,0:T(8,128)(2,1)S(1)}, u32[]{:S(2)}, u32[]{:S(2)}) collective-permute-start(bf16[32,768]{1,0:T(8,128)(2,1)S(1)} %get-tuple-element.34), channel_id=1, source_target_pairs={{0,4},{1,5},{2,6},{3,7},{4,0},{5,1},{6,2},{7,3},{8,12},{9,13},{10,... | collective-permute-start | bytes 147464 | tf_op jit(solution)/shard_map/ppermute | solution.py:321
  29.7 7.0 %collective-permute-start.12 = (bf16[32,768]{1,0:T(8,128)(2,1)S(1)}, bf16[32,768]{1,0:T(8,128)(2,1)S(1)}, u32[]{:S(2)}, u32[]{:S(2)}) collective-permute-start(bf16[32,768]{1,0:T(8,128)(2,1)S(1)} %get-tuple-element.35), channel_id=1, source_target_pairs={{0,5},{1,4},{2,7},{3,6},{4,1},{5,0},{6,3},{7,2},{8,13},{9,12},{10,... | collective-permute-start | bytes 147464 | tf_op jit(solution)/shard_map/ppermute | solution.py:321
  29.7 7.0 %collective-permute-start.13 = (bf16[32,768]{1,0:T(8,128)(2,1)S(1)}, bf16[32,768]{1,0:T(8,128)(2,1)S(1)}, u32[]{:S(2)}, u32[]{:S(2)}) collective-permute-start(bf16[32,768]{1,0:T(8,128)(2,1)S(1)} %get-tuple-element.36), channel_id=1, source_target_pairs={{0,6},{1,7},{2,4},{3,5},{4,2},{5,3},{6,0},{7,1},{8,14},{9,15},{10,... | collective-permute-start | bytes 147464 | tf_op jit(solution)/shard_map/ppermute | solution.py:321
  32.4 5.5 %collective-permute-start.14 = (bf16[32,768]{1,0:T(8,128)(2,1)S(1)}, bf16[32,768]{1,0:T(8,128)(2,1)S(1)}, u32[]{:S(2)}, u32[]{:S(2)}) collective-permute-start(bf16[32,768]{1,0:T(8,128)(2,1)S(1)} %get-tuple-element.37), channel_id=1, source_target_pairs={{0,7},{1,6},{2,5},{3,4},{4,3},{5,2},{6,1},{7,0},{8,15},{9,14},{10,... | collective-permute-start | bytes 147464 | tf_op jit(solution)/shard_map/ppermute | solution.py:321
  34.3 5.1 %collective-permute-start.15 = (bf16[32,768]{1,0:T(8,128)(2,1)S(1)}, bf16[32,768]{1,0:T(8,128)(2,1)S(1)}, u32[]{:S(2)}, u32[]{:S(2)}) collective-permute-start(bf16[32,768]{1,0:T(8,128)(2,1)S(1)} %get-tuple-element.38), channel_id=1, source_target_pairs={{0,2},{1,3},{2,0},{3,1},{4,6},{5,7},{6,4},{7,5},{8,10},{9,11},{10,... | collective-permute-start | bytes 147464 | tf_op jit(solution)/shard_map/ppermute | solution.py:321
  34.3 5.1 %collective-permute-start.16 = (bf16[32,768]{1,0:T(8,128)(2,1)S(1)}, bf16[32,768]{1,0:T(8,128)(2,1)S(1)}, u32[]{:S(2)}, u32[]{:S(2)}) collective-permute-start(bf16[32,768]{1,0:T(8,128)(2,1)S(1)} %get-tuple-element.39), channel_id=1, source_target_pairs={{0,3},{1,2},{2,1},{3,0},{4,7},{5,6},{6,5},{7,4},{8,11},{9,10},{10,... | collective-permute-start | bytes 147464 | tf_op jit(solution)/shard_map/ppermute | solution.py:321
  36.7 2.7 %collective-permute-start.17 = (bf16[32,768]{1,0:T(8,128)(2,1)S(1)}, bf16[32,768]{1,0:T(8,128)(2,1)S(1)}, u32[]{:S(2)}, u32[]{:S(2)}) collective-permute-start(bf16[32,768]{1,0:T(8,128)(2,1)S(1)} %get-tuple-element.40), channel_id=1, source_target_pairs={{0,1},{1,0},{2,3},{3,2},{4,5},{5,4},{6,7},{7,6},{8,9},{9,8},{10,11... | collective-permute-start | bytes 147464 | tf_op jit(solution)/shard_map/ppermute | solution.py:321
  39.5 4.2 %collective-permute-start.18 = (bf16[32,768]{1,0:T(8,128)(2,1)S(1)}, bf16[32,768]{1,0:T(8,128)(2,1)S(1)}, u32[]{:S(2)}, u32[]{:S(2)}) collective-permute-start(bf16[32,768]{1,0:T(8,128)(2,1)S(1)} %get-tuple-element.42), channel_id=1, source_target_pairs={{0,16},{8,24},{16,0},{24,8},{1,17},{9,25},{17,1},{25,9},{2,18},{10... | collective-permute-start | bytes 147464 | tf_op jit(solution)/shard_map/ppermute | solution.py:316
  41.1 5.4 %collective-permute-start.19 = (bf16[32,768]{1,0:T(8,128)(2,1)S(1)}, bf16[32,768]{1,0:T(8,128)(2,1)S(1)}, u32[]{:S(2)}, u32[]{:S(2)}) collective-permute-start(bf16[32,768]{1,0:T(8,128)(2,1)S(1)} %get-tuple-element.43), channel_id=1, source_target_pairs={{0,24},{8,16},{16,8},{24,0},{1,25},{9,17},{17,9},{25,1},{2,26},{10... | collective-permute-start | bytes 147464 | tf_op jit(solution)/shard_map/ppermute | solution.py:316
  42.5 4.1 %collective-permute-start.20 = (bf16[32,768]{1,0:T(8,128)(2,1)S(1)}, bf16[32,768]{1,0:T(8,128)(2,1)S(1)}, u32[]{:S(2)}, u32[]{:S(2)}) collective-permute-start(bf16[32,768]{1,0:T(8,128)(2,1)S(1)} %get-tuple-element.44), channel_id=1, source_target_pairs={{0,8},{8,0},{16,24},{24,16},{1,9},{9,1},{17,25},{25,17},{2,10},{10... | collective-permute-start | bytes 147464 | tf_op jit(solution)/shard_map/ppermute | solution.py:316

commit v12 on v11

--- a/solution.py
+++ b/solution.py
@@ -104,7 +104,7 @@
 
 
 def merge_kernel(order, keep, cap, orbitals, core_ref, when, *refs):
-    ins, (same_ref, other_ref, weight_ref, pick_ref) = refs[: len(order)], refs[len(order) :]
+    ins, (same_ref, other_ref, same2_ref, other2_ref, weight_ref, pick_ref) = refs[: len(order)], refs[len(order) :]
     half = keep // 2
     rows = ins[0].shape[0] // cap
     slab = half * rows
@@ -138,6 +138,8 @@
                 out[at : at + rows, :] = block[:, c * LANES : (c + 1) * LANES].astype(BF16)
         tail = [p[i * chunks : (i + 1) * chunks] for i in range(2) for p in picked]
         out[chunks * slab :, :] = jnp.concatenate(tail, axis=0).astype(BF16)
+    same2_ref[...] = same_ref[...]
+    other2_ref[...] = other_ref[...]
 
 
 def power(size):
@@ -155,6 +157,10 @@
     chips = n // 2
     far = list(range(chips // 2, chips)) + list(range(1, chips // 2))
     return [(0, 0)] + [(s, e) for s in far for e in range(2)] + [(0, 1)]
+
+
+def after_kernel(source_ref, when_ref, out_ref):
+    out_ref[...] = source_ref[...]
 
 
 def arrivals(n):
@@ -366,9 +372,9 @@
     )
     routed = [to_list(routed[s], s) if s else kept for s in order]
     payload = shape((chunks * slab + 2 * half * chunks, LANES), BF16)
-    same, other, weight_sum, pick = call(
+    same, other, same2, other2, weight_sum, pick = call(
         functools.partial(merge_kernel, order, keep, cap, orbitals),
-        [payload, payload, shape((8, LANES), F32), shape((groups * keep, LANES), F32)],
+        [payload] * 4 + [shape((8, LANES), F32), shape((groups * keep, LANES), F32)],
         [core],
         [own],
         routed,
@@ -384,14 +390,21 @@
         [pltpu.SemaphoreType.DMA((1,))],
         "hold",
     )
+    relayed = {leading(s, n // 2) for s, _ in hops(n) if leading(s, n // 2) != s}
     gathered = {}
-    for s, e in arrivals(n):
-        if leading(s, n // 2) == s:
+    for s, e in hops(n):
+        if s in relayed:
             gathered[s, e] = to_block(other if e else same, s, e)
-    for s, e in arrivals(n):
+    for s, e in hops(n):
+        if leading(s, n // 2) == s and s not in relayed and (s, e) != (0, 1):
+            gathered[s, e] = to_block(other2 if e else same2, s, e)
+    for s, e in hops(n):
         top = leading(s, n // 2)
         if top != s:
             gathered[s, e] = to_block(gathered[top, e], s ^ top, 0)
+    late = gathered.get((1, 1), same2)
+    (last,) = call(after_kernel, [payload], [], [], [other2, late], [], "after")
+    gathered[0, 1] = to_block(last, 0, 1)
     gathered = [gathered[hop] for hop in arrivals(n)]
     held = F32 if rows % 16 else BF16
     parts = call(

time: 48.2 us -> 48.2 us (level)
  waiting for transfers between devices: 15.7 us -> 14.6 us
  starting transfers between devices: 22 us -> 23 us
    ppermute x15, waiting for transfers between devices: 10.7 us -> 9.45 us  [to_block(): lax.ppermute(x, 'blk', [(i, 2 * moved(i // 2, s, n // 2, 1) + (i % 2 ^ e)...]
    ppermute x15, starting transfers between devices: 14.3 us -> 15.3 us  [to_block(): lax.ppermute(x, 'blk', [(i, 2 * moved(i // 2, s, n // 2, 1) + (i % 2 ^ e)...]
    pallas_call x8 -> x9, Pallas kernels: 7.68 us -> 7.72 us  [call(): pl.pallas_call(kernel, out_shape=outs, in_specs=[smem] * len(scalars) + [...]
where the time goes in v12:
time: 48.2 us; the launch traced here: 48 us
  starting transfers between devices  23 us (48%)
  waiting for transfers between devices  14.6 us (30%)
  Pallas kernels  7.72 us (16%)
  local copies, waits for them, and re-layouts  2.5 us (5%)
    ppermute x15, starting transfers between devices, to_block(): lax.ppermute(x, 'blk', [(i, 2 * moved(i // 2, s, n // 2, 1) + (i % 2 ^ e)...  15.3 us
    ppermute x15, waiting for transfers between devices, to_block(): lax.ppermute(x, 'blk', [(i, 2 * moved(i // 2, s, n // 2, 1) + (i % 2 ^ e)...  9.45 us
    pallas_call x9, Pallas kernels, call(): pl.pallas_call(kernel, out_shape=outs, in_specs=[smem] * len(scalars) + [...  7.72 us
    ppermute x6, starting transfers between devices, to_list(): lax.ppermute(x, 'grp', [(i, moved(i, s, groups, 1)) for i in range(groups)])  7.68 us
    ppermute x6, waiting for transfers between devices, to_list(): lax.ppermute(x, 'grp', [(i, moved(i, s, groups, 1)) for i in range(groups)])  5.14 us
    unnamed x10, local copies, waits for them, and re-layouts  2.5 us
  transfers between devices with their start and end apart: 21, of which 12 were waited for; matrix products, arithmetic and copies ran while one was open for 0% of the time, Pallas kernels for 5%

profile of v12, /device:TPU:0, one launch (start us, length us, event | category | flops | bytes accessed | tf_op | source)
XLA Modules:
  0.0 48.0 jit_solution(16498297772239953016)
XLA Ops:
  0.0 0.5 collective-permute-start.3
  0.5 1.9 %route.1 = (bf16[32,896]{1,0:T(8,128)(2,1)}, bf16[32,896]{1,0:T(8,128)(2,1)}, bf16[32,896]{1,0:T(8,128)(2,1)}, bf16[32,896]{1,0:T(8,128)(2,1)}) custom-call(s32[1]{0:T(128)} %bitcast.me_ref, s32[8]{0:T(128)} %target_ref.1, f32[8]{0:T(128)} %weights_ref.1, bf16[16,8,768]{2,1,0:T(8,128)(2,1)} %walkers_any.1, f32[8,12]{1,0:T(8,128)} %fields_any.1, ...), custom_call_target="tpu_custom_call" | custom-call | bytes 229376 | tf_op jit(solution)/shard_map/route/pallas_call | solution.py:296
  2.4 2.6 %collective-permute-start = (bf16[32,896]{1,0:T(8,128)(2,1)}, bf16[32,896]{1,0:T(8,128)(2,1)S(1)}, u32[]{:S(2)}, u32[]{:S(2)}) collective-permute-start(bf16[32,896]{1,0:T(8,128)(2,1)} %get-tuple-element.28), channel_id=1, source_target_pairs={{0,16},{8,24},{16,0},{24,8},{1,17},{9,25},{17,1},{25,9},{2,18},{10... | collective-permute-start | bytes 172040 | tf_op jit(solution)/shard_map/ppermute | solution.py:322
  5.0 1.4 %collective-permute-start.1 = (bf16[32,896]{1,0:T(8,128)(2,1)}, bf16[32,896]{1,0:T(8,128)(2,1)S(1)}, u32[]{:S(2)}, u32[]{:S(2)}) collective-permute-start(bf16[32,896]{1,0:T(8,128)(2,1)} %get-tuple-element.29), channel_id=1, source_target_pairs={{0,24},{8,16},{16,8},{24,0},{1,25},{9,17},{17,9},{25,1},{2,26},{10... | collective-permute-start | bytes 172040 | tf_op jit(solution)/shard_map/ppermute | solution.py:322
  6.4 0.1 collective-permute-start.2
  6.5 0.8 %copy-done.2 = bf16[32,896]{1,0:T(8,128)(2,1)S(1)} copy-done((bf16[32,896]{1,0:T(8,128)(2,1)S(1)}, bf16[32,896]{1,0:T(8,128)(2,1)}, u32[]{:S(2)}) %copy-start.2) | copy-done | bytes 57368
  7.4 0.0 copy-start
  7.4 1.7 %copy-done = bf16[12,128,768]{2,1,0:T(8,128)(2,1)S(1)} copy-done((bf16[12,128,768]{2,1,0:T(8,128)(2,1)S(1)}, bf16[12,128,768]{2,1,0:T(8,128)(2,1)}, u32[]{:S(2)}) %copy-start) | copy-done | bytes 2359320
  9.0 0.2 stage.1.when.own_ref
  9.2 0.0 copy-start.1
  9.2 0.0 collective-permute-done.refs_1_
  9.2 1.2 %collective-permute-done.1.refs_2_ = bf16[32,896]{1,0:T(8,128)(2,1)S(1)} collective-permute-done((bf16[32,896]{1,0:T(8,128)(2,1)}, bf16[32,896]{1,0:T(8,128)(2,1)S(1)}, u32[]{:S(2)}, u32[]{:S(2)}) %collective-permute-start.1) | collective-permute-done | bytes 57376 | tf_op jit(solution)/shard_map/ppermute | solution.py:322
  10.5 0.3 collective-permute-done.2.refs_3_
  10.8 0.1 merge.1
  10.9 1.5 %collective-permute-start.7 = (bf16[216,128]{1,0:T(8,128)(2,1)S(1)}, bf16[216,128]{1,0:T(8,128)(2,1)S(1)}, u32[]{:S(2)}, u32[]{:S(2)}) collective-permute-start(bf16[216,128]{1,0:T(8,128)(2,1)S(1)} %get-tuple-element.35), channel_id=1, source_target_pairs={{0,5},{1,4},{2,7},{3,6},{4,1},{5,0},{6,3},{7,2},{8,13},{9,12},{10,... | collective-permute-start | bytes 165896 | tf_op jit(solution)/shard_map/ppermute | solution.py:327
  12.4 1.3 %collective-permute-start.9 = (bf16[216,128]{1,0:T(8,128)(2,1)S(1)}, bf16[216,128]{1,0:T(8,128)(2,1)S(1)}, u32[]{:S(2)}, u32[]{:S(2)}) collective-permute-start(bf16[216,128]{1,0:T(8,128)(2,1)S(1)} %get-tuple-element.36), channel_id=1, source_target_pairs={{0,4},{1,5},{2,6},{3,7},{4,0},{5,1},{6,2},{7,3},{8,12},{9,13},{10,... | collective-permute-start | bytes 165896 | tf_op jit(solution)/shard_map/ppermute | solution.py:327
  13.6 1.3 %collective-permute-start.4 = (bf16[216,128]{1,0:T(8,128)(2,1)S(1)}, bf16[216,128]{1,0:T(8,128)(2,1)S(1)}, u32[]{:S(2)}, u32[]{:S(2)}) collective-permute-start(bf16[216,128]{1,0:T(8,128)(2,1)S(1)} %get-tuple-element.34.source_ref), channel_id=1, source_target_pairs={{0,3},{1,2},{2,1},{3,0},{4,7},{5,6},{6,5},{7,4},{8,11},{9,10},{10,... | collective-permute-start | bytes 165896 | tf_op jit(solution)/shard_map/ppermute | solution.py:327
  14.9 0.4 collective-permute-start.6
  15.3 0.4 collective-permute-done.7.refs_6_
  15.8 2.6 %collective-permute-start.8 = (bf16[216,128]{1,0:T(8,128)(2,1)S(1)}, bf16[216,128]{1,0:T(8,128)(2,1)S(1)}, u32[]{:S(2)}, u32[]{:S(2)}) collective-permute-start(bf16[216,128]{1,0:T(8,128)(2,1)S(1)} %collective-permute-done.7.refs_6_), channel_id=1, source_target_pairs={{0,2},{1,3},{2,0},{3,1},{4,6},{5,7},{6,4},{7,5},{8,10},{9,11},{10,... | collective-permute-start | bytes 165896 | tf_op jit(solution)/shard_map/ppermute | solution.py:327
  18.4 1.2 %collective-permute-done.9.refs_7_ = bf16[216,128]{1,0:T(8,128)(2,1)S(1)} collective-permute-done((bf16[216,128]{1,0:T(8,128)(2,1)S(1)}, bf16[216,128]{1,0:T(8,128)(2,1)S(1)}, u32[]{:S(2)}, u32[]{:S(2)}) %collective-permute-start.9) | collective-permute-done | bytes 55328 | tf_op jit(solution)/shard_map/ppermute | solution.py:327
  19.7 0.1 collective-permute-start.5
  19.8 0.3 hold.1.body_ref
  20.0 0.0 copy-start.3
  20.1 0.0 copy-start.4
  20.1 0.4 collective-permute-done.6.refs_3_
  20.5 0.9 %collective-permute-done.8.refs_4_ = bf16[216,128]{1,0:T(8,128)(2,1)S(1)} collective-permute-done((bf16[216,128]{1,0:T(8,128)(2,1)S(1)}, bf16[216,128]{1,0:T(8,128)(2,1)S(1)}, u32[]{:S(2)}, u32[]{:S(2)}) %collective-permute-start.8) | collective-permute-done | bytes 55328 | tf_op jit(solution)/shard_map/ppermute | solution.py:327
  21.4 2.4 %collective-permute-done.10.refs_5_ = bf16[216,128]{1,0:T(8,128)(2,1)S(1)} collective-permute-done((bf16[216,128]{1,0:T(8,128)(2,1)S(1)}, bf16[216,128]{1,0:T(8,128)(2,1)S(1)}, u32[]{:S(2)}, u32[]{:S(2)}) %collective-permute-start.10) | collective-permute-done | bytes 55328 | tf_op jit(solution)/shard_map/ppermute | solution.py:327
  23.8 3.7 %fock.1 = (bf16[32,768]{1,0:T(8,128)(2,1)S(1)}, bf16[32,768]{1,0:T(8,128)(2,1)S(1)}, bf16[32,768]{1,0:T(8,128)(2,1)S(1)}, bf16[32,768]{1,0:T(8,128)(2,1)S(1)}, b...) custom-call(s32[1]{0:T(128)} %bitcast.1.blk_ref, ...), custom_call_target="tpu_custom_call" | custom-call | flops 2717908992 | bytes 6733824 | tf_op jit(solution)/shard_map/fock/pallas_call | solution.py:296
  27.6 2.4 %collective-permute-start.11 = (bf16[32,768]{1,0:T(8,128)(2,1)S(1)}, bf16[32,768]{1,0:T(8,128)(2,1)S(1)}, u32[]{:S(2)}, u32[]{:S(2)}) collective-permute-start(bf16[32,768]{1,0:T(8,128)(2,1)S(1)} %get-tuple-element.38), channel_id=1, source_target_pairs={{0,4},{1,5},{2,6},{3,7},{4,0},{5,1},{6,2},{7,3},{8,12},{9,13},{10,... | collective-permute-start | bytes 147464 | tf_op jit(solution)/shard_map/ppermute | solution.py:327
  30.0 0.0 collective-permute-start.12
  30.0 2.5 %collective-permute-start.13 = (bf16[32,768]{1,0:T(8,128)(2,1)S(1)}, bf16[32,768]{1,0:T(8,128)(2,1)S(1)}, u32[]{:S(2)}, u32[]{:S(2)}) collective-permute-start(bf16[32,768]{1,0:T(8,128)(2,1)S(1)} %get-tuple-element.40), channel_id=1, source_target_pairs={{0,6},{1,7},{2,4},{3,5},{4,2},{5,3},{6,0},{7,1},{8,14},{9,15},{10,... | collective-permute-start | bytes 147464 | tf_op jit(solution)/shard_map/ppermute | solution.py:327
  32.5 1.3 %collective-permute-start.14 = (bf16[32,768]{1,0:T(8,128)(2,1)S(1)}, bf16[32,768]{1,0:T(8,128)(2,1)S(1)}, u32[]{:S(2)}, u32[]{:S(2)}) collective-permute-start(bf16[32,768]{1,0:T(8,128)(2,1)S(1)} %get-tuple-element.41), channel_id=1, source_target_pairs={{0,7},{1,6},{2,5},{3,4},{4,3},{5,2},{6,1},{7,0},{8,15},{9,14},{10,... | collective-permute-start | bytes 147464 | tf_op jit(solution)/shard_map/ppermute | solution.py:327
  33.8 0.0 collective-permute-start.15
  33.8 0.0 collective-permute-done.11.refs_1_
  33.8 1.4 %collective-permute-start.16 = (bf16[32,768]{1,0:T(8,128)(2,1)S(1)}, bf16[32,768]{1,0:T(8,128)(2,1)S(1)}, u32[]{:S(2)}, u32[]{:S(2)}) collective-permute-start(bf16[32,768]{1,0:T(8,128)(2,1)S(1)} %get-tuple-element.43), channel_id=1, source_target_pairs={{0,3},{1,2},{2,1},{3,0},{4,7},{5,6},{6,5},{7,4},{8,11},{9,10},{10,... | collective-permute-start | bytes 147464 | tf_op jit(solution)/shard_map/ppermute | solution.py:327
  35.3 1.5 %collective-permute-done.12.refs_2_ = bf16[32,768]{1,0:T(8,128)(2,1)S(1)} collective-permute-done((bf16[32,768]{1,0:T(8,128)(2,1)S(1)}, bf16[32,768]{1,0:T(8,128)(2,1)S(1)}, u32[]{:S(2)}, u32[]{:S(2)}) %collective-permute-start.12) | collective-permute-done | bytes 49184 | tf_op jit(solution)/shard_map/ppermute | solution.py:327
  36.8 1.2 %collective-permute-done.14.refs_4_ = bf16[32,768]{1,0:T(8,128)(2,1)S(1)} collective-permute-done((bf16[32,768]{1,0:T(8,128)(2,1)S(1)}, bf16[32,768]{1,0:T(8,128)(2,1)S(1)}, u32[]{:S(2)}, u32[]{:S(2)}) %collective-permute-start.14) | collective-permute-done | bytes 49184 | tf_op jit(solution)/shard_map/ppermute | solution.py:327
  38.0 1.3 %collective-permute-done.15.refs_5_ = bf16[32,768]{1,0:T(8,128)(2,1)S(1)} collective-permute-done((bf16[32,768]{1,0:T(8,128)(2,1)S(1)}, bf16[32,768]{1,0:T(8,128)(2,1)S(1)}, u32[]{:S(2)}, u32[]{:S(2)}) %collective-permute-start.15) | collective-permute-done | bytes 49184 | tf_op jit(solution)/shard_map/ppermute | solution.py:327
  39.3 0.0 collective-permute-done.16.refs_6_
  39.3 0.1 sum.1
  39.4 1.6 %collective-permute-start.18 = (bf16[32,768]{1,0:T(8,128)(2,1)S(1)}, bf16[32,768]{1,0:T(8,128)(2,1)S(1)}, u32[]{:S(2)}, u32[]{:S(2)}) collective-permute-start(bf16[32,768]{1,0:T(8,128)(2,1)S(1)} %get-tuple-element.46), channel_id=1, source_target_pairs={{0,16},{8,24},{16,0},{24,8},{1,17},{9,25},{17,1},{25,9},{2,18},{10... | collective-permute-start | bytes 147464 | tf_op jit(solution)/shard_map/ppermute | solution.py:322
  41.0 1.4 %collective-permute-start.19 = (bf16[32,768]{1,0:T(8,128)(2,1)S(1)}, bf16[32,768]{1,0:T(8,128)(2,1)S(1)}, u32[]{:S(2)}, u32[]{:S(2)}) collective-permute-start(bf16[32,768]{1,0:T(8,128)(2,1)S(1)} %get-tuple-element.47), channel_id=1, source_target_pairs={{0,24},{8,16},{16,8},{24,0},{1,25},{9,17},{17,9},{25,1},{2,26},{10... | collective-permute-start | bytes 147464 | tf_op jit(solution)/shard_map/ppermute | solution.py:322
  42.4 0.5 %collective-permute-start.20 = (bf16[32,768]{1,0:T(8,128)(2,1)S(1)}, bf16[32,768]{1,0:T(8,128)(2,1)S(1)}, u32[]{:S(2)}, u32[]{:S(2)}) collective-permute-start(bf16[32,768]{1,0:T(8,128)(2,1)S(1)} %get-tuple-element.48), channel_id=1, source_target_pairs={{0,8},{8,0},{16,24},{24,16},{1,9},{9,1},{17,25},{25,17},{2,10},{10... | collective-permute-start | bytes 147464 | tf_op jit(solution)/shard_map/ppermute | solution.py:322
  42.9 0.6 %collective-permute-done.18.refs_1_ = bf16[32,768]{1,0:T(8,128)(2,1)S(1)} collective-permute-done((bf16[32,768]{1,0:T(8,128)(2,1)S(1)}, bf16[32,768]{1,0:T(8,128)(2,1)S(1)}, u32[]{:S(2)}, u32[]{:S(2)}) %collective-permute-start.18) | collective-permute-done | bytes 49184 | tf_op jit(solution)/shard_map/ppermute | solution.py:322
  43.5 3.0 %collective-permute-done.19.refs_2_ = bf16[32,768]{1,0:T(8,128)(2,1)S(1)} collective-permute-done((bf16[32,768]{1,0:T(8,128)(2,1)S(1)}, bf16[32,768]{1,0:T(8,128)(2,1)S(1)}, u32[]{:S(2)}, u32[]{:S(2)}) %collective-permute-start.19) | collective-permute-done | bytes 49184 | tf_op jit(solution)/shard_map/ppermute | solution.py:322
  46.5 0.0 collective-permute-done.20.refs_3_
  46.5 1.4 %deal.1 = bf16[16,8,768]{2,1,0:T(8,128)(2,1)} custom-call(s32[1]{0:T(128)} %bitcast.me_ref, s32[8]{0:T(128)S(1)} %copy-done.3, f32[8]{0:T(128)S(1)} %copy-done.4, f32[8,128]{1,0:T(8,128)S(1)} %get-tuple-element.31.refs_1_.total_ref, bf16[32,768]{1,0:T(8,128)(2,1)S(1)} %get-tuple-element.45.refs_0_, bf16[32,768]{1,0:T(8,128)(2,1)S(1)} %collective-permute-done.18.refs_1_, ...), custom_call_target="tpu_custom_call" | custom-call | bytes 397312 | tf_op jit(solution)/shard_map/deal/pallas_call | solution.py:296
  (13 shorter events, 0.1 us)
Async XLA Ops:
  0.0 23.8 %collective-permute-start.3 = (bf16[12,128,768]{2,1,0:T(8,128)(2,1)}, bf16[12,128,768]{2,1,0:T(8,128)(2,1)S(1)}, u32[]{:S(2)}, u32[]{:S(2)}) collective-permute-start(bf16[12,128,768]{2,1,0:T(8,128)(2,1)} %refs_0_.2), channel_id=1, source_target_pairs={{0,1},{1,0},{2,3},{3,2},{4,5},{5,4},{6,7},{7,6},{8,9},{9,8},{10,11... | collective-permute-start | bytes 7077896 | tf_op jit(solution)/shard_map/ppermute | solution.py:327
  2.4 6.9 %collective-permute-start = (bf16[32,896]{1,0:T(8,128)(2,1)}, bf16[32,896]{1,0:T(8,128)(2,1)S(1)}, u32[]{:S(2)}, u32[]{:S(2)}) collective-permute-start(bf16[32,896]{1,0:T(8,128)(2,1)} %get-tuple-element.28), channel_id=1, source_target_pairs={{0,16},{8,24},{16,0},{24,8},{1,17},{9,25},{17,1},{25,9},{2,18},{10... | collective-permute-start | bytes 172040 | tf_op jit(solution)/shard_map/ppermute | solution.py:322
  5.0 5.5 %collective-permute-start.1 = (bf16[32,896]{1,0:T(8,128)(2,1)}, bf16[32,896]{1,0:T(8,128)(2,1)S(1)}, u32[]{:S(2)}, u32[]{:S(2)}) collective-permute-start(bf16[32,896]{1,0:T(8,128)(2,1)} %get-tuple-element.29), channel_id=1, source_target_pairs={{0,24},{8,16},{16,8},{24,0},{1,25},{9,17},{17,9},{25,1},{2,26},{10... | collective-permute-start | bytes 172040 | tf_op jit(solution)/shard_map/ppermute | solution.py:322
  6.4 4.4 %collective-permute-start.2 = (bf16[32,896]{1,0:T(8,128)(2,1)}, bf16[32,896]{1,0:T(8,128)(2,1)S(1)}, u32[]{:S(2)}, u32[]{:S(2)}) collective-permute-start(bf16[32,896]{1,0:T(8,128)(2,1)} %get-tuple-element.30), channel_id=1, source_target_pairs={{0,8},{8,0},{16,24},{24,16},{1,9},{9,1},{17,25},{25,17},{2,10},{10... | collective-permute-start | bytes 172040 | tf_op jit(solution)/shard_map/ppermute | solution.py:322
  6.5 0.8 %copy-start.2 = (bf16[32,896]{1,0:T(8,128)(2,1)S(1)}, bf16[32,896]{1,0:T(8,128)(2,1)}, u32[]{:S(2)}) copy-start(bf16[32,896]{1,0:T(8,128)(2,1)} %get-tuple-element.27.refs_0_) | copy-start | bytes 172036
  7.4 1.7 %copy-start = (bf16[12,128,768]{2,1,0:T(8,128)(2,1)S(1)}, bf16[12,128,768]{2,1,0:T(8,128)(2,1)}, u32[]{:S(2)}) copy-start(bf16[12,128,768]{2,1,0:T(8,128)(2,1)} %refs_0_.2) | copy-start | bytes 7077892
  9.2 10.6 %copy-start.1 = (bf16[768,768]{1,0:T(8,128)(2,1)S(1)}, bf16[768,768]{1,0:T(8,128)(2,1)}, u32[]{:S(2)}) copy-start(bf16[768,768]{1,0:T(8,128)(2,1)} %refs_0_.3) | copy-start | bytes 3538948
  10.9 4.9 %collective-permute-start.7 = (bf16[216,128]{1,0:T(8,128)(2,1)S(1)}, bf16[216,128]{1,0:T(8,128)(2,1)S(1)}, u32[]{:S(2)}, u32[]{:S(2)}) collective-permute-start(bf16[216,128]{1,0:T(8,128)(2,1)S(1)} %get-tuple-element.35), channel_id=1, source_target_pairs={{0,5},{1,4},{2,7},{3,6},{4,1},{5,0},{6,3},{7,2},{8,13},{9,12},{10,... | collective-permute-start | bytes 165896 | tf_op jit(solution)/shard_map/ppermute | solution.py:327
  12.4 7.3 %collective-permute-start.9 = (bf16[216,128]{1,0:T(8,128)(2,1)S(1)}, bf16[216,128]{1,0:T(8,128)(2,1)S(1)}, u32[]{:S(2)}, u32[]{:S(2)}) collective-permute-start(bf16[216,128]{1,0:T(8,128)(2,1)S(1)} %get-tuple-element.36), channel_id=1, source_target_pairs={{0,4},{1,5},{2,6},{3,7},{4,0},{5,1},{6,2},{7,3},{8,12},{9,13},{10,... | collective-permute-start | bytes 165896 | tf_op jit(solution)/shard_map/ppermute | solution.py:327
  13.6 6.0 %collective-permute-start.4 = (bf16[216,128]{1,0:T(8,128)(2,1)S(1)}, bf16[216,128]{1,0:T(8,128)(2,1)S(1)}, u32[]{:S(2)}, u32[]{:S(2)}) collective-permute-start(bf16[216,128]{1,0:T(8,128)(2,1)S(1)} %get-tuple-element.34.source_ref), channel_id=1, source_target_pairs={{0,3},{1,2},{2,1},{3,0},{4,7},{5,6},{6,5},{7,4},{8,11},{9,10},{10,... | collective-permute-start | bytes 165896 | tf_op jit(solution)/shard_map/ppermute | solution.py:327
  14.9 5.6 %collective-permute-start.6 = (bf16[216,128]{1,0:T(8,128)(2,1)S(1)}, bf16[216,128]{1,0:T(8,128)(2,1)S(1)}, u32[]{:S(2)}, u32[]{:S(2)}) collective-permute-start(bf16[216,128]{1,0:T(8,128)(2,1)S(1)} %get-tuple-element.33.refs_0_), channel_id=1, source_target_pairs={{0,2},{1,3},{2,0},{3,1},{4,6},{5,7},{6,4},{7,5},{8,10},{9,11},{10,... | collective-permute-start | bytes 165896 | tf_op jit(solution)/shard_map/ppermute | solution.py:327
  15.8 5.7 %collective-permute-start.8 = (bf16[216,128]{1,0:T(8,128)(2,1)S(1)}, bf16[216,128]{1,0:T(8,128)(2,1)S(1)}, u32[]{:S(2)}, u32[]{:S(2)}) collective-permute-start(bf16[216,128]{1,0:T(8,128)(2,1)S(1)} %collective-permute-done.7.refs_6_), channel_id=1, source_target_pairs={{0,2},{1,3},{2,0},{3,1},{4,6},{5,7},{6,4},{7,5},{8,10},{9,11},{10,... | collective-permute-start | bytes 165896 | tf_op jit(solution)/shard_map/ppermute | solution.py:327
  19.7 4.2 %collective-permute-start.10 = (bf16[216,128]{1,0:T(8,128)(2,1)S(1)}, bf16[216,128]{1,0:T(8,128)(2,1)S(1)}, u32[]{:S(2)}, u32[]{:S(2)}) collective-permute-start(bf16[216,128]{1,0:T(8,128)(2,1)S(1)} %collective-permute-done.9.refs_7_), channel_id=1, source_target_pairs={{0,2},{1,3},{2,0},{3,1},{4,6},{5,7},{6,4},{7,5},{8,10},{9,11},{10,... | collective-permute-start | bytes 165896 | tf_op jit(solution)/shard_map/ppermute | solution.py:327
  19.7 4.1 %collective-permute-start.5 = (bf16[216,128]{1,0:T(8,128)(2,1)S(1)}, bf16[216,128]{1,0:T(8,128)(2,1)S(1)}, u32[]{:S(2)}, u32[]{:S(2)}) collective-permute-start(bf16[216,128]{1,0:T(8,128)(2,1)S(1)} %after.1), channel_id=1, source_target_pairs={{0,1},{1,0},{2,3},{3,2},{4,5},{5,4},{6,7},{7,6},{8,9},{9,8},{10,11... | collective-permute-start | bytes 165896 | tf_op jit(solution)/shard_map/ppermute | solution.py:327
  20.0 26.5 %copy-start.3 = (s32[8]{0:T(128)S(1)}, s32[8]{0:T(128)}, u32[]{:S(2)}) copy-start(s32[8]{0:T(128)} %target_ref.1) | copy-start | bytes 100
  20.1 26.5 %copy-start.4 = (f32[8]{0:T(128)S(1)}, f32[8]{0:T(128)}, u32[]{:S(2)}) copy-start(f32[8]{0:T(128)} %weights_ref.1) | copy-start | bytes 100
  27.6 6.3 %collective-permute-start.11 = (bf16[32,768]{1,0:T(8,128)(2,1)S(1)}, bf16[32,768]{1,0:T(8,128)(2,1)S(1)}, u32[]{:S(2)}, u32[]{:S(2)}) collective-permute-start(bf16[32,768]{1,0:T(8,128)(2,1)S(1)} %get-tuple-element.38), channel_id=1, source_target_pairs={{0,4},{1,5},{2,6},{3,7},{4,0},{5,1},{6,2},{7,3},{8,12},{9,13},{10,... | collective-permute-start | bytes 147464 | tf_op jit(solution)/shard_map/ppermute | solution.py:327
  30.0 6.8 %collective-permute-start.12 = (bf16[32,768]{1,0:T(8,128)(2,1)S(1)}, bf16[32,768]{1,0:T(8,128)(2,1)S(1)}, u32[]{:S(2)}, u32[]{:S(2)}) collective-permute-start(bf16[32,768]{1,0:T(8,128)(2,1)S(1)} %get-tuple-element.39), channel_id=1, source_target_pairs={{0,5},{1,4},{2,7},{3,6},{4,1},{5,0},{6,3},{7,2},{8,13},{9,12},{10,... | collective-permute-start | bytes 147464 | tf_op jit(solution)/shard_map/ppermute | solution.py:327
  30.0 6.8 %collective-permute-start.13 = (bf16[32,768]{1,0:T(8,128)(2,1)S(1)}, bf16[32,768]{1,0:T(8,128)(2,1)S(1)}, u32[]{:S(2)}, u32[]{:S(2)}) collective-permute-start(bf16[32,768]{1,0:T(8,128)(2,1)S(1)} %get-tuple-element.40), channel_id=1, source_target_pairs={{0,6},{1,7},{2,4},{3,5},{4,2},{5,3},{6,0},{7,1},{8,14},{9,15},{10,... | collective-permute-start | bytes 147464 | tf_op jit(solution)/shard_map/ppermute | solution.py:327
  32.5 5.5 %collective-permute-start.14 = (bf16[32,768]{1,0:T(8,128)(2,1)S(1)}, bf16[32,768]{1,0:T(8,128)(2,1)S(1)}, u32[]{:S(2)}, u32[]{:S(2)}) collective-permute-start(bf16[32,768]{1,0:T(8,128)(2,1)S(1)} %get-tuple-element.41), channel_id=1, source_target_pairs={{0,7},{1,6},{2,5},{3,4},{4,3},{5,2},{6,1},{7,0},{8,15},{9,14},{10,... | collective-permute-start | bytes 147464 | tf_op jit(solution)/shard_map/ppermute | solution.py:327
  33.8 5.4 %collective-permute-start.15 = (bf16[32,768]{1,0:T(8,128)(2,1)S(1)}, bf16[32,768]{1,0:T(8,128)(2,1)S(1)}, u32[]{:S(2)}, u32[]{:S(2)}) collective-permute-start(bf16[32,768]{1,0:T(8,128)(2,1)S(1)} %get-tuple-element.42), channel_id=1, source_target_pairs={{0,2},{1,3},{2,0},{3,1},{4,6},{5,7},{6,4},{7,5},{8,10},{9,11},{10,... | collective-permute-start | bytes 147464 | tf_op jit(solution)/shard_map/ppermute | solution.py:327
  33.8 5.4 %collective-permute-start.16 = (bf16[32,768]{1,0:T(8,128)(2,1)S(1)}, bf16[32,768]{1,0:T(8,128)(2,1)S(1)}, u32[]{:S(2)}, u32[]{:S(2)}) collective-permute-start(bf16[32,768]{1,0:T(8,128)(2,1)S(1)} %get-tuple-element.43), channel_id=1, source_target_pairs={{0,3},{1,2},{2,1},{3,0},{4,7},{5,6},{6,5},{7,4},{8,11},{9,10},{10,... | collective-permute-start | bytes 147464 | tf_op jit(solution)/shard_map/ppermute | solution.py:327
  36.8 2.5 %collective-permute-start.17 = (bf16[32,768]{1,0:T(8,128)(2,1)S(1)}, bf16[32,768]{1,0:T(8,128)(2,1)S(1)}, u32[]{:S(2)}, u32[]{:S(2)}) collective-permute-start(bf16[32,768]{1,0:T(8,128)(2,1)S(1)} %get-tuple-element.44), channel_id=1, source_target_pairs={{0,1},{1,0},{2,3},{3,2},{4,5},{5,4},{6,7},{7,6},{8,9},{9,8},{10,11... | collective-permute-start | bytes 147464 | tf_op jit(solution)/shard_map/ppermute | solution.py:327
  39.4 4.2 %collective-permute-start.18 = (bf16[32,768]{1,0:T(8,128)(2,1)S(1)}, bf16[32,768]{1,0:T(8,128)(2,1)S(1)}, u32[]{:S(2)}, u32[]{:S(2)}) collective-permute-start(bf16[32,768]{1,0:T(8,128)(2,1)S(1)} %get-tuple-element.46), channel_id=1, source_target_pairs={{0,16},{8,24},{16,0},{24,8},{1,17},{9,25},{17,1},{25,9},{2,18},{10... | collective-permute-start | bytes 147464 | tf_op jit(solution)/shard_map/ppermute | solution.py:322
  41.0 5.5 %collective-permute-start.19 = (bf16[32,768]{1,0:T(8,128)(2,1)S(1)}, bf16[32,768]{1,0:T(8,128)(2,1)S(1)}, u32[]{:S(2)}, u32[]{:S(2)}) collective-permute-start(bf16[32,768]{1,0:T(8,128)(2,1)S(1)} %get-tuple-element.47), channel_id=1, source_target_pairs={{0,24},{8,16},{16,8},{24,0},{1,25},{9,17},{17,9},{25,1},{2,26},{10... | collective-permute-start | bytes 147464 | tf_op jit(solution)/shard_map/ppermute | solution.py:322
  42.4 4.1 %collective-permute-start.20 = (bf16[32,768]{1,0:T(8,128)(2,1)S(1)}, bf16[32,768]{1,0:T(8,128)(2,1)S(1)}, u32[]{:S(2)}, u32[]{:S(2)}) collective-permute-start(bf16[32,768]{1,0:T(8,128)(2,1)S(1)} %get-tuple-element.48), channel_id=1, source_target_pairs={{0,8},{8,0},{16,24},{24,16},{1,9},{9,1},{17,25},{25,17},{2,10},{10... | collective-permute-start | bytes 147464 | tf_op jit(solution)/shard_map/ppermute | solution.py:322

commit v13 on v12

--- a/solution.py
+++ b/solution.py
@@ -167,9 +167,23 @@
     return hops(n)[:1] + hops(n)[:0:-1]
 
 
-def leading(s, chips):
-    top = 1 << (s.bit_length() - 1) if s else 0
-    return top if power(chips) else s
+def leading(s, e, chips):
+    return 1 << (s.bit_length() - 1) if s and e and power(chips) else s
+
+
+def returns(n):
+    return [(s, e) for s, e in hops(n) if leading(s, e, n // 2) == s]
+
+
+def add_kernel(count, *refs):
+    outs = refs[len(refs) - 1 - count :]
+    ins = refs[: len(refs) - 1 - count]
+    total = ins[count][...].astype(F32)
+    for ref in ins[count + 1 :]:
+        total = total + ref[...].astype(F32)
+    outs[0][...] = total.astype(BF16)
+    for i in range(count):
+        outs[1 + i][...] = ins[i][...]
 
 
 def partner(blk, s, e, n, sign):
@@ -234,13 +248,14 @@
 
 
 def sum_kernel(n, keep, cap, groups, core_ref, pick_ref, *refs):
-    ins, outs = refs[:n], refs[n:]
+    known = returns(n)
+    ins, outs = refs[: len(known)], refs[len(known) :]
     slab, orbitals = ins[0].shape
     half = keep // 2
     rows = slab // half
     halves = []
     for e in range(2):
-        same = [ref for ref, (_, other) in zip(ins, hops(n)) if other == e]
+        same = [ref for ref, (_, other) in zip(ins, known) if other == e]
         total = same[0][...].astype(F32)
         for ref in same[1:]:
             total = total + ref[...].astype(F32)
@@ -390,20 +405,19 @@
         [pltpu.SemaphoreType.DMA((1,))],
         "hold",
     )
-    relayed = {leading(s, n // 2) for s, _ in hops(n) if leading(s, n // 2) != s}
+    chips = n // 2
     gathered = {}
-    for s, e in hops(n):
-        if s in relayed:
+    for s, e in [hop for hop in hops(n) if hop[1]] + [hop for hop in hops(n) if not hop[1]]:
+        if leading(s, e, chips) == s and 2 * s >= chips:
             gathered[s, e] = to_block(other if e else same, s, e)
     for s, e in hops(n):
-        if leading(s, n // 2) == s and s not in relayed and (s, e) != (0, 1):
+        if leading(s, e, chips) == s and 2 * s < chips and (s, e) != (0, 1):
             gathered[s, e] = to_block(other2 if e else same2, s, e)
     for s, e in hops(n):
-        top = leading(s, n // 2)
+        top = leading(s, e, chips)
         if top != s:
             gathered[s, e] = to_block(gathered[top, e], s ^ top, 0)
-    late = gathered.get((1, 1), same2)
-    (last,) = call(after_kernel, [payload], [], [], [other2, late], [], "after")
+    (last,) = call(after_kernel, [payload], [], [], [other2, gathered.get((chips // 2, 0), same2)], [], "after")
     gathered[0, 1] = to_block(last, 0, 1)
     gathered = [gathered[hop] for hop in arrivals(n)]
     held = F32 if rows % 16 else BF16
@@ -422,7 +436,22 @@
         "fock",
         flops=2 * n * slab * orbitals * (orbitals + 4 * vec_count * occupied),
     )
-    backs = [to_block(x, s, e) for x, (s, e) in zip(parts, hops(n))]
+    parts = dict(zip(hops(n), parts))
+    for s, e in returns(n):
+        via = [hop for hop in hops(n) if hop[1] == e and hop[0] != s and leading(*hop, chips) == s]
+        if via:
+            later = [hop for hop in returns(n) if hop[0] < s and hop != (0, 0) and (hop[1] == e or 2 * hop[0] < chips)]
+            out = call(
+                functools.partial(add_kernel, len(later)),
+                [shape((slab, orbitals), BF16)] * (1 + len(later)),
+                [],
+                [],
+                [parts[hop] for hop in later] + [parts[s, e]] + [to_block(parts[hop], hop[0] ^ s, 0) for hop in via],
+                [],
+                "add",
+            )
+            parts.update(zip([(s, e)] + later, out))
+    backs = [to_block(parts[hop], *hop) for hop in returns(n)]
     back = call(
         functools.partial(sum_kernel, n, keep, cap, groups),
         [shape((cap * rows, orbitals), BF16)] * groups,

time: 48.2 us -> 47.8 us (level)
  waiting for transfers between devices: 14.6 us -> 11.4 us
  starting transfers between devices: 23 us -> 25.8 us
    ppermute x15, waiting for transfers between devices: 9.45 us -> 6.64 us  [to_block(): lax.ppermute(x, 'blk', [(i, 2 * moved(i // 2, s, n // 2, 1) + (i % 2 ^ e)...]
    ppermute x15, starting transfers between devices: 15.3 us -> 18.1 us  [to_block(): lax.ppermute(x, 'blk', [(i, 2 * moved(i // 2, s, n // 2, 1) + (i % 2 ^ e)...]
    pallas_call x9 -> x10, Pallas kernels: 7.72 us -> 7.74 us  [call(): pl.pallas_call(kernel, out_shape=outs, in_specs=[smem] * len(scalars) + [...]
  transfers between devices with their start and end apart: 21 -> 21, of which waited for: 12 -> 10; matrix products, arithmetic and copies ran while one was open for 0% -> 0% of each run, Pallas kernels for 5% -> 5%
where the time goes in v13:
time: 47.8 us; the launch traced here: 47.5 us
  starting transfers between devices  25.8 us (54%)
  waiting for transfers between devices  11.4 us (24%)
  Pallas kernels  7.74 us (16%)
  local copies, waits for them, and re-layouts  2.5 us (5%)
    ppermute x15, starting transfers between devices, to_block(): lax.ppermute(x, 'blk', [(i, 2 * moved(i // 2, s, n // 2, 1) + (i % 2 ^ e)...  18.1 us
    pallas_call x10, Pallas kernels, call(): pl.pallas_call(kernel, out_shape=outs, in_specs=[smem] * len(scalars) + [...  7.74 us
    ppermute x6, starting transfers between devices, to_list(): lax.ppermute(x, 'grp', [(i, moved(i, s, groups, 1)) for i in range(groups)])  7.68 us
    ppermute x15, waiting for transfers between devices, to_block(): lax.ppermute(x, 'blk', [(i, 2 * moved(i // 2, s, n // 2, 1) + (i % 2 ^ e)...  6.64 us
    ppermute x6, waiting for transfers between devices, to_list(): lax.ppermute(x, 'grp', [(i, moved(i, s, groups, 1)) for i in range(groups)])  4.77 us
    unnamed x10, local copies, waits for them, and re-layouts  2.5 us
  transfers between devices with their start and end apart: 21, of which 10 were waited for; matrix products, arithmetic and copies ran while one was open for 0% of the time, Pallas kernels for 5%

profile of v13, /device:TPU:0, one launch (start us, length us, event | category | flops | bytes accessed | tf_op | source)
XLA Modules:
  0.0 47.5 jit_solution(11324735563707738293)
XLA Ops:
  0.0 0.5 collective-permute-start.3
  0.5 1.9 %route.1 = (bf16[32,896]{1,0:T(8,128)(2,1)}, bf16[32,896]{1,0:T(8,128)(2,1)}, bf16[32,896]{1,0:T(8,128)(2,1)}, bf16[32,896]{1,0:T(8,128)(2,1)}) custom-call(s32[1]{0:T(128)} %bitcast.me_ref, s32[8]{0:T(128)} %target_ref.1, f32[8]{0:T(128)} %weights_ref.1, bf16[16,8,768]{2,1,0:T(8,128)(2,1)} %walkers_any.1, f32[8,12]{1,0:T(8,128)} %fields_any.1, ...), custom_call_target="tpu_custom_call" | custom-call | bytes 229376 | tf_op jit(solution)/shard_map/route/pallas_call | solution.py:311
  2.4 2.6 %collective-permute-start = (bf16[32,896]{1,0:T(8,128)(2,1)}, bf16[32,896]{1,0:T(8,128)(2,1)S(1)}, u32[]{:S(2)}, u32[]{:S(2)}) collective-permute-start(bf16[32,896]{1,0:T(8,128)(2,1)} %get-tuple-element.32), channel_id=1, source_target_pairs={{0,16},{8,24},{16,0},{24,8},{1,17},{9,25},{17,1},{25,9},{2,18},{10... | collective-permute-start | bytes 172040 | tf_op jit(solution)/shard_map/ppermute | solution.py:337
  5.0 1.4 %collective-permute-start.1 = (bf16[32,896]{1,0:T(8,128)(2,1)}, bf16[32,896]{1,0:T(8,128)(2,1)S(1)}, u32[]{:S(2)}, u32[]{:S(2)}) collective-permute-start(bf16[32,896]{1,0:T(8,128)(2,1)} %get-tuple-element.33), channel_id=1, source_target_pairs={{0,24},{8,16},{16,8},{24,0},{1,25},{9,17},{17,9},{25,1},{2,26},{10... | collective-permute-start | bytes 172040 | tf_op jit(solution)/shard_map/ppermute | solution.py:337
  6.4 0.1 collective-permute-start.2
  6.5 0.8 %copy-done.2 = bf16[32,896]{1,0:T(8,128)(2,1)S(1)} copy-done((bf16[32,896]{1,0:T(8,128)(2,1)S(1)}, bf16[32,896]{1,0:T(8,128)(2,1)}, u32[]{:S(2)}) %copy-start.2) | copy-done | bytes 57368
  7.4 0.0 copy-start
  7.4 1.7 %copy-done = bf16[12,128,768]{2,1,0:T(8,128)(2,1)S(1)} copy-done((bf16[12,128,768]{2,1,0:T(8,128)(2,1)S(1)}, bf16[12,128,768]{2,1,0:T(8,128)(2,1)}, u32[]{:S(2)}) %copy-start) | copy-done | bytes 2359320
  9.0 0.2 stage.1.when.own_ref
  9.2 0.0 copy-start.1
  9.2 0.0 collective-permute-done.refs_1_
  9.2 1.2 %collective-permute-done.1.refs_2_ = bf16[32,896]{1,0:T(8,128)(2,1)S(1)} collective-permute-done((bf16[32,896]{1,0:T(8,128)(2,1)}, bf16[32,896]{1,0:T(8,128)(2,1)S(1)}, u32[]{:S(2)}, u32[]{:S(2)}) %collective-permute-start.1) | collective-permute-done | bytes 57376 | tf_op jit(solution)/shard_map/ppermute | solution.py:337
  10.5 0.3 collective-permute-done.2.refs_3_
  10.8 0.1 merge.1
  10.9 1.5 %collective-permute-start.8 = (bf16[216,128]{1,0:T(8,128)(2,1)S(1)}, bf16[216,128]{1,0:T(8,128)(2,1)S(1)}, u32[]{:S(2)}, u32[]{:S(2)}) collective-permute-start(bf16[216,128]{1,0:T(8,128)(2,1)S(1)} %get-tuple-element.40), channel_id=1, source_target_pairs={{0,5},{1,4},{2,7},{3,6},{4,1},{5,0},{6,3},{7,2},{8,13},{9,12},{10,... | collective-permute-start | bytes 165896 | tf_op jit(solution)/shard_map/ppermute | solution.py:342
  12.4 1.2 %collective-permute-start.4 = (bf16[216,128]{1,0:T(8,128)(2,1)S(1)}, bf16[216,128]{1,0:T(8,128)(2,1)S(1)}, u32[]{:S(2)}, u32[]{:S(2)}) collective-permute-start(bf16[216,128]{1,0:T(8,128)(2,1)S(1)} %get-tuple-element.39), channel_id=1, source_target_pairs={{0,4},{1,5},{2,6},{3,7},{4,0},{5,1},{6,2},{7,3},{8,12},{9,13},{10,... | collective-permute-start | bytes 165896 | tf_op jit(solution)/shard_map/ppermute | solution.py:342
  13.6 1.6 %collective-permute-start.7 = (bf16[216,128]{1,0:T(8,128)(2,1)S(1)}, bf16[216,128]{1,0:T(8,128)(2,1)S(1)}, u32[]{:S(2)}, u32[]{:S(2)}) collective-permute-start(bf16[216,128]{1,0:T(8,128)(2,1)S(1)} %get-tuple-element.37.refs_0_), channel_id=1, source_target_pairs={{0,2},{1,3},{2,0},{3,1},{4,6},{5,7},{6,4},{7,5},{8,10},{9,11},{10,... | collective-permute-start | bytes 165896 | tf_op jit(solution)/shard_map/ppermute | solution.py:342
  15.2 1.6 %collective-permute-start.10 = (bf16[216,128]{1,0:T(8,128)(2,1)S(1)}, bf16[216,128]{1,0:T(8,128)(2,1)S(1)}, u32[]{:S(2)}, u32[]{:S(2)}) collective-permute-start(bf16[216,128]{1,0:T(8,128)(2,1)S(1)} %get-tuple-element.39), channel_id=1, source_target_pairs={{0,6},{1,7},{2,4},{3,5},{4,2},{5,3},{6,0},{7,1},{8,14},{9,15},{10,... | collective-permute-start | bytes 165896 | tf_op jit(solution)/shard_map/ppermute | solution.py:342
  16.8 0.0 collective-permute-done.8.refs_6_
  16.8 1.5 %collective-permute-start.6 = (bf16[216,128]{1,0:T(8,128)(2,1)S(1)}, bf16[216,128]{1,0:T(8,128)(2,1)S(1)}, u32[]{:S(2)}, u32[]{:S(2)}) collective-permute-start(bf16[216,128]{1,0:T(8,128)(2,1)S(1)} %get-tuple-element.38.source_ref), channel_id=1, source_target_pairs={{0,3},{1,2},{2,1},{3,0},{4,7},{5,6},{6,5},{7,4},{8,11},{9,10},{10,... | collective-permute-start | bytes 165896 | tf_op jit(solution)/shard_map/ppermute | solution.py:342
  18.3 1.3 %collective-permute-done.4.when_ref.refs_7_ = bf16[216,128]{1,0:T(8,128)(2,1)S(1)} collective-permute-done((bf16[216,128]{1,0:T(8,128)(2,1)S(1)}, bf16[216,128]{1,0:T(8,128)(2,1)S(1)}, u32[]{:S(2)}, u32[]{:S(2)}) %collective-permute-start.4) | collective-permute-done | bytes 55328 | tf_op jit(solution)/shard_map/ppermute | solution.py:342
  19.6 1.1 %collective-permute-start.9 = (bf16[216,128]{1,0:T(8,128)(2,1)S(1)}, bf16[216,128]{1,0:T(8,128)(2,1)S(1)}, u32[]{:S(2)}, u32[]{:S(2)}) collective-permute-start(bf16[216,128]{1,0:T(8,128)(2,1)S(1)} %collective-permute-done.8.refs_6_), channel_id=1, source_target_pairs={{0,2},{1,3},{2,0},{3,1},{4,6},{5,7},{6,4},{7,5},{8,10},{9,11},{10,... | collective-permute-start | bytes 165896 | tf_op jit(solution)/shard_map/ppermute | solution.py:342
  20.7 0.0 collective-permute-done.7.refs_3_
  20.7 0.1 collective-permute-start.5
  20.8 0.3 hold.1.body_ref
  21.1 0.0 copy-start.3
  21.1 0.0 copy-start.4
  21.1 0.5 %collective-permute-done.6.refs_2_ = bf16[216,128]{1,0:T(8,128)(2,1)S(1)} collective-permute-done((bf16[216,128]{1,0:T(8,128)(2,1)S(1)}, bf16[216,128]{1,0:T(8,128)(2,1)S(1)}, u32[]{:S(2)}, u32[]{:S(2)}) %collective-permute-start.6) | collective-permute-done | bytes 55328 | tf_op jit(solution)/shard_map/ppermute | solution.py:342
  21.6 0.0 collective-permute-done.10.refs_5_
  21.6 2.1 %collective-permute-done.9.refs_4_ = bf16[216,128]{1,0:T(8,128)(2,1)S(1)} collective-permute-done((bf16[216,128]{1,0:T(8,128)(2,1)S(1)}, bf16[216,128]{1,0:T(8,128)(2,1)S(1)}, u32[]{:S(2)}, u32[]{:S(2)}) %collective-permute-start.9) | collective-permute-done | bytes 55328 | tf_op jit(solution)/shard_map/ppermute | solution.py:342
  23.8 3.7 %fock.1 = (bf16[32,768]{1,0:T(8,128)(2,1)S(1)}, bf16[32,768]{1,0:T(8,128)(2,1)S(1)}, bf16[32,768]{1,0:T(8,128)(2,1)S(1)}, bf16[32,768]{1,0:T(8,128)(2,1)S(1)}, b...) custom-call(s32[1]{0:T(128)} %bitcast.1.blk_ref, ...), custom_call_target="tpu_custom_call" | custom-call | flops 2717908992 | bytes 6733824 | tf_op jit(solution)/shard_map/fock/pallas_call | solution.py:311
  27.5 1.2 %collective-permute-start.12 = (bf16[32,768]{1,0:T(8,128)(2,1)S(1)}, bf16[32,768]{1,0:T(8,128)(2,1)S(1)}, u32[]{:S(2)}, u32[]{:S(2)}) collective-permute-start(bf16[32,768]{1,0:T(8,128)(2,1)S(1)} %get-tuple-element.47), channel_id=1, source_target_pairs={{0,2},{1,3},{2,0},{3,1},{4,6},{5,7},{6,4},{7,5},{8,10},{9,11},{10,... | collective-permute-start | bytes 147464 | tf_op jit(solution)/shard_map/ppermute | solution.py:342
  28.7 3.6 %collective-permute-start.11 = (bf16[32,768]{1,0:T(8,128)(2,1)S(1)}, bf16[32,768]{1,0:T(8,128)(2,1)S(1)}, u32[]{:S(2)}, u32[]{:S(2)}) collective-permute-start(bf16[32,768]{1,0:T(8,128)(2,1)S(1)} %get-tuple-element.42), channel_id=1, source_target_pairs={{0,4},{1,5},{2,6},{3,7},{4,0},{5,1},{6,2},{7,3},{8,12},{9,13},{10,... | collective-permute-start | bytes 147464 | tf_op jit(solution)/shard_map/ppermute | solution.py:342
  32.2 0.0 collective-permute-start.14
  32.3 0.1 collective-permute-start.13
  32.4 2.0 %collective-permute-start.15 = (bf16[32,768]{1,0:T(8,128)(2,1)S(1)}, bf16[32,768]{1,0:T(8,128)(2,1)S(1)}, u32[]{:S(2)}, u32[]{:S(2)}) collective-permute-start(bf16[32,768]{1,0:T(8,128)(2,1)S(1)} %get-tuple-element.50), channel_id=1, source_target_pairs={{0,2},{1,3},{2,0},{3,1},{4,6},{5,7},{6,4},{7,5},{8,10},{9,11},{10,... | collective-permute-start | bytes 147464 | tf_op jit(solution)/shard_map/ppermute | solution.py:342
  34.4 2.1 %collective-permute-start.16 = (bf16[32,768]{1,0:T(8,128)(2,1)S(1)}, bf16[32,768]{1,0:T(8,128)(2,1)S(1)}, u32[]{:S(2)}, u32[]{:S(2)}) collective-permute-start(bf16[32,768]{1,0:T(8,128)(2,1)S(1)} %get-tuple-element.51), channel_id=1, source_target_pairs={{0,3},{1,2},{2,1},{3,0},{4,7},{5,6},{6,5},{7,4},{8,11},{9,10},{10,... | collective-permute-start | bytes 147464 | tf_op jit(solution)/shard_map/ppermute | solution.py:342
  36.5 0.1 collective-permute-start.17
  36.6 1.9 %collective-permute-done.14.refs_3_ = bf16[32,768]{1,0:T(8,128)(2,1)S(1)} collective-permute-done((bf16[32,768]{1,0:T(8,128)(2,1)S(1)}, bf16[32,768]{1,0:T(8,128)(2,1)S(1)}, u32[]{:S(2)}, u32[]{:S(2)}) %collective-permute-start.14) | collective-permute-done | bytes 49184 | tf_op jit(solution)/shard_map/ppermute | solution.py:342
  38.5 0.7 %collective-permute-done.16.refs_5_ = bf16[32,768]{1,0:T(8,128)(2,1)S(1)} collective-permute-done((bf16[32,768]{1,0:T(8,128)(2,1)S(1)}, bf16[32,768]{1,0:T(8,128)(2,1)S(1)}, u32[]{:S(2)}, u32[]{:S(2)}) %collective-permute-start.16) | collective-permute-done | bytes 49184 | tf_op jit(solution)/shard_map/ppermute | solution.py:342
  39.2 0.1 sum.1
  39.3 1.5 %collective-permute-start.18 = (bf16[32,768]{1,0:T(8,128)(2,1)S(1)}, bf16[32,768]{1,0:T(8,128)(2,1)S(1)}, u32[]{:S(2)}, u32[]{:S(2)}) collective-permute-start(bf16[32,768]{1,0:T(8,128)(2,1)S(1)} %get-tuple-element.54), channel_id=1, source_target_pairs={{0,16},{8,24},{16,0},{24,8},{1,17},{9,25},{17,1},{25,9},{2,18},{10... | collective-permute-start | bytes 147464 | tf_op jit(solution)/shard_map/ppermute | solution.py:337
  40.8 1.2 %collective-permute-start.19 = (bf16[32,768]{1,0:T(8,128)(2,1)S(1)}, bf16[32,768]{1,0:T(8,128)(2,1)S(1)}, u32[]{:S(2)}, u32[]{:S(2)}) collective-permute-start(bf16[32,768]{1,0:T(8,128)(2,1)S(1)} %get-tuple-element.55), channel_id=1, source_target_pairs={{0,24},{8,16},{16,8},{24,0},{1,25},{9,17},{17,9},{25,1},{2,26},{10... | collective-permute-start | bytes 147464 | tf_op jit(solution)/shard_map/ppermute | solution.py:337
  42.0 0.9 %collective-permute-start.20 = (bf16[32,768]{1,0:T(8,128)(2,1)S(1)}, bf16[32,768]{1,0:T(8,128)(2,1)S(1)}, u32[]{:S(2)}, u32[]{:S(2)}) collective-permute-start(bf16[32,768]{1,0:T(8,128)(2,1)S(1)} %get-tuple-element.56), channel_id=1, source_target_pairs={{0,8},{8,0},{16,24},{24,16},{1,9},{9,1},{17,25},{25,17},{2,10},{10... | collective-permute-start | bytes 147464 | tf_op jit(solution)/shard_map/ppermute | solution.py:337
  42.9 1.0 %collective-permute-done.18.refs_1_ = bf16[32,768]{1,0:T(8,128)(2,1)S(1)} collective-permute-done((bf16[32,768]{1,0:T(8,128)(2,1)S(1)}, bf16[32,768]{1,0:T(8,128)(2,1)S(1)}, u32[]{:S(2)}, u32[]{:S(2)}) %collective-permute-start.18) | collective-permute-done | bytes 49184 | tf_op jit(solution)/shard_map/ppermute | solution.py:337
  43.9 1.9 %collective-permute-done.19.refs_2_ = bf16[32,768]{1,0:T(8,128)(2,1)S(1)} collective-permute-done((bf16[32,768]{1,0:T(8,128)(2,1)S(1)}, bf16[32,768]{1,0:T(8,128)(2,1)S(1)}, u32[]{:S(2)}, u32[]{:S(2)}) %collective-permute-start.19) | collective-permute-done | bytes 49184 | tf_op jit(solution)/shard_map/ppermute | solution.py:337
  45.8 0.3 collective-permute-done.20.refs_3_
  46.1 1.4 %deal.1 = bf16[16,8,768]{2,1,0:T(8,128)(2,1)} custom-call(s32[1]{0:T(128)} %bitcast.me_ref, s32[8]{0:T(128)S(1)} %copy-done.3, f32[8]{0:T(128)S(1)} %copy-done.4, f32[8,128]{1,0:T(8,128)S(1)} %get-tuple-element.35.refs_1_.total_ref, bf16[32,768]{1,0:T(8,128)(2,1)S(1)} %get-tuple-element.53.refs_0_, bf16[32,768]{1,0:T(8,128)(2,1)S(1)} %collective-permute-done.18.refs_1_, ...), custom_call_target="tpu_custom_call" | custom-call | bytes 397312 | tf_op jit(solution)/shard_map/deal/pallas_call | solution.py:311
  (14 shorter events, 0.1 us)
Async XLA Ops:
  0.0 23.8 %collective-permute-start.3 = (bf16[12,128,768]{2,1,0:T(8,128)(2,1)}, bf16[12,128,768]{2,1,0:T(8,128)(2,1)S(1)}, u32[]{:S(2)}, u32[]{:S(2)}) collective-permute-start(bf16[12,128,768]{2,1,0:T(8,128)(2,1)} %refs_0_.2), channel_id=1, source_target_pairs={{0,1},{1,0},{2,3},{3,2},{4,5},{5,4},{6,7},{7,6},{8,9},{9,8},{10,11... | collective-permute-start | bytes 7077896 | tf_op jit(solution)/shard_map/ppermute | solution.py:342
  2.4 6.9 %collective-permute-start = (bf16[32,896]{1,0:T(8,128)(2,1)}, bf16[32,896]{1,0:T(8,128)(2,1)S(1)}, u32[]{:S(2)}, u32[]{:S(2)}) collective-permute-start(bf16[32,896]{1,0:T(8,128)(2,1)} %get-tuple-element.32), channel_id=1, source_target_pairs={{0,16},{8,24},{16,0},{24,8},{1,17},{9,25},{17,1},{25,9},{2,18},{10... | collective-permute-start | bytes 172040 | tf_op jit(solution)/shard_map/ppermute | solution.py:337
  5.0 5.5 %collective-permute-start.1 = (bf16[32,896]{1,0:T(8,128)(2,1)}, bf16[32,896]{1,0:T(8,128)(2,1)S(1)}, u32[]{:S(2)}, u32[]{:S(2)}) collective-permute-start(bf16[32,896]{1,0:T(8,128)(2,1)} %get-tuple-element.33), channel_id=1, source_target_pairs={{0,24},{8,16},{16,8},{24,0},{1,25},{9,17},{17,9},{25,1},{2,26},{10... | collective-permute-start | bytes 172040 | tf_op jit(solution)/shard_map/ppermute | solution.py:337
  6.4 4.4 %collective-permute-start.2 = (bf16[32,896]{1,0:T(8,128)(2,1)}, bf16[32,896]{1,0:T(8,128)(2,1)S(1)}, u32[]{:S(2)}, u32[]{:S(2)}) collective-permute-start(bf16[32,896]{1,0:T(8,128)(2,1)} %get-tuple-element.34), channel_id=1, source_target_pairs={{0,8},{8,0},{16,24},{24,16},{1,9},{9,1},{17,25},{25,17},{2,10},{10... | collective-permute-start | bytes 172040 | tf_op jit(solution)/shard_map/ppermute | solution.py:337
  6.5 0.8 %copy-start.2 = (bf16[32,896]{1,0:T(8,128)(2,1)S(1)}, bf16[32,896]{1,0:T(8,128)(2,1)}, u32[]{:S(2)}) copy-start(bf16[32,896]{1,0:T(8,128)(2,1)} %get-tuple-element.31.refs_0_) | copy-start | bytes 172036
  7.4 1.7 %copy-start = (bf16[12,128,768]{2,1,0:T(8,128)(2,1)S(1)}, bf16[12,128,768]{2,1,0:T(8,128)(2,1)}, u32[]{:S(2)}) copy-start(bf16[12,128,768]{2,1,0:T(8,128)(2,1)} %refs_0_.2) | copy-start | bytes 7077892
  9.2 11.6 %copy-start.1 = (bf16[768,768]{1,0:T(8,128)(2,1)S(1)}, bf16[768,768]{1,0:T(8,128)(2,1)}, u32[]{:S(2)}) copy-start(bf16[768,768]{1,0:T(8,128)(2,1)} %refs_0_.3) | copy-start | bytes 3538948
  10.9 5.9 %collective-permute-start.8 = (bf16[216,128]{1,0:T(8,128)(2,1)S(1)}, bf16[216,128]{1,0:T(8,128)(2,1)S(1)}, u32[]{:S(2)}, u32[]{:S(2)}) collective-permute-start(bf16[216,128]{1,0:T(8,128)(2,1)S(1)} %get-tuple-element.40), channel_id=1, source_target_pairs={{0,5},{1,4},{2,7},{3,6},{4,1},{5,0},{6,3},{7,2},{8,13},{9,12},{10,... | collective-permute-start | bytes 165896 | tf_op jit(solution)/shard_map/ppermute | solution.py:342
  12.4 7.2 %collective-permute-start.4 = (bf16[216,128]{1,0:T(8,128)(2,1)S(1)}, bf16[216,128]{1,0:T(8,128)(2,1)S(1)}, u32[]{:S(2)}, u32[]{:S(2)}) collective-permute-start(bf16[216,128]{1,0:T(8,128)(2,1)S(1)} %get-tuple-element.39), channel_id=1, source_target_pairs={{0,4},{1,5},{2,6},{3,7},{4,0},{5,1},{6,2},{7,3},{8,12},{9,13},{10,... | collective-permute-start | bytes 165896 | tf_op jit(solution)/shard_map/ppermute | solution.py:342
  13.6 7.1 %collective-permute-start.7 = (bf16[216,128]{1,0:T(8,128)(2,1)S(1)}, bf16[216,128]{1,0:T(8,128)(2,1)S(1)}, u32[]{:S(2)}, u32[]{:S(2)}) collective-permute-start(bf16[216,128]{1,0:T(8,128)(2,1)S(1)} %get-tuple-element.37.refs_0_), channel_id=1, source_target_pairs={{0,2},{1,3},{2,0},{3,1},{4,6},{5,7},{6,4},{7,5},{8,10},{9,11},{10,... | collective-permute-start | bytes 165896 | tf_op jit(solution)/shard_map/ppermute | solution.py:342
  15.2 6.4 %collective-permute-start.10 = (bf16[216,128]{1,0:T(8,128)(2,1)S(1)}, bf16[216,128]{1,0:T(8,128)(2,1)S(1)}, u32[]{:S(2)}, u32[]{:S(2)}) collective-permute-start(bf16[216,128]{1,0:T(8,128)(2,1)S(1)} %get-tuple-element.39), channel_id=1, source_target_pairs={{0,6},{1,7},{2,4},{3,5},{4,2},{5,3},{6,0},{7,1},{8,14},{9,15},{10,... | collective-permute-start | bytes 165896 | tf_op jit(solution)/shard_map/ppermute | solution.py:342
  16.8 4.8 %collective-permute-start.6 = (bf16[216,128]{1,0:T(8,128)(2,1)S(1)}, bf16[216,128]{1,0:T(8,128)(2,1)S(1)}, u32[]{:S(2)}, u32[]{:S(2)}) collective-permute-start(bf16[216,128]{1,0:T(8,128)(2,1)S(1)} %get-tuple-element.38.source_ref), channel_id=1, source_target_pairs={{0,3},{1,2},{2,1},{3,0},{4,7},{5,6},{6,5},{7,4},{8,11},{9,10},{10,... | collective-permute-start | bytes 165896 | tf_op jit(solution)/shard_map/ppermute | solution.py:342
  19.6 4.2 %collective-permute-start.9 = (bf16[216,128]{1,0:T(8,128)(2,1)S(1)}, bf16[216,128]{1,0:T(8,128)(2,1)S(1)}, u32[]{:S(2)}, u32[]{:S(2)}) collective-permute-start(bf16[216,128]{1,0:T(8,128)(2,1)S(1)} %collective-permute-done.8.refs_6_), channel_id=1, source_target_pairs={{0,2},{1,3},{2,0},{3,1},{4,6},{5,7},{6,4},{7,5},{8,10},{9,11},{10,... | collective-permute-start | bytes 165896 | tf_op jit(solution)/shard_map/ppermute | solution.py:342
  20.7 3.0 %collective-permute-start.5 = (bf16[216,128]{1,0:T(8,128)(2,1)S(1)}, bf16[216,128]{1,0:T(8,128)(2,1)S(1)}, u32[]{:S(2)}, u32[]{:S(2)}) collective-permute-start(bf16[216,128]{1,0:T(8,128)(2,1)S(1)} %after.1), channel_id=1, source_target_pairs={{0,1},{1,0},{2,3},{3,2},{4,5},{5,4},{6,7},{7,6},{8,9},{9,8},{10,11... | collective-permute-start | bytes 165896 | tf_op jit(solution)/shard_map/ppermute | solution.py:342
  21.1 25.0 %copy-start.3 = (s32[8]{0:T(128)S(1)}, s32[8]{0:T(128)}, u32[]{:S(2)}) copy-start(s32[8]{0:T(128)} %target_ref.1) | copy-start | bytes 100
  21.1 25.0 %copy-start.4 = (f32[8]{0:T(128)S(1)}, f32[8]{0:T(128)}, u32[]{:S(2)}) copy-start(f32[8]{0:T(128)} %weights_ref.1) | copy-start | bytes 100
  27.5 4.8 %collective-permute-start.12 = (bf16[32,768]{1,0:T(8,128)(2,1)S(1)}, bf16[32,768]{1,0:T(8,128)(2,1)S(1)}, u32[]{:S(2)}, u32[]{:S(2)}) collective-permute-start(bf16[32,768]{1,0:T(8,128)(2,1)S(1)} %get-tuple-element.47), channel_id=1, source_target_pairs={{0,2},{1,3},{2,0},{3,1},{4,6},{5,7},{6,4},{7,5},{8,10},{9,11},{10,... | collective-permute-start | bytes 147464 | tf_op jit(solution)/shard_map/ppermute | solution.py:342
  28.7 7.8 %collective-permute-start.11 = (bf16[32,768]{1,0:T(8,128)(2,1)S(1)}, bf16[32,768]{1,0:T(8,128)(2,1)S(1)}, u32[]{:S(2)}, u32[]{:S(2)}) collective-permute-start(bf16[32,768]{1,0:T(8,128)(2,1)S(1)} %get-tuple-element.42), channel_id=1, source_target_pairs={{0,4},{1,5},{2,6},{3,7},{4,0},{5,1},{6,2},{7,3},{8,12},{9,13},{10,... | collective-permute-start | bytes 147464 | tf_op jit(solution)/shard_map/ppermute | solution.py:342
  32.2 6.2 %collective-permute-start.14 = (bf16[32,768]{1,0:T(8,128)(2,1)S(1)}, bf16[32,768]{1,0:T(8,128)(2,1)S(1)}, u32[]{:S(2)}, u32[]{:S(2)}) collective-permute-start(bf16[32,768]{1,0:T(8,128)(2,1)S(1)} %get-tuple-element.49), channel_id=1, source_target_pairs={{0,6},{1,7},{2,4},{3,5},{4,2},{5,3},{6,0},{7,1},{8,14},{9,15},{10,... | collective-permute-start | bytes 147464 | tf_op jit(solution)/shard_map/ppermute | solution.py:342
  32.3 6.2 %collective-permute-start.13 = (bf16[32,768]{1,0:T(8,128)(2,1)S(1)}, bf16[32,768]{1,0:T(8,128)(2,1)S(1)}, u32[]{:S(2)}, u32[]{:S(2)}) collective-permute-start(bf16[32,768]{1,0:T(8,128)(2,1)S(1)} %get-tuple-element.48), channel_id=1, source_target_pairs={{0,5},{1,4},{2,7},{3,6},{4,1},{5,0},{6,3},{7,2},{8,13},{9,12},{10,... | collective-permute-start | bytes 147464 | tf_op jit(solution)/shard_map/ppermute | solution.py:342
  32.4 6.1 %collective-permute-start.15 = (bf16[32,768]{1,0:T(8,128)(2,1)S(1)}, bf16[32,768]{1,0:T(8,128)(2,1)S(1)}, u32[]{:S(2)}, u32[]{:S(2)}) collective-permute-start(bf16[32,768]{1,0:T(8,128)(2,1)S(1)} %get-tuple-element.50), channel_id=1, source_target_pairs={{0,2},{1,3},{2,0},{3,1},{4,6},{5,7},{6,4},{7,5},{8,10},{9,11},{10,... | collective-permute-start | bytes 147464 | tf_op jit(solution)/shard_map/ppermute | solution.py:342
  34.4 4.8 %collective-permute-start.16 = (bf16[32,768]{1,0:T(8,128)(2,1)S(1)}, bf16[32,768]{1,0:T(8,128)(2,1)S(1)}, u32[]{:S(2)}, u32[]{:S(2)}) collective-permute-start(bf16[32,768]{1,0:T(8,128)(2,1)S(1)} %get-tuple-element.51), channel_id=1, source_target_pairs={{0,3},{1,2},{2,1},{3,0},{4,7},{5,6},{6,5},{7,4},{8,11},{9,10},{10,... | collective-permute-start | bytes 147464 | tf_op jit(solution)/shard_map/ppermute | solution.py:342
  36.5 2.8 %collective-permute-start.17 = (bf16[32,768]{1,0:T(8,128)(2,1)S(1)}, bf16[32,768]{1,0:T(8,128)(2,1)S(1)}, u32[]{:S(2)}, u32[]{:S(2)}) collective-permute-start(bf16[32,768]{1,0:T(8,128)(2,1)S(1)} %get-tuple-element.52), channel_id=1, source_target_pairs={{0,1},{1,0},{2,3},{3,2},{4,5},{5,4},{6,7},{7,6},{8,9},{9,8},{10,11... | collective-permute-start | bytes 147464 | tf_op jit(solution)/shard_map/ppermute | solution.py:342
  39.3 4.6 %collective-permute-start.18 = (bf16[32,768]{1,0:T(8,128)(2,1)S(1)}, bf16[32,768]{1,0:T(8,128)(2,1)S(1)}, u32[]{:S(2)}, u32[]{:S(2)}) collective-permute-start(bf16[32,768]{1,0:T(8,128)(2,1)S(1)} %get-tuple-element.54), channel_id=1, source_target_pairs={{0,16},{8,24},{16,0},{24,8},{1,17},{9,25},{17,1},{25,9},{2,18},{10... | collective-permute-start | bytes 147464 | tf_op jit(solution)/shard_map/ppermute | solution.py:337
  40.8 5.0 %collective-permute-start.19 = (bf16[32,768]{1,0:T(8,128)(2,1)S(1)}, bf16[32,768]{1,0:T(8,128)(2,1)S(1)}, u32[]{:S(2)}, u32[]{:S(2)}) collective-permute-start(bf16[32,768]{1,0:T(8,128)(2,1)S(1)} %get-tuple-element.55), channel_id=1, source_target_pairs={{0,24},{8,16},{16,8},{24,0},{1,25},{9,17},{17,9},{25,1},{2,26},{10... | collective-permute-start | bytes 147464 | tf_op jit(solution)/shard_map/ppermute | solution.py:337
  42.0 4.1 %collective-permute-start.20 = (bf16[32,768]{1,0:T(8,128)(2,1)S(1)}, bf16[32,768]{1,0:T(8,128)(2,1)S(1)}, u32[]{:S(2)}, u32[]{:S(2)}) collective-permute-start(bf16[32,768]{1,0:T(8,128)(2,1)S(1)} %get-tuple-element.56), channel_id=1, source_target_pairs={{0,8},{8,0},{16,24},{24,16},{1,9},{9,1},{17,25},{25,17},{2,10},{10... | collective-permute-start | bytes 147464 | tf_op jit(solution)/shard_map/ppermute | solution.py:337

commit v14 on v13

--- a/solution.py
+++ b/solution.py
@@ -164,7 +164,7 @@
 
 
 def arrivals(n):
-    return hops(n)[:1] + hops(n)[:0:-1]
+    return hops(n)
 
 
 def leading(s, e, chips):
@@ -417,7 +417,7 @@
         top = leading(s, e, chips)
         if top != s:
             gathered[s, e] = to_block(gathered[top, e], s ^ top, 0)
-    (last,) = call(after_kernel, [payload], [], [], [other2, gathered.get((chips // 2, 0), same2)], [], "after")
+    (last,) = call(after_kernel, [payload], [], [], [other2, gathered.get((1, 0), same2)], [], "after")
     gathered[0, 1] = to_block(last, 0, 1)
     gathered = [gathered[hop] for hop in arrivals(n)]
     held = F32 if rows % 16 else BF16

time: 47.8 us -> 47.9 us (level)
  waiting for transfers between devices: 11.4 us -> 13.2 us
  starting transfers between devices: 25.8 us -> 24.1 us
    ppermute x15, starting transfers between devices: 18.1 us -> 16.5 us  [to_block(): lax.ppermute(x, 'blk', [(i, 2 * moved(i // 2, s, n // 2, 1) + (i % 2 ^ e)...]
    ppermute x15, waiting for transfers between devices: 6.64 us -> 8.04 us  [to_block(): lax.ppermute(x, 'blk', [(i, 2 * moved(i // 2, s, n // 2, 1) + (i % 2 ^ e)...]
  transfers between devices with their start and end apart: 21 -> 21, of which waited for: 10 -> 12; matrix products, arithmetic and copies ran while one was open for 0% -> 0% of each run, Pallas kernels for 5% -> 5%
where the time goes in v14:
time: 47.9 us; the launch traced here: 47.6 us
  starting transfers between devices  24.1 us (50%)
  waiting for transfers between devices  13.2 us (28%)
  Pallas kernels  7.74 us (16%)
  local copies, waits for them, and re-layouts  2.5 us (5%)
    ppermute x15, starting transfers between devices, to_block(): lax.ppermute(x, 'blk', [(i, 2 * moved(i // 2, s, n // 2, 1) + (i % 2 ^ e)...  16.5 us
    ppermute x15, waiting for transfers between devices, to_block(): lax.ppermute(x, 'blk', [(i, 2 * moved(i // 2, s, n // 2, 1) + (i % 2 ^ e)...  8.04 us
    pallas_call x10, Pallas kernels, call(): pl.pallas_call(kernel, out_shape=outs, in_specs=[smem] * len(scalars) + [...  7.74 us
    ppermute x6, starting transfers between devices, to_list(): lax.ppermute(x, 'grp', [(i, moved(i, s, groups, 1)) for i in range(groups)])  7.68 us
    ppermute x6, waiting for transfers between devices, to_list(): lax.ppermute(x, 'grp', [(i, moved(i, s, groups, 1)) for i in range(groups)])  5.12 us
    unnamed x10, local copies, waits for them, and re-layouts  2.5 us
  transfers between devices with their start and end apart: 21, of which 12 were waited for; matrix products, arithmetic and copies ran while one was open for 0% of the time, Pallas kernels for 5%

profile of v14, /device:TPU:0, one launch (start us, length us, event | category | flops | bytes accessed | tf_op | source)
XLA Modules:
  0.0 47.6 jit_solution(6140175202601737282)
XLA Ops:
  0.0 0.5 collective-permute-start.3
  0.5 1.9 %route.1 = (bf16[32,896]{1,0:T(8,128)(2,1)}, bf16[32,896]{1,0:T(8,128)(2,1)}, bf16[32,896]{1,0:T(8,128)(2,1)}, bf16[32,896]{1,0:T(8,128)(2,1)}) custom-call(s32[1]{0:T(128)} %bitcast.me_ref, s32[8]{0:T(128)} %target_ref.1, f32[8]{0:T(128)} %weights_ref.1, bf16[16,8,768]{2,1,0:T(8,128)(2,1)} %walkers_any.1, f32[8,12]{1,0:T(8,128)} %fields_any.1, ...), custom_call_target="tpu_custom_call" | custom-call | bytes 229376 | tf_op jit(solution)/shard_map/route/pallas_call | solution.py:311
  2.4 2.6 %collective-permute-start = (bf16[32,896]{1,0:T(8,128)(2,1)}, bf16[32,896]{1,0:T(8,128)(2,1)S(1)}, u32[]{:S(2)}, u32[]{:S(2)}) collective-permute-start(bf16[32,896]{1,0:T(8,128)(2,1)} %get-tuple-element.32), channel_id=1, source_target_pairs={{0,16},{8,24},{16,0},{24,8},{1,17},{9,25},{17,1},{25,9},{2,18},{10... | collective-permute-start | bytes 172040 | tf_op jit(solution)/shard_map/ppermute | solution.py:337
  5.0 1.4 %collective-permute-start.1 = (bf16[32,896]{1,0:T(8,128)(2,1)}, bf16[32,896]{1,0:T(8,128)(2,1)S(1)}, u32[]{:S(2)}, u32[]{:S(2)}) collective-permute-start(bf16[32,896]{1,0:T(8,128)(2,1)} %get-tuple-element.33), channel_id=1, source_target_pairs={{0,24},{8,16},{16,8},{24,0},{1,25},{9,17},{17,9},{25,1},{2,26},{10... | collective-permute-start | bytes 172040 | tf_op jit(solution)/shard_map/ppermute | solution.py:337
  6.4 0.1 collective-permute-start.2
  6.5 0.8 %copy-done.2 = bf16[32,896]{1,0:T(8,128)(2,1)S(1)} copy-done((bf16[32,896]{1,0:T(8,128)(2,1)S(1)}, bf16[32,896]{1,0:T(8,128)(2,1)}, u32[]{:S(2)}) %copy-start.2) | copy-done | bytes 57368
  7.4 0.0 copy-start
  7.4 1.7 %copy-done = bf16[12,128,768]{2,1,0:T(8,128)(2,1)S(1)} copy-done((bf16[12,128,768]{2,1,0:T(8,128)(2,1)S(1)}, bf16[12,128,768]{2,1,0:T(8,128)(2,1)}, u32[]{:S(2)}) %copy-start) | copy-done | bytes 2359320
  9.0 0.2 stage.1.when.own_ref
  9.2 0.0 copy-start.1
  9.2 0.0 collective-permute-done.refs_1_
  9.2 1.2 %collective-permute-done.1.refs_2_ = bf16[32,896]{1,0:T(8,128)(2,1)S(1)} collective-permute-done((bf16[32,896]{1,0:T(8,128)(2,1)}, bf16[32,896]{1,0:T(8,128)(2,1)S(1)}, u32[]{:S(2)}, u32[]{:S(2)}) %collective-permute-start.1) | collective-permute-done | bytes 57376 | tf_op jit(solution)/shard_map/ppermute | solution.py:337
  10.5 0.3 collective-permute-done.2.refs_3_
  10.8 0.1 merge.1
  10.9 1.5 %collective-permute-start.5 = (bf16[216,128]{1,0:T(8,128)(2,1)S(1)}, bf16[216,128]{1,0:T(8,128)(2,1)S(1)}, u32[]{:S(2)}, u32[]{:S(2)}) collective-permute-start(bf16[216,128]{1,0:T(8,128)(2,1)S(1)} %get-tuple-element.39), channel_id=1, source_target_pairs={{0,5},{1,4},{2,7},{3,6},{4,1},{5,0},{6,3},{7,2},{8,13},{9,12},{10,... | collective-permute-start | bytes 165896 | tf_op jit(solution)/shard_map/ppermute | solution.py:342
  12.4 1.6 %collective-permute-start.8 = (bf16[216,128]{1,0:T(8,128)(2,1)S(1)}, bf16[216,128]{1,0:T(8,128)(2,1)S(1)}, u32[]{:S(2)}, u32[]{:S(2)}) collective-permute-start(bf16[216,128]{1,0:T(8,128)(2,1)S(1)} %get-tuple-element.37.refs_0_), channel_id=1, source_target_pairs={{0,2},{1,3},{2,0},{3,1},{4,6},{5,7},{6,4},{7,5},{8,10},{9,11},{10,... | collective-permute-start | bytes 165896 | tf_op jit(solution)/shard_map/ppermute | solution.py:342
  14.0 1.1 %collective-permute-start.6 = (bf16[216,128]{1,0:T(8,128)(2,1)S(1)}, bf16[216,128]{1,0:T(8,128)(2,1)S(1)}, u32[]{:S(2)}, u32[]{:S(2)}) collective-permute-start(bf16[216,128]{1,0:T(8,128)(2,1)S(1)} %get-tuple-element.38), channel_id=1, source_target_pairs={{0,6},{1,7},{2,4},{3,5},{4,2},{5,3},{6,0},{7,1},{8,14},{9,15},{10,... | collective-permute-start | bytes 165896 | tf_op jit(solution)/shard_map/ppermute | solution.py:342
  15.1 0.8 %collective-permute-start.4 = (bf16[216,128]{1,0:T(8,128)(2,1)S(1)}, bf16[216,128]{1,0:T(8,128)(2,1)S(1)}, u32[]{:S(2)}, u32[]{:S(2)}) collective-permute-start(bf16[216,128]{1,0:T(8,128)(2,1)S(1)} %get-tuple-element.38), channel_id=1, source_target_pairs={{0,4},{1,5},{2,6},{3,7},{4,0},{5,1},{6,2},{7,3},{8,12},{9,13},{10,... | collective-permute-start | bytes 165896 | tf_op jit(solution)/shard_map/ppermute | solution.py:342
  15.9 0.0 collective-permute-done.5.refs_2_
  15.9 2.5 %collective-permute-start.9 = (bf16[216,128]{1,0:T(8,128)(2,1)S(1)}, bf16[216,128]{1,0:T(8,128)(2,1)S(1)}, u32[]{:S(2)}, u32[]{:S(2)}) collective-permute-start(bf16[216,128]{1,0:T(8,128)(2,1)S(1)} %get-tuple-element.40.source_ref), channel_id=1, source_target_pairs={{0,3},{1,2},{2,1},{3,0},{4,7},{5,6},{6,5},{7,4},{8,11},{9,10},{10,... | collective-permute-start | bytes 165896 | tf_op jit(solution)/shard_map/ppermute | solution.py:342
  18.4 0.0 collective-permute-done.8.when_ref.refs_5_
  18.4 0.2 collective-permute-start.7
  18.6 2.1 %collective-permute-done.6.refs_3_ = bf16[216,128]{1,0:T(8,128)(2,1)S(1)} collective-permute-done((bf16[216,128]{1,0:T(8,128)(2,1)S(1)}, bf16[216,128]{1,0:T(8,128)(2,1)S(1)}, u32[]{:S(2)}, u32[]{:S(2)}) %collective-permute-start.6) | collective-permute-done | bytes 55328 | tf_op jit(solution)/shard_map/ppermute | solution.py:342
  20.7 0.2 hold.1.body_ref
  21.0 0.0 copy-start.3
  21.0 0.0 copy-start.4
  21.0 1.4 %collective-permute-done.4.refs_1_ = bf16[216,128]{1,0:T(8,128)(2,1)S(1)} collective-permute-done((bf16[216,128]{1,0:T(8,128)(2,1)S(1)}, bf16[216,128]{1,0:T(8,128)(2,1)S(1)}, u32[]{:S(2)}, u32[]{:S(2)}) %collective-permute-start.4) | collective-permute-done | bytes 55328 | tf_op jit(solution)/shard_map/ppermute | solution.py:342
  22.4 1.1 %collective-permute-done.7.refs_4_ = bf16[216,128]{1,0:T(8,128)(2,1)S(1)} collective-permute-done((bf16[216,128]{1,0:T(8,128)(2,1)S(1)}, bf16[216,128]{1,0:T(8,128)(2,1)S(1)}, u32[]{:S(2)}, u32[]{:S(2)}) %collective-permute-start.7) | collective-permute-done | bytes 55328 | tf_op jit(solution)/shard_map/ppermute | solution.py:342
  23.5 3.7 %fock.1 = (bf16[32,768]{1,0:T(8,128)(2,1)S(1)}, bf16[32,768]{1,0:T(8,128)(2,1)S(1)}, bf16[32,768]{1,0:T(8,128)(2,1)S(1)}, bf16[32,768]{1,0:T(8,128)(2,1)S(1)}, b...) custom-call(s32[1]{0:T(128)} %bitcast.1.blk_ref, ...), custom_call_target="tpu_custom_call" | custom-call | flops 2717908992 | bytes 6733824 | tf_op jit(solution)/shard_map/fock/pallas_call | solution.py:311
  27.2 0.3 collective-permute-start.12
  27.5 3.6 %collective-permute-start.11 = (bf16[32,768]{1,0:T(8,128)(2,1)S(1)}, bf16[32,768]{1,0:T(8,128)(2,1)S(1)}, u32[]{:S(2)}, u32[]{:S(2)}) collective-permute-start(bf16[32,768]{1,0:T(8,128)(2,1)S(1)} %get-tuple-element.42), channel_id=1, source_target_pairs={{0,4},{1,5},{2,6},{3,7},{4,0},{5,1},{6,2},{7,3},{8,12},{9,13},{10,... | collective-permute-start | bytes 147464 | tf_op jit(solution)/shard_map/ppermute | solution.py:342
  31.1 0.6 %collective-permute-start.14 = (bf16[32,768]{1,0:T(8,128)(2,1)S(1)}, bf16[32,768]{1,0:T(8,128)(2,1)S(1)}, u32[]{:S(2)}, u32[]{:S(2)}) collective-permute-start(bf16[32,768]{1,0:T(8,128)(2,1)S(1)} %get-tuple-element.49), channel_id=1, source_target_pairs={{0,6},{1,7},{2,4},{3,5},{4,2},{5,3},{6,0},{7,1},{8,14},{9,15},{10,... | collective-permute-start | bytes 147464 | tf_op jit(solution)/shard_map/ppermute | solution.py:342
  31.7 0.2 collective-permute-start.13
  31.9 2.4 %collective-permute-start.15 = (bf16[32,768]{1,0:T(8,128)(2,1)S(1)}, bf16[32,768]{1,0:T(8,128)(2,1)S(1)}, u32[]{:S(2)}, u32[]{:S(2)}) collective-permute-start(bf16[32,768]{1,0:T(8,128)(2,1)S(1)} %get-tuple-element.50), channel_id=1, source_target_pairs={{0,2},{1,3},{2,0},{3,1},{4,6},{5,7},{6,4},{7,5},{8,10},{9,11},{10,... | collective-permute-start | bytes 147464 | tf_op jit(solution)/shard_map/ppermute | solution.py:342
  34.2 1.2 %collective-permute-start.16 = (bf16[32,768]{1,0:T(8,128)(2,1)S(1)}, bf16[32,768]{1,0:T(8,128)(2,1)S(1)}, u32[]{:S(2)}, u32[]{:S(2)}) collective-permute-start(bf16[32,768]{1,0:T(8,128)(2,1)S(1)} %get-tuple-element.51), channel_id=1, source_target_pairs={{0,3},{1,2},{2,1},{3,0},{4,7},{5,6},{6,5},{7,4},{8,11},{9,10},{10,... | collective-permute-start | bytes 147464 | tf_op jit(solution)/shard_map/ppermute | solution.py:342
  35.5 0.1 collective-permute-start.17
  35.6 1.7 %collective-permute-done.14.refs_3_ = bf16[32,768]{1,0:T(8,128)(2,1)S(1)} collective-permute-done((bf16[32,768]{1,0:T(8,128)(2,1)S(1)}, bf16[32,768]{1,0:T(8,128)(2,1)S(1)}, u32[]{:S(2)}, u32[]{:S(2)}) %collective-permute-start.14) | collective-permute-done | bytes 49184 | tf_op jit(solution)/shard_map/ppermute | solution.py:342
  37.2 0.8 %collective-permute-done.13.refs_2_ = bf16[32,768]{1,0:T(8,128)(2,1)S(1)} collective-permute-done((bf16[32,768]{1,0:T(8,128)(2,1)S(1)}, bf16[32,768]{1,0:T(8,128)(2,1)S(1)}, u32[]{:S(2)}, u32[]{:S(2)}) %collective-permute-start.13) | collective-permute-done | bytes 49184 | tf_op jit(solution)/shard_map/ppermute | solution.py:342
  38.0 0.1 collective-permute-done.15.refs_4_
  38.1 0.9 %collective-permute-done.16.refs_5_ = bf16[32,768]{1,0:T(8,128)(2,1)S(1)} collective-permute-done((bf16[32,768]{1,0:T(8,128)(2,1)S(1)}, bf16[32,768]{1,0:T(8,128)(2,1)S(1)}, u32[]{:S(2)}, u32[]{:S(2)}) %collective-permute-start.16) | collective-permute-done | bytes 49184 | tf_op jit(solution)/shard_map/ppermute | solution.py:342
  39.0 0.1 sum.1
  39.1 1.4 %collective-permute-start.18 = (bf16[32,768]{1,0:T(8,128)(2,1)S(1)}, bf16[32,768]{1,0:T(8,128)(2,1)S(1)}, u32[]{:S(2)}, u32[]{:S(2)}) collective-permute-start(bf16[32,768]{1,0:T(8,128)(2,1)S(1)} %get-tuple-element.54), channel_id=1, source_target_pairs={{0,16},{8,24},{16,0},{24,8},{1,17},{9,25},{17,1},{25,9},{2,18},{10... | collective-permute-start | bytes 147464 | tf_op jit(solution)/shard_map/ppermute | solution.py:337
  40.4 1.7 %collective-permute-start.19 = (bf16[32,768]{1,0:T(8,128)(2,1)S(1)}, bf16[32,768]{1,0:T(8,128)(2,1)S(1)}, u32[]{:S(2)}, u32[]{:S(2)}) collective-permute-start(bf16[32,768]{1,0:T(8,128)(2,1)S(1)} %get-tuple-element.55), channel_id=1, source_target_pairs={{0,24},{8,16},{16,8},{24,0},{1,25},{9,17},{17,9},{25,1},{2,26},{10... | collective-permute-start | bytes 147464 | tf_op jit(solution)/shard_map/ppermute | solution.py:337
  42.1 0.5 %collective-permute-start.20 = (bf16[32,768]{1,0:T(8,128)(2,1)S(1)}, bf16[32,768]{1,0:T(8,128)(2,1)S(1)}, u32[]{:S(2)}, u32[]{:S(2)}) collective-permute-start(bf16[32,768]{1,0:T(8,128)(2,1)S(1)} %get-tuple-element.56), channel_id=1, source_target_pairs={{0,8},{8,0},{16,24},{24,16},{1,9},{9,1},{17,25},{25,17},{2,10},{10... | collective-permute-start | bytes 147464 | tf_op jit(solution)/shard_map/ppermute | solution.py:337
  42.6 0.6 %collective-permute-done.18.refs_1_ = bf16[32,768]{1,0:T(8,128)(2,1)S(1)} collective-permute-done((bf16[32,768]{1,0:T(8,128)(2,1)S(1)}, bf16[32,768]{1,0:T(8,128)(2,1)S(1)}, u32[]{:S(2)}, u32[]{:S(2)}) %collective-permute-start.18) | collective-permute-done | bytes 49184 | tf_op jit(solution)/shard_map/ppermute | solution.py:337
  43.2 2.6 %collective-permute-done.19.refs_2_ = bf16[32,768]{1,0:T(8,128)(2,1)S(1)} collective-permute-done((bf16[32,768]{1,0:T(8,128)(2,1)S(1)}, bf16[32,768]{1,0:T(8,128)(2,1)S(1)}, u32[]{:S(2)}, u32[]{:S(2)}) %collective-permute-start.19) | collective-permute-done | bytes 49184 | tf_op jit(solution)/shard_map/ppermute | solution.py:337
  45.8 0.4 collective-permute-done.20.refs_3_
  46.2 1.4 %deal.1 = bf16[16,8,768]{2,1,0:T(8,128)(2,1)} custom-call(s32[1]{0:T(128)} %bitcast.me_ref, s32[8]{0:T(128)S(1)} %copy-done.3, f32[8]{0:T(128)S(1)} %copy-done.4, f32[8,128]{1,0:T(8,128)S(1)} %get-tuple-element.35.refs_1_.total_ref, bf16[32,768]{1,0:T(8,128)(2,1)S(1)} %get-tuple-element.53.refs_0_, bf16[32,768]{1,0:T(8,128)(2,1)S(1)} %collective-permute-done.18.refs_1_, ...), custom_call_target="tpu_custom_call" | custom-call | bytes 397312 | tf_op jit(solution)/shard_map/deal/pallas_call | solution.py:311
  (14 shorter events, 0.1 us)
Async XLA Ops:
  0.0 23.5 %collective-permute-start.3 = (bf16[12,128,768]{2,1,0:T(8,128)(2,1)}, bf16[12,128,768]{2,1,0:T(8,128)(2,1)S(1)}, u32[]{:S(2)}, u32[]{:S(2)}) collective-permute-start(bf16[12,128,768]{2,1,0:T(8,128)(2,1)} %refs_0_.2), channel_id=1, source_target_pairs={{0,1},{1,0},{2,3},{3,2},{4,5},{5,4},{6,7},{7,6},{8,9},{9,8},{10,11... | collective-permute-start | bytes 7077896 | tf_op jit(solution)/shard_map/ppermute | solution.py:342
  2.4 6.9 %collective-permute-start = (bf16[32,896]{1,0:T(8,128)(2,1)}, bf16[32,896]{1,0:T(8,128)(2,1)S(1)}, u32[]{:S(2)}, u32[]{:S(2)}) collective-permute-start(bf16[32,896]{1,0:T(8,128)(2,1)} %get-tuple-element.32), channel_id=1, source_target_pairs={{0,16},{8,24},{16,0},{24,8},{1,17},{9,25},{17,1},{25,9},{2,18},{10... | collective-permute-start | bytes 172040 | tf_op jit(solution)/shard_map/ppermute | solution.py:337
  5.0 5.5 %collective-permute-start.1 = (bf16[32,896]{1,0:T(8,128)(2,1)}, bf16[32,896]{1,0:T(8,128)(2,1)S(1)}, u32[]{:S(2)}, u32[]{:S(2)}) collective-permute-start(bf16[32,896]{1,0:T(8,128)(2,1)} %get-tuple-element.33), channel_id=1, source_target_pairs={{0,24},{8,16},{16,8},{24,0},{1,25},{9,17},{17,9},{25,1},{2,26},{10... | collective-permute-start | bytes 172040 | tf_op jit(solution)/shard_map/ppermute | solution.py:337
  6.4 4.4 %collective-permute-start.2 = (bf16[32,896]{1,0:T(8,128)(2,1)}, bf16[32,896]{1,0:T(8,128)(2,1)S(1)}, u32[]{:S(2)}, u32[]{:S(2)}) collective-permute-start(bf16[32,896]{1,0:T(8,128)(2,1)} %get-tuple-element.34), channel_id=1, source_target_pairs={{0,8},{8,0},{16,24},{24,16},{1,9},{9,1},{17,25},{25,17},{2,10},{10... | collective-permute-start | bytes 172040 | tf_op jit(solution)/shard_map/ppermute | solution.py:337
  6.5 0.8 %copy-start.2 = (bf16[32,896]{1,0:T(8,128)(2,1)S(1)}, bf16[32,896]{1,0:T(8,128)(2,1)}, u32[]{:S(2)}) copy-start(bf16[32,896]{1,0:T(8,128)(2,1)} %get-tuple-element.31.refs_0_) | copy-start | bytes 172036
  7.4 1.7 %copy-start = (bf16[12,128,768]{2,1,0:T(8,128)(2,1)S(1)}, bf16[12,128,768]{2,1,0:T(8,128)(2,1)}, u32[]{:S(2)}) copy-start(bf16[12,128,768]{2,1,0:T(8,128)(2,1)} %refs_0_.2) | copy-start | bytes 7077892
  9.2 11.5 %copy-start.1 = (bf16[768,768]{1,0:T(8,128)(2,1)S(1)}, bf16[768,768]{1,0:T(8,128)(2,1)}, u32[]{:S(2)}) copy-start(bf16[768,768]{1,0:T(8,128)(2,1)} %refs_0_.3) | copy-start | bytes 3538948
  10.9 5.0 %collective-permute-start.5 = (bf16[216,128]{1,0:T(8,128)(2,1)S(1)}, bf16[216,128]{1,0:T(8,128)(2,1)S(1)}, u32[]{:S(2)}, u32[]{:S(2)}) collective-permute-start(bf16[216,128]{1,0:T(8,128)(2,1)S(1)} %get-tuple-element.39), channel_id=1, source_target_pairs={{0,5},{1,4},{2,7},{3,6},{4,1},{5,0},{6,3},{7,2},{8,13},{9,12},{10,... | collective-permute-start | bytes 165896 | tf_op jit(solution)/shard_map/ppermute | solution.py:342
  12.4 6.0 %collective-permute-start.8 = (bf16[216,128]{1,0:T(8,128)(2,1)S(1)}, bf16[216,128]{1,0:T(8,128)(2,1)S(1)}, u32[]{:S(2)}, u32[]{:S(2)}) collective-permute-start(bf16[216,128]{1,0:T(8,128)(2,1)S(1)} %get-tuple-element.37.refs_0_), channel_id=1, source_target_pairs={{0,2},{1,3},{2,0},{3,1},{4,6},{5,7},{6,4},{7,5},{8,10},{9,11},{10,... | collective-permute-start | bytes 165896 | tf_op jit(solution)/shard_map/ppermute | solution.py:342
  14.0 6.7 %collective-permute-start.6 = (bf16[216,128]{1,0:T(8,128)(2,1)S(1)}, bf16[216,128]{1,0:T(8,128)(2,1)S(1)}, u32[]{:S(2)}, u32[]{:S(2)}) collective-permute-start(bf16[216,128]{1,0:T(8,128)(2,1)S(1)} %get-tuple-element.38), channel_id=1, source_target_pairs={{0,6},{1,7},{2,4},{3,5},{4,2},{5,3},{6,0},{7,1},{8,14},{9,15},{10,... | collective-permute-start | bytes 165896 | tf_op jit(solution)/shard_map/ppermute | solution.py:342
  15.1 7.3 %collective-permute-start.4 = (bf16[216,128]{1,0:T(8,128)(2,1)S(1)}, bf16[216,128]{1,0:T(8,128)(2,1)S(1)}, u32[]{:S(2)}, u32[]{:S(2)}) collective-permute-start(bf16[216,128]{1,0:T(8,128)(2,1)S(1)} %get-tuple-element.38), channel_id=1, source_target_pairs={{0,4},{1,5},{2,6},{3,7},{4,0},{5,1},{6,2},{7,3},{8,12},{9,13},{10,... | collective-permute-start | bytes 165896 | tf_op jit(solution)/shard_map/ppermute | solution.py:342
  15.9 6.5 %collective-permute-start.9 = (bf16[216,128]{1,0:T(8,128)(2,1)S(1)}, bf16[216,128]{1,0:T(8,128)(2,1)S(1)}, u32[]{:S(2)}, u32[]{:S(2)}) collective-permute-start(bf16[216,128]{1,0:T(8,128)(2,1)S(1)} %get-tuple-element.40.source_ref), channel_id=1, source_target_pairs={{0,3},{1,2},{2,1},{3,0},{4,7},{5,6},{6,5},{7,4},{8,11},{9,10},{10,... | collective-permute-start | bytes 165896 | tf_op jit(solution)/shard_map/ppermute | solution.py:342
  18.4 5.1 %collective-permute-start.7 = (bf16[216,128]{1,0:T(8,128)(2,1)S(1)}, bf16[216,128]{1,0:T(8,128)(2,1)S(1)}, u32[]{:S(2)}, u32[]{:S(2)}) collective-permute-start(bf16[216,128]{1,0:T(8,128)(2,1)S(1)} %collective-permute-done.5.refs_2_), channel_id=1, source_target_pairs={{0,2},{1,3},{2,0},{3,1},{4,6},{5,7},{6,4},{7,5},{8,10},{9,11},{10,... | collective-permute-start | bytes 165896 | tf_op jit(solution)/shard_map/ppermute | solution.py:342
  20.7 2.8 %collective-permute-start.10 = (bf16[216,128]{1,0:T(8,128)(2,1)S(1)}, bf16[216,128]{1,0:T(8,128)(2,1)S(1)}, u32[]{:S(2)}, u32[]{:S(2)}) collective-permute-start(bf16[216,128]{1,0:T(8,128)(2,1)S(1)} %after.1), channel_id=1, source_target_pairs={{0,1},{1,0},{2,3},{3,2},{4,5},{5,4},{6,7},{7,6},{8,9},{9,8},{10,11... | collective-permute-start | bytes 165896 | tf_op jit(solution)/shard_map/ppermute | solution.py:342
  21.0 25.3 %copy-start.3 = (s32[8]{0:T(128)S(1)}, s32[8]{0:T(128)}, u32[]{:S(2)}) copy-start(s32[8]{0:T(128)} %target_ref.1) | copy-start | bytes 100
  21.0 25.3 %copy-start.4 = (f32[8]{0:T(128)S(1)}, f32[8]{0:T(128)}, u32[]{:S(2)}) copy-start(f32[8]{0:T(128)} %weights_ref.1) | copy-start | bytes 100
  27.2 4.5 %collective-permute-start.12 = (bf16[32,768]{1,0:T(8,128)(2,1)S(1)}, bf16[32,768]{1,0:T(8,128)(2,1)S(1)}, u32[]{:S(2)}, u32[]{:S(2)}) collective-permute-start(bf16[32,768]{1,0:T(8,128)(2,1)S(1)} %get-tuple-element.47), channel_id=1, source_target_pairs={{0,2},{1,3},{2,0},{3,1},{4,6},{5,7},{6,4},{7,5},{8,10},{9,11},{10,... | collective-permute-start | bytes 147464 | tf_op jit(solution)/shard_map/ppermute | solution.py:342
  27.5 8.0 %collective-permute-start.11 = (bf16[32,768]{1,0:T(8,128)(2,1)S(1)}, bf16[32,768]{1,0:T(8,128)(2,1)S(1)}, u32[]{:S(2)}, u32[]{:S(2)}) collective-permute-start(bf16[32,768]{1,0:T(8,128)(2,1)S(1)} %get-tuple-element.42), channel_id=1, source_target_pairs={{0,4},{1,5},{2,6},{3,7},{4,0},{5,1},{6,2},{7,3},{8,12},{9,13},{10,... | collective-permute-start | bytes 147464 | tf_op jit(solution)/shard_map/ppermute | solution.py:342
  31.1 6.2 %collective-permute-start.14 = (bf16[32,768]{1,0:T(8,128)(2,1)S(1)}, bf16[32,768]{1,0:T(8,128)(2,1)S(1)}, u32[]{:S(2)}, u32[]{:S(2)}) collective-permute-start(bf16[32,768]{1,0:T(8,128)(2,1)S(1)} %get-tuple-element.49), channel_id=1, source_target_pairs={{0,6},{1,7},{2,4},{3,5},{4,2},{5,3},{6,0},{7,1},{8,14},{9,15},{10,... | collective-permute-start | bytes 147464 | tf_op jit(solution)/shard_map/ppermute | solution.py:342
  31.7 6.4 %collective-permute-start.13 = (bf16[32,768]{1,0:T(8,128)(2,1)S(1)}, bf16[32,768]{1,0:T(8,128)(2,1)S(1)}, u32[]{:S(2)}, u32[]{:S(2)}) collective-permute-start(bf16[32,768]{1,0:T(8,128)(2,1)S(1)} %get-tuple-element.48), channel_id=1, source_target_pairs={{0,5},{1,4},{2,7},{3,6},{4,1},{5,0},{6,3},{7,2},{8,13},{9,12},{10,... | collective-permute-start | bytes 147464 | tf_op jit(solution)/shard_map/ppermute | solution.py:342
  31.9 6.2 %collective-permute-start.15 = (bf16[32,768]{1,0:T(8,128)(2,1)S(1)}, bf16[32,768]{1,0:T(8,128)(2,1)S(1)}, u32[]{:S(2)}, u32[]{:S(2)}) collective-permute-start(bf16[32,768]{1,0:T(8,128)(2,1)S(1)} %get-tuple-element.50), channel_id=1, source_target_pairs={{0,2},{1,3},{2,0},{3,1},{4,6},{5,7},{6,4},{7,5},{8,10},{9,11},{10,... | collective-permute-start | bytes 147464 | tf_op jit(solution)/shard_map/ppermute | solution.py:342
  34.2 4.7 %collective-permute-start.16 = (bf16[32,768]{1,0:T(8,128)(2,1)S(1)}, bf16[32,768]{1,0:T(8,128)(2,1)S(1)}, u32[]{:S(2)}, u32[]{:S(2)}) collective-permute-start(bf16[32,768]{1,0:T(8,128)(2,1)S(1)} %get-tuple-element.51), channel_id=1, source_target_pairs={{0,3},{1,2},{2,1},{3,0},{4,7},{5,6},{6,5},{7,4},{8,11},{9,10},{10,... | collective-permute-start | bytes 147464 | tf_op jit(solution)/shard_map/ppermute | solution.py:342
  35.5 3.5 %collective-permute-start.17 = (bf16[32,768]{1,0:T(8,128)(2,1)S(1)}, bf16[32,768]{1,0:T(8,128)(2,1)S(1)}, u32[]{:S(2)}, u32[]{:S(2)}) collective-permute-start(bf16[32,768]{1,0:T(8,128)(2,1)S(1)} %get-tuple-element.52), channel_id=1, source_target_pairs={{0,1},{1,0},{2,3},{3,2},{4,5},{5,4},{6,7},{7,6},{8,9},{9,8},{10,11... | collective-permute-start | bytes 147464 | tf_op jit(solution)/shard_map/ppermute | solution.py:342
  39.1 4.2 %collective-permute-start.18 = (bf16[32,768]{1,0:T(8,128)(2,1)S(1)}, bf16[32,768]{1,0:T(8,128)(2,1)S(1)}, u32[]{:S(2)}, u32[]{:S(2)}) collective-permute-start(bf16[32,768]{1,0:T(8,128)(2,1)S(1)} %get-tuple-element.54), channel_id=1, source_target_pairs={{0,16},{8,24},{16,0},{24,8},{1,17},{9,25},{17,1},{25,9},{2,18},{10... | collective-permute-start | bytes 147464 | tf_op jit(solution)/shard_map/ppermute | solution.py:337
  40.4 5.4 %collective-permute-start.19 = (bf16[32,768]{1,0:T(8,128)(2,1)S(1)}, bf16[32,768]{1,0:T(8,128)(2,1)S(1)}, u32[]{:S(2)}, u32[]{:S(2)}) collective-permute-start(bf16[32,768]{1,0:T(8,128)(2,1)S(1)} %get-tuple-element.55), channel_id=1, source_target_pairs={{0,24},{8,16},{16,8},{24,0},{1,25},{9,17},{17,9},{25,1},{2,26},{10... | collective-permute-start | bytes 147464 | tf_op jit(solution)/shard_map/ppermute | solution.py:337
  42.1 4.1 %collective-permute-start.20 = (bf16[32,768]{1,0:T(8,128)(2,1)S(1)}, bf16[32,768]{1,0:T(8,128)(2,1)S(1)}, u32[]{:S(2)}, u32[]{:S(2)}) collective-permute-start(bf16[32,768]{1,0:T(8,128)(2,1)S(1)} %get-tuple-element.56), channel_id=1, source_target_pairs={{0,8},{8,0},{16,24},{24,16},{1,9},{9,1},{17,25},{25,17},{2,10},{10... | collective-permute-start | bytes 147464 | tf_op jit(solution)/shard_map/ppermute | solution.py:337

commit v15 on v14

--- a/solution.py
+++ b/solution.py
@@ -159,10 +159,6 @@
     return [(0, 0)] + [(s, e) for s in far for e in range(2)] + [(0, 1)]
 
 
-def after_kernel(source_ref, when_ref, out_ref):
-    out_ref[...] = source_ref[...]
-
-
 def arrivals(n):
     return hops(n)
 
@@ -213,7 +209,7 @@
                 prop[w, source, :, c * LANES : (c + 1) * LANES] = piece.astype(prop.dtype)
     scaled = jnp.concatenate([prop[w, i] for w in range(half) for i in range(n)], axis=0).astype(BF16)
     carried[...] = jnp.dot(scaled, body_ref[...], preferred_element_type=F32).astype(BF16)
-    batch = math.gcd(vec_count, 4)
+    batch = vec_count
     for c, ref in enumerate((own_ref, sib_ref)):
         for g in range(0, vec_count, batch):
             left = ref[g : g + batch].reshape(batch * occupied, orbitals)
@@ -386,6 +382,7 @@
         vmem=STAGE_VMEM,
     )
     routed = [to_list(routed[s], s) if s else kept for s in order]
+    routed[1], sibling = lax.optimization_barrier((routed[1], sibling))
     payload = shape((chunks * slab + 2 * half * chunks, LANES), BF16)
     same, other, same2, other2, weight_sum, pick = call(
         functools.partial(merge_kernel, order, keep, cap, orbitals),
@@ -411,14 +408,17 @@
         if leading(s, e, chips) == s and 2 * s >= chips:
             gathered[s, e] = to_block(other if e else same, s, e)
     for s, e in hops(n):
-        if leading(s, e, chips) == s and 2 * s < chips and (s, e) != (0, 1):
+        if leading(s, e, chips) == s and 2 * s < chips and (s, e) not in ((0, 1), (1, 1)):
             gathered[s, e] = to_block(other2 if e else same2, s, e)
+    first = (chips // 2, 1)
+    gathered[first], later = lax.optimization_barrier((gathered[first], other2))
+    gathered[1, 0], latest = lax.optimization_barrier((gathered[1, 0], later))
     for s, e in hops(n):
         top = leading(s, e, chips)
         if top != s:
             gathered[s, e] = to_block(gathered[top, e], s ^ top, 0)
-    (last,) = call(after_kernel, [payload], [], [], [other2, gathered.get((1, 0), same2)], [], "after")
-    gathered[0, 1] = to_block(last, 0, 1)
+    gathered[1, 1] = to_block(later, 1, 1)
+    gathered[0, 1] = to_block(latest, 0, 1)
     gathered = [gathered[hop] for hop in arrivals(n)]
     held = F32 if rows % 16 else BF16
     parts = call(

time: 47.9 us -> 47.8 us (level)
  starting transfers between devices: 24.1 us -> 22.6 us
  waiting for transfers between devices: 13.2 us -> 14.6 us
    ppermute x15, waiting for transfers between devices: 8.04 us -> 9.73 us  [to_block(): lax.ppermute(x, 'blk', [(i, 2 * moved(i // 2, s, n // 2, 1) + (i % 2 ^ e)...]
    ppermute x15, starting transfers between devices: 16.5 us -> 14.9 us  [to_block(): lax.ppermute(x, 'blk', [(i, 2 * moved(i // 2, s, n // 2, 1) + (i % 2 ^ e)...]
    pallas_call x10 -> x9, Pallas kernels: 7.74 us -> 7.81 us  [call(): pl.pallas_call(kernel, out_shape=outs, in_specs=[smem] * len(scalars) + [...]
  transfers between devices with their start and end apart: 21 -> 21, of which waited for: 12 -> 13; matrix products, arithmetic and copies ran while one was open for 0% -> 0% of each run, Pallas kernels for 5% -> 5%
where the time goes in v15:
time: 47.8 us; the launch traced here: 47.6 us
  starting transfers between devices  22.6 us (47%)
  waiting for transfers between devices  14.6 us (31%)
  Pallas kernels  7.81 us (16%)
  local copies, waits for them, and re-layouts  2.5 us (5%)
    ppermute x15, starting transfers between devices, to_block(): lax.ppermute(x, 'blk', [(i, 2 * moved(i // 2, s, n // 2, 1) + (i % 2 ^ e)...  14.9 us
    ppermute x15, waiting for transfers between devices, to_block(): lax.ppermute(x, 'blk', [(i, 2 * moved(i // 2, s, n // 2, 1) + (i % 2 ^ e)...  9.73 us
    pallas_call x9, Pallas kernels, call(): pl.pallas_call(kernel, out_shape=outs, in_specs=[smem] * len(scalars) + [...  7.81 us
    ppermute x6, starting transfers between devices, to_list(): lax.ppermute(x, 'grp', [(i, moved(i, s, groups, 1)) for i in range(groups)])  7.68 us
    ppermute x6, waiting for transfers between devices, to_list(): lax.ppermute(x, 'grp', [(i, moved(i, s, groups, 1)) for i in range(groups)])  4.86 us
    unnamed x10, local copies, waits for them, and re-layouts  2.5 us
  transfers between devices with their start and end apart: 21, of which 13 were waited for; matrix products, arithmetic and copies ran while one was open for 0% of the time, Pallas kernels for 5%

profile of v15, /device:TPU:0, one launch (start us, length us, event | category | flops | bytes accessed | tf_op | source)
XLA Modules:
  0.0 47.6 jit_solution(14536196766389193088)
XLA Ops:
  0.0 0.5 collective-permute-start.1
  0.5 1.9 %route.1 = (bf16[32,896]{1,0:T(8,128)(2,1)}, bf16[32,896]{1,0:T(8,128)(2,1)}, bf16[32,896]{1,0:T(8,128)(2,1)}, bf16[32,896]{1,0:T(8,128)(2,1)}) custom-call(s32[1]{0:T(128)} %bitcast.me_ref, s32[8]{0:T(128)} %target_ref.1, f32[8]{0:T(128)} %weights_ref.1, bf16[16,8,768]{2,1,0:T(8,128)(2,1)} %walkers_any.1, f32[8,12]{1,0:T(8,128)} %fields_any.1, ...), custom_call_target="tpu_custom_call" | custom-call | bytes 229376 | tf_op jit(solution)/shard_map/route/pallas_call | solution.py:307
  2.4 2.6 %collective-permute-start = (bf16[32,896]{1,0:T(8,128)(2,1)}, bf16[32,896]{1,0:T(8,128)(2,1)S(1)}, u32[]{:S(2)}, u32[]{:S(2)}) collective-permute-start(bf16[32,896]{1,0:T(8,128)(2,1)} %get-tuple-element.38), channel_id=1, source_target_pairs={{0,16},{8,24},{16,0},{24,8},{1,17},{9,25},{17,1},{25,9},{2,18},{10... | collective-permute-start | bytes 172040 | tf_op jit(solution)/shard_map/ppermute | solution.py:333
  5.0 1.4 %collective-permute-start.2 = (bf16[32,896]{1,0:T(8,128)(2,1)}, bf16[32,896]{1,0:T(8,128)(2,1)S(1)}, u32[]{:S(2)}, u32[]{:S(2)}) collective-permute-start(bf16[32,896]{1,0:T(8,128)(2,1)} %get-tuple-element.40), channel_id=1, source_target_pairs={{0,24},{8,16},{16,8},{24,0},{1,25},{9,17},{17,9},{25,1},{2,26},{10... | collective-permute-start | bytes 172040 | tf_op jit(solution)/shard_map/ppermute | solution.py:333
  6.4 0.1 collective-permute-start.3
  6.5 0.8 %copy-done.2 = bf16[32,896]{1,0:T(8,128)(2,1)S(1)} copy-done((bf16[32,896]{1,0:T(8,128)(2,1)S(1)}, bf16[32,896]{1,0:T(8,128)(2,1)}, u32[]{:S(2)}) %copy-start.2) | copy-done | bytes 57368
  7.4 0.0 copy-start
  7.4 1.7 %copy-done = bf16[12,128,768]{2,1,0:T(8,128)(2,1)S(1)} copy-done((bf16[12,128,768]{2,1,0:T(8,128)(2,1)S(1)}, bf16[12,128,768]{2,1,0:T(8,128)(2,1)}, u32[]{:S(2)}) %copy-start) | copy-done | bytes 2359320
  9.0 0.2 stage.1.when.own_ref
  9.2 0.0 copy-start.1
  9.2 0.0 collective-permute-done.refs_1_
  9.3 1.2 %collective-permute-done.2.refs_2_ = bf16[32,896]{1,0:T(8,128)(2,1)S(1)} collective-permute-done((bf16[32,896]{1,0:T(8,128)(2,1)}, bf16[32,896]{1,0:T(8,128)(2,1)S(1)}, u32[]{:S(2)}, u32[]{:S(2)}) %collective-permute-start.2) | collective-permute-done | bytes 57376 | tf_op jit(solution)/shard_map/ppermute | solution.py:333
  10.5 0.3 collective-permute-done.3.refs_3_
  10.8 0.1 merge.1
  10.9 1.5 %collective-permute-start.5 = (bf16[216,128]{1,0:T(8,128)(2,1)S(1)}, bf16[216,128]{1,0:T(8,128)(2,1)S(1)}, u32[]{:S(2)}, u32[]{:S(2)}) collective-permute-start(bf16[216,128]{1,0:T(8,128)(2,1)S(1)} %get-tuple-element.47), channel_id=1, source_target_pairs={{0,5},{1,4},{2,7},{3,6},{4,1},{5,0},{6,3},{7,2},{8,13},{9,12},{10,... | collective-permute-start | bytes 165896 | tf_op jit(solution)/shard_map/ppermute | solution.py:338
  12.4 1.6 %collective-permute-start.8 = (bf16[216,128]{1,0:T(8,128)(2,1)S(1)}, bf16[216,128]{1,0:T(8,128)(2,1)S(1)}, u32[]{:S(2)}, u32[]{:S(2)}) collective-permute-start(bf16[216,128]{1,0:T(8,128)(2,1)S(1)} %get-tuple-element.45.refs_0_), channel_id=1, source_target_pairs={{0,2},{1,3},{2,0},{3,1},{4,6},{5,7},{6,4},{7,5},{8,10},{9,11},{10,... | collective-permute-start | bytes 165896 | tf_op jit(solution)/shard_map/ppermute | solution.py:338
  14.0 1.1 %collective-permute-start.6 = (bf16[216,128]{1,0:T(8,128)(2,1)S(1)}, bf16[216,128]{1,0:T(8,128)(2,1)S(1)}, u32[]{:S(2)}, u32[]{:S(2)}) collective-permute-start(bf16[216,128]{1,0:T(8,128)(2,1)S(1)} %get-tuple-element.46), channel_id=1, source_target_pairs={{0,6},{1,7},{2,4},{3,5},{4,2},{5,3},{6,0},{7,1},{8,14},{9,15},{10,... | collective-permute-start | bytes 165896 | tf_op jit(solution)/shard_map/ppermute | solution.py:338
  15.1 0.8 %collective-permute-start.4 = (bf16[216,128]{1,0:T(8,128)(2,1)S(1)}, bf16[216,128]{1,0:T(8,128)(2,1)S(1)}, u32[]{:S(2)}, u32[]{:S(2)}) collective-permute-start(bf16[216,128]{1,0:T(8,128)(2,1)S(1)} %get-tuple-element.46), channel_id=1, source_target_pairs={{0,4},{1,5},{2,6},{3,7},{4,0},{5,1},{6,2},{7,3},{8,12},{9,13},{10,... | collective-permute-start | bytes 165896 | tf_op jit(solution)/shard_map/ppermute | solution.py:338
  15.9 2.5 %collective-permute-start.7 = (bf16[216,128]{1,0:T(8,128)(2,1)S(1)}, bf16[216,128]{1,0:T(8,128)(2,1)S(1)}, u32[]{:S(2)}, u32[]{:S(2)}) collective-permute-start(bf16[216,128]{1,0:T(8,128)(2,1)S(1)} %collective-permute-done.5.refs_2_), channel_id=1, source_target_pairs={{0,2},{1,3},{2,0},{3,1},{4,6},{5,7},{6,4},{7,5},{8,10},{9,11},{10,... | collective-permute-start | bytes 165896 | tf_op jit(solution)/shard_map/ppermute | solution.py:338
  18.4 0.1 collective-permute-start.9
  18.4 0.1 collective-permute-start.10
  18.5 0.2 hold.1.body_ref
  18.8 0.0 copy-start.3
  18.8 0.0 copy-start.4
  18.8 1.9 %collective-permute-done.6.refs_3_ = bf16[216,128]{1,0:T(8,128)(2,1)S(1)} collective-permute-done((bf16[216,128]{1,0:T(8,128)(2,1)S(1)}, bf16[216,128]{1,0:T(8,128)(2,1)S(1)}, u32[]{:S(2)}, u32[]{:S(2)}) %collective-permute-start.6) | collective-permute-done | bytes 55328 | tf_op jit(solution)/shard_map/ppermute | solution.py:338
  20.7 1.7 %collective-permute-done.4.refs_1_ = bf16[216,128]{1,0:T(8,128)(2,1)S(1)} collective-permute-done((bf16[216,128]{1,0:T(8,128)(2,1)S(1)}, bf16[216,128]{1,0:T(8,128)(2,1)S(1)}, u32[]{:S(2)}, u32[]{:S(2)}) %collective-permute-start.4) | collective-permute-done | bytes 55328 | tf_op jit(solution)/shard_map/ppermute | solution.py:338
  22.4 1.1 %collective-permute-done.9.refs_6_ = bf16[216,128]{1,0:T(8,128)(2,1)S(1)} collective-permute-done((bf16[216,128]{1,0:T(8,128)(2,1)S(1)}, bf16[216,128]{1,0:T(8,128)(2,1)S(1)}, u32[]{:S(2)}, u32[]{:S(2)}) %collective-permute-start.9) | collective-permute-done | bytes 55328 | tf_op jit(solution)/shard_map/ppermute | solution.py:338
  23.5 3.8 %fock.1 = (bf16[32,768]{1,0:T(8,128)(2,1)S(1)}, bf16[32,768]{1,0:T(8,128)(2,1)S(1)}, bf16[32,768]{1,0:T(8,128)(2,1)S(1)}, bf16[32,768]{1,0:T(8,128)(2,1)S(1)}, b...) custom-call(s32[1]{0:T(128)} %bitcast.1.blk_ref, ...), custom_call_target="tpu_custom_call" | custom-call | flops 2717908992 | bytes 6733824 | tf_op jit(solution)/shard_map/fock/pallas_call | solution.py:307
  27.3 0.1 collective-permute-start.12
  27.3 2.8 %collective-permute-start.11 = (bf16[32,768]{1,0:T(8,128)(2,1)S(1)}, bf16[32,768]{1,0:T(8,128)(2,1)S(1)}, u32[]{:S(2)}, u32[]{:S(2)}) collective-permute-start(bf16[32,768]{1,0:T(8,128)(2,1)S(1)} %get-tuple-element.54), channel_id=1, source_target_pairs={{0,4},{1,5},{2,6},{3,7},{4,0},{5,1},{6,2},{7,3},{8,12},{9,13},{10,... | collective-permute-start | bytes 147464 | tf_op jit(solution)/shard_map/ppermute | solution.py:338
  30.2 1.5 %collective-permute-start.14 = (bf16[32,768]{1,0:T(8,128)(2,1)S(1)}, bf16[32,768]{1,0:T(8,128)(2,1)S(1)}, u32[]{:S(2)}, u32[]{:S(2)}) collective-permute-start(bf16[32,768]{1,0:T(8,128)(2,1)S(1)} %get-tuple-element.61), channel_id=1, source_target_pairs={{0,6},{1,7},{2,4},{3,5},{4,2},{5,3},{6,0},{7,1},{8,14},{9,15},{10,... | collective-permute-start | bytes 147464 | tf_op jit(solution)/shard_map/ppermute | solution.py:338
  31.7 0.6 %collective-permute-done.12.refs_4_ = bf16[32,768]{1,0:T(8,128)(2,1)S(1)} collective-permute-done((bf16[32,768]{1,0:T(8,128)(2,1)S(1)}, bf16[32,768]{1,0:T(8,128)(2,1)S(1)}, u32[]{:S(2)}, u32[]{:S(2)}) %collective-permute-start.12) | collective-permute-done | bytes 49184 | tf_op jit(solution)/shard_map/ppermute | solution.py:338
  32.3 0.1 collective-permute-start.13
  32.4 1.5 %collective-permute-start.15 = (bf16[32,768]{1,0:T(8,128)(2,1)S(1)}, bf16[32,768]{1,0:T(8,128)(2,1)S(1)}, u32[]{:S(2)}, u32[]{:S(2)}) collective-permute-start(bf16[32,768]{1,0:T(8,128)(2,1)S(1)} %get-tuple-element.62), channel_id=1, source_target_pairs={{0,2},{1,3},{2,0},{3,1},{4,6},{5,7},{6,4},{7,5},{8,10},{9,11},{10,... | collective-permute-start | bytes 147464 | tf_op jit(solution)/shard_map/ppermute | solution.py:338
  33.9 0.8 %collective-permute-start.16 = (bf16[32,768]{1,0:T(8,128)(2,1)S(1)}, bf16[32,768]{1,0:T(8,128)(2,1)S(1)}, u32[]{:S(2)}, u32[]{:S(2)}) collective-permute-start(bf16[32,768]{1,0:T(8,128)(2,1)S(1)} %get-tuple-element.63), channel_id=1, source_target_pairs={{0,3},{1,2},{2,1},{3,0},{4,7},{5,6},{6,5},{7,4},{8,11},{9,10},{10,... | collective-permute-start | bytes 147464 | tf_op jit(solution)/shard_map/ppermute | solution.py:338
  34.6 0.1 collective-permute-start.17
  34.7 1.4 %collective-permute-done.14.refs_3_ = bf16[32,768]{1,0:T(8,128)(2,1)S(1)} collective-permute-done((bf16[32,768]{1,0:T(8,128)(2,1)S(1)}, bf16[32,768]{1,0:T(8,128)(2,1)S(1)}, u32[]{:S(2)}, u32[]{:S(2)}) %collective-permute-start.14) | collective-permute-done | bytes 49184 | tf_op jit(solution)/shard_map/ppermute | solution.py:338
  36.2 1.6 %collective-permute-done.13.refs_2_ = bf16[32,768]{1,0:T(8,128)(2,1)S(1)} collective-permute-done((bf16[32,768]{1,0:T(8,128)(2,1)S(1)}, bf16[32,768]{1,0:T(8,128)(2,1)S(1)}, u32[]{:S(2)}, u32[]{:S(2)}) %collective-permute-start.13) | collective-permute-done | bytes 49184 | tf_op jit(solution)/shard_map/ppermute | solution.py:338
  37.8 0.4 collective-permute-done.15.refs_4_
  38.2 1.0 %collective-permute-done.16.refs_5_ = bf16[32,768]{1,0:T(8,128)(2,1)S(1)} collective-permute-done((bf16[32,768]{1,0:T(8,128)(2,1)S(1)}, bf16[32,768]{1,0:T(8,128)(2,1)S(1)}, u32[]{:S(2)}, u32[]{:S(2)}) %collective-permute-start.16) | collective-permute-done | bytes 49184 | tf_op jit(solution)/shard_map/ppermute | solution.py:338
  39.2 0.1 sum.1
  39.3 1.2 %collective-permute-start.18 = (bf16[32,768]{1,0:T(8,128)(2,1)S(1)}, bf16[32,768]{1,0:T(8,128)(2,1)S(1)}, u32[]{:S(2)}, u32[]{:S(2)}) collective-permute-start(bf16[32,768]{1,0:T(8,128)(2,1)S(1)} %get-tuple-element.66), channel_id=1, source_target_pairs={{0,16},{8,24},{16,0},{24,8},{1,17},{9,25},{17,1},{25,9},{2,18},{10... | collective-permute-start | bytes 147464 | tf_op jit(solution)/shard_map/ppermute | solution.py:333
  40.6 1.6 %collective-permute-start.19 = (bf16[32,768]{1,0:T(8,128)(2,1)S(1)}, bf16[32,768]{1,0:T(8,128)(2,1)S(1)}, u32[]{:S(2)}, u32[]{:S(2)}) collective-permute-start(bf16[32,768]{1,0:T(8,128)(2,1)S(1)} %get-tuple-element.67), channel_id=1, source_target_pairs={{0,24},{8,16},{16,8},{24,0},{1,25},{9,17},{17,9},{25,1},{2,26},{10... | collective-permute-start | bytes 147464 | tf_op jit(solution)/shard_map/ppermute | solution.py:333
  42.1 0.8 %collective-permute-start.20 = (bf16[32,768]{1,0:T(8,128)(2,1)S(1)}, bf16[32,768]{1,0:T(8,128)(2,1)S(1)}, u32[]{:S(2)}, u32[]{:S(2)}) collective-permute-start(bf16[32,768]{1,0:T(8,128)(2,1)S(1)} %get-tuple-element.68), channel_id=1, source_target_pairs={{0,8},{8,0},{16,24},{24,16},{1,9},{9,1},{17,25},{25,17},{2,10},{10... | collective-permute-start | bytes 147464 | tf_op jit(solution)/shard_map/ppermute | solution.py:333
  42.9 0.6 %collective-permute-done.18.refs_1_ = bf16[32,768]{1,0:T(8,128)(2,1)S(1)} collective-permute-done((bf16[32,768]{1,0:T(8,128)(2,1)S(1)}, bf16[32,768]{1,0:T(8,128)(2,1)S(1)}, u32[]{:S(2)}, u32[]{:S(2)}) %collective-permute-start.18) | collective-permute-done | bytes 49184 | tf_op jit(solution)/shard_map/ppermute | solution.py:333
  43.5 2.6 %collective-permute-done.19.refs_2_ = bf16[32,768]{1,0:T(8,128)(2,1)S(1)} collective-permute-done((bf16[32,768]{1,0:T(8,128)(2,1)S(1)}, bf16[32,768]{1,0:T(8,128)(2,1)S(1)}, u32[]{:S(2)}, u32[]{:S(2)}) %collective-permute-start.19) | collective-permute-done | bytes 49184 | tf_op jit(solution)/shard_map/ppermute | solution.py:333
  46.1 0.1 collective-permute-done.20.refs_3_
  46.2 1.4 %deal.1 = bf16[16,8,768]{2,1,0:T(8,128)(2,1)} custom-call(s32[1]{0:T(128)} %bitcast.me_ref, s32[8]{0:T(128)S(1)} %copy-done.3, f32[8]{0:T(128)S(1)} %copy-done.4, f32[8,128]{1,0:T(8,128)S(1)} %get-tuple-element.42.refs_1_.total_ref, bf16[32,768]{1,0:T(8,128)(2,1)S(1)} %get-tuple-element.65.refs_0_, bf16[32,768]{1,0:T(8,128)(2,1)S(1)} %collective-permute-done.18.refs_1_, ...), custom_call_target="tpu_custom_call" | custom-call | bytes 397312 | tf_op jit(solution)/shard_map/deal/pallas_call | solution.py:307
  (13 shorter events, 0.1 us)
Async XLA Ops:
  0.0 9.2 %collective-permute-start.1 = (bf16[12,128,768]{2,1,0:T(8,128)(2,1)}, bf16[12,128,768]{2,1,0:T(8,128)(2,1)S(1)}, u32[]{:S(2)}, u32[]{:S(2)}) collective-permute-start(bf16[12,128,768]{2,1,0:T(8,128)(2,1)} %refs_0_.2), channel_id=1, source_target_pairs={{0,1},{1,0},{2,3},{3,2},{4,5},{5,4},{6,7},{7,6},{8,9},{9,8},{10,11... | collective-permute-start | bytes 7077896 | tf_op jit(solution)/shard_map/ppermute | solution.py:338
  2.4 6.9 %collective-permute-start = (bf16[32,896]{1,0:T(8,128)(2,1)}, bf16[32,896]{1,0:T(8,128)(2,1)S(1)}, u32[]{:S(2)}, u32[]{:S(2)}) collective-permute-start(bf16[32,896]{1,0:T(8,128)(2,1)} %get-tuple-element.38), channel_id=1, source_target_pairs={{0,16},{8,24},{16,0},{24,8},{1,17},{9,25},{17,1},{25,9},{2,18},{10... | collective-permute-start | bytes 172040 | tf_op jit(solution)/shard_map/ppermute | solution.py:333
  5.0 5.5 %collective-permute-start.2 = (bf16[32,896]{1,0:T(8,128)(2,1)}, bf16[32,896]{1,0:T(8,128)(2,1)S(1)}, u32[]{:S(2)}, u32[]{:S(2)}) collective-permute-start(bf16[32,896]{1,0:T(8,128)(2,1)} %get-tuple-element.40), channel_id=1, source_target_pairs={{0,24},{8,16},{16,8},{24,0},{1,25},{9,17},{17,9},{25,1},{2,26},{10... | collective-permute-start | bytes 172040 | tf_op jit(solution)/shard_map/ppermute | solution.py:333
  6.4 4.4 %collective-permute-start.3 = (bf16[32,896]{1,0:T(8,128)(2,1)}, bf16[32,896]{1,0:T(8,128)(2,1)S(1)}, u32[]{:S(2)}, u32[]{:S(2)}) collective-permute-start(bf16[32,896]{1,0:T(8,128)(2,1)} %get-tuple-element.41), channel_id=1, source_target_pairs={{0,8},{8,0},{16,24},{24,16},{1,9},{9,1},{17,25},{25,17},{2,10},{10... | collective-permute-start | bytes 172040 | tf_op jit(solution)/shard_map/ppermute | solution.py:333
  6.5 0.8 %copy-start.2 = (bf16[32,896]{1,0:T(8,128)(2,1)S(1)}, bf16[32,896]{1,0:T(8,128)(2,1)}, u32[]{:S(2)}) copy-start(bf16[32,896]{1,0:T(8,128)(2,1)} %get-tuple-element.37.refs_0_) | copy-start | bytes 172036
  7.4 1.7 %copy-start = (bf16[12,128,768]{2,1,0:T(8,128)(2,1)S(1)}, bf16[12,128,768]{2,1,0:T(8,128)(2,1)}, u32[]{:S(2)}) copy-start(bf16[12,128,768]{2,1,0:T(8,128)(2,1)} %refs_0_.2) | copy-start | bytes 7077892
  9.2 9.3 %copy-start.1 = (bf16[768,768]{1,0:T(8,128)(2,1)S(1)}, bf16[768,768]{1,0:T(8,128)(2,1)}, u32[]{:S(2)}) copy-start(bf16[768,768]{1,0:T(8,128)(2,1)} %refs_0_.3) | copy-start | bytes 3538948
  10.9 5.0 %collective-permute-start.5 = (bf16[216,128]{1,0:T(8,128)(2,1)S(1)}, bf16[216,128]{1,0:T(8,128)(2,1)S(1)}, u32[]{:S(2)}, u32[]{:S(2)}) collective-permute-start(bf16[216,128]{1,0:T(8,128)(2,1)S(1)} %get-tuple-element.47), channel_id=1, source_target_pairs={{0,5},{1,4},{2,7},{3,6},{4,1},{5,0},{6,3},{7,2},{8,13},{9,12},{10,... | collective-permute-start | bytes 165896 | tf_op jit(solution)/shard_map/ppermute | solution.py:338
  12.4 6.0 %collective-permute-start.8 = (bf16[216,128]{1,0:T(8,128)(2,1)S(1)}, bf16[216,128]{1,0:T(8,128)(2,1)S(1)}, u32[]{:S(2)}, u32[]{:S(2)}) collective-permute-start(bf16[216,128]{1,0:T(8,128)(2,1)S(1)} %get-tuple-element.45.refs_0_), channel_id=1, source_target_pairs={{0,2},{1,3},{2,0},{3,1},{4,6},{5,7},{6,4},{7,5},{8,10},{9,11},{10,... | collective-permute-start | bytes 165896 | tf_op jit(solution)/shard_map/ppermute | solution.py:338
  14.0 6.7 %collective-permute-start.6 = (bf16[216,128]{1,0:T(8,128)(2,1)S(1)}, bf16[216,128]{1,0:T(8,128)(2,1)S(1)}, u32[]{:S(2)}, u32[]{:S(2)}) collective-permute-start(bf16[216,128]{1,0:T(8,128)(2,1)S(1)} %get-tuple-element.46), channel_id=1, source_target_pairs={{0,6},{1,7},{2,4},{3,5},{4,2},{5,3},{6,0},{7,1},{8,14},{9,15},{10,... | collective-permute-start | bytes 165896 | tf_op jit(solution)/shard_map/ppermute | solution.py:338
  15.1 7.3 %collective-permute-start.4 = (bf16[216,128]{1,0:T(8,128)(2,1)S(1)}, bf16[216,128]{1,0:T(8,128)(2,1)S(1)}, u32[]{:S(2)}, u32[]{:S(2)}) collective-permute-start(bf16[216,128]{1,0:T(8,128)(2,1)S(1)} %get-tuple-element.46), channel_id=1, source_target_pairs={{0,4},{1,5},{2,6},{3,7},{4,0},{5,1},{6,2},{7,3},{8,12},{9,13},{10,... | collective-permute-start | bytes 165896 | tf_op jit(solution)/shard_map/ppermute | solution.py:338
  15.9 6.5 %collective-permute-start.7 = (bf16[216,128]{1,0:T(8,128)(2,1)S(1)}, bf16[216,128]{1,0:T(8,128)(2,1)S(1)}, u32[]{:S(2)}, u32[]{:S(2)}) collective-permute-start(bf16[216,128]{1,0:T(8,128)(2,1)S(1)} %collective-permute-done.5.refs_2_), channel_id=1, source_target_pairs={{0,2},{1,3},{2,0},{3,1},{4,6},{5,7},{6,4},{7,5},{8,10},{9,11},{10,... | collective-permute-start | bytes 165896 | tf_op jit(solution)/shard_map/ppermute | solution.py:338
  18.4 5.1 %collective-permute-start.9 = (bf16[216,128]{1,0:T(8,128)(2,1)S(1)}, bf16[216,128]{1,0:T(8,128)(2,1)S(1)}, u32[]{:S(2)}, u32[]{:S(2)}) collective-permute-start(bf16[216,128]{1,0:T(8,128)(2,1)S(1)} %get-tuple-element.52), channel_id=1, source_target_pairs={{0,3},{1,2},{2,1},{3,0},{4,7},{5,6},{6,5},{7,4},{8,11},{9,10},{10,... | collective-permute-start | bytes 165896 | tf_op jit(solution)/shard_map/ppermute | solution.py:338
  18.4 5.0 %collective-permute-start.10 = (bf16[216,128]{1,0:T(8,128)(2,1)S(1)}, bf16[216,128]{1,0:T(8,128)(2,1)S(1)}, u32[]{:S(2)}, u32[]{:S(2)}) collective-permute-start(bf16[216,128]{1,0:T(8,128)(2,1)S(1)} %get-tuple-element.52), channel_id=1, source_target_pairs={{0,1},{1,0},{2,3},{3,2},{4,5},{5,4},{6,7},{7,6},{8,9},{9,8},{10,11... | collective-permute-start | bytes 165896 | tf_op jit(solution)/shard_map/ppermute | solution.py:338
  18.8 27.4 %copy-start.3 = (s32[8]{0:T(128)S(1)}, s32[8]{0:T(128)}, u32[]{:S(2)}) copy-start(s32[8]{0:T(128)} %target_ref.1) | copy-start | bytes 100
  18.8 27.4 %copy-start.4 = (f32[8]{0:T(128)S(1)}, f32[8]{0:T(128)}, u32[]{:S(2)}) copy-start(f32[8]{0:T(128)} %weights_ref.1) | copy-start | bytes 100
  27.3 5.0 %collective-permute-start.12 = (bf16[32,768]{1,0:T(8,128)(2,1)S(1)}, bf16[32,768]{1,0:T(8,128)(2,1)S(1)}, u32[]{:S(2)}, u32[]{:S(2)}) collective-permute-start(bf16[32,768]{1,0:T(8,128)(2,1)S(1)} %get-tuple-element.59), channel_id=1, source_target_pairs={{0,2},{1,3},{2,0},{3,1},{4,6},{5,7},{6,4},{7,5},{8,10},{9,11},{10,... | collective-permute-start | bytes 147464 | tf_op jit(solution)/shard_map/ppermute | solution.py:338
  27.3 7.3 %collective-permute-start.11 = (bf16[32,768]{1,0:T(8,128)(2,1)S(1)}, bf16[32,768]{1,0:T(8,128)(2,1)S(1)}, u32[]{:S(2)}, u32[]{:S(2)}) collective-permute-start(bf16[32,768]{1,0:T(8,128)(2,1)S(1)} %get-tuple-element.54), channel_id=1, source_target_pairs={{0,4},{1,5},{2,6},{3,7},{4,0},{5,1},{6,2},{7,3},{8,12},{9,13},{10,... | collective-permute-start | bytes 147464 | tf_op jit(solution)/shard_map/ppermute | solution.py:338
  30.2 6.0 %collective-permute-start.14 = (bf16[32,768]{1,0:T(8,128)(2,1)S(1)}, bf16[32,768]{1,0:T(8,128)(2,1)S(1)}, u32[]{:S(2)}, u32[]{:S(2)}) collective-permute-start(bf16[32,768]{1,0:T(8,128)(2,1)S(1)} %get-tuple-element.61), channel_id=1, source_target_pairs={{0,6},{1,7},{2,4},{3,5},{4,2},{5,3},{6,0},{7,1},{8,14},{9,15},{10,... | collective-permute-start | bytes 147464 | tf_op jit(solution)/shard_map/ppermute | solution.py:338
  32.3 5.5 %collective-permute-start.13 = (bf16[32,768]{1,0:T(8,128)(2,1)S(1)}, bf16[32,768]{1,0:T(8,128)(2,1)S(1)}, u32[]{:S(2)}, u32[]{:S(2)}) collective-permute-start(bf16[32,768]{1,0:T(8,128)(2,1)S(1)} %get-tuple-element.60), channel_id=1, source_target_pairs={{0,5},{1,4},{2,7},{3,6},{4,1},{5,0},{6,3},{7,2},{8,13},{9,12},{10,... | collective-permute-start | bytes 147464 | tf_op jit(solution)/shard_map/ppermute | solution.py:338
  32.4 5.8 %collective-permute-start.15 = (bf16[32,768]{1,0:T(8,128)(2,1)S(1)}, bf16[32,768]{1,0:T(8,128)(2,1)S(1)}, u32[]{:S(2)}, u32[]{:S(2)}) collective-permute-start(bf16[32,768]{1,0:T(8,128)(2,1)S(1)} %get-tuple-element.62), channel_id=1, source_target_pairs={{0,2},{1,3},{2,0},{3,1},{4,6},{5,7},{6,4},{7,5},{8,10},{9,11},{10,... | collective-permute-start | bytes 147464 | tf_op jit(solution)/shard_map/ppermute | solution.py:338
  33.9 5.4 %collective-permute-start.16 = (bf16[32,768]{1,0:T(8,128)(2,1)S(1)}, bf16[32,768]{1,0:T(8,128)(2,1)S(1)}, u32[]{:S(2)}, u32[]{:S(2)}) collective-permute-start(bf16[32,768]{1,0:T(8,128)(2,1)S(1)} %get-tuple-element.63), channel_id=1, source_target_pairs={{0,3},{1,2},{2,1},{3,0},{4,7},{5,6},{6,5},{7,4},{8,11},{9,10},{10,... | collective-permute-start | bytes 147464 | tf_op jit(solution)/shard_map/ppermute | solution.py:338
  34.6 4.6 %collective-permute-start.17 = (bf16[32,768]{1,0:T(8,128)(2,1)S(1)}, bf16[32,768]{1,0:T(8,128)(2,1)S(1)}, u32[]{:S(2)}, u32[]{:S(2)}) collective-permute-start(bf16[32,768]{1,0:T(8,128)(2,1)S(1)} %get-tuple-element.64), channel_id=1, source_target_pairs={{0,1},{1,0},{2,3},{3,2},{4,5},{5,4},{6,7},{7,6},{8,9},{9,8},{10,11... | collective-permute-start | bytes 147464 | tf_op jit(solution)/shard_map/ppermute | solution.py:338
  39.3 4.2 %collective-permute-start.18 = (bf16[32,768]{1,0:T(8,128)(2,1)S(1)}, bf16[32,768]{1,0:T(8,128)(2,1)S(1)}, u32[]{:S(2)}, u32[]{:S(2)}) collective-permute-start(bf16[32,768]{1,0:T(8,128)(2,1)S(1)} %get-tuple-element.66), channel_id=1, source_target_pairs={{0,16},{8,24},{16,0},{24,8},{1,17},{9,25},{17,1},{25,9},{2,18},{10... | collective-permute-start | bytes 147464 | tf_op jit(solution)/shard_map/ppermute | solution.py:333
  40.6 5.5 %collective-permute-start.19 = (bf16[32,768]{1,0:T(8,128)(2,1)S(1)}, bf16[32,768]{1,0:T(8,128)(2,1)S(1)}, u32[]{:S(2)}, u32[]{:S(2)}) collective-permute-start(bf16[32,768]{1,0:T(8,128)(2,1)S(1)} %get-tuple-element.67), channel_id=1, source_target_pairs={{0,24},{8,16},{16,8},{24,0},{1,25},{9,17},{17,9},{25,1},{2,26},{10... | collective-permute-start | bytes 147464 | tf_op jit(solution)/shard_map/ppermute | solution.py:333
  42.1 4.1 %collective-permute-start.20 = (bf16[32,768]{1,0:T(8,128)(2,1)S(1)}, bf16[32,768]{1,0:T(8,128)(2,1)S(1)}, u32[]{:S(2)}, u32[]{:S(2)}) collective-permute-start(bf16[32,768]{1,0:T(8,128)(2,1)S(1)} %get-tuple-element.68), channel_id=1, source_target_pairs={{0,8},{8,0},{16,24},{24,16},{1,9},{9,1},{17,25},{25,17},{2,10},{10... | collective-permute-start | bytes 147464 | tf_op jit(solution)/shard_map/ppermute | solution.py:333

commit v16 on v15

--- a/solution.py
+++ b/solution.py
@@ -209,7 +209,7 @@
                 prop[w, source, :, c * LANES : (c + 1) * LANES] = piece.astype(prop.dtype)
     scaled = jnp.concatenate([prop[w, i] for w in range(half) for i in range(n)], axis=0).astype(BF16)
     carried[...] = jnp.dot(scaled, body_ref[...], preferred_element_type=F32).astype(BF16)
-    batch = vec_count
+    batch = math.gcd(vec_count, 4)
     for c, ref in enumerate((own_ref, sib_ref)):
         for g in range(0, vec_count, batch):
             left = ref[g : g + batch].reshape(batch * occupied, orbitals)

time: 47.8 us -> 47.8 us (level)
  no operation moved by 1% of the time
where the time goes in v16:
time: 47.8 us; the launch traced here: 47.5 us
  starting transfers between devices  22.6 us (47%)
  waiting for transfers between devices  14.6 us (31%)
  Pallas kernels  7.73 us (16%)
  local copies, waits for them, and re-layouts  2.5 us (5%)
    ppermute x15, starting transfers between devices, to_block(): lax.ppermute(x, 'blk', [(i, 2 * moved(i // 2, s, n // 2, 1) + (i % 2 ^ e)...  14.9 us
    ppermute x15, waiting for transfers between devices, to_block(): lax.ppermute(x, 'blk', [(i, 2 * moved(i // 2, s, n // 2, 1) + (i % 2 ^ e)...  9.74 us
    pallas_call x9, Pallas kernels, call(): pl.pallas_call(kernel, out_shape=outs, in_specs=[smem] * len(scalars) + [...  7.73 us
    ppermute x6, starting transfers between devices, to_list(): lax.ppermute(x, 'grp', [(i, moved(i, s, groups, 1)) for i in range(groups)])  7.68 us
    ppermute x6, waiting for transfers between devices, to_list(): lax.ppermute(x, 'grp', [(i, moved(i, s, groups, 1)) for i in range(groups)])  4.86 us
    unnamed x10, local copies, waits for them, and re-layouts  2.5 us
  transfers between devices with their start and end apart: 21, of which 13 were waited for; matrix products, arithmetic and copies ran while one was open for 0% of the time, Pallas kernels for 5%

profile of v16, /device:TPU:0, one launch (start us, length us, event | category | flops | bytes accessed | tf_op | source)
XLA Modules:
  0.0 47.5 jit_solution(9298090646350816033)
XLA Ops:
  0.0 0.5 collective-permute-start.1
  0.5 1.9 %route.1 = (bf16[32,896]{1,0:T(8,128)(2,1)}, bf16[32,896]{1,0:T(8,128)(2,1)}, bf16[32,896]{1,0:T(8,128)(2,1)}, bf16[32,896]{1,0:T(8,128)(2,1)}) custom-call(s32[1]{0:T(128)} %bitcast.me_ref, s32[8]{0:T(128)} %target_ref.1, f32[8]{0:T(128)} %weights_ref.1, bf16[16,8,768]{2,1,0:T(8,128)(2,1)} %walkers_any.1, f32[8,12]{1,0:T(8,128)} %fields_any.1, ...), custom_call_target="tpu_custom_call" | custom-call | bytes 229376 | tf_op jit(solution)/shard_map/route/pallas_call | solution.py:307
  2.4 2.6 %collective-permute-start = (bf16[32,896]{1,0:T(8,128)(2,1)}, bf16[32,896]{1,0:T(8,128)(2,1)S(1)}, u32[]{:S(2)}, u32[]{:S(2)}) collective-permute-start(bf16[32,896]{1,0:T(8,128)(2,1)} %get-tuple-element.38), channel_id=1, source_target_pairs={{0,16},{8,24},{16,0},{24,8},{1,17},{9,25},{17,1},{25,9},{2,18},{10... | collective-permute-start | bytes 172040 | tf_op jit(solution)/shard_map/ppermute | solution.py:333
  5.0 1.4 %collective-permute-start.2 = (bf16[32,896]{1,0:T(8,128)(2,1)}, bf16[32,896]{1,0:T(8,128)(2,1)S(1)}, u32[]{:S(2)}, u32[]{:S(2)}) collective-permute-start(bf16[32,896]{1,0:T(8,128)(2,1)} %get-tuple-element.40), channel_id=1, source_target_pairs={{0,24},{8,16},{16,8},{24,0},{1,25},{9,17},{17,9},{25,1},{2,26},{10... | collective-permute-start | bytes 172040 | tf_op jit(solution)/shard_map/ppermute | solution.py:333
  6.4 0.1 collective-permute-start.3
  6.5 0.8 %copy-done.2 = bf16[32,896]{1,0:T(8,128)(2,1)S(1)} copy-done((bf16[32,896]{1,0:T(8,128)(2,1)S(1)}, bf16[32,896]{1,0:T(8,128)(2,1)}, u32[]{:S(2)}) %copy-start.2) | copy-done | bytes 57368
  7.4 0.0 copy-start
  7.4 1.7 %copy-done = bf16[12,128,768]{2,1,0:T(8,128)(2,1)S(1)} copy-done((bf16[12,128,768]{2,1,0:T(8,128)(2,1)S(1)}, bf16[12,128,768]{2,1,0:T(8,128)(2,1)}, u32[]{:S(2)}) %copy-start) | copy-done | bytes 2359320
  9.0 0.2 stage.1.when.own_ref
  9.2 0.0 copy-start.1
  9.2 0.0 collective-permute-done.refs_1_
  9.3 1.2 %collective-permute-done.2.refs_2_ = bf16[32,896]{1,0:T(8,128)(2,1)S(1)} collective-permute-done((bf16[32,896]{1,0:T(8,128)(2,1)}, bf16[32,896]{1,0:T(8,128)(2,1)S(1)}, u32[]{:S(2)}, u32[]{:S(2)}) %collective-permute-start.2) | collective-permute-done | bytes 57376 | tf_op jit(solution)/shard_map/ppermute | solution.py:333
  10.5 0.3 collective-permute-done.3.refs_3_
  10.8 0.1 merge.1
  10.9 1.5 %collective-permute-start.5 = (bf16[216,128]{1,0:T(8,128)(2,1)S(1)}, bf16[216,128]{1,0:T(8,128)(2,1)S(1)}, u32[]{:S(2)}, u32[]{:S(2)}) collective-permute-start(bf16[216,128]{1,0:T(8,128)(2,1)S(1)} %get-tuple-element.47), channel_id=1, source_target_pairs={{0,5},{1,4},{2,7},{3,6},{4,1},{5,0},{6,3},{7,2},{8,13},{9,12},{10,... | collective-permute-start | bytes 165896 | tf_op jit(solution)/shard_map/ppermute | solution.py:338
  12.4 1.6 %collective-permute-start.8 = (bf16[216,128]{1,0:T(8,128)(2,1)S(1)}, bf16[216,128]{1,0:T(8,128)(2,1)S(1)}, u32[]{:S(2)}, u32[]{:S(2)}) collective-permute-start(bf16[216,128]{1,0:T(8,128)(2,1)S(1)} %get-tuple-element.45.refs_0_), channel_id=1, source_target_pairs={{0,2},{1,3},{2,0},{3,1},{4,6},{5,7},{6,4},{7,5},{8,10},{9,11},{10,... | collective-permute-start | bytes 165896 | tf_op jit(solution)/shard_map/ppermute | solution.py:338
  14.0 1.1 %collective-permute-start.6 = (bf16[216,128]{1,0:T(8,128)(2,1)S(1)}, bf16[216,128]{1,0:T(8,128)(2,1)S(1)}, u32[]{:S(2)}, u32[]{:S(2)}) collective-permute-start(bf16[216,128]{1,0:T(8,128)(2,1)S(1)} %get-tuple-element.46), channel_id=1, source_target_pairs={{0,6},{1,7},{2,4},{3,5},{4,2},{5,3},{6,0},{7,1},{8,14},{9,15},{10,... | collective-permute-start | bytes 165896 | tf_op jit(solution)/shard_map/ppermute | solution.py:338
  15.1 0.8 %collective-permute-start.4 = (bf16[216,128]{1,0:T(8,128)(2,1)S(1)}, bf16[216,128]{1,0:T(8,128)(2,1)S(1)}, u32[]{:S(2)}, u32[]{:S(2)}) collective-permute-start(bf16[216,128]{1,0:T(8,128)(2,1)S(1)} %get-tuple-element.46), channel_id=1, source_target_pairs={{0,4},{1,5},{2,6},{3,7},{4,0},{5,1},{6,2},{7,3},{8,12},{9,13},{10,... | collective-permute-start | bytes 165896 | tf_op jit(solution)/shard_map/ppermute | solution.py:338
  15.9 2.5 %collective-permute-start.7 = (bf16[216,128]{1,0:T(8,128)(2,1)S(1)}, bf16[216,128]{1,0:T(8,128)(2,1)S(1)}, u32[]{:S(2)}, u32[]{:S(2)}) collective-permute-start(bf16[216,128]{1,0:T(8,128)(2,1)S(1)} %collective-permute-done.5.refs_2_), channel_id=1, source_target_pairs={{0,2},{1,3},{2,0},{3,1},{4,6},{5,7},{6,4},{7,5},{8,10},{9,11},{10,... | collective-permute-start | bytes 165896 | tf_op jit(solution)/shard_map/ppermute | solution.py:338
  18.4 0.1 collective-permute-start.9
  18.4 0.1 collective-permute-start.10
  18.5 0.2 hold.1.body_ref
  18.8 0.0 copy-start.3
  18.8 0.0 copy-start.4
  18.8 1.9 %collective-permute-done.6.refs_3_ = bf16[216,128]{1,0:T(8,128)(2,1)S(1)} collective-permute-done((bf16[216,128]{1,0:T(8,128)(2,1)S(1)}, bf16[216,128]{1,0:T(8,128)(2,1)S(1)}, u32[]{:S(2)}, u32[]{:S(2)}) %collective-permute-start.6) | collective-permute-done | bytes 55328 | tf_op jit(solution)/shard_map/ppermute | solution.py:338
  20.7 1.7 %collective-permute-done.4.refs_1_ = bf16[216,128]{1,0:T(8,128)(2,1)S(1)} collective-permute-done((bf16[216,128]{1,0:T(8,128)(2,1)S(1)}, bf16[216,128]{1,0:T(8,128)(2,1)S(1)}, u32[]{:S(2)}, u32[]{:S(2)}) %collective-permute-start.4) | collective-permute-done | bytes 55328 | tf_op jit(solution)/shard_map/ppermute | solution.py:338
  22.4 1.1 %collective-permute-done.9.refs_6_ = bf16[216,128]{1,0:T(8,128)(2,1)S(1)} collective-permute-done((bf16[216,128]{1,0:T(8,128)(2,1)S(1)}, bf16[216,128]{1,0:T(8,128)(2,1)S(1)}, u32[]{:S(2)}, u32[]{:S(2)}) %collective-permute-start.9) | collective-permute-done | bytes 55328 | tf_op jit(solution)/shard_map/ppermute | solution.py:338
  23.5 3.7 %fock.1 = (bf16[32,768]{1,0:T(8,128)(2,1)S(1)}, bf16[32,768]{1,0:T(8,128)(2,1)S(1)}, bf16[32,768]{1,0:T(8,128)(2,1)S(1)}, bf16[32,768]{1,0:T(8,128)(2,1)S(1)}, b...) custom-call(s32[1]{0:T(128)} %bitcast.1.blk_ref, ...), custom_call_target="tpu_custom_call" | custom-call | flops 2717908992 | bytes 6733824 | tf_op jit(solution)/shard_map/fock/pallas_call | solution.py:307
  27.2 0.1 collective-permute-start.12
  27.3 2.8 %collective-permute-start.11 = (bf16[32,768]{1,0:T(8,128)(2,1)S(1)}, bf16[32,768]{1,0:T(8,128)(2,1)S(1)}, u32[]{:S(2)}, u32[]{:S(2)}) collective-permute-start(bf16[32,768]{1,0:T(8,128)(2,1)S(1)} %get-tuple-element.54), channel_id=1, source_target_pairs={{0,4},{1,5},{2,6},{3,7},{4,0},{5,1},{6,2},{7,3},{8,12},{9,13},{10,... | collective-permute-start | bytes 147464 | tf_op jit(solution)/shard_map/ppermute | solution.py:338
  30.1 1.5 %collective-permute-start.14 = (bf16[32,768]{1,0:T(8,128)(2,1)S(1)}, bf16[32,768]{1,0:T(8,128)(2,1)S(1)}, u32[]{:S(2)}, u32[]{:S(2)}) collective-permute-start(bf16[32,768]{1,0:T(8,128)(2,1)S(1)} %get-tuple-element.61), channel_id=1, source_target_pairs={{0,6},{1,7},{2,4},{3,5},{4,2},{5,3},{6,0},{7,1},{8,14},{9,15},{10,... | collective-permute-start | bytes 147464 | tf_op jit(solution)/shard_map/ppermute | solution.py:338
  31.6 0.6 %collective-permute-done.12.refs_4_ = bf16[32,768]{1,0:T(8,128)(2,1)S(1)} collective-permute-done((bf16[32,768]{1,0:T(8,128)(2,1)S(1)}, bf16[32,768]{1,0:T(8,128)(2,1)S(1)}, u32[]{:S(2)}, u32[]{:S(2)}) %collective-permute-start.12) | collective-permute-done | bytes 49184 | tf_op jit(solution)/shard_map/ppermute | solution.py:338
  32.2 0.1 collective-permute-start.13
  32.3 1.5 %collective-permute-start.15 = (bf16[32,768]{1,0:T(8,128)(2,1)S(1)}, bf16[32,768]{1,0:T(8,128)(2,1)S(1)}, u32[]{:S(2)}, u32[]{:S(2)}) collective-permute-start(bf16[32,768]{1,0:T(8,128)(2,1)S(1)} %get-tuple-element.62), channel_id=1, source_target_pairs={{0,2},{1,3},{2,0},{3,1},{4,6},{5,7},{6,4},{7,5},{8,10},{9,11},{10,... | collective-permute-start | bytes 147464 | tf_op jit(solution)/shard_map/ppermute | solution.py:338
  33.8 0.8 %collective-permute-start.16 = (bf16[32,768]{1,0:T(8,128)(2,1)S(1)}, bf16[32,768]{1,0:T(8,128)(2,1)S(1)}, u32[]{:S(2)}, u32[]{:S(2)}) collective-permute-start(bf16[32,768]{1,0:T(8,128)(2,1)S(1)} %get-tuple-element.63), channel_id=1, source_target_pairs={{0,3},{1,2},{2,1},{3,0},{4,7},{5,6},{6,5},{7,4},{8,11},{9,10},{10,... | collective-permute-start | bytes 147464 | tf_op jit(solution)/shard_map/ppermute | solution.py:338
  34.6 0.1 collective-permute-start.17
  34.6 1.4 %collective-permute-done.14.refs_3_ = bf16[32,768]{1,0:T(8,128)(2,1)S(1)} collective-permute-done((bf16[32,768]{1,0:T(8,128)(2,1)S(1)}, bf16[32,768]{1,0:T(8,128)(2,1)S(1)}, u32[]{:S(2)}, u32[]{:S(2)}) %collective-permute-start.14) | collective-permute-done | bytes 49184 | tf_op jit(solution)/shard_map/ppermute | solution.py:338
  36.1 1.6 %collective-permute-done.13.refs_2_ = bf16[32,768]{1,0:T(8,128)(2,1)S(1)} collective-permute-done((bf16[32,768]{1,0:T(8,128)(2,1)S(1)}, bf16[32,768]{1,0:T(8,128)(2,1)S(1)}, u32[]{:S(2)}, u32[]{:S(2)}) %collective-permute-start.13) | collective-permute-done | bytes 49184 | tf_op jit(solution)/shard_map/ppermute | solution.py:338
  37.7 0.4 collective-permute-done.15.refs_4_
  38.1 1.0 %collective-permute-done.16.refs_5_ = bf16[32,768]{1,0:T(8,128)(2,1)S(1)} collective-permute-done((bf16[32,768]{1,0:T(8,128)(2,1)S(1)}, bf16[32,768]{1,0:T(8,128)(2,1)S(1)}, u32[]{:S(2)}, u32[]{:S(2)}) %collective-permute-start.16) | collective-permute-done | bytes 49184 | tf_op jit(solution)/shard_map/ppermute | solution.py:338
  39.2 0.1 sum.1
  39.2 1.2 %collective-permute-start.18 = (bf16[32,768]{1,0:T(8,128)(2,1)S(1)}, bf16[32,768]{1,0:T(8,128)(2,1)S(1)}, u32[]{:S(2)}, u32[]{:S(2)}) collective-permute-start(bf16[32,768]{1,0:T(8,128)(2,1)S(1)} %get-tuple-element.66), channel_id=1, source_target_pairs={{0,16},{8,24},{16,0},{24,8},{1,17},{9,25},{17,1},{25,9},{2,18},{10... | collective-permute-start | bytes 147464 | tf_op jit(solution)/shard_map/ppermute | solution.py:333
  40.5 1.5 %collective-permute-start.19 = (bf16[32,768]{1,0:T(8,128)(2,1)S(1)}, bf16[32,768]{1,0:T(8,128)(2,1)S(1)}, u32[]{:S(2)}, u32[]{:S(2)}) collective-permute-start(bf16[32,768]{1,0:T(8,128)(2,1)S(1)} %get-tuple-element.67), channel_id=1, source_target_pairs={{0,24},{8,16},{16,8},{24,0},{1,25},{9,17},{17,9},{25,1},{2,26},{10... | collective-permute-start | bytes 147464 | tf_op jit(solution)/shard_map/ppermute | solution.py:333
  42.0 0.8 %collective-permute-start.20 = (bf16[32,768]{1,0:T(8,128)(2,1)S(1)}, bf16[32,768]{1,0:T(8,128)(2,1)S(1)}, u32[]{:S(2)}, u32[]{:S(2)}) collective-permute-start(bf16[32,768]{1,0:T(8,128)(2,1)S(1)} %get-tuple-element.68), channel_id=1, source_target_pairs={{0,8},{8,0},{16,24},{24,16},{1,9},{9,1},{17,25},{25,17},{2,10},{10... | collective-permute-start | bytes 147464 | tf_op jit(solution)/shard_map/ppermute | solution.py:333
  42.8 0.6 %collective-permute-done.18.refs_1_ = bf16[32,768]{1,0:T(8,128)(2,1)S(1)} collective-permute-done((bf16[32,768]{1,0:T(8,128)(2,1)S(1)}, bf16[32,768]{1,0:T(8,128)(2,1)S(1)}, u32[]{:S(2)}, u32[]{:S(2)}) %collective-permute-start.18) | collective-permute-done | bytes 49184 | tf_op jit(solution)/shard_map/ppermute | solution.py:333
  43.4 2.6 %collective-permute-done.19.refs_2_ = bf16[32,768]{1,0:T(8,128)(2,1)S(1)} collective-permute-done((bf16[32,768]{1,0:T(8,128)(2,1)S(1)}, bf16[32,768]{1,0:T(8,128)(2,1)S(1)}, u32[]{:S(2)}, u32[]{:S(2)}) %collective-permute-start.19) | collective-permute-done | bytes 49184 | tf_op jit(solution)/shard_map/ppermute | solution.py:333
  46.0 0.1 collective-permute-done.20.refs_3_
  46.1 1.4 %deal.1 = bf16[16,8,768]{2,1,0:T(8,128)(2,1)} custom-call(s32[1]{0:T(128)} %bitcast.me_ref, s32[8]{0:T(128)S(1)} %copy-done.3, f32[8]{0:T(128)S(1)} %copy-done.4, f32[8,128]{1,0:T(8,128)S(1)} %get-tuple-element.42.refs_1_.total_ref, bf16[32,768]{1,0:T(8,128)(2,1)S(1)} %get-tuple-element.65.refs_0_, bf16[32,768]{1,0:T(8,128)(2,1)S(1)} %collective-permute-done.18.refs_1_, ...), custom_call_target="tpu_custom_call" | custom-call | bytes 397312 | tf_op jit(solution)/shard_map/deal/pallas_call | solution.py:307
  (13 shorter events, 0.1 us)
Async XLA Ops:
  0.0 9.2 %collective-permute-start.1 = (bf16[12,128,768]{2,1,0:T(8,128)(2,1)}, bf16[12,128,768]{2,1,0:T(8,128)(2,1)S(1)}, u32[]{:S(2)}, u32[]{:S(2)}) collective-permute-start(bf16[12,128,768]{2,1,0:T(8,128)(2,1)} %refs_0_.2), channel_id=1, source_target_pairs={{0,1},{1,0},{2,3},{3,2},{4,5},{5,4},{6,7},{7,6},{8,9},{9,8},{10,11... | collective-permute-start | bytes 7077896 | tf_op jit(solution)/shard_map/ppermute | solution.py:338
  2.4 6.9 %collective-permute-start = (bf16[32,896]{1,0:T(8,128)(2,1)}, bf16[32,896]{1,0:T(8,128)(2,1)S(1)}, u32[]{:S(2)}, u32[]{:S(2)}) collective-permute-start(bf16[32,896]{1,0:T(8,128)(2,1)} %get-tuple-element.38), channel_id=1, source_target_pairs={{0,16},{8,24},{16,0},{24,8},{1,17},{9,25},{17,1},{25,9},{2,18},{10... | collective-permute-start | bytes 172040 | tf_op jit(solution)/shard_map/ppermute | solution.py:333
  5.0 5.5 %collective-permute-start.2 = (bf16[32,896]{1,0:T(8,128)(2,1)}, bf16[32,896]{1,0:T(8,128)(2,1)S(1)}, u32[]{:S(2)}, u32[]{:S(2)}) collective-permute-start(bf16[32,896]{1,0:T(8,128)(2,1)} %get-tuple-element.40), channel_id=1, source_target_pairs={{0,24},{8,16},{16,8},{24,0},{1,25},{9,17},{17,9},{25,1},{2,26},{10... | collective-permute-start | bytes 172040 | tf_op jit(solution)/shard_map/ppermute | solution.py:333
  6.4 4.4 %collective-permute-start.3 = (bf16[32,896]{1,0:T(8,128)(2,1)}, bf16[32,896]{1,0:T(8,128)(2,1)S(1)}, u32[]{:S(2)}, u32[]{:S(2)}) collective-permute-start(bf16[32,896]{1,0:T(8,128)(2,1)} %get-tuple-element.41), channel_id=1, source_target_pairs={{0,8},{8,0},{16,24},{24,16},{1,9},{9,1},{17,25},{25,17},{2,10},{10... | collective-permute-start | bytes 172040 | tf_op jit(solution)/shard_map/ppermute | solution.py:333
  6.5 0.8 %copy-start.2 = (bf16[32,896]{1,0:T(8,128)(2,1)S(1)}, bf16[32,896]{1,0:T(8,128)(2,1)}, u32[]{:S(2)}) copy-start(bf16[32,896]{1,0:T(8,128)(2,1)} %get-tuple-element.37.refs_0_) | copy-start | bytes 172036
  7.4 1.7 %copy-start = (bf16[12,128,768]{2,1,0:T(8,128)(2,1)S(1)}, bf16[12,128,768]{2,1,0:T(8,128)(2,1)}, u32[]{:S(2)}) copy-start(bf16[12,128,768]{2,1,0:T(8,128)(2,1)} %refs_0_.2) | copy-start | bytes 7077892
  9.2 9.3 %copy-start.1 = (bf16[768,768]{1,0:T(8,128)(2,1)S(1)}, bf16[768,768]{1,0:T(8,128)(2,1)}, u32[]{:S(2)}) copy-start(bf16[768,768]{1,0:T(8,128)(2,1)} %refs_0_.3) | copy-start | bytes 3538948
  10.9 5.0 %collective-permute-start.5 = (bf16[216,128]{1,0:T(8,128)(2,1)S(1)}, bf16[216,128]{1,0:T(8,128)(2,1)S(1)}, u32[]{:S(2)}, u32[]{:S(2)}) collective-permute-start(bf16[216,128]{1,0:T(8,128)(2,1)S(1)} %get-tuple-element.47), channel_id=1, source_target_pairs={{0,5},{1,4},{2,7},{3,6},{4,1},{5,0},{6,3},{7,2},{8,13},{9,12},{10,... | collective-permute-start | bytes 165896 | tf_op jit(solution)/shard_map/ppermute | solution.py:338
  12.4 6.0 %collective-permute-start.8 = (bf16[216,128]{1,0:T(8,128)(2,1)S(1)}, bf16[216,128]{1,0:T(8,128)(2,1)S(1)}, u32[]{:S(2)}, u32[]{:S(2)}) collective-permute-start(bf16[216,128]{1,0:T(8,128)(2,1)S(1)} %get-tuple-element.45.refs_0_), channel_id=1, source_target_pairs={{0,2},{1,3},{2,0},{3,1},{4,6},{5,7},{6,4},{7,5},{8,10},{9,11},{10,... | collective-permute-start | bytes 165896 | tf_op jit(solution)/shard_map/ppermute | solution.py:338
  14.0 6.7 %collective-permute-start.6 = (bf16[216,128]{1,0:T(8,128)(2,1)S(1)}, bf16[216,128]{1,0:T(8,128)(2,1)S(1)}, u32[]{:S(2)}, u32[]{:S(2)}) collective-permute-start(bf16[216,128]{1,0:T(8,128)(2,1)S(1)} %get-tuple-element.46), channel_id=1, source_target_pairs={{0,6},{1,7},{2,4},{3,5},{4,2},{5,3},{6,0},{7,1},{8,14},{9,15},{10,... | collective-permute-start | bytes 165896 | tf_op jit(solution)/shard_map/ppermute | solution.py:338
  15.1 7.3 %collective-permute-start.4 = (bf16[216,128]{1,0:T(8,128)(2,1)S(1)}, bf16[216,128]{1,0:T(8,128)(2,1)S(1)}, u32[]{:S(2)}, u32[]{:S(2)}) collective-permute-start(bf16[216,128]{1,0:T(8,128)(2,1)S(1)} %get-tuple-element.46), channel_id=1, source_target_pairs={{0,4},{1,5},{2,6},{3,7},{4,0},{5,1},{6,2},{7,3},{8,12},{9,13},{10,... | collective-permute-start | bytes 165896 | tf_op jit(solution)/shard_map/ppermute | solution.py:338
  15.9 6.5 %collective-permute-start.7 = (bf16[216,128]{1,0:T(8,128)(2,1)S(1)}, bf16[216,128]{1,0:T(8,128)(2,1)S(1)}, u32[]{:S(2)}, u32[]{:S(2)}) collective-permute-start(bf16[216,128]{1,0:T(8,128)(2,1)S(1)} %collective-permute-done.5.refs_2_), channel_id=1, source_target_pairs={{0,2},{1,3},{2,0},{3,1},{4,6},{5,7},{6,4},{7,5},{8,10},{9,11},{10,... | collective-permute-start | bytes 165896 | tf_op jit(solution)/shard_map/ppermute | solution.py:338
  18.4 5.1 %collective-permute-start.9 = (bf16[216,128]{1,0:T(8,128)(2,1)S(1)}, bf16[216,128]{1,0:T(8,128)(2,1)S(1)}, u32[]{:S(2)}, u32[]{:S(2)}) collective-permute-start(bf16[216,128]{1,0:T(8,128)(2,1)S(1)} %get-tuple-element.52), channel_id=1, source_target_pairs={{0,3},{1,2},{2,1},{3,0},{4,7},{5,6},{6,5},{7,4},{8,11},{9,10},{10,... | collective-permute-start | bytes 165896 | tf_op jit(solution)/shard_map/ppermute | solution.py:338
  18.4 5.0 %collective-permute-start.10 = (bf16[216,128]{1,0:T(8,128)(2,1)S(1)}, bf16[216,128]{1,0:T(8,128)(2,1)S(1)}, u32[]{:S(2)}, u32[]{:S(2)}) collective-permute-start(bf16[216,128]{1,0:T(8,128)(2,1)S(1)} %get-tuple-element.52), channel_id=1, source_target_pairs={{0,1},{1,0},{2,3},{3,2},{4,5},{5,4},{6,7},{7,6},{8,9},{9,8},{10,11... | collective-permute-start | bytes 165896 | tf_op jit(solution)/shard_map/ppermute | solution.py:338
  18.8 27.3 %copy-start.3 = (s32[8]{0:T(128)S(1)}, s32[8]{0:T(128)}, u32[]{:S(2)}) copy-start(s32[8]{0:T(128)} %target_ref.1) | copy-start | bytes 100
  18.8 27.3 %copy-start.4 = (f32[8]{0:T(128)S(1)}, f32[8]{0:T(128)}, u32[]{:S(2)}) copy-start(f32[8]{0:T(128)} %weights_ref.1) | copy-start | bytes 100
  27.2 5.0 %collective-permute-start.12 = (bf16[32,768]{1,0:T(8,128)(2,1)S(1)}, bf16[32,768]{1,0:T(8,128)(2,1)S(1)}, u32[]{:S(2)}, u32[]{:S(2)}) collective-permute-start(bf16[32,768]{1,0:T(8,128)(2,1)S(1)} %get-tuple-element.59), channel_id=1, source_target_pairs={{0,2},{1,3},{2,0},{3,1},{4,6},{5,7},{6,4},{7,5},{8,10},{9,11},{10,... | collective-permute-start | bytes 147464 | tf_op jit(solution)/shard_map/ppermute | solution.py:338
  27.3 7.3 %collective-permute-start.11 = (bf16[32,768]{1,0:T(8,128)(2,1)S(1)}, bf16[32,768]{1,0:T(8,128)(2,1)S(1)}, u32[]{:S(2)}, u32[]{:S(2)}) collective-permute-start(bf16[32,768]{1,0:T(8,128)(2,1)S(1)} %get-tuple-element.54), channel_id=1, source_target_pairs={{0,4},{1,5},{2,6},{3,7},{4,0},{5,1},{6,2},{7,3},{8,12},{9,13},{10,... | collective-permute-start | bytes 147464 | tf_op jit(solution)/shard_map/ppermute | solution.py:338
  30.1 6.0 %collective-permute-start.14 = (bf16[32,768]{1,0:T(8,128)(2,1)S(1)}, bf16[32,768]{1,0:T(8,128)(2,1)S(1)}, u32[]{:S(2)}, u32[]{:S(2)}) collective-permute-start(bf16[32,768]{1,0:T(8,128)(2,1)S(1)} %get-tuple-element.61), channel_id=1, source_target_pairs={{0,6},{1,7},{2,4},{3,5},{4,2},{5,3},{6,0},{7,1},{8,14},{9,15},{10,... | collective-permute-start | bytes 147464 | tf_op jit(solution)/shard_map/ppermute | solution.py:338
  32.2 5.4 %collective-permute-start.13 = (bf16[32,768]{1,0:T(8,128)(2,1)S(1)}, bf16[32,768]{1,0:T(8,128)(2,1)S(1)}, u32[]{:S(2)}, u32[]{:S(2)}) collective-permute-start(bf16[32,768]{1,0:T(8,128)(2,1)S(1)} %get-tuple-element.60), channel_id=1, source_target_pairs={{0,5},{1,4},{2,7},{3,6},{4,1},{5,0},{6,3},{7,2},{8,13},{9,12},{10,... | collective-permute-start | bytes 147464 | tf_op jit(solution)/shard_map/ppermute | solution.py:338
  32.3 5.8 %collective-permute-start.15 = (bf16[32,768]{1,0:T(8,128)(2,1)S(1)}, bf16[32,768]{1,0:T(8,128)(2,1)S(1)}, u32[]{:S(2)}, u32[]{:S(2)}) collective-permute-start(bf16[32,768]{1,0:T(8,128)(2,1)S(1)} %get-tuple-element.62), channel_id=1, source_target_pairs={{0,2},{1,3},{2,0},{3,1},{4,6},{5,7},{6,4},{7,5},{8,10},{9,11},{10,... | collective-permute-start | bytes 147464 | tf_op jit(solution)/shard_map/ppermute | solution.py:338
  33.8 5.4 %collective-permute-start.16 = (bf16[32,768]{1,0:T(8,128)(2,1)S(1)}, bf16[32,768]{1,0:T(8,128)(2,1)S(1)}, u32[]{:S(2)}, u32[]{:S(2)}) collective-permute-start(bf16[32,768]{1,0:T(8,128)(2,1)S(1)} %get-tuple-element.63), channel_id=1, source_target_pairs={{0,3},{1,2},{2,1},{3,0},{4,7},{5,6},{6,5},{7,4},{8,11},{9,10},{10,... | collective-permute-start | bytes 147464 | tf_op jit(solution)/shard_map/ppermute | solution.py:338
  34.6 4.6 %collective-permute-start.17 = (bf16[32,768]{1,0:T(8,128)(2,1)S(1)}, bf16[32,768]{1,0:T(8,128)(2,1)S(1)}, u32[]{:S(2)}, u32[]{:S(2)}) collective-permute-start(bf16[32,768]{1,0:T(8,128)(2,1)S(1)} %get-tuple-element.64), channel_id=1, source_target_pairs={{0,1},{1,0},{2,3},{3,2},{4,5},{5,4},{6,7},{7,6},{8,9},{9,8},{10,11... | collective-permute-start | bytes 147464 | tf_op jit(solution)/shard_map/ppermute | solution.py:338
  39.2 4.2 %collective-permute-start.18 = (bf16[32,768]{1,0:T(8,128)(2,1)S(1)}, bf16[32,768]{1,0:T(8,128)(2,1)S(1)}, u32[]{:S(2)}, u32[]{:S(2)}) collective-permute-start(bf16[32,768]{1,0:T(8,128)(2,1)S(1)} %get-tuple-element.66), channel_id=1, source_target_pairs={{0,16},{8,24},{16,0},{24,8},{1,17},{9,25},{17,1},{25,9},{2,18},{10... | collective-permute-start | bytes 147464 | tf_op jit(solution)/shard_map/ppermute | solution.py:333
  40.5 5.5 %collective-permute-start.19 = (bf16[32,768]{1,0:T(8,128)(2,1)S(1)}, bf16[32,768]{1,0:T(8,128)(2,1)S(1)}, u32[]{:S(2)}, u32[]{:S(2)}) collective-permute-start(bf16[32,768]{1,0:T(8,128)(2,1)S(1)} %get-tuple-element.67), channel_id=1, source_target_pairs={{0,24},{8,16},{16,8},{24,0},{1,25},{9,17},{17,9},{25,1},{2,26},{10... | collective-permute-start | bytes 147464 | tf_op jit(solution)/shard_map/ppermute | solution.py:333
  42.0 4.1 %collective-permute-start.20 = (bf16[32,768]{1,0:T(8,128)(2,1)S(1)}, bf16[32,768]{1,0:T(8,128)(2,1)S(1)}, u32[]{:S(2)}, u32[]{:S(2)}) collective-permute-start(bf16[32,768]{1,0:T(8,128)(2,1)S(1)} %get-tuple-element.68), channel_id=1, source_target_pairs={{0,8},{8,0},{16,24},{24,16},{1,9},{9,1},{17,25},{25,17},{2,10},{10... | collective-permute-start | bytes 147464 | tf_op jit(solution)/shard_map/ppermute | solution.py:333

commit v17 on v13

--- a/solution.py
+++ b/solution.py
@@ -386,6 +386,7 @@
         vmem=STAGE_VMEM,
     )
     routed = [to_list(routed[s], s) if s else kept for s in order]
+    routed[1], sibling = lax.optimization_barrier((routed[1], sibling))
     payload = shape((chunks * slab + 2 * half * chunks, LANES), BF16)
     same, other, same2, other2, weight_sum, pick = call(
         functools.partial(merge_kernel, order, keep, cap, orbitals),

time: 47.8 us -> 48.9 us (1.023)
  waiting for transfers between devices: 11.4 us -> 15.1 us
  starting transfers between devices: 25.8 us -> 23.3 us
    ppermute x15, waiting for transfers between devices: 6.64 us -> 10 us  [to_block(): lax.ppermute(x, 'blk', [(i, 2 * moved(i // 2, s, n // 2, 1) + (i % 2 ^ e)...]
    ppermute x15, starting transfers between devices: 18.1 us -> 15.6 us  [to_block(): lax.ppermute(x, 'blk', [(i, 2 * moved(i // 2, s, n // 2, 1) + (i % 2 ^ e)...]
  transfers between devices with their start and end apart: 21 -> 21, of which waited for: 10 -> 14; matrix products, arithmetic and copies ran while one was open for 0% -> 0% of each run, Pallas kernels for 5% -> 5%
where the time goes in v17:
time: 48.9 us; the launch traced here: 48.7 us
  starting transfers between devices  23.3 us (48%)
  waiting for transfers between devices  15.1 us (31%)
  Pallas kernels  7.74 us (16%)
  local copies, waits for them, and re-layouts  2.5 us (5%)
    ppermute x15, starting transfers between devices, to_block(): lax.ppermute(x, 'blk', [(i, 2 * moved(i // 2, s, n // 2, 1) + (i % 2 ^ e)...  15.6 us
    ppermute x15, waiting for transfers between devices, to_block(): lax.ppermute(x, 'blk', [(i, 2 * moved(i // 2, s, n // 2, 1) + (i % 2 ^ e)...  10 us
    pallas_call x10, Pallas kernels, call(): pl.pallas_call(kernel, out_shape=outs, in_specs=[smem] * len(scalars) + [...  7.74 us
    ppermute x6, starting transfers between devices, to_list(): lax.ppermute(x, 'grp', [(i, moved(i, s, groups, 1)) for i in range(groups)])  7.68 us
    ppermute x6, waiting for transfers between devices, to_list(): lax.ppermute(x, 'grp', [(i, moved(i, s, groups, 1)) for i in range(groups)])  5.08 us
    unnamed x10, local copies, waits for them, and re-layouts  2.5 us
  transfers between devices with their start and end apart: 21, of which 14 were waited for; matrix products, arithmetic and copies ran while one was open for 0% of the time, Pallas kernels for 5%

profile of v17, /device:TPU:0, one launch (start us, length us, event | category | flops | bytes accessed | tf_op | source)
XLA Modules:
  0.0 48.7 jit_solution(10475178511980398054)
XLA Ops:
  0.0 0.5 collective-permute-start.1
  0.5 1.9 %route.1 = (bf16[32,896]{1,0:T(8,128)(2,1)}, bf16[32,896]{1,0:T(8,128)(2,1)}, bf16[32,896]{1,0:T(8,128)(2,1)}, bf16[32,896]{1,0:T(8,128)(2,1)}) custom-call(s32[1]{0:T(128)} %bitcast.me_ref, s32[8]{0:T(128)} %target_ref.1, f32[8]{0:T(128)} %weights_ref.1, bf16[16,8,768]{2,1,0:T(8,128)(2,1)} %walkers_any.1, f32[8,12]{1,0:T(8,128)} %fields_any.1, ...), custom_call_target="tpu_custom_call" | custom-call | bytes 229376 | tf_op jit(solution)/shard_map/route/pallas_call | solution.py:311
  2.4 2.6 %collective-permute-start = (bf16[32,896]{1,0:T(8,128)(2,1)}, bf16[32,896]{1,0:T(8,128)(2,1)S(1)}, u32[]{:S(2)}, u32[]{:S(2)}) collective-permute-start(bf16[32,896]{1,0:T(8,128)(2,1)} %get-tuple-element.34), channel_id=1, source_target_pairs={{0,16},{8,24},{16,0},{24,8},{1,17},{9,25},{17,1},{25,9},{2,18},{10... | collective-permute-start | bytes 172040 | tf_op jit(solution)/shard_map/ppermute | solution.py:337
  5.0 1.4 %collective-permute-start.2 = (bf16[32,896]{1,0:T(8,128)(2,1)}, bf16[32,896]{1,0:T(8,128)(2,1)S(1)}, u32[]{:S(2)}, u32[]{:S(2)}) collective-permute-start(bf16[32,896]{1,0:T(8,128)(2,1)} %get-tuple-element.36), channel_id=1, source_target_pairs={{0,24},{8,16},{16,8},{24,0},{1,25},{9,17},{17,9},{25,1},{2,26},{10... | collective-permute-start | bytes 172040 | tf_op jit(solution)/shard_map/ppermute | solution.py:337
  6.4 0.1 collective-permute-start.3
  6.5 0.8 %copy-done.2 = bf16[32,896]{1,0:T(8,128)(2,1)S(1)} copy-done((bf16[32,896]{1,0:T(8,128)(2,1)S(1)}, bf16[32,896]{1,0:T(8,128)(2,1)}, u32[]{:S(2)}) %copy-start.2) | copy-done | bytes 57368
  7.4 0.0 copy-start
  7.4 1.7 %copy-done = bf16[12,128,768]{2,1,0:T(8,128)(2,1)S(1)} copy-done((bf16[12,128,768]{2,1,0:T(8,128)(2,1)S(1)}, bf16[12,128,768]{2,1,0:T(8,128)(2,1)}, u32[]{:S(2)}) %copy-start) | copy-done | bytes 2359320
  9.1 0.2 stage.1.when.own_ref
  9.2 0.0 copy-start.1
  9.2 0.0 collective-permute-done.refs_1_
  9.3 1.2 %collective-permute-done.2.refs_2_ = bf16[32,896]{1,0:T(8,128)(2,1)S(1)} collective-permute-done((bf16[32,896]{1,0:T(8,128)(2,1)}, bf16[32,896]{1,0:T(8,128)(2,1)S(1)}, u32[]{:S(2)}, u32[]{:S(2)}) %collective-permute-start.2) | collective-permute-done | bytes 57376 | tf_op jit(solution)/shard_map/ppermute | solution.py:337
  10.5 0.3 collective-permute-done.3.refs_3_
  10.8 0.1 merge.1
  10.9 1.5 %collective-permute-start.8 = (bf16[216,128]{1,0:T(8,128)(2,1)S(1)}, bf16[216,128]{1,0:T(8,128)(2,1)S(1)}, u32[]{:S(2)}, u32[]{:S(2)}) collective-permute-start(bf16[216,128]{1,0:T(8,128)(2,1)S(1)} %get-tuple-element.44), channel_id=1, source_target_pairs={{0,5},{1,4},{2,7},{3,6},{4,1},{5,0},{6,3},{7,2},{8,13},{9,12},{10,... | collective-permute-start | bytes 165896 | tf_op jit(solution)/shard_map/ppermute | solution.py:342
  12.4 1.2 %collective-permute-start.4 = (bf16[216,128]{1,0:T(8,128)(2,1)S(1)}, bf16[216,128]{1,0:T(8,128)(2,1)S(1)}, u32[]{:S(2)}, u32[]{:S(2)}) collective-permute-start(bf16[216,128]{1,0:T(8,128)(2,1)S(1)} %get-tuple-element.43), channel_id=1, source_target_pairs={{0,4},{1,5},{2,6},{3,7},{4,0},{5,1},{6,2},{7,3},{8,12},{9,13},{10,... | collective-permute-start | bytes 165896 | tf_op jit(solution)/shard_map/ppermute | solution.py:342
  13.6 2.7 %collective-permute-start.10 = (bf16[216,128]{1,0:T(8,128)(2,1)S(1)}, bf16[216,128]{1,0:T(8,128)(2,1)S(1)}, u32[]{:S(2)}, u32[]{:S(2)}) collective-permute-start(bf16[216,128]{1,0:T(8,128)(2,1)S(1)} %get-tuple-element.43), channel_id=1, source_target_pairs={{0,6},{1,7},{2,4},{3,5},{4,2},{5,3},{6,0},{7,1},{8,14},{9,15},{10,... | collective-permute-start | bytes 165896 | tf_op jit(solution)/shard_map/ppermute | solution.py:342
  16.3 2.1 %collective-permute-start.6 = (bf16[216,128]{1,0:T(8,128)(2,1)S(1)}, bf16[216,128]{1,0:T(8,128)(2,1)S(1)}, u32[]{:S(2)}, u32[]{:S(2)}) collective-permute-start(bf16[216,128]{1,0:T(8,128)(2,1)S(1)} %get-tuple-element.42.source_ref), channel_id=1, source_target_pairs={{0,3},{1,2},{2,1},{3,0},{4,7},{5,6},{6,5},{7,4},{8,11},{9,10},{10,... | collective-permute-start | bytes 165896 | tf_op jit(solution)/shard_map/ppermute | solution.py:342
  18.4 0.3 collective-permute-start.9
  18.7 2.2 %collective-permute-done.4.when_ref.refs_7_ = bf16[216,128]{1,0:T(8,128)(2,1)S(1)} collective-permute-done((bf16[216,128]{1,0:T(8,128)(2,1)S(1)}, bf16[216,128]{1,0:T(8,128)(2,1)S(1)}, u32[]{:S(2)}, u32[]{:S(2)}) %collective-permute-start.4) | collective-permute-done | bytes 55328 | tf_op jit(solution)/shard_map/ppermute | solution.py:342
  20.9 0.0 collective-permute-start.5
  20.9 0.2 hold.1.body_ref
  21.2 0.0 copy-start.3
  21.2 0.0 copy-start.4
  21.2 0.8 %collective-permute-done.7.refs_3_ = bf16[216,128]{1,0:T(8,128)(2,1)S(1)} collective-permute-done((bf16[216,128]{1,0:T(8,128)(2,1)S(1)}, bf16[216,128]{1,0:T(8,128)(2,1)S(1)}, u32[]{:S(2)}, u32[]{:S(2)}) %collective-permute-start.7) | collective-permute-done | bytes 55328 | tf_op jit(solution)/shard_map/ppermute | solution.py:342
  22.0 1.1 %collective-permute-done.6.refs_2_ = bf16[216,128]{1,0:T(8,128)(2,1)S(1)} collective-permute-done((bf16[216,128]{1,0:T(8,128)(2,1)S(1)}, bf16[216,128]{1,0:T(8,128)(2,1)S(1)}, u32[]{:S(2)}, u32[]{:S(2)}) %collective-permute-start.6) | collective-permute-done | bytes 55328 | tf_op jit(solution)/shard_map/ppermute | solution.py:342
  23.1 1.2 %collective-permute-done.9.refs_4_ = bf16[216,128]{1,0:T(8,128)(2,1)S(1)} collective-permute-done((bf16[216,128]{1,0:T(8,128)(2,1)S(1)}, bf16[216,128]{1,0:T(8,128)(2,1)S(1)}, u32[]{:S(2)}, u32[]{:S(2)}) %collective-permute-start.9) | collective-permute-done | bytes 55328 | tf_op jit(solution)/shard_map/ppermute | solution.py:342
  24.3 3.7 %fock.1 = (bf16[32,768]{1,0:T(8,128)(2,1)S(1)}, bf16[32,768]{1,0:T(8,128)(2,1)S(1)}, bf16[32,768]{1,0:T(8,128)(2,1)S(1)}, bf16[32,768]{1,0:T(8,128)(2,1)S(1)}, b...) custom-call(s32[1]{0:T(128)} %bitcast.1.blk_ref, ...), custom_call_target="tpu_custom_call" | custom-call | flops 2717908992 | bytes 6733824 | tf_op jit(solution)/shard_map/fock/pallas_call | solution.py:311
  28.1 0.4 collective-permute-start.12
  28.4 2.8 %collective-permute-start.11 = (bf16[32,768]{1,0:T(8,128)(2,1)S(1)}, bf16[32,768]{1,0:T(8,128)(2,1)S(1)}, u32[]{:S(2)}, u32[]{:S(2)}) collective-permute-start(bf16[32,768]{1,0:T(8,128)(2,1)S(1)} %get-tuple-element.46), channel_id=1, source_target_pairs={{0,4},{1,5},{2,6},{3,7},{4,0},{5,1},{6,2},{7,3},{8,12},{9,13},{10,... | collective-permute-start | bytes 147464 | tf_op jit(solution)/shard_map/ppermute | solution.py:342
  31.3 1.2 %collective-permute-start.14 = (bf16[32,768]{1,0:T(8,128)(2,1)S(1)}, bf16[32,768]{1,0:T(8,128)(2,1)S(1)}, u32[]{:S(2)}, u32[]{:S(2)}) collective-permute-start(bf16[32,768]{1,0:T(8,128)(2,1)S(1)} %get-tuple-element.53), channel_id=1, source_target_pairs={{0,6},{1,7},{2,4},{3,5},{4,2},{5,3},{6,0},{7,1},{8,14},{9,15},{10,... | collective-permute-start | bytes 147464 | tf_op jit(solution)/shard_map/ppermute | solution.py:342
  32.5 0.2 collective-permute-done.12.refs_4_
  32.8 0.1 collective-permute-start.13
  32.8 1.4 %collective-permute-start.15 = (bf16[32,768]{1,0:T(8,128)(2,1)S(1)}, bf16[32,768]{1,0:T(8,128)(2,1)S(1)}, u32[]{:S(2)}, u32[]{:S(2)}) collective-permute-start(bf16[32,768]{1,0:T(8,128)(2,1)S(1)} %get-tuple-element.54), channel_id=1, source_target_pairs={{0,2},{1,3},{2,0},{3,1},{4,6},{5,7},{6,4},{7,5},{8,10},{9,11},{10,... | collective-permute-start | bytes 147464 | tf_op jit(solution)/shard_map/ppermute | solution.py:342
  34.2 1.3 %collective-permute-start.16 = (bf16[32,768]{1,0:T(8,128)(2,1)S(1)}, bf16[32,768]{1,0:T(8,128)(2,1)S(1)}, u32[]{:S(2)}, u32[]{:S(2)}) collective-permute-start(bf16[32,768]{1,0:T(8,128)(2,1)S(1)} %get-tuple-element.55), channel_id=1, source_target_pairs={{0,3},{1,2},{2,1},{3,0},{4,7},{5,6},{6,5},{7,4},{8,11},{9,10},{10,... | collective-permute-start | bytes 147464 | tf_op jit(solution)/shard_map/ppermute | solution.py:342
  35.5 0.1 collective-permute-start.17
  35.6 1.7 %collective-permute-done.14.refs_3_ = bf16[32,768]{1,0:T(8,128)(2,1)S(1)} collective-permute-done((bf16[32,768]{1,0:T(8,128)(2,1)S(1)}, bf16[32,768]{1,0:T(8,128)(2,1)S(1)}, u32[]{:S(2)}, u32[]{:S(2)}) %collective-permute-start.14) | collective-permute-done | bytes 49184 | tf_op jit(solution)/shard_map/ppermute | solution.py:342
  37.3 1.4 %collective-permute-done.13.refs_2_ = bf16[32,768]{1,0:T(8,128)(2,1)S(1)} collective-permute-done((bf16[32,768]{1,0:T(8,128)(2,1)S(1)}, bf16[32,768]{1,0:T(8,128)(2,1)S(1)}, u32[]{:S(2)}, u32[]{:S(2)}) %collective-permute-start.13) | collective-permute-done | bytes 49184 | tf_op jit(solution)/shard_map/ppermute | solution.py:342
  38.7 0.1 collective-permute-done.15.refs_4_
  38.8 1.3 %collective-permute-done.16.refs_5_ = bf16[32,768]{1,0:T(8,128)(2,1)S(1)} collective-permute-done((bf16[32,768]{1,0:T(8,128)(2,1)S(1)}, bf16[32,768]{1,0:T(8,128)(2,1)S(1)}, u32[]{:S(2)}, u32[]{:S(2)}) %collective-permute-start.16) | collective-permute-done | bytes 49184 | tf_op jit(solution)/shard_map/ppermute | solution.py:342
  40.1 0.1 sum.1
  40.2 1.5 %collective-permute-start.18 = (bf16[32,768]{1,0:T(8,128)(2,1)S(1)}, bf16[32,768]{1,0:T(8,128)(2,1)S(1)}, u32[]{:S(2)}, u32[]{:S(2)}) collective-permute-start(bf16[32,768]{1,0:T(8,128)(2,1)S(1)} %get-tuple-element.58), channel_id=1, source_target_pairs={{0,16},{8,24},{16,0},{24,8},{1,17},{9,25},{17,1},{25,9},{2,18},{10... | collective-permute-start | bytes 147464 | tf_op jit(solution)/shard_map/ppermute | solution.py:337
  41.7 1.5 %collective-permute-start.19 = (bf16[32,768]{1,0:T(8,128)(2,1)S(1)}, bf16[32,768]{1,0:T(8,128)(2,1)S(1)}, u32[]{:S(2)}, u32[]{:S(2)}) collective-permute-start(bf16[32,768]{1,0:T(8,128)(2,1)S(1)} %get-tuple-element.59), channel_id=1, source_target_pairs={{0,24},{8,16},{16,8},{24,0},{1,25},{9,17},{17,9},{25,1},{2,26},{10... | collective-permute-start | bytes 147464 | tf_op jit(solution)/shard_map/ppermute | solution.py:337
  43.2 0.5 %collective-permute-start.20 = (bf16[32,768]{1,0:T(8,128)(2,1)S(1)}, bf16[32,768]{1,0:T(8,128)(2,1)S(1)}, u32[]{:S(2)}, u32[]{:S(2)}) collective-permute-start(bf16[32,768]{1,0:T(8,128)(2,1)S(1)} %get-tuple-element.60), channel_id=1, source_target_pairs={{0,8},{8,0},{16,24},{24,16},{1,9},{9,1},{17,25},{25,17},{2,10},{10... | collective-permute-start | bytes 147464 | tf_op jit(solution)/shard_map/ppermute | solution.py:337
  43.7 0.6 %collective-permute-done.18.refs_1_ = bf16[32,768]{1,0:T(8,128)(2,1)S(1)} collective-permute-done((bf16[32,768]{1,0:T(8,128)(2,1)S(1)}, bf16[32,768]{1,0:T(8,128)(2,1)S(1)}, u32[]{:S(2)}, u32[]{:S(2)}) %collective-permute-start.18) | collective-permute-done | bytes 49184 | tf_op jit(solution)/shard_map/ppermute | solution.py:337
  44.3 2.4 %collective-permute-done.19.refs_2_ = bf16[32,768]{1,0:T(8,128)(2,1)S(1)} collective-permute-done((bf16[32,768]{1,0:T(8,128)(2,1)S(1)}, bf16[32,768]{1,0:T(8,128)(2,1)S(1)}, u32[]{:S(2)}, u32[]{:S(2)}) %collective-permute-start.19) | collective-permute-done | bytes 49184 | tf_op jit(solution)/shard_map/ppermute | solution.py:337
  46.8 0.5 %collective-permute-done.20.refs_3_ = bf16[32,768]{1,0:T(8,128)(2,1)S(1)} collective-permute-done((bf16[32,768]{1,0:T(8,128)(2,1)S(1)}, bf16[32,768]{1,0:T(8,128)(2,1)S(1)}, u32[]{:S(2)}, u32[]{:S(2)}) %collective-permute-start.20) | collective-permute-done | bytes 49184 | tf_op jit(solution)/shard_map/ppermute | solution.py:337
  47.3 1.4 %deal.1 = bf16[16,8,768]{2,1,0:T(8,128)(2,1)} custom-call(s32[1]{0:T(128)} %bitcast.me_ref, s32[8]{0:T(128)S(1)} %copy-done.3, f32[8]{0:T(128)S(1)} %copy-done.4, f32[8,128]{1,0:T(8,128)S(1)} %get-tuple-element.38.refs_1_.total_ref, bf16[32,768]{1,0:T(8,128)(2,1)S(1)} %get-tuple-element.57.refs_0_, bf16[32,768]{1,0:T(8,128)(2,1)S(1)} %collective-permute-done.18.refs_1_, ...), custom_call_target="tpu_custom_call" | custom-call | bytes 397312 | tf_op jit(solution)/shard_map/deal/pallas_call | solution.py:311
  (14 shorter events, 0.1 us)
Async XLA Ops:
  0.0 9.3 %collective-permute-start.1 = (bf16[12,128,768]{2,1,0:T(8,128)(2,1)}, bf16[12,128,768]{2,1,0:T(8,128)(2,1)S(1)}, u32[]{:S(2)}, u32[]{:S(2)}) collective-permute-start(bf16[12,128,768]{2,1,0:T(8,128)(2,1)} %refs_0_.2), channel_id=1, source_target_pairs={{0,1},{1,0},{2,3},{3,2},{4,5},{5,4},{6,7},{7,6},{8,9},{9,8},{10,11... | collective-permute-start | bytes 7077896 | tf_op jit(solution)/shard_map/ppermute | solution.py:342
  2.4 6.9 %collective-permute-start = (bf16[32,896]{1,0:T(8,128)(2,1)}, bf16[32,896]{1,0:T(8,128)(2,1)S(1)}, u32[]{:S(2)}, u32[]{:S(2)}) collective-permute-start(bf16[32,896]{1,0:T(8,128)(2,1)} %get-tuple-element.34), channel_id=1, source_target_pairs={{0,16},{8,24},{16,0},{24,8},{1,17},{9,25},{17,1},{25,9},{2,18},{10... | collective-permute-start | bytes 172040 | tf_op jit(solution)/shard_map/ppermute | solution.py:337
  5.0 5.5 %collective-permute-start.2 = (bf16[32,896]{1,0:T(8,128)(2,1)}, bf16[32,896]{1,0:T(8,128)(2,1)S(1)}, u32[]{:S(2)}, u32[]{:S(2)}) collective-permute-start(bf16[32,896]{1,0:T(8,128)(2,1)} %get-tuple-element.36), channel_id=1, source_target_pairs={{0,24},{8,16},{16,8},{24,0},{1,25},{9,17},{17,9},{25,1},{2,26},{10... | collective-permute-start | bytes 172040 | tf_op jit(solution)/shard_map/ppermute | solution.py:337
  6.4 4.4 %collective-permute-start.3 = (bf16[32,896]{1,0:T(8,128)(2,1)}, bf16[32,896]{1,0:T(8,128)(2,1)S(1)}, u32[]{:S(2)}, u32[]{:S(2)}) collective-permute-start(bf16[32,896]{1,0:T(8,128)(2,1)} %get-tuple-element.37), channel_id=1, source_target_pairs={{0,8},{8,0},{16,24},{24,16},{1,9},{9,1},{17,25},{25,17},{2,10},{10... | collective-permute-start | bytes 172040 | tf_op jit(solution)/shard_map/ppermute | solution.py:337
  6.5 0.8 %copy-start.2 = (bf16[32,896]{1,0:T(8,128)(2,1)S(1)}, bf16[32,896]{1,0:T(8,128)(2,1)}, u32[]{:S(2)}) copy-start(bf16[32,896]{1,0:T(8,128)(2,1)} %get-tuple-element.33.refs_0_) | copy-start | bytes 172036
  7.4 1.7 %copy-start = (bf16[12,128,768]{2,1,0:T(8,128)(2,1)S(1)}, bf16[12,128,768]{2,1,0:T(8,128)(2,1)}, u32[]{:S(2)}) copy-start(bf16[12,128,768]{2,1,0:T(8,128)(2,1)} %refs_0_.2) | copy-start | bytes 7077892
  9.2 11.7 %copy-start.1 = (bf16[768,768]{1,0:T(8,128)(2,1)S(1)}, bf16[768,768]{1,0:T(8,128)(2,1)}, u32[]{:S(2)}) copy-start(bf16[768,768]{1,0:T(8,128)(2,1)} %refs_0_.3) | copy-start | bytes 3538948
  10.9 7.5 %collective-permute-start.8 = (bf16[216,128]{1,0:T(8,128)(2,1)S(1)}, bf16[216,128]{1,0:T(8,128)(2,1)S(1)}, u32[]{:S(2)}, u32[]{:S(2)}) collective-permute-start(bf16[216,128]{1,0:T(8,128)(2,1)S(1)} %get-tuple-element.44), channel_id=1, source_target_pairs={{0,5},{1,4},{2,7},{3,6},{4,1},{5,0},{6,3},{7,2},{8,13},{9,12},{10,... | collective-permute-start | bytes 165896 | tf_op jit(solution)/shard_map/ppermute | solution.py:342
  12.4 8.5 %collective-permute-start.4 = (bf16[216,128]{1,0:T(8,128)(2,1)S(1)}, bf16[216,128]{1,0:T(8,128)(2,1)S(1)}, u32[]{:S(2)}, u32[]{:S(2)}) collective-permute-start(bf16[216,128]{1,0:T(8,128)(2,1)S(1)} %get-tuple-element.43), channel_id=1, source_target_pairs={{0,4},{1,5},{2,6},{3,7},{4,0},{5,1},{6,2},{7,3},{8,12},{9,13},{10,... | collective-permute-start | bytes 165896 | tf_op jit(solution)/shard_map/ppermute | solution.py:342
  13.6 9.5 %collective-permute-start.10 = (bf16[216,128]{1,0:T(8,128)(2,1)S(1)}, bf16[216,128]{1,0:T(8,128)(2,1)S(1)}, u32[]{:S(2)}, u32[]{:S(2)}) collective-permute-start(bf16[216,128]{1,0:T(8,128)(2,1)S(1)} %get-tuple-element.43), channel_id=1, source_target_pairs={{0,6},{1,7},{2,4},{3,5},{4,2},{5,3},{6,0},{7,1},{8,14},{9,15},{10,... | collective-permute-start | bytes 165896 | tf_op jit(solution)/shard_map/ppermute | solution.py:342
  16.3 5.6 %collective-permute-start.7 = (bf16[216,128]{1,0:T(8,128)(2,1)S(1)}, bf16[216,128]{1,0:T(8,128)(2,1)S(1)}, u32[]{:S(2)}, u32[]{:S(2)}) collective-permute-start(bf16[216,128]{1,0:T(8,128)(2,1)S(1)} %get-tuple-element.41.refs_0_), channel_id=1, source_target_pairs={{0,2},{1,3},{2,0},{3,1},{4,6},{5,7},{6,4},{7,5},{8,10},{9,11},{10,... | collective-permute-start | bytes 165896 | tf_op jit(solution)/shard_map/ppermute | solution.py:342
  16.3 6.8 %collective-permute-start.6 = (bf16[216,128]{1,0:T(8,128)(2,1)S(1)}, bf16[216,128]{1,0:T(8,128)(2,1)S(1)}, u32[]{:S(2)}, u32[]{:S(2)}) collective-permute-start(bf16[216,128]{1,0:T(8,128)(2,1)S(1)} %get-tuple-element.42.source_ref), channel_id=1, source_target_pairs={{0,3},{1,2},{2,1},{3,0},{4,7},{5,6},{6,5},{7,4},{8,11},{9,10},{10,... | collective-permute-start | bytes 165896 | tf_op jit(solution)/shard_map/ppermute | solution.py:342
  18.4 5.9 %collective-permute-start.9 = (bf16[216,128]{1,0:T(8,128)(2,1)S(1)}, bf16[216,128]{1,0:T(8,128)(2,1)S(1)}, u32[]{:S(2)}, u32[]{:S(2)}) collective-permute-start(bf16[216,128]{1,0:T(8,128)(2,1)S(1)} %collective-permute-done.8.refs_6_), channel_id=1, source_target_pairs={{0,2},{1,3},{2,0},{3,1},{4,6},{5,7},{6,4},{7,5},{8,10},{9,11},{10,... | collective-permute-start | bytes 165896 | tf_op jit(solution)/shard_map/ppermute | solution.py:342
  20.9 3.5 %collective-permute-start.5 = (bf16[216,128]{1,0:T(8,128)(2,1)S(1)}, bf16[216,128]{1,0:T(8,128)(2,1)S(1)}, u32[]{:S(2)}, u32[]{:S(2)}) collective-permute-start(bf16[216,128]{1,0:T(8,128)(2,1)S(1)} %after.1), channel_id=1, source_target_pairs={{0,1},{1,0},{2,3},{3,2},{4,5},{5,4},{6,7},{7,6},{8,9},{9,8},{10,11... | collective-permute-start | bytes 165896 | tf_op jit(solution)/shard_map/ppermute | solution.py:342
  21.2 26.1 %copy-start.3 = (s32[8]{0:T(128)S(1)}, s32[8]{0:T(128)}, u32[]{:S(2)}) copy-start(s32[8]{0:T(128)} %target_ref.1) | copy-start | bytes 100
  21.2 26.1 %copy-start.4 = (f32[8]{0:T(128)S(1)}, f32[8]{0:T(128)}, u32[]{:S(2)}) copy-start(f32[8]{0:T(128)} %weights_ref.1) | copy-start | bytes 100
  28.1 4.7 %collective-permute-start.12 = (bf16[32,768]{1,0:T(8,128)(2,1)S(1)}, bf16[32,768]{1,0:T(8,128)(2,1)S(1)}, u32[]{:S(2)}, u32[]{:S(2)}) collective-permute-start(bf16[32,768]{1,0:T(8,128)(2,1)S(1)} %get-tuple-element.51), channel_id=1, source_target_pairs={{0,2},{1,3},{2,0},{3,1},{4,6},{5,7},{6,4},{7,5},{8,10},{9,11},{10,... | collective-permute-start | bytes 147464 | tf_op jit(solution)/shard_map/ppermute | solution.py:342
  28.4 7.1 %collective-permute-start.11 = (bf16[32,768]{1,0:T(8,128)(2,1)S(1)}, bf16[32,768]{1,0:T(8,128)(2,1)S(1)}, u32[]{:S(2)}, u32[]{:S(2)}) collective-permute-start(bf16[32,768]{1,0:T(8,128)(2,1)S(1)} %get-tuple-element.46), channel_id=1, source_target_pairs={{0,4},{1,5},{2,6},{3,7},{4,0},{5,1},{6,2},{7,3},{8,12},{9,13},{10,... | collective-permute-start | bytes 147464 | tf_op jit(solution)/shard_map/ppermute | solution.py:342
  31.3 6.0 %collective-permute-start.14 = (bf16[32,768]{1,0:T(8,128)(2,1)S(1)}, bf16[32,768]{1,0:T(8,128)(2,1)S(1)}, u32[]{:S(2)}, u32[]{:S(2)}) collective-permute-start(bf16[32,768]{1,0:T(8,128)(2,1)S(1)} %get-tuple-element.53), channel_id=1, source_target_pairs={{0,6},{1,7},{2,4},{3,5},{4,2},{5,3},{6,0},{7,1},{8,14},{9,15},{10,... | collective-permute-start | bytes 147464 | tf_op jit(solution)/shard_map/ppermute | solution.py:342
  32.8 5.9 %collective-permute-start.13 = (bf16[32,768]{1,0:T(8,128)(2,1)S(1)}, bf16[32,768]{1,0:T(8,128)(2,1)S(1)}, u32[]{:S(2)}, u32[]{:S(2)}) collective-permute-start(bf16[32,768]{1,0:T(8,128)(2,1)S(1)} %get-tuple-element.52), channel_id=1, source_target_pairs={{0,5},{1,4},{2,7},{3,6},{4,1},{5,0},{6,3},{7,2},{8,13},{9,12},{10,... | collective-permute-start | bytes 147464 | tf_op jit(solution)/shard_map/ppermute | solution.py:342
  32.8 6.0 %collective-permute-start.15 = (bf16[32,768]{1,0:T(8,128)(2,1)S(1)}, bf16[32,768]{1,0:T(8,128)(2,1)S(1)}, u32[]{:S(2)}, u32[]{:S(2)}) collective-permute-start(bf16[32,768]{1,0:T(8,128)(2,1)S(1)} %get-tuple-element.54), channel_id=1, source_target_pairs={{0,2},{1,3},{2,0},{3,1},{4,6},{5,7},{6,4},{7,5},{8,10},{9,11},{10,... | collective-permute-start | bytes 147464 | tf_op jit(solution)/shard_map/ppermute | solution.py:342
  34.2 5.8 %collective-permute-start.16 = (bf16[32,768]{1,0:T(8,128)(2,1)S(1)}, bf16[32,768]{1,0:T(8,128)(2,1)S(1)}, u32[]{:S(2)}, u32[]{:S(2)}) collective-permute-start(bf16[32,768]{1,0:T(8,128)(2,1)S(1)} %get-tuple-element.55), channel_id=1, source_target_pairs={{0,3},{1,2},{2,1},{3,0},{4,7},{5,6},{6,5},{7,4},{8,11},{9,10},{10,... | collective-permute-start | bytes 147464 | tf_op jit(solution)/shard_map/ppermute | solution.py:342
  35.5 4.6 %collective-permute-start.17 = (bf16[32,768]{1,0:T(8,128)(2,1)S(1)}, bf16[32,768]{1,0:T(8,128)(2,1)S(1)}, u32[]{:S(2)}, u32[]{:S(2)}) collective-permute-start(bf16[32,768]{1,0:T(8,128)(2,1)S(1)} %get-tuple-element.56), channel_id=1, source_target_pairs={{0,1},{1,0},{2,3},{3,2},{4,5},{5,4},{6,7},{7,6},{8,9},{9,8},{10,11... | collective-permute-start | bytes 147464 | tf_op jit(solution)/shard_map/ppermute | solution.py:342
  40.2 4.2 %collective-permute-start.18 = (bf16[32,768]{1,0:T(8,128)(2,1)S(1)}, bf16[32,768]{1,0:T(8,128)(2,1)S(1)}, u32[]{:S(2)}, u32[]{:S(2)}) collective-permute-start(bf16[32,768]{1,0:T(8,128)(2,1)S(1)} %get-tuple-element.58), channel_id=1, source_target_pairs={{0,16},{8,24},{16,0},{24,8},{1,17},{9,25},{17,1},{25,9},{2,18},{10... | collective-permute-start | bytes 147464 | tf_op jit(solution)/shard_map/ppermute | solution.py:337
  41.7 5.1 %collective-permute-start.19 = (bf16[32,768]{1,0:T(8,128)(2,1)S(1)}, bf16[32,768]{1,0:T(8,128)(2,1)S(1)}, u32[]{:S(2)}, u32[]{:S(2)}) collective-permute-start(bf16[32,768]{1,0:T(8,128)(2,1)S(1)} %get-tuple-element.59), channel_id=1, source_target_pairs={{0,24},{8,16},{16,8},{24,0},{1,25},{9,17},{17,9},{25,1},{2,26},{10... | collective-permute-start | bytes 147464 | tf_op jit(solution)/shard_map/ppermute | solution.py:337
  43.2 4.1 %collective-permute-start.20 = (bf16[32,768]{1,0:T(8,128)(2,1)S(1)}, bf16[32,768]{1,0:T(8,128)(2,1)S(1)}, u32[]{:S(2)}, u32[]{:S(2)}) collective-permute-start(bf16[32,768]{1,0:T(8,128)(2,1)S(1)} %get-tuple-element.60), channel_id=1, source_target_pairs={{0,8},{8,0},{16,24},{24,16},{1,9},{9,1},{17,25},{25,17},{2,10},{10... | collective-permute-start | bytes 147464 | tf_op jit(solution)/shard_map/ppermute | solution.py:337

commit v18 on v13

--- a/solution.py
+++ b/solution.py
@@ -461,9 +461,10 @@
         [],
         "sum",
     )
-    back = [to_list(back[s], s) for s in order]
+    last_order = [0] + sorted(range(1, groups), key=lambda s: -bin(s).count("1"))
+    back = [to_list(back[s], s) for s in last_order]
     (out,) = call(
-        functools.partial(deal_kernel, order, keep, cap),
+        functools.partial(deal_kernel, last_order, keep, cap),
         [shape(walkers.shape, BF16)],
         [grp, target, weights],
         [],

time: 47.8 us -> 48 us (level)
  no operation moved by 1% of the time
where the time goes in v18:
time: 48 us; the launch traced here: 47.8 us
  starting transfers between devices  25.8 us (54%)
  waiting for transfers between devices  11.7 us (24%)
  Pallas kernels  7.74 us (16%)
  local copies, waits for them, and re-layouts  2.5 us (5%)
    ppermute x15, starting transfers between devices, to_block(): lax.ppermute(x, 'blk', [(i, 2 * moved(i // 2, s, n // 2, 1) + (i % 2 ^ e)...  18.1 us
    pallas_call x10, Pallas kernels, call(): pl.pallas_call(kernel, out_shape=outs, in_specs=[smem] * len(scalars) + [...  7.74 us
    ppermute x6, starting transfers between devices, to_list(): lax.ppermute(x, 'grp', [(i, moved(i, s, groups, 1)) for i in range(groups)])  7.68 us
    ppermute x15, waiting for transfers between devices, to_block(): lax.ppermute(x, 'blk', [(i, 2 * moved(i // 2, s, n // 2, 1) + (i % 2 ^ e)...  6.64 us
    ppermute x6, waiting for transfers between devices, to_list(): lax.ppermute(x, 'grp', [(i, moved(i, s, groups, 1)) for i in range(groups)])  5.03 us
    unnamed x10, local copies, waits for them, and re-layouts  2.5 us
  transfers between devices with their start and end apart: 21, of which 10 were waited for; matrix products, arithmetic and copies ran while one was open for 0% of the time, Pallas kernels for 5%

profile of v18, /device:TPU:0, one launch (start us, length us, event | category | flops | bytes accessed | tf_op | source)
XLA Modules:
  0.0 47.8 jit_solution(16680885565103795029)
XLA Ops:
  0.0 0.5 collective-permute-start.3
  0.5 1.9 %route.1 = (bf16[32,896]{1,0:T(8,128)(2,1)}, bf16[32,896]{1,0:T(8,128)(2,1)}, bf16[32,896]{1,0:T(8,128)(2,1)}, bf16[32,896]{1,0:T(8,128)(2,1)}) custom-call(s32[1]{0:T(128)} %bitcast.me_ref, s32[8]{0:T(128)} %target_ref.1, f32[8]{0:T(128)} %weights_ref.1, bf16[16,8,768]{2,1,0:T(8,128)(2,1)} %walkers_any.1, f32[8,12]{1,0:T(8,128)} %fields_any.1, ...), custom_call_target="tpu_custom_call" | custom-call | bytes 229376 | tf_op jit(solution)/shard_map/route/pallas_call | solution.py:311
  2.4 2.6 %collective-permute-start = (bf16[32,896]{1,0:T(8,128)(2,1)}, bf16[32,896]{1,0:T(8,128)(2,1)S(1)}, u32[]{:S(2)}, u32[]{:S(2)}) collective-permute-start(bf16[32,896]{1,0:T(8,128)(2,1)} %get-tuple-element.32), channel_id=1, source_target_pairs={{0,16},{8,24},{16,0},{24,8},{1,17},{9,25},{17,1},{25,9},{2,18},{10... | collective-permute-start | bytes 172040 | tf_op jit(solution)/shard_map/ppermute | solution.py:337
  5.0 1.4 %collective-permute-start.1 = (bf16[32,896]{1,0:T(8,128)(2,1)}, bf16[32,896]{1,0:T(8,128)(2,1)S(1)}, u32[]{:S(2)}, u32[]{:S(2)}) collective-permute-start(bf16[32,896]{1,0:T(8,128)(2,1)} %get-tuple-element.33), channel_id=1, source_target_pairs={{0,24},{8,16},{16,8},{24,0},{1,25},{9,17},{17,9},{25,1},{2,26},{10... | collective-permute-start | bytes 172040 | tf_op jit(solution)/shard_map/ppermute | solution.py:337
  6.4 0.1 collective-permute-start.2
  6.5 0.8 %copy-done.2 = bf16[32,896]{1,0:T(8,128)(2,1)S(1)} copy-done((bf16[32,896]{1,0:T(8,128)(2,1)S(1)}, bf16[32,896]{1,0:T(8,128)(2,1)}, u32[]{:S(2)}) %copy-start.2) | copy-done | bytes 57368
  7.4 0.0 copy-start
  7.4 1.7 %copy-done = bf16[12,128,768]{2,1,0:T(8,128)(2,1)S(1)} copy-done((bf16[12,128,768]{2,1,0:T(8,128)(2,1)S(1)}, bf16[12,128,768]{2,1,0:T(8,128)(2,1)}, u32[]{:S(2)}) %copy-start) | copy-done | bytes 2359320
  9.0 0.2 stage.1.when.own_ref
  9.2 0.0 copy-start.1
  9.2 0.0 collective-permute-done.refs_1_
  9.2 1.2 %collective-permute-done.1.refs_2_ = bf16[32,896]{1,0:T(8,128)(2,1)S(1)} collective-permute-done((bf16[32,896]{1,0:T(8,128)(2,1)}, bf16[32,896]{1,0:T(8,128)(2,1)S(1)}, u32[]{:S(2)}, u32[]{:S(2)}) %collective-permute-start.1) | collective-permute-done | bytes 57376 | tf_op jit(solution)/shard_map/ppermute | solution.py:337
  10.5 0.3 collective-permute-done.2.refs_3_
  10.8 0.1 merge.1
  10.9 1.5 %collective-permute-start.8 = (bf16[216,128]{1,0:T(8,128)(2,1)S(1)}, bf16[216,128]{1,0:T(8,128)(2,1)S(1)}, u32[]{:S(2)}, u32[]{:S(2)}) collective-permute-start(bf16[216,128]{1,0:T(8,128)(2,1)S(1)} %get-tuple-element.40), channel_id=1, source_target_pairs={{0,5},{1,4},{2,7},{3,6},{4,1},{5,0},{6,3},{7,2},{8,13},{9,12},{10,... | collective-permute-start | bytes 165896 | tf_op jit(solution)/shard_map/ppermute | solution.py:342
  12.4 1.2 %collective-permute-start.4 = (bf16[216,128]{1,0:T(8,128)(2,1)S(1)}, bf16[216,128]{1,0:T(8,128)(2,1)S(1)}, u32[]{:S(2)}, u32[]{:S(2)}) collective-permute-start(bf16[216,128]{1,0:T(8,128)(2,1)S(1)} %get-tuple-element.39), channel_id=1, source_target_pairs={{0,4},{1,5},{2,6},{3,7},{4,0},{5,1},{6,2},{7,3},{8,12},{9,13},{10,... | collective-permute-start | bytes 165896 | tf_op jit(solution)/shard_map/ppermute | solution.py:342
  13.6 1.6 %collective-permute-start.7 = (bf16[216,128]{1,0:T(8,128)(2,1)S(1)}, bf16[216,128]{1,0:T(8,128)(2,1)S(1)}, u32[]{:S(2)}, u32[]{:S(2)}) collective-permute-start(bf16[216,128]{1,0:T(8,128)(2,1)S(1)} %get-tuple-element.37.refs_0_), channel_id=1, source_target_pairs={{0,2},{1,3},{2,0},{3,1},{4,6},{5,7},{6,4},{7,5},{8,10},{9,11},{10,... | collective-permute-start | bytes 165896 | tf_op jit(solution)/shard_map/ppermute | solution.py:342
  15.2 1.6 %collective-permute-start.10 = (bf16[216,128]{1,0:T(8,128)(2,1)S(1)}, bf16[216,128]{1,0:T(8,128)(2,1)S(1)}, u32[]{:S(2)}, u32[]{:S(2)}) collective-permute-start(bf16[216,128]{1,0:T(8,128)(2,1)S(1)} %get-tuple-element.39), channel_id=1, source_target_pairs={{0,6},{1,7},{2,4},{3,5},{4,2},{5,3},{6,0},{7,1},{8,14},{9,15},{10,... | collective-permute-start | bytes 165896 | tf_op jit(solution)/shard_map/ppermute | solution.py:342
  16.8 0.0 collective-permute-done.8.refs_6_
  16.8 1.5 %collective-permute-start.6 = (bf16[216,128]{1,0:T(8,128)(2,1)S(1)}, bf16[216,128]{1,0:T(8,128)(2,1)S(1)}, u32[]{:S(2)}, u32[]{:S(2)}) collective-permute-start(bf16[216,128]{1,0:T(8,128)(2,1)S(1)} %get-tuple-element.38.source_ref), channel_id=1, source_target_pairs={{0,3},{1,2},{2,1},{3,0},{4,7},{5,6},{6,5},{7,4},{8,11},{9,10},{10,... | collective-permute-start | bytes 165896 | tf_op jit(solution)/shard_map/ppermute | solution.py:342
  18.3 1.3 %collective-permute-done.4.when_ref.refs_7_ = bf16[216,128]{1,0:T(8,128)(2,1)S(1)} collective-permute-done((bf16[216,128]{1,0:T(8,128)(2,1)S(1)}, bf16[216,128]{1,0:T(8,128)(2,1)S(1)}, u32[]{:S(2)}, u32[]{:S(2)}) %collective-permute-start.4) | collective-permute-done | bytes 55328 | tf_op jit(solution)/shard_map/ppermute | solution.py:342
  19.6 1.1 %collective-permute-start.9 = (bf16[216,128]{1,0:T(8,128)(2,1)S(1)}, bf16[216,128]{1,0:T(8,128)(2,1)S(1)}, u32[]{:S(2)}, u32[]{:S(2)}) collective-permute-start(bf16[216,128]{1,0:T(8,128)(2,1)S(1)} %collective-permute-done.8.refs_6_), channel_id=1, source_target_pairs={{0,2},{1,3},{2,0},{3,1},{4,6},{5,7},{6,4},{7,5},{8,10},{9,11},{10,... | collective-permute-start | bytes 165896 | tf_op jit(solution)/shard_map/ppermute | solution.py:342
  20.7 0.1 collective-permute-start.5
  20.8 0.3 hold.1.body_ref
  21.1 0.0 copy-start.3
  21.1 0.0 copy-start.4
  21.1 0.5 %collective-permute-done.6.refs_2_ = bf16[216,128]{1,0:T(8,128)(2,1)S(1)} collective-permute-done((bf16[216,128]{1,0:T(8,128)(2,1)S(1)}, bf16[216,128]{1,0:T(8,128)(2,1)S(1)}, u32[]{:S(2)}, u32[]{:S(2)}) %collective-permute-start.6) | collective-permute-done | bytes 55328 | tf_op jit(solution)/shard_map/ppermute | solution.py:342
  21.6 2.1 %collective-permute-done.9.refs_4_ = bf16[216,128]{1,0:T(8,128)(2,1)S(1)} collective-permute-done((bf16[216,128]{1,0:T(8,128)(2,1)S(1)}, bf16[216,128]{1,0:T(8,128)(2,1)S(1)}, u32[]{:S(2)}, u32[]{:S(2)}) %collective-permute-start.9) | collective-permute-done | bytes 55328 | tf_op jit(solution)/shard_map/ppermute | solution.py:342
  23.7 0.0 collective-permute-done.5.refs_1_
  23.7 0.0 collective-permute-done.3.sib_ref
  23.8 3.7 %fock.1 = (bf16[32,768]{1,0:T(8,128)(2,1)S(1)}, bf16[32,768]{1,0:T(8,128)(2,1)S(1)}, bf16[32,768]{1,0:T(8,128)(2,1)S(1)}, bf16[32,768]{1,0:T(8,128)(2,1)S(1)}, b...) custom-call(s32[1]{0:T(128)} %bitcast.1.blk_ref, ...), custom_call_target="tpu_custom_call" | custom-call | flops 2717908992 | bytes 6733824 | tf_op jit(solution)/shard_map/fock/pallas_call | solution.py:311
  27.5 1.2 %collective-permute-start.12 = (bf16[32,768]{1,0:T(8,128)(2,1)S(1)}, bf16[32,768]{1,0:T(8,128)(2,1)S(1)}, u32[]{:S(2)}, u32[]{:S(2)}) collective-permute-start(bf16[32,768]{1,0:T(8,128)(2,1)S(1)} %get-tuple-element.47), channel_id=1, source_target_pairs={{0,2},{1,3},{2,0},{3,1},{4,6},{5,7},{6,4},{7,5},{8,10},{9,11},{10,... | collective-permute-start | bytes 147464 | tf_op jit(solution)/shard_map/ppermute | solution.py:342
  28.7 3.6 %collective-permute-start.11 = (bf16[32,768]{1,0:T(8,128)(2,1)S(1)}, bf16[32,768]{1,0:T(8,128)(2,1)S(1)}, u32[]{:S(2)}, u32[]{:S(2)}) collective-permute-start(bf16[32,768]{1,0:T(8,128)(2,1)S(1)} %get-tuple-element.42), channel_id=1, source_target_pairs={{0,4},{1,5},{2,6},{3,7},{4,0},{5,1},{6,2},{7,3},{8,12},{9,13},{10,... | collective-permute-start | bytes 147464 | tf_op jit(solution)/shard_map/ppermute | solution.py:342
  32.2 0.0 collective-permute-start.14
  32.3 0.1 collective-permute-start.13
  32.4 2.0 %collective-permute-start.15 = (bf16[32,768]{1,0:T(8,128)(2,1)S(1)}, bf16[32,768]{1,0:T(8,128)(2,1)S(1)}, u32[]{:S(2)}, u32[]{:S(2)}) collective-permute-start(bf16[32,768]{1,0:T(8,128)(2,1)S(1)} %get-tuple-element.50), channel_id=1, source_target_pairs={{0,2},{1,3},{2,0},{3,1},{4,6},{5,7},{6,4},{7,5},{8,10},{9,11},{10,... | collective-permute-start | bytes 147464 | tf_op jit(solution)/shard_map/ppermute | solution.py:342
  34.4 2.1 %collective-permute-start.16 = (bf16[32,768]{1,0:T(8,128)(2,1)S(1)}, bf16[32,768]{1,0:T(8,128)(2,1)S(1)}, u32[]{:S(2)}, u32[]{:S(2)}) collective-permute-start(bf16[32,768]{1,0:T(8,128)(2,1)S(1)} %get-tuple-element.51), channel_id=1, source_target_pairs={{0,3},{1,2},{2,1},{3,0},{4,7},{5,6},{6,5},{7,4},{8,11},{9,10},{10,... | collective-permute-start | bytes 147464 | tf_op jit(solution)/shard_map/ppermute | solution.py:342
  36.5 0.1 collective-permute-start.17
  36.6 1.9 %collective-permute-done.14.refs_3_ = bf16[32,768]{1,0:T(8,128)(2,1)S(1)} collective-permute-done((bf16[32,768]{1,0:T(8,128)(2,1)S(1)}, bf16[32,768]{1,0:T(8,128)(2,1)S(1)}, u32[]{:S(2)}, u32[]{:S(2)}) %collective-permute-start.14) | collective-permute-done | bytes 49184 | tf_op jit(solution)/shard_map/ppermute | solution.py:342
  38.5 0.7 %collective-permute-done.16.refs_5_ = bf16[32,768]{1,0:T(8,128)(2,1)S(1)} collective-permute-done((bf16[32,768]{1,0:T(8,128)(2,1)S(1)}, bf16[32,768]{1,0:T(8,128)(2,1)S(1)}, u32[]{:S(2)}, u32[]{:S(2)}) %collective-permute-start.16) | collective-permute-done | bytes 49184 | tf_op jit(solution)/shard_map/ppermute | solution.py:342
  39.2 0.1 sum.1
  39.3 2.3 %collective-permute-start.18 = (bf16[32,768]{1,0:T(8,128)(2,1)S(1)}, bf16[32,768]{1,0:T(8,128)(2,1)S(1)}, u32[]{:S(2)}, u32[]{:S(2)}) collective-permute-start(bf16[32,768]{1,0:T(8,128)(2,1)S(1)} %get-tuple-element.54), channel_id=1, source_target_pairs={{0,24},{8,16},{16,8},{24,0},{1,25},{9,17},{17,9},{25,1},{2,26},{10... | collective-permute-start | bytes 147464 | tf_op jit(solution)/shard_map/ppermute | solution.py:337
  41.6 0.7 %collective-permute-start.19 = (bf16[32,768]{1,0:T(8,128)(2,1)S(1)}, bf16[32,768]{1,0:T(8,128)(2,1)S(1)}, u32[]{:S(2)}, u32[]{:S(2)}) collective-permute-start(bf16[32,768]{1,0:T(8,128)(2,1)S(1)} %get-tuple-element.55), channel_id=1, source_target_pairs={{0,8},{8,0},{16,24},{24,16},{1,9},{9,1},{17,25},{25,17},{2,10},{10... | collective-permute-start | bytes 147464 | tf_op jit(solution)/shard_map/ppermute | solution.py:337
  42.3 0.6 %collective-permute-start.20 = (bf16[32,768]{1,0:T(8,128)(2,1)S(1)}, bf16[32,768]{1,0:T(8,128)(2,1)S(1)}, u32[]{:S(2)}, u32[]{:S(2)}) collective-permute-start(bf16[32,768]{1,0:T(8,128)(2,1)S(1)} %get-tuple-element.56), channel_id=1, source_target_pairs={{0,16},{8,24},{16,0},{24,8},{1,17},{9,25},{17,1},{25,9},{2,18},{10... | collective-permute-start | bytes 147464 | tf_op jit(solution)/shard_map/ppermute | solution.py:337
  42.9 2.0 %collective-permute-done.18.refs_1_ = bf16[32,768]{1,0:T(8,128)(2,1)S(1)} collective-permute-done((bf16[32,768]{1,0:T(8,128)(2,1)S(1)}, bf16[32,768]{1,0:T(8,128)(2,1)S(1)}, u32[]{:S(2)}, u32[]{:S(2)}) %collective-permute-start.18) | collective-permute-done | bytes 49184 | tf_op jit(solution)/shard_map/ppermute | solution.py:337
  44.9 0.9 %collective-permute-done.19.refs_2_ = bf16[32,768]{1,0:T(8,128)(2,1)S(1)} collective-permute-done((bf16[32,768]{1,0:T(8,128)(2,1)S(1)}, bf16[32,768]{1,0:T(8,128)(2,1)S(1)}, u32[]{:S(2)}, u32[]{:S(2)}) %collective-permute-start.19) | collective-permute-done | bytes 49184 | tf_op jit(solution)/shard_map/ppermute | solution.py:337
  45.8 0.5 %collective-permute-done.20.refs_3_ = bf16[32,768]{1,0:T(8,128)(2,1)S(1)} collective-permute-done((bf16[32,768]{1,0:T(8,128)(2,1)S(1)}, bf16[32,768]{1,0:T(8,128)(2,1)S(1)}, u32[]{:S(2)}, u32[]{:S(2)}) %collective-permute-start.20) | collective-permute-done | bytes 49184 | tf_op jit(solution)/shard_map/ppermute | solution.py:337
  46.4 1.4 %deal.1 = bf16[16,8,768]{2,1,0:T(8,128)(2,1)} custom-call(s32[1]{0:T(128)} %bitcast.me_ref, s32[8]{0:T(128)S(1)} %copy-done.3, f32[8]{0:T(128)S(1)} %copy-done.4, f32[8,128]{1,0:T(8,128)S(1)} %get-tuple-element.35.refs_1_.total_ref, bf16[32,768]{1,0:T(8,128)(2,1)S(1)} %get-tuple-element.53.refs_0_, bf16[32,768]{1,0:T(8,128)(2,1)S(1)} %collective-permute-done.18.refs_1_, ...), custom_call_target="tpu_custom_call" | custom-call | bytes 397312 | tf_op jit(solution)/shard_map/deal/pallas_call | solution.py:311
  (14 shorter events, 0.1 us)
Async XLA Ops:
  0.0 23.8 %collective-permute-start.3 = (bf16[12,128,768]{2,1,0:T(8,128)(2,1)}, bf16[12,128,768]{2,1,0:T(8,128)(2,1)S(1)}, u32[]{:S(2)}, u32[]{:S(2)}) collective-permute-start(bf16[12,128,768]{2,1,0:T(8,128)(2,1)} %refs_0_.2), channel_id=1, source_target_pairs={{0,1},{1,0},{2,3},{3,2},{4,5},{5,4},{6,7},{7,6},{8,9},{9,8},{10,11... | collective-permute-start | bytes 7077896 | tf_op jit(solution)/shard_map/ppermute | solution.py:342
  2.4 6.9 %collective-permute-start = (bf16[32,896]{1,0:T(8,128)(2,1)}, bf16[32,896]{1,0:T(8,128)(2,1)S(1)}, u32[]{:S(2)}, u32[]{:S(2)}) collective-permute-start(bf16[32,896]{1,0:T(8,128)(2,1)} %get-tuple-element.32), channel_id=1, source_target_pairs={{0,16},{8,24},{16,0},{24,8},{1,17},{9,25},{17,1},{25,9},{2,18},{10... | collective-permute-start | bytes 172040 | tf_op jit(solution)/shard_map/ppermute | solution.py:337
  5.0 5.5 %collective-permute-start.1 = (bf16[32,896]{1,0:T(8,128)(2,1)}, bf16[32,896]{1,0:T(8,128)(2,1)S(1)}, u32[]{:S(2)}, u32[]{:S(2)}) collective-permute-start(bf16[32,896]{1,0:T(8,128)(2,1)} %get-tuple-element.33), channel_id=1, source_target_pairs={{0,24},{8,16},{16,8},{24,0},{1,25},{9,17},{17,9},{25,1},{2,26},{10... | collective-permute-start | bytes 172040 | tf_op jit(solution)/shard_map/ppermute | solution.py:337
  6.4 4.4 %collective-permute-start.2 = (bf16[32,896]{1,0:T(8,128)(2,1)}, bf16[32,896]{1,0:T(8,128)(2,1)S(1)}, u32[]{:S(2)}, u32[]{:S(2)}) collective-permute-start(bf16[32,896]{1,0:T(8,128)(2,1)} %get-tuple-element.34), channel_id=1, source_target_pairs={{0,8},{8,0},{16,24},{24,16},{1,9},{9,1},{17,25},{25,17},{2,10},{10... | collective-permute-start | bytes 172040 | tf_op jit(solution)/shard_map/ppermute | solution.py:337
  6.5 0.8 %copy-start.2 = (bf16[32,896]{1,0:T(8,128)(2,1)S(1)}, bf16[32,896]{1,0:T(8,128)(2,1)}, u32[]{:S(2)}) copy-start(bf16[32,896]{1,0:T(8,128)(2,1)} %get-tuple-element.31.refs_0_) | copy-start | bytes 172036
  7.4 1.7 %copy-start = (bf16[12,128,768]{2,1,0:T(8,128)(2,1)S(1)}, bf16[12,128,768]{2,1,0:T(8,128)(2,1)}, u32[]{:S(2)}) copy-start(bf16[12,128,768]{2,1,0:T(8,128)(2,1)} %refs_0_.2) | copy-start | bytes 7077892
  9.2 11.6 %copy-start.1 = (bf16[768,768]{1,0:T(8,128)(2,1)S(1)}, bf16[768,768]{1,0:T(8,128)(2,1)}, u32[]{:S(2)}) copy-start(bf16[768,768]{1,0:T(8,128)(2,1)} %refs_0_.3) | copy-start | bytes 3538948
  10.9 5.9 %collective-permute-start.8 = (bf16[216,128]{1,0:T(8,128)(2,1)S(1)}, bf16[216,128]{1,0:T(8,128)(2,1)S(1)}, u32[]{:S(2)}, u32[]{:S(2)}) collective-permute-start(bf16[216,128]{1,0:T(8,128)(2,1)S(1)} %get-tuple-element.40), channel_id=1, source_target_pairs={{0,5},{1,4},{2,7},{3,6},{4,1},{5,0},{6,3},{7,2},{8,13},{9,12},{10,... | collective-permute-start | bytes 165896 | tf_op jit(solution)/shard_map/ppermute | solution.py:342
  12.4 7.2 %collective-permute-start.4 = (bf16[216,128]{1,0:T(8,128)(2,1)S(1)}, bf16[216,128]{1,0:T(8,128)(2,1)S(1)}, u32[]{:S(2)}, u32[]{:S(2)}) collective-permute-start(bf16[216,128]{1,0:T(8,128)(2,1)S(1)} %get-tuple-element.39), channel_id=1, source_target_pairs={{0,4},{1,5},{2,6},{3,7},{4,0},{5,1},{6,2},{7,3},{8,12},{9,13},{10,... | collective-permute-start | bytes 165896 | tf_op jit(solution)/shard_map/ppermute | solution.py:342
  13.6 7.1 %collective-permute-start.7 = (bf16[216,128]{1,0:T(8,128)(2,1)S(1)}, bf16[216,128]{1,0:T(8,128)(2,1)S(1)}, u32[]{:S(2)}, u32[]{:S(2)}) collective-permute-start(bf16[216,128]{1,0:T(8,128)(2,1)S(1)} %get-tuple-element.37.refs_0_), channel_id=1, source_target_pairs={{0,2},{1,3},{2,0},{3,1},{4,6},{5,7},{6,4},{7,5},{8,10},{9,11},{10,... | collective-permute-start | bytes 165896 | tf_op jit(solution)/shard_map/ppermute | solution.py:342
  15.2 6.4 %collective-permute-start.10 = (bf16[216,128]{1,0:T(8,128)(2,1)S(1)}, bf16[216,128]{1,0:T(8,128)(2,1)S(1)}, u32[]{:S(2)}, u32[]{:S(2)}) collective-permute-start(bf16[216,128]{1,0:T(8,128)(2,1)S(1)} %get-tuple-element.39), channel_id=1, source_target_pairs={{0,6},{1,7},{2,4},{3,5},{4,2},{5,3},{6,0},{7,1},{8,14},{9,15},{10,... | collective-permute-start | bytes 165896 | tf_op jit(solution)/shard_map/ppermute | solution.py:342
  16.8 4.8 %collective-permute-start.6 = (bf16[216,128]{1,0:T(8,128)(2,1)S(1)}, bf16[216,128]{1,0:T(8,128)(2,1)S(1)}, u32[]{:S(2)}, u32[]{:S(2)}) collective-permute-start(bf16[216,128]{1,0:T(8,128)(2,1)S(1)} %get-tuple-element.38.source_ref), channel_id=1, source_target_pairs={{0,3},{1,2},{2,1},{3,0},{4,7},{5,6},{6,5},{7,4},{8,11},{9,10},{10,... | collective-permute-start | bytes 165896 | tf_op jit(solution)/shard_map/ppermute | solution.py:342
  19.6 4.2 %collective-permute-start.9 = (bf16[216,128]{1,0:T(8,128)(2,1)S(1)}, bf16[216,128]{1,0:T(8,128)(2,1)S(1)}, u32[]{:S(2)}, u32[]{:S(2)}) collective-permute-start(bf16[216,128]{1,0:T(8,128)(2,1)S(1)} %collective-permute-done.8.refs_6_), channel_id=1, source_target_pairs={{0,2},{1,3},{2,0},{3,1},{4,6},{5,7},{6,4},{7,5},{8,10},{9,11},{10,... | collective-permute-start | bytes 165896 | tf_op jit(solution)/shard_map/ppermute | solution.py:342
  20.7 3.0 %collective-permute-start.5 = (bf16[216,128]{1,0:T(8,128)(2,1)S(1)}, bf16[216,128]{1,0:T(8,128)(2,1)S(1)}, u32[]{:S(2)}, u32[]{:S(2)}) collective-permute-start(bf16[216,128]{1,0:T(8,128)(2,1)S(1)} %after.1), channel_id=1, source_target_pairs={{0,1},{1,0},{2,3},{3,2},{4,5},{5,4},{6,7},{7,6},{8,9},{9,8},{10,11... | collective-permute-start | bytes 165896 | tf_op jit(solution)/shard_map/ppermute | solution.py:342
  21.1 25.3 %copy-start.3 = (s32[8]{0:T(128)S(1)}, s32[8]{0:T(128)}, u32[]{:S(2)}) copy-start(s32[8]{0:T(128)} %target_ref.1) | copy-start | bytes 100
  21.1 25.3 %copy-start.4 = (f32[8]{0:T(128)S(1)}, f32[8]{0:T(128)}, u32[]{:S(2)}) copy-start(f32[8]{0:T(128)} %weights_ref.1) | copy-start | bytes 100
  27.5 4.8 %collective-permute-start.12 = (bf16[32,768]{1,0:T(8,128)(2,1)S(1)}, bf16[32,768]{1,0:T(8,128)(2,1)S(1)}, u32[]{:S(2)}, u32[]{:S(2)}) collective-permute-start(bf16[32,768]{1,0:T(8,128)(2,1)S(1)} %get-tuple-element.47), channel_id=1, source_target_pairs={{0,2},{1,3},{2,0},{3,1},{4,6},{5,7},{6,4},{7,5},{8,10},{9,11},{10,... | collective-permute-start | bytes 147464 | tf_op jit(solution)/shard_map/ppermute | solution.py:342
  28.7 7.8 %collective-permute-start.11 = (bf16[32,768]{1,0:T(8,128)(2,1)S(1)}, bf16[32,768]{1,0:T(8,128)(2,1)S(1)}, u32[]{:S(2)}, u32[]{:S(2)}) collective-permute-start(bf16[32,768]{1,0:T(8,128)(2,1)S(1)} %get-tuple-element.42), channel_id=1, source_target_pairs={{0,4},{1,5},{2,6},{3,7},{4,0},{5,1},{6,2},{7,3},{8,12},{9,13},{10,... | collective-permute-start | bytes 147464 | tf_op jit(solution)/shard_map/ppermute | solution.py:342
  32.2 6.2 %collective-permute-start.14 = (bf16[32,768]{1,0:T(8,128)(2,1)S(1)}, bf16[32,768]{1,0:T(8,128)(2,1)S(1)}, u32[]{:S(2)}, u32[]{:S(2)}) collective-permute-start(bf16[32,768]{1,0:T(8,128)(2,1)S(1)} %get-tuple-element.49), channel_id=1, source_target_pairs={{0,6},{1,7},{2,4},{3,5},{4,2},{5,3},{6,0},{7,1},{8,14},{9,15},{10,... | collective-permute-start | bytes 147464 | tf_op jit(solution)/shard_map/ppermute | solution.py:342
  32.3 6.2 %collective-permute-start.13 = (bf16[32,768]{1,0:T(8,128)(2,1)S(1)}, bf16[32,768]{1,0:T(8,128)(2,1)S(1)}, u32[]{:S(2)}, u32[]{:S(2)}) collective-permute-start(bf16[32,768]{1,0:T(8,128)(2,1)S(1)} %get-tuple-element.48), channel_id=1, source_target_pairs={{0,5},{1,4},{2,7},{3,6},{4,1},{5,0},{6,3},{7,2},{8,13},{9,12},{10,... | collective-permute-start | bytes 147464 | tf_op jit(solution)/shard_map/ppermute | solution.py:342
  32.4 6.1 %collective-permute-start.15 = (bf16[32,768]{1,0:T(8,128)(2,1)S(1)}, bf16[32,768]{1,0:T(8,128)(2,1)S(1)}, u32[]{:S(2)}, u32[]{:S(2)}) collective-permute-start(bf16[32,768]{1,0:T(8,128)(2,1)S(1)} %get-tuple-element.50), channel_id=1, source_target_pairs={{0,2},{1,3},{2,0},{3,1},{4,6},{5,7},{6,4},{7,5},{8,10},{9,11},{10,... | collective-permute-start | bytes 147464 | tf_op jit(solution)/shard_map/ppermute | solution.py:342
  34.4 4.8 %collective-permute-start.16 = (bf16[32,768]{1,0:T(8,128)(2,1)S(1)}, bf16[32,768]{1,0:T(8,128)(2,1)S(1)}, u32[]{:S(2)}, u32[]{:S(2)}) collective-permute-start(bf16[32,768]{1,0:T(8,128)(2,1)S(1)} %get-tuple-element.51), channel_id=1, source_target_pairs={{0,3},{1,2},{2,1},{3,0},{4,7},{5,6},{6,5},{7,4},{8,11},{9,10},{10,... | collective-permute-start | bytes 147464 | tf_op jit(solution)/shard_map/ppermute | solution.py:342
  36.5 2.8 %collective-permute-start.17 = (bf16[32,768]{1,0:T(8,128)(2,1)S(1)}, bf16[32,768]{1,0:T(8,128)(2,1)S(1)}, u32[]{:S(2)}, u32[]{:S(2)}) collective-permute-start(bf16[32,768]{1,0:T(8,128)(2,1)S(1)} %get-tuple-element.52), channel_id=1, source_target_pairs={{0,1},{1,0},{2,3},{3,2},{4,5},{5,4},{6,7},{7,6},{8,9},{9,8},{10,11... | collective-permute-start | bytes 147464 | tf_op jit(solution)/shard_map/ppermute | solution.py:342
  39.3 5.6 %collective-permute-start.18 = (bf16[32,768]{1,0:T(8,128)(2,1)S(1)}, bf16[32,768]{1,0:T(8,128)(2,1)S(1)}, u32[]{:S(2)}, u32[]{:S(2)}) collective-permute-start(bf16[32,768]{1,0:T(8,128)(2,1)S(1)} %get-tuple-element.54), channel_id=1, source_target_pairs={{0,24},{8,16},{16,8},{24,0},{1,25},{9,17},{17,9},{25,1},{2,26},{10... | collective-permute-start | bytes 147464 | tf_op jit(solution)/shard_map/ppermute | solution.py:337
  41.6 4.2 %collective-permute-start.19 = (bf16[32,768]{1,0:T(8,128)(2,1)S(1)}, bf16[32,768]{1,0:T(8,128)(2,1)S(1)}, u32[]{:S(2)}, u32[]{:S(2)}) collective-permute-start(bf16[32,768]{1,0:T(8,128)(2,1)S(1)} %get-tuple-element.55), channel_id=1, source_target_pairs={{0,8},{8,0},{16,24},{24,16},{1,9},{9,1},{17,25},{25,17},{2,10},{10... | collective-permute-start | bytes 147464 | tf_op jit(solution)/shard_map/ppermute | solution.py:337
  42.3 4.1 %collective-permute-start.20 = (bf16[32,768]{1,0:T(8,128)(2,1)S(1)}, bf16[32,768]{1,0:T(8,128)(2,1)S(1)}, u32[]{:S(2)}, u32[]{:S(2)}) collective-permute-start(bf16[32,768]{1,0:T(8,128)(2,1)S(1)} %get-tuple-element.56), channel_id=1, source_target_pairs={{0,16},{8,24},{16,0},{24,8},{1,17},{9,25},{17,1},{25,9},{2,18},{10... | collective-permute-start | bytes 147464 | tf_op jit(solution)/shard_map/ppermute | solution.py:337

commit v19 on v13

--- a/solution.py
+++ b/solution.py
@@ -417,7 +417,7 @@
         top = leading(s, e, chips)
         if top != s:
             gathered[s, e] = to_block(gathered[top, e], s ^ top, 0)
-    (last,) = call(after_kernel, [payload], [], [], [other2, gathered.get((chips // 2, 0), same2)], [], "after")
+    (last,) = call(after_kernel, [payload], [], [], [other2, gathered.get((chips - 1, 0), same2)], [], "after")
     gathered[0, 1] = to_block(last, 0, 1)
     gathered = [gathered[hop] for hop in arrivals(n)]
     held = F32 if rows % 16 else BF16

time: 47.8 us -> 48.5 us (1.015)
  starting transfers between devices: 25.8 us -> 26.8 us
    ppermute x15, starting transfers between devices: 18.1 us -> 19.1 us  [to_block(): lax.ppermute(x, 'blk', [(i, 2 * moved(i // 2, s, n // 2, 1) + (i % 2 ^ e)...]
  transfers between devices with their start and end apart: 21 -> 21, of which waited for: 10 -> 12; matrix products, arithmetic and copies ran while one was open for 0% -> 0% of each run, Pallas kernels for 5% -> 5%
where the time goes in v19:
time: 48.5 us; the launch traced here: 48.3 us
  starting transfers between devices  26.8 us (55%)
  waiting for transfers between devices  11.2 us (23%)
  Pallas kernels  7.74 us (16%)
  local copies, waits for them, and re-layouts  2.5 us (5%)
    ppermute x15, starting transfers between devices, to_block(): lax.ppermute(x, 'blk', [(i, 2 * moved(i // 2, s, n // 2, 1) + (i % 2 ^ e)...  19.1 us
    pallas_call x10, Pallas kernels, call(): pl.pallas_call(kernel, out_shape=outs, in_specs=[smem] * len(scalars) + [...  7.74 us
    ppermute x6, starting transfers between devices, to_list(): lax.ppermute(x, 'grp', [(i, moved(i, s, groups, 1)) for i in range(groups)])  7.68 us
    ppermute x15, waiting for transfers between devices, to_block(): lax.ppermute(x, 'blk', [(i, 2 * moved(i // 2, s, n // 2, 1) + (i % 2 ^ e)...  6.29 us
    ppermute x6, waiting for transfers between devices, to_list(): lax.ppermute(x, 'grp', [(i, moved(i, s, groups, 1)) for i in range(groups)])  4.9 us
    unnamed x10, local copies, waits for them, and re-layouts  2.5 us
  transfers between devices with their start and end apart: 21, of which 12 were waited for; matrix products, arithmetic and copies ran while one was open for 0% of the time, Pallas kernels for 5%

profile of v19, /device:TPU:0, one launch (start us, length us, event | category | flops | bytes accessed | tf_op | source)
XLA Modules:
  0.0 48.3 jit_solution(13520840626641304086)
XLA Ops:
  0.0 0.5 collective-permute-start.3
  0.5 1.9 %route.1 = (bf16[32,896]{1,0:T(8,128)(2,1)}, bf16[32,896]{1,0:T(8,128)(2,1)}, bf16[32,896]{1,0:T(8,128)(2,1)}, bf16[32,896]{1,0:T(8,128)(2,1)}) custom-call(s32[1]{0:T(128)} %bitcast.me_ref, s32[8]{0:T(128)} %target_ref.1, f32[8]{0:T(128)} %weights_ref.1, bf16[16,8,768]{2,1,0:T(8,128)(2,1)} %walkers_any.1, f32[8,12]{1,0:T(8,128)} %fields_any.1, ...), custom_call_target="tpu_custom_call" | custom-call | bytes 229376 | tf_op jit(solution)/shard_map/route/pallas_call | solution.py:311
  2.4 2.6 %collective-permute-start = (bf16[32,896]{1,0:T(8,128)(2,1)}, bf16[32,896]{1,0:T(8,128)(2,1)S(1)}, u32[]{:S(2)}, u32[]{:S(2)}) collective-permute-start(bf16[32,896]{1,0:T(8,128)(2,1)} %get-tuple-element.32), channel_id=1, source_target_pairs={{0,16},{8,24},{16,0},{24,8},{1,17},{9,25},{17,1},{25,9},{2,18},{10... | collective-permute-start | bytes 172040 | tf_op jit(solution)/shard_map/ppermute | solution.py:337
  5.0 1.4 %collective-permute-start.1 = (bf16[32,896]{1,0:T(8,128)(2,1)}, bf16[32,896]{1,0:T(8,128)(2,1)S(1)}, u32[]{:S(2)}, u32[]{:S(2)}) collective-permute-start(bf16[32,896]{1,0:T(8,128)(2,1)} %get-tuple-element.33), channel_id=1, source_target_pairs={{0,24},{8,16},{16,8},{24,0},{1,25},{9,17},{17,9},{25,1},{2,26},{10... | collective-permute-start | bytes 172040 | tf_op jit(solution)/shard_map/ppermute | solution.py:337
  6.4 0.1 collective-permute-start.2
  6.5 0.8 %copy-done.2 = bf16[32,896]{1,0:T(8,128)(2,1)S(1)} copy-done((bf16[32,896]{1,0:T(8,128)(2,1)S(1)}, bf16[32,896]{1,0:T(8,128)(2,1)}, u32[]{:S(2)}) %copy-start.2) | copy-done | bytes 57368
  7.4 0.0 copy-start
  7.4 1.7 %copy-done = bf16[12,128,768]{2,1,0:T(8,128)(2,1)S(1)} copy-done((bf16[12,128,768]{2,1,0:T(8,128)(2,1)S(1)}, bf16[12,128,768]{2,1,0:T(8,128)(2,1)}, u32[]{:S(2)}) %copy-start) | copy-done | bytes 2359320
  9.0 0.2 stage.1.when.own_ref
  9.2 0.0 copy-start.1
  9.2 0.0 collective-permute-done.refs_1_
  9.2 1.2 %collective-permute-done.1.refs_2_ = bf16[32,896]{1,0:T(8,128)(2,1)S(1)} collective-permute-done((bf16[32,896]{1,0:T(8,128)(2,1)}, bf16[32,896]{1,0:T(8,128)(2,1)S(1)}, u32[]{:S(2)}, u32[]{:S(2)}) %collective-permute-start.1) | collective-permute-done | bytes 57376 | tf_op jit(solution)/shard_map/ppermute | solution.py:337
  10.5 0.3 collective-permute-done.2.refs_3_
  10.8 0.1 merge.1
  10.9 1.5 %collective-permute-start.8 = (bf16[216,128]{1,0:T(8,128)(2,1)S(1)}, bf16[216,128]{1,0:T(8,128)(2,1)S(1)}, u32[]{:S(2)}, u32[]{:S(2)}) collective-permute-start(bf16[216,128]{1,0:T(8,128)(2,1)S(1)} %get-tuple-element.40), channel_id=1, source_target_pairs={{0,5},{1,4},{2,7},{3,6},{4,1},{5,0},{6,3},{7,2},{8,13},{9,12},{10,... | collective-permute-start | bytes 165896 | tf_op jit(solution)/shard_map/ppermute | solution.py:342
  12.4 2.3 %collective-permute-start.4 = (bf16[216,128]{1,0:T(8,128)(2,1)S(1)}, bf16[216,128]{1,0:T(8,128)(2,1)S(1)}, u32[]{:S(2)}, u32[]{:S(2)}) collective-permute-start(bf16[216,128]{1,0:T(8,128)(2,1)S(1)} %get-tuple-element.39), channel_id=1, source_target_pairs={{0,6},{1,7},{2,4},{3,5},{4,2},{5,3},{6,0},{7,1},{8,14},{9,15},{10,... | collective-permute-start | bytes 165896 | tf_op jit(solution)/shard_map/ppermute | solution.py:342
  14.7 2.1 %collective-permute-start.10 = (bf16[216,128]{1,0:T(8,128)(2,1)S(1)}, bf16[216,128]{1,0:T(8,128)(2,1)S(1)}, u32[]{:S(2)}, u32[]{:S(2)}) collective-permute-start(bf16[216,128]{1,0:T(8,128)(2,1)S(1)} %get-tuple-element.39), channel_id=1, source_target_pairs={{0,4},{1,5},{2,6},{3,7},{4,0},{5,1},{6,2},{7,3},{8,12},{9,13},{10,... | collective-permute-start | bytes 165896 | tf_op jit(solution)/shard_map/ppermute | solution.py:342
  16.8 0.0 collective-permute-done.8.refs_6_
  16.8 1.4 %collective-permute-start.6 = (bf16[216,128]{1,0:T(8,128)(2,1)S(1)}, bf16[216,128]{1,0:T(8,128)(2,1)S(1)}, u32[]{:S(2)}, u32[]{:S(2)}) collective-permute-start(bf16[216,128]{1,0:T(8,128)(2,1)S(1)} %get-tuple-element.38.source_ref), channel_id=1, source_target_pairs={{0,3},{1,2},{2,1},{3,0},{4,7},{5,6},{6,5},{7,4},{8,11},{9,10},{10,... | collective-permute-start | bytes 165896 | tf_op jit(solution)/shard_map/ppermute | solution.py:342
  18.2 0.6 %collective-permute-done.4.when_ref.refs_5_ = bf16[216,128]{1,0:T(8,128)(2,1)S(1)} collective-permute-done((bf16[216,128]{1,0:T(8,128)(2,1)S(1)}, bf16[216,128]{1,0:T(8,128)(2,1)S(1)}, u32[]{:S(2)}, u32[]{:S(2)}) %collective-permute-start.4) | collective-permute-done | bytes 55328 | tf_op jit(solution)/shard_map/ppermute | solution.py:342
  18.8 1.8 %collective-permute-start.9 = (bf16[216,128]{1,0:T(8,128)(2,1)S(1)}, bf16[216,128]{1,0:T(8,128)(2,1)S(1)}, u32[]{:S(2)}, u32[]{:S(2)}) collective-permute-start(bf16[216,128]{1,0:T(8,128)(2,1)S(1)} %collective-permute-done.8.refs_6_), channel_id=1, source_target_pairs={{0,2},{1,3},{2,0},{3,1},{4,6},{5,7},{6,4},{7,5},{8,10},{9,11},{10,... | collective-permute-start | bytes 165896 | tf_op jit(solution)/shard_map/ppermute | solution.py:342
  20.6 0.0 collective-permute-done.7.refs_3_
  20.6 0.2 collective-permute-start.5
  20.8 0.2 hold.1.body_ref
  21.1 0.0 copy-start.3
  21.1 0.0 copy-start.4
  21.1 0.4 collective-permute-done.6.refs_2_
  21.5 0.5 collective-permute-done.10.refs_7_
  21.9 1.3 %collective-permute-done.9.refs_4_ = bf16[216,128]{1,0:T(8,128)(2,1)S(1)} collective-permute-done((bf16[216,128]{1,0:T(8,128)(2,1)S(1)}, bf16[216,128]{1,0:T(8,128)(2,1)S(1)}, u32[]{:S(2)}, u32[]{:S(2)}) %collective-permute-start.9) | collective-permute-done | bytes 55328 | tf_op jit(solution)/shard_map/ppermute | solution.py:342
  23.3 0.0 collective-permute-done.5.refs_1_
  23.3 3.7 %fock.1 = (bf16[32,768]{1,0:T(8,128)(2,1)S(1)}, bf16[32,768]{1,0:T(8,128)(2,1)S(1)}, bf16[32,768]{1,0:T(8,128)(2,1)S(1)}, bf16[32,768]{1,0:T(8,128)(2,1)S(1)}, b...) custom-call(s32[1]{0:T(128)} %bitcast.1.blk_ref, ...), custom_call_target="tpu_custom_call" | custom-call | flops 2717908992 | bytes 6733824 | tf_op jit(solution)/shard_map/fock/pallas_call | solution.py:311
  27.0 1.6 %collective-permute-start.12 = (bf16[32,768]{1,0:T(8,128)(2,1)S(1)}, bf16[32,768]{1,0:T(8,128)(2,1)S(1)}, u32[]{:S(2)}, u32[]{:S(2)}) collective-permute-start(bf16[32,768]{1,0:T(8,128)(2,1)S(1)} %get-tuple-element.47), channel_id=1, source_target_pairs={{0,2},{1,3},{2,0},{3,1},{4,6},{5,7},{6,4},{7,5},{8,10},{9,11},{10,... | collective-permute-start | bytes 147464 | tf_op jit(solution)/shard_map/ppermute | solution.py:342
  28.6 3.0 %collective-permute-start.11 = (bf16[32,768]{1,0:T(8,128)(2,1)S(1)}, bf16[32,768]{1,0:T(8,128)(2,1)S(1)}, u32[]{:S(2)}, u32[]{:S(2)}) collective-permute-start(bf16[32,768]{1,0:T(8,128)(2,1)S(1)} %get-tuple-element.42), channel_id=1, source_target_pairs={{0,4},{1,5},{2,6},{3,7},{4,0},{5,1},{6,2},{7,3},{8,12},{9,13},{10,... | collective-permute-start | bytes 147464 | tf_op jit(solution)/shard_map/ppermute | solution.py:342
  31.6 0.5 %collective-permute-start.14 = (bf16[32,768]{1,0:T(8,128)(2,1)S(1)}, bf16[32,768]{1,0:T(8,128)(2,1)S(1)}, u32[]{:S(2)}, u32[]{:S(2)}) collective-permute-start(bf16[32,768]{1,0:T(8,128)(2,1)S(1)} %get-tuple-element.49), channel_id=1, source_target_pairs={{0,6},{1,7},{2,4},{3,5},{4,2},{5,3},{6,0},{7,1},{8,14},{9,15},{10,... | collective-permute-start | bytes 147464 | tf_op jit(solution)/shard_map/ppermute | solution.py:342
  32.2 0.4 collective-permute-start.13
  32.6 2.4 %collective-permute-start.15 = (bf16[32,768]{1,0:T(8,128)(2,1)S(1)}, bf16[32,768]{1,0:T(8,128)(2,1)S(1)}, u32[]{:S(2)}, u32[]{:S(2)}) collective-permute-start(bf16[32,768]{1,0:T(8,128)(2,1)S(1)} %get-tuple-element.50), channel_id=1, source_target_pairs={{0,2},{1,3},{2,0},{3,1},{4,6},{5,7},{6,4},{7,5},{8,10},{9,11},{10,... | collective-permute-start | bytes 147464 | tf_op jit(solution)/shard_map/ppermute | solution.py:342
  34.9 1.4 %collective-permute-start.16 = (bf16[32,768]{1,0:T(8,128)(2,1)S(1)}, bf16[32,768]{1,0:T(8,128)(2,1)S(1)}, u32[]{:S(2)}, u32[]{:S(2)}) collective-permute-start(bf16[32,768]{1,0:T(8,128)(2,1)S(1)} %get-tuple-element.51), channel_id=1, source_target_pairs={{0,3},{1,2},{2,1},{3,0},{4,7},{5,6},{6,5},{7,4},{8,11},{9,10},{10,... | collective-permute-start | bytes 147464 | tf_op jit(solution)/shard_map/ppermute | solution.py:342
  36.3 1.4 %collective-permute-done.14.refs_3_ = bf16[32,768]{1,0:T(8,128)(2,1)S(1)} collective-permute-done((bf16[32,768]{1,0:T(8,128)(2,1)S(1)}, bf16[32,768]{1,0:T(8,128)(2,1)S(1)}, u32[]{:S(2)}, u32[]{:S(2)}) %collective-permute-start.14) | collective-permute-done | bytes 49184 | tf_op jit(solution)/shard_map/ppermute | solution.py:342
  37.8 1.0 %collective-permute-done.13.refs_2_ = bf16[32,768]{1,0:T(8,128)(2,1)S(1)} collective-permute-done((bf16[32,768]{1,0:T(8,128)(2,1)S(1)}, bf16[32,768]{1,0:T(8,128)(2,1)S(1)}, u32[]{:S(2)}, u32[]{:S(2)}) %collective-permute-start.13) | collective-permute-done | bytes 49184 | tf_op jit(solution)/shard_map/ppermute | solution.py:342
  38.8 1.1 %collective-permute-done.16.refs_5_ = bf16[32,768]{1,0:T(8,128)(2,1)S(1)} collective-permute-done((bf16[32,768]{1,0:T(8,128)(2,1)S(1)}, bf16[32,768]{1,0:T(8,128)(2,1)S(1)}, u32[]{:S(2)}, u32[]{:S(2)}) %collective-permute-start.16) | collective-permute-done | bytes 49184 | tf_op jit(solution)/shard_map/ppermute | solution.py:342
  39.9 0.1 sum.1
  40.0 0.6 %collective-permute-start.18 = (bf16[32,768]{1,0:T(8,128)(2,1)S(1)}, bf16[32,768]{1,0:T(8,128)(2,1)S(1)}, u32[]{:S(2)}, u32[]{:S(2)}) collective-permute-start(bf16[32,768]{1,0:T(8,128)(2,1)S(1)} %get-tuple-element.54), channel_id=1, source_target_pairs={{0,16},{8,24},{16,0},{24,8},{1,17},{9,25},{17,1},{25,9},{2,18},{10... | collective-permute-start | bytes 147464 | tf_op jit(solution)/shard_map/ppermute | solution.py:337
  40.6 2.2 %collective-permute-start.19 = (bf16[32,768]{1,0:T(8,128)(2,1)S(1)}, bf16[32,768]{1,0:T(8,128)(2,1)S(1)}, u32[]{:S(2)}, u32[]{:S(2)}) collective-permute-start(bf16[32,768]{1,0:T(8,128)(2,1)S(1)} %get-tuple-element.55), channel_id=1, source_target_pairs={{0,24},{8,16},{16,8},{24,0},{1,25},{9,17},{17,9},{25,1},{2,26},{10... | collective-permute-start | bytes 147464 | tf_op jit(solution)/shard_map/ppermute | solution.py:337
  42.8 0.7 %collective-permute-start.20 = (bf16[32,768]{1,0:T(8,128)(2,1)S(1)}, bf16[32,768]{1,0:T(8,128)(2,1)S(1)}, u32[]{:S(2)}, u32[]{:S(2)}) collective-permute-start(bf16[32,768]{1,0:T(8,128)(2,1)S(1)} %get-tuple-element.56), channel_id=1, source_target_pairs={{0,8},{8,0},{16,24},{24,16},{1,9},{9,1},{17,25},{25,17},{2,10},{10... | collective-permute-start | bytes 147464 | tf_op jit(solution)/shard_map/ppermute | solution.py:337
  43.5 0.6 %collective-permute-done.18.refs_1_ = bf16[32,768]{1,0:T(8,128)(2,1)S(1)} collective-permute-done((bf16[32,768]{1,0:T(8,128)(2,1)S(1)}, bf16[32,768]{1,0:T(8,128)(2,1)S(1)}, u32[]{:S(2)}, u32[]{:S(2)}) %collective-permute-start.18) | collective-permute-done | bytes 49184 | tf_op jit(solution)/shard_map/ppermute | solution.py:337
  44.1 1.4 %collective-permute-done.19.refs_2_ = bf16[32,768]{1,0:T(8,128)(2,1)S(1)} collective-permute-done((bf16[32,768]{1,0:T(8,128)(2,1)S(1)}, bf16[32,768]{1,0:T(8,128)(2,1)S(1)}, u32[]{:S(2)}, u32[]{:S(2)}) %collective-permute-start.19) | collective-permute-done | bytes 49184 | tf_op jit(solution)/shard_map/ppermute | solution.py:337
  45.6 1.3 %collective-permute-done.20.refs_3_ = bf16[32,768]{1,0:T(8,128)(2,1)S(1)} collective-permute-done((bf16[32,768]{1,0:T(8,128)(2,1)S(1)}, bf16[32,768]{1,0:T(8,128)(2,1)S(1)}, u32[]{:S(2)}, u32[]{:S(2)}) %collective-permute-start.20) | collective-permute-done | bytes 49184 | tf_op jit(solution)/shard_map/ppermute | solution.py:337
  46.9 1.4 %deal.1 = bf16[16,8,768]{2,1,0:T(8,128)(2,1)} custom-call(s32[1]{0:T(128)} %bitcast.me_ref, s32[8]{0:T(128)S(1)} %copy-done.3, f32[8]{0:T(128)S(1)} %copy-done.4, f32[8,128]{1,0:T(8,128)S(1)} %get-tuple-element.35.refs_1_.total_ref, bf16[32,768]{1,0:T(8,128)(2,1)S(1)} %get-tuple-element.53.refs_0_, bf16[32,768]{1,0:T(8,128)(2,1)S(1)} %collective-permute-done.18.refs_1_, ...), custom_call_target="tpu_custom_call" | custom-call | bytes 397312 | tf_op jit(solution)/shard_map/deal/pallas_call | solution.py:311
  (14 shorter events, 0.1 us)
Async XLA Ops:
  0.0 23.3 %collective-permute-start.3 = (bf16[12,128,768]{2,1,0:T(8,128)(2,1)}, bf16[12,128,768]{2,1,0:T(8,128)(2,1)S(1)}, u32[]{:S(2)}, u32[]{:S(2)}) collective-permute-start(bf16[12,128,768]{2,1,0:T(8,128)(2,1)} %refs_0_.2), channel_id=1, source_target_pairs={{0,1},{1,0},{2,3},{3,2},{4,5},{5,4},{6,7},{7,6},{8,9},{9,8},{10,11... | collective-permute-start | bytes 7077896 | tf_op jit(solution)/shard_map/ppermute | solution.py:342
  2.4 6.9 %collective-permute-start = (bf16[32,896]{1,0:T(8,128)(2,1)}, bf16[32,896]{1,0:T(8,128)(2,1)S(1)}, u32[]{:S(2)}, u32[]{:S(2)}) collective-permute-start(bf16[32,896]{1,0:T(8,128)(2,1)} %get-tuple-element.32), channel_id=1, source_target_pairs={{0,16},{8,24},{16,0},{24,8},{1,17},{9,25},{17,1},{25,9},{2,18},{10... | collective-permute-start | bytes 172040 | tf_op jit(solution)/shard_map/ppermute | solution.py:337
  5.0 5.5 %collective-permute-start.1 = (bf16[32,896]{1,0:T(8,128)(2,1)}, bf16[32,896]{1,0:T(8,128)(2,1)S(1)}, u32[]{:S(2)}, u32[]{:S(2)}) collective-permute-start(bf16[32,896]{1,0:T(8,128)(2,1)} %get-tuple-element.33), channel_id=1, source_target_pairs={{0,24},{8,16},{16,8},{24,0},{1,25},{9,17},{17,9},{25,1},{2,26},{10... | collective-permute-start | bytes 172040 | tf_op jit(solution)/shard_map/ppermute | solution.py:337
  6.4 4.4 %collective-permute-start.2 = (bf16[32,896]{1,0:T(8,128)(2,1)}, bf16[32,896]{1,0:T(8,128)(2,1)S(1)}, u32[]{:S(2)}, u32[]{:S(2)}) collective-permute-start(bf16[32,896]{1,0:T(8,128)(2,1)} %get-tuple-element.34), channel_id=1, source_target_pairs={{0,8},{8,0},{16,24},{24,16},{1,9},{9,1},{17,25},{25,17},{2,10},{10... | collective-permute-start | bytes 172040 | tf_op jit(solution)/shard_map/ppermute | solution.py:337
  6.5 0.8 %copy-start.2 = (bf16[32,896]{1,0:T(8,128)(2,1)S(1)}, bf16[32,896]{1,0:T(8,128)(2,1)}, u32[]{:S(2)}) copy-start(bf16[32,896]{1,0:T(8,128)(2,1)} %get-tuple-element.31.refs_0_) | copy-start | bytes 172036
  7.4 1.7 %copy-start = (bf16[12,128,768]{2,1,0:T(8,128)(2,1)S(1)}, bf16[12,128,768]{2,1,0:T(8,128)(2,1)}, u32[]{:S(2)}) copy-start(bf16[12,128,768]{2,1,0:T(8,128)(2,1)} %refs_0_.2) | copy-start | bytes 7077892
  9.2 11.6 %copy-start.1 = (bf16[768,768]{1,0:T(8,128)(2,1)S(1)}, bf16[768,768]{1,0:T(8,128)(2,1)}, u32[]{:S(2)}) copy-start(bf16[768,768]{1,0:T(8,128)(2,1)} %refs_0_.3) | copy-start | bytes 3538948
  10.9 5.9 %collective-permute-start.8 = (bf16[216,128]{1,0:T(8,128)(2,1)S(1)}, bf16[216,128]{1,0:T(8,128)(2,1)S(1)}, u32[]{:S(2)}, u32[]{:S(2)}) collective-permute-start(bf16[216,128]{1,0:T(8,128)(2,1)S(1)} %get-tuple-element.40), channel_id=1, source_target_pairs={{0,5},{1,4},{2,7},{3,6},{4,1},{5,0},{6,3},{7,2},{8,13},{9,12},{10,... | collective-permute-start | bytes 165896 | tf_op jit(solution)/shard_map/ppermute | solution.py:342
  12.4 6.4 %collective-permute-start.4 = (bf16[216,128]{1,0:T(8,128)(2,1)S(1)}, bf16[216,128]{1,0:T(8,128)(2,1)S(1)}, u32[]{:S(2)}, u32[]{:S(2)}) collective-permute-start(bf16[216,128]{1,0:T(8,128)(2,1)S(1)} %get-tuple-element.39), channel_id=1, source_target_pairs={{0,6},{1,7},{2,4},{3,5},{4,2},{5,3},{6,0},{7,1},{8,14},{9,15},{10,... | collective-permute-start | bytes 165896 | tf_op jit(solution)/shard_map/ppermute | solution.py:342
  14.7 5.9 %collective-permute-start.7 = (bf16[216,128]{1,0:T(8,128)(2,1)S(1)}, bf16[216,128]{1,0:T(8,128)(2,1)S(1)}, u32[]{:S(2)}, u32[]{:S(2)}) collective-permute-start(bf16[216,128]{1,0:T(8,128)(2,1)S(1)} %get-tuple-element.37.refs_0_), channel_id=1, source_target_pairs={{0,2},{1,3},{2,0},{3,1},{4,6},{5,7},{6,4},{7,5},{8,10},{9,11},{10,... | collective-permute-start | bytes 165896 | tf_op jit(solution)/shard_map/ppermute | solution.py:342
  14.7 7.3 %collective-permute-start.10 = (bf16[216,128]{1,0:T(8,128)(2,1)S(1)}, bf16[216,128]{1,0:T(8,128)(2,1)S(1)}, u32[]{:S(2)}, u32[]{:S(2)}) collective-permute-start(bf16[216,128]{1,0:T(8,128)(2,1)S(1)} %get-tuple-element.39), channel_id=1, source_target_pairs={{0,4},{1,5},{2,6},{3,7},{4,0},{5,1},{6,2},{7,3},{8,12},{9,13},{10,... | collective-permute-start | bytes 165896 | tf_op jit(solution)/shard_map/ppermute | solution.py:342
  16.8 4.7 %collective-permute-start.6 = (bf16[216,128]{1,0:T(8,128)(2,1)S(1)}, bf16[216,128]{1,0:T(8,128)(2,1)S(1)}, u32[]{:S(2)}, u32[]{:S(2)}) collective-permute-start(bf16[216,128]{1,0:T(8,128)(2,1)S(1)} %get-tuple-element.38.source_ref), channel_id=1, source_target_pairs={{0,3},{1,2},{2,1},{3,0},{4,7},{5,6},{6,5},{7,4},{8,11},{9,10},{10,... | collective-permute-start | bytes 165896 | tf_op jit(solution)/shard_map/ppermute | solution.py:342
  18.8 4.5 %collective-permute-start.9 = (bf16[216,128]{1,0:T(8,128)(2,1)S(1)}, bf16[216,128]{1,0:T(8,128)(2,1)S(1)}, u32[]{:S(2)}, u32[]{:S(2)}) collective-permute-start(bf16[216,128]{1,0:T(8,128)(2,1)S(1)} %collective-permute-done.8.refs_6_), channel_id=1, source_target_pairs={{0,2},{1,3},{2,0},{3,1},{4,6},{5,7},{6,4},{7,5},{8,10},{9,11},{10,... | collective-permute-start | bytes 165896 | tf_op jit(solution)/shard_map/ppermute | solution.py:342
  20.6 2.7 %collective-permute-start.5 = (bf16[216,128]{1,0:T(8,128)(2,1)S(1)}, bf16[216,128]{1,0:T(8,128)(2,1)S(1)}, u32[]{:S(2)}, u32[]{:S(2)}) collective-permute-start(bf16[216,128]{1,0:T(8,128)(2,1)S(1)} %after.1), channel_id=1, source_target_pairs={{0,1},{1,0},{2,3},{3,2},{4,5},{5,4},{6,7},{7,6},{8,9},{9,8},{10,11... | collective-permute-start | bytes 165896 | tf_op jit(solution)/shard_map/ppermute | solution.py:342
  21.1 25.8 %copy-start.3 = (s32[8]{0:T(128)S(1)}, s32[8]{0:T(128)}, u32[]{:S(2)}) copy-start(s32[8]{0:T(128)} %target_ref.1) | copy-start | bytes 100
  21.1 25.8 %copy-start.4 = (f32[8]{0:T(128)S(1)}, f32[8]{0:T(128)}, u32[]{:S(2)}) copy-start(f32[8]{0:T(128)} %weights_ref.1) | copy-start | bytes 100
  27.0 5.2 %collective-permute-start.12 = (bf16[32,768]{1,0:T(8,128)(2,1)S(1)}, bf16[32,768]{1,0:T(8,128)(2,1)S(1)}, u32[]{:S(2)}, u32[]{:S(2)}) collective-permute-start(bf16[32,768]{1,0:T(8,128)(2,1)S(1)} %get-tuple-element.47), channel_id=1, source_target_pairs={{0,2},{1,3},{2,0},{3,1},{4,6},{5,7},{6,4},{7,5},{8,10},{9,11},{10,... | collective-permute-start | bytes 147464 | tf_op jit(solution)/shard_map/ppermute | solution.py:342
  28.6 7.7 %collective-permute-start.11 = (bf16[32,768]{1,0:T(8,128)(2,1)S(1)}, bf16[32,768]{1,0:T(8,128)(2,1)S(1)}, u32[]{:S(2)}, u32[]{:S(2)}) collective-permute-start(bf16[32,768]{1,0:T(8,128)(2,1)S(1)} %get-tuple-element.42), channel_id=1, source_target_pairs={{0,4},{1,5},{2,6},{3,7},{4,0},{5,1},{6,2},{7,3},{8,12},{9,13},{10,... | collective-permute-start | bytes 147464 | tf_op jit(solution)/shard_map/ppermute | solution.py:342
  31.6 6.2 %collective-permute-start.14 = (bf16[32,768]{1,0:T(8,128)(2,1)S(1)}, bf16[32,768]{1,0:T(8,128)(2,1)S(1)}, u32[]{:S(2)}, u32[]{:S(2)}) collective-permute-start(bf16[32,768]{1,0:T(8,128)(2,1)S(1)} %get-tuple-element.49), channel_id=1, source_target_pairs={{0,6},{1,7},{2,4},{3,5},{4,2},{5,3},{6,0},{7,1},{8,14},{9,15},{10,... | collective-permute-start | bytes 147464 | tf_op jit(solution)/shard_map/ppermute | solution.py:342
  32.2 6.6 %collective-permute-start.13 = (bf16[32,768]{1,0:T(8,128)(2,1)S(1)}, bf16[32,768]{1,0:T(8,128)(2,1)S(1)}, u32[]{:S(2)}, u32[]{:S(2)}) collective-permute-start(bf16[32,768]{1,0:T(8,128)(2,1)S(1)} %get-tuple-element.48), channel_id=1, source_target_pairs={{0,5},{1,4},{2,7},{3,6},{4,1},{5,0},{6,3},{7,2},{8,13},{9,12},{10,... | collective-permute-start | bytes 147464 | tf_op jit(solution)/shard_map/ppermute | solution.py:342
  32.6 6.2 %collective-permute-start.15 = (bf16[32,768]{1,0:T(8,128)(2,1)S(1)}, bf16[32,768]{1,0:T(8,128)(2,1)S(1)}, u32[]{:S(2)}, u32[]{:S(2)}) collective-permute-start(bf16[32,768]{1,0:T(8,128)(2,1)S(1)} %get-tuple-element.50), channel_id=1, source_target_pairs={{0,2},{1,3},{2,0},{3,1},{4,6},{5,7},{6,4},{7,5},{8,10},{9,11},{10,... | collective-permute-start | bytes 147464 | tf_op jit(solution)/shard_map/ppermute | solution.py:342
  34.9 4.9 %collective-permute-start.16 = (bf16[32,768]{1,0:T(8,128)(2,1)S(1)}, bf16[32,768]{1,0:T(8,128)(2,1)S(1)}, u32[]{:S(2)}, u32[]{:S(2)}) collective-permute-start(bf16[32,768]{1,0:T(8,128)(2,1)S(1)} %get-tuple-element.51), channel_id=1, source_target_pairs={{0,3},{1,2},{2,1},{3,0},{4,7},{5,6},{6,5},{7,4},{8,11},{9,10},{10,... | collective-permute-start | bytes 147464 | tf_op jit(solution)/shard_map/ppermute | solution.py:342
  36.3 3.6 %collective-permute-start.17 = (bf16[32,768]{1,0:T(8,128)(2,1)S(1)}, bf16[32,768]{1,0:T(8,128)(2,1)S(1)}, u32[]{:S(2)}, u32[]{:S(2)}) collective-permute-start(bf16[32,768]{1,0:T(8,128)(2,1)S(1)} %get-tuple-element.52), channel_id=1, source_target_pairs={{0,1},{1,0},{2,3},{3,2},{4,5},{5,4},{6,7},{7,6},{8,9},{9,8},{10,11... | collective-permute-start | bytes 147464 | tf_op jit(solution)/shard_map/ppermute | solution.py:342
  40.0 4.2 %collective-permute-start.18 = (bf16[32,768]{1,0:T(8,128)(2,1)S(1)}, bf16[32,768]{1,0:T(8,128)(2,1)S(1)}, u32[]{:S(2)}, u32[]{:S(2)}) collective-permute-start(bf16[32,768]{1,0:T(8,128)(2,1)S(1)} %get-tuple-element.54), channel_id=1, source_target_pairs={{0,16},{8,24},{16,0},{24,8},{1,17},{9,25},{17,1},{25,9},{2,18},{10... | collective-permute-start | bytes 147464 | tf_op jit(solution)/shard_map/ppermute | solution.py:337
  40.6 5.0 %collective-permute-start.19 = (bf16[32,768]{1,0:T(8,128)(2,1)S(1)}, bf16[32,768]{1,0:T(8,128)(2,1)S(1)}, u32[]{:S(2)}, u32[]{:S(2)}) collective-permute-start(bf16[32,768]{1,0:T(8,128)(2,1)S(1)} %get-tuple-element.55), channel_id=1, source_target_pairs={{0,24},{8,16},{16,8},{24,0},{1,25},{9,17},{17,9},{25,1},{2,26},{10... | collective-permute-start | bytes 147464 | tf_op jit(solution)/shard_map/ppermute | solution.py:337
  42.8 4.1 %collective-permute-start.20 = (bf16[32,768]{1,0:T(8,128)(2,1)S(1)}, bf16[32,768]{1,0:T(8,128)(2,1)S(1)}, u32[]{:S(2)}, u32[]{:S(2)}) collective-permute-start(bf16[32,768]{1,0:T(8,128)(2,1)S(1)} %get-tuple-element.56), channel_id=1, source_target_pairs={{0,8},{8,0},{16,24},{24,16},{1,9},{9,1},{17,25},{25,17},{2,10},{10... | collective-permute-start | bytes 147464 | tf_op jit(solution)/shard_map/ppermute | solution.py:337
